TPU v7x, 128 devices: a whole 4x4x4 slice. The times are simulated.
128 devices in a mesh: dp: 4 (over z), tp: 32 (over y, x, core).
Axes of the slice: x: 4, y: 4, z: 4, core: 2. Of those that a mesh axis runs over, the one named last changes fastest.
Arguments:
- layer_input: bfloat16 [512, 7168], P(('dp', 'tp')), may hold values from -16 to 16
- query: bfloat16 [512, 64, 576], P(('dp', 'tp')), may hold values from -48 to 48
- cache: bfloat16 [512, 2048, 576], P(('dp', 'tp')), may hold values from -8 to 8
- lengths: int32 [512], P(('dp', 'tp')), may hold values from 2 to 2048, as said below
- counts: int32 [128], P(('dp', 'tp')), may hold values from 1 to 4, as said below
- value_weight: bfloat16 [64, 512, 128], P('tp'), may hold values from -0.25 to 0.25
- output_weight: bfloat16 [8192, 7168], P('tp'), may hold values from -0.0625 to 0.0625
- norm_gain: float32 [7168], replicated, may hold values from 0.1 to 1.9
- gate_weight: bfloat16 [7168, 9216], P(None, 'tp'), may hold values from -0.0625 to 0.0625
- up_weight: bfloat16 [7168, 9216], P(None, 'tp'), may hold values from -0.0625 to 0.0625
- down_weight: bfloat16 [9216, 7168], P('tp', 'dp'), may hold values from -0.0625 to 0.0625
Outputs:
- layer_output: bfloat16 [512, 7168], P(('dp', 'tp'))
Inputs may be any that keep to these rules, and one draw needn't show every extreme that they name: `counts`: one device holds 4 live slots and another one. `lengths`: on every device some live slot has 2048 valid positions.
All inputs are finite; a program needn't handle non-finite values.
Results may differ from a plain program's by a relative error of at most 0.014.
Values may be sent and summed in bfloat16 or wider, within the bound.
No kernel may reach another device: no remote copies, remote signals or barrier semaphores. Data moves between devices by JAX's collectives and lax.ppermute only.
A program may use at most 128 MiB of HBM per device.

v0:
```python
import jax
import jax.numpy as jnp
from jax import lax
from jax.sharding import PartitionSpec as P

score_scale = 1.0 / 192.0**0.5
norm_eps = 1e-06


def normalize(residual, norm_gain):
    wide = residual.astype(jnp.float32)
    square_mean = jnp.mean(wide * wide, axis=1, keepdims=True)
    return (wide * lax.rsqrt(square_mean + norm_eps) * norm_gain[None, :]).astype(jnp.bfloat16)


def on_device(
    layer_input,
    query,
    cache,
    lengths,
    counts,
    value_weight,
    output_weight,
    norm_gain,
    gate_weight,
    up_weight,
    down_weight,
):
    slot_count = layer_input.shape[0]
    latent_width = value_weight.shape[1]
    positions = jnp.arange(cache.shape[1], dtype=jnp.int32)
    visible = positions[None, None, :] < lengths[:, None, None]
    scores = (
        jnp.einsum("rhc,rtc->rht", query, cache, preferred_element_type=jnp.float32) * score_scale
    )
    scores = jnp.where(visible, scores, jnp.float32(-1e30))
    peak = jnp.max(scores, axis=2, keepdims=True)
    raised = jnp.where(visible, jnp.exp(scores - peak), jnp.float32(0.0))
    attention = (raised / jnp.sum(raised, axis=2, keepdims=True)).astype(jnp.bfloat16)
    latent = jnp.einsum(
        "rht,rta->rha", attention, cache[:, :, :latent_width], preferred_element_type=jnp.float32
    ).astype(jnp.bfloat16)
    arrived = lax.all_to_all(latent, "tp", split_axis=1, concat_axis=0, tiled=True)
    values = jnp.einsum(
        "gha,had->ghd", arrived, value_weight, preferred_element_type=jnp.float32
    ).astype(jnp.bfloat16)
    flat = values.reshape(values.shape[0], values.shape[1] * values.shape[2])
    begin = lax.axis_index("tp") * slot_count
    attended = lax.psum(jnp.dot(flat, output_weight, preferred_element_type=jnp.float32), "tp")
    every_input = lax.all_gather(layer_input, "tp", axis=0, tiled=True)
    residual_group = (every_input.astype(jnp.float32) + attended).astype(jnp.bfloat16)
    normed_group = normalize(residual_group, norm_gain)
    residual = lax.dynamic_slice_in_dim(residual_group, begin, slot_count, 0)
    gate = jnp.dot(normed_group, gate_weight, preferred_element_type=jnp.float32)
    upward = jnp.dot(normed_group, up_weight, preferred_element_type=jnp.float32)
    inner = (jax.nn.silu(gate) * upward).astype(jnp.bfloat16)
    partial_value = jnp.dot(
        inner,
        lax.all_gather(down_weight, "dp", axis=1, tiled=True),
        preferred_element_type=jnp.float32,
    )
    feed = lax.psum_scatter(
        partial_value.astype(jnp.bfloat16), "tp", scatter_dimension=0, tiled=True
    ).astype(jnp.float32)
    mixed = residual.astype(jnp.float32) + feed
    live = jnp.arange(slot_count, dtype=jnp.int32) < counts[0]
    return jnp.where(live[:, None], mixed, jnp.float32(0.0)).astype(jnp.bfloat16)


def solution(mesh):
    placed = (
        P(("dp", "tp"), None),
        P(("dp", "tp"), None, None),
        P(("dp", "tp"), None, None),
        P(("dp", "tp")),
        P(("dp", "tp")),
        P("tp", None, None),
        P("tp", None),
        P(),
        P(None, "tp"),
        P(None, "tp"),
        P("tp", "dp"),
    )
    return jax.shard_map(
        on_device, mesh=mesh, in_specs=placed, out_specs=P(("dp", "tp"), None), check_vma=False
    )
```

profile of v0, /device:TPU:1, one launch (start us, length us, event | category | flops | bytes accessed | tf_op | source)
XLA Modules:
  0.0 342.8 jit_solution(5176916486490649174)
XLA Ops:
  6.5 0.7 all-gather.6.cloned.1.call-update
  7.3 0.0 all-reduce.4.cloned.1.call-start
  7.3 0.7 iota_compare_fusion
  8.1 6.1 %fusion.26 = (f32[4,64]{1,0:T(4,128)S(1)}, f32[4,64,2048]{2,1,0:T(8,128)S(1)}) fusion(pred[4,2048]{1,0:T(4,128)(4,1)S(1)} %iota_compare_fusion, bf16[4,64,576]{2,1,0:T(8,128)(2,1)S(1)} %copy-done, bf16[4,2048,576]{1,2,0:T(8,128)(2,1)} %param.13), kind=kOutput, calls=%fused_computation.34 | convolution fusion | flops 606603264 | bytes 11838464 | tf_op jit(solution)/shard_map/sub | solution.py:38
  14.1 6.1 %fusion.10 = bf16[4,64,512]{2,1,0:T(8,128)(2,1)S(1)} fusion(bf16[4,2048,576]{1,2,0:T(8,128)(2,1)} %param.13, f32[4,64,2048]{2,1,0:T(8,128)S(1)} %get-tuple-element.8, f32[4,64]{1,0:T(4,128)S(1)} %get-tuple-element.7), kind=kOutput, calls=%fused_computation.16 | convolution fusion | flops 538050560 | bytes 10748928 | tf_op jit(solution)/shard_map/rht,rta->rha/dot_general | solution.py:40
  20.2 0.2 copy.16
  20.4 17.4 %all_to_all.18 = bf16[4,64,512]{2,0,1:T(4,128)(2,1)S(1)} all-to-all(bf16[4,64,512]{2,0,1:T(4,128)(2,1)S(1)} %copy.16), channel_id=1, replica_groups=mesh['dp'=4,'tp'=32] {'tp'}, dimensions={1} | all-to-all | bytes 524288 | tf_op jit(solution)/shard_map/all_to_all | solution.py:43
  37.8 0.1 copy.22
  37.9 0.1 all_to_all.16
  38.0 0.3 convolution_convert_fusion.1
  38.3 4.7 %fusion.27 = f32[128,7168]{1,0:T(8,128)} fusion(bf16[128,256]{0,1:T(8,128)(2,1)S(1)} %bitcast.24, bf16[256,7168]{1,0:T(8,128)(2,1)} %param.17), kind=kOutput, calls=%fused_computation.35 | convolution fusion | flops 469762048 | bytes 7405568 | tf_op jit(solution)/shard_map/dot_general | solution.py:49
  43.0 0.0 all-gather.4.cloned.1.call-start
  43.0 0.7 all-gather.4.cloned.1.call-update
  43.8 13.7 %all-gather.6.cloned.1.call-done = bf16[32,4,7168]{2,1,0:T(4,128)(2,1)} async-done(((bf16[1,4,7168]{2,1,0:T(4,128)(2,1)}), bf16[32,4,7168]{2,1,0:T(4,128)(2,1)}) %all-gather.6.cloned.1.call-update) | async-done | bytes 1835024 | tf_op jit(solution)/shard_map/all_gather | solution.py:50
  57.5 4.2 %reshape.42 = f32[128,7168]{1,0:T(8,128)} reshape(bf16[32,4,7168]{2,1,0:T(4,128)(2,1)} %all-gather.6.cloned.1.call-done) | data formatting | bytes 5505024 | tf_op jit(solution)/shard_map/convert_element_type | solution.py:51
  61.7 108.4 %all-reduce.4.cloned.1.call-done = f32[128,7168]{1,0:T(8,128)} async-done(((f32[128,7168]{1,0:T(8,128)}), f32[128,7168]{1,0:T(8,128)}) %all-reduce.4.cloned.1.call-update) | async-done | bytes 3670032 | tf_op jit(solution)/shard_map/psum | solution.py:49
  170.1 3.9 %fusion.3 = (f32[128]{0:T(128)S(1)}, bf16[128,7168]{1,0:T(8,128)(2,1)S(1)}) fusion(f32[128,7168]{1,0:T(8,128)} %reshape.42, f32[128,7168]{1,0:T(8,128)} %all-reduce.4.cloned.1.call-done), kind=kLoop, calls=%fused_computation.6 | loop fusion | flops 4587392 | bytes 9175552 | tf_op jit(solution)/shard_map/reduce_sum | solution.py:12
  174.0 0.4 copy-done.3
  174.4 1.4 fusion.17
  175.8 43.7 %all-gather.4.cloned.1.call-done = bf16[288,7168]{1,0:T(8,128)(2,1)} async-done(((bf16[288,1792]{1,0:T(8,128)(2,1)}), bf16[288,7168]{1,0:T(8,128)(2,1)}) %all-gather.4.cloned.1.call-update) | async-done | bytes 4128784 | tf_op jit(solution)/shard_map/all_gather | solution.py:59
  219.5 9.0 %convolution_convert_fusion = bf16[128,7168]{1,0:T(8,128)(2,1)} fusion(bf16[288,7168]{1,0:T(8,128)(2,1)} %all-gather.4.cloned.1.call-done, bf16[7168,288]{0,1:T(8,128)(2,1)} %param.20, bf16[128,7168]{1,0:T(8,128)(2,1)S(1)} %get-tuple-element.6, f32[7168]{0:T(1024)S(1)} %copy-done.2, f32[128]{0:T(128)S(1)} %add_rsqrt_fusion, f32[128,288]{0,1:T(8,128)S(1)} %fusion.17), kind=kOutput, calls=%fused_computation.1 | convolution fusion | flops 1061773312 | bytes 12104192 | tf_op jit(solution)/shard_map/dot_general | solution.py:57
  229.2 0.6 dynamic-slice
  230.4 104.2 %all-reduce.6.cloned.1.call-done = bf16[128,7168]{1,0:T(8,128)(2,1)} async-done(((bf16[128,7168]{1,0:T(8,128)(2,1)}), bf16[128,7168]{1,0:T(8,128)(2,1)}) %all-reduce.6.cloned.1.call-update) | async-done | bytes 1835024
  334.7 1.6 select_convert_fusion
  (15 shorter events, 0.1 us)
Async XLA Ops:
  6.5 1.5 copy-start
  6.5 51.0 %all-gather.6.cloned.1.call-start = ((), (), s32[]{:S(2)}) async-start(), calls=%async_computation.3 | async-start | bytes 1892352 | tf_op jit(solution)/shard_map/all_gather | solution.py:50
  7.3 162.8 %all-reduce.4.cloned.1.call-start = ((), (), s32[]{:S(2)}) async-start(), calls=%async_computation.1 | async-start | bytes 7340032 | tf_op jit(solution)/shard_map/psum | solution.py:49
  14.1 23.9 %copy-start.1 = (bf16[2,512,128]{2,1,0:T(8,128)(2,1)S(1)}, bf16[2,512,128]{2,1,0:T(8,128)(2,1)}, u32[]{:S(2)}) copy-start(bf16[2,512,128]{2,1,0:T(8,128)(2,1)} %param.16) | copy-start | bytes 786436
  43.0 176.5 %all-gather.4.cloned.1.call-start = ((), (), s32[]{:S(2)}) async-start(), calls=%async_computation.2 | async-start | bytes 5160960 | tf_op jit(solution)/shard_map/all_gather | solution.py:59
  43.7 290.9 %all-reduce.6.cloned.1.call-start = ((), (), s32[]{:S(2)}) async-start(), calls=%async_computation.4 | async-start | bytes 3670016
  61.7 112.3 %copy-start.2 = (f32[7168]{0:T(1024)S(1)}, f32[7168]{0:T(1024)}, u32[]{:S(2)}) copy-start(f32[7168]{0:T(1024)} %param.18) | copy-start | bytes 86020
  170.1 4.3 %copy-start.3 = (bf16[7168,288]{0,1:T(8,128)(2,1)S(1)}, bf16[7168,288]{0,1:T(8,128)(2,1)}, u32[]{:S(2)}) copy-start(bf16[7168,288]{0,1:T(8,128)(2,1)} %param.19) | copy-start | bytes 12386308
  175.8 53.4 %copy-start.4 = (u32[128]{0:T(128)S(1)}, u32[128]{0:T(128)}, u32[]{:S(2)}) copy-start(u32[128]{0:T(128)} %constant.34) | copy-start | bytes 1540
Sparse Core Ops, SparseCore 0:
  9.6 47.8 all-gather.5
  60.9 109.1 all-reduce.3
  171.8 47.7 all-gather.3
  228.6 105.9 all-reduce.5
where the time goes:
time: 343 us
  waiting for transfers between devices  271 us (79%)
  matrix products  27.5 us (8%)
  blocking collectives  17.4 us (5%)
  between operations  14.5 us (4%)
  other arithmetic  6.22 us (2%)
  local copies, waits for them, and re-layouts  5.61 us (2%)
    psum x1, waiting for transfers between devices, on_device(): lax.psum(jnp.dot(flat, output_weight, preferred_element_type=jnp.float32)...  108 us
    unnamed x5, waiting for transfers between devices  106 us
    all_gather x1, waiting for transfers between devices, on_device(): lax.all_gather(down_weight, 'dp', axis=1, tiled=True)  43.7 us
    all_to_all x1, blocking collectives, on_device(): lax.all_to_all(latent, 'tp', split_axis=1, concat_axis=0, tiled=True)  17.4 us
    all_gather x1, waiting for transfers between devices, on_device(): every_input = lax.all_gather(layer_input, 'tp', axis=0, tiled=True)  13.7 us
    dot_general x1, matrix products, on_device(): jnp.dot(inner, lax.all_gather(down_weight, 'dp', axis=1, tiled=True), pre...  8.98 us
  transfers between devices with their start and end apart: 4, of which 4 were waited for; matrix products, arithmetic and copies ran while one was open for 8% of the time, Pallas kernels for 0%

commit v1 on v0

v1 whole, which is shorter than its diff:
```python
import jax
import jax.numpy as jnp
from jax import lax
from jax.sharding import PartitionSpec as P

score_scale = 1.0 / 192.0**0.5
norm_eps = 1e-06


def core_swap(x, width):
    return lax.ppermute(x, "tp", [(i, i ^ 1) for i in range(width)])


def between_chips(x, width):
    groups = [[2 * chip + core for chip in range(width // 2)] for core in range(2)]
    return lax.all_to_all(x, "tp", 0, 0, tiled=True, axis_index_groups=groups)


def attend(query, cache, lengths, latent_width):
    positions = jnp.arange(cache.shape[1], dtype=jnp.int32)
    visible = positions[None, None, :] < lengths[:, None, None]
    scores = (
        jnp.einsum("rhc,rtc->rht", query, cache, preferred_element_type=jnp.float32) * score_scale
    )
    scores = jnp.where(visible, scores, jnp.float32(-1e30))
    peak = jnp.max(scores, axis=2, keepdims=True)
    raised = jnp.where(visible, jnp.exp(scores - peak), jnp.float32(0.0))
    attention = (raised / jnp.sum(raised, axis=2, keepdims=True)).astype(jnp.bfloat16)
    return jnp.einsum(
        "rht,rta->rha", attention, cache[:, :, :latent_width], preferred_element_type=jnp.float32
    ).astype(jnp.bfloat16)


def on_device(
    layer_input,
    query,
    cache,
    lengths,
    counts,
    value_weight,
    output_weight,
    norm_gain,
    gate_weight,
    up_weight,
    down_weight,
    width,
):
    slots, model = layer_input.shape
    half = model // 2
    chips = width // 2
    heads_here, latent_width, head = value_weight.shape
    heads = 2 * heads_here
    chip_slots = 2 * slots
    rows = chips * chip_slots
    core = lax.axis_index("tp") % 2
    upper = core == 1

    down_parts = lax.all_gather(down_weight, "dp", axis=0, tiled=False)
    value_other = core_swap(value_weight, width)
    output_mine = lax.dynamic_slice_in_dim(output_weight, core * half, half, 1)
    output_other = core_swap(
        lax.dynamic_slice_in_dim(output_weight, (1 - core) * half, half, 1), width
    )
    input_mine = lax.dynamic_slice_in_dim(layer_input, core * half, half, 1)
    input_other = core_swap(
        lax.dynamic_slice_in_dim(layer_input, (1 - core) * half, half, 1), width
    )

    latent = attend(query, cache, lengths, latent_width)
    leaving = latent.reshape(slots, chips, heads, latent_width).transpose(1, 2, 0, 3)
    arrived = between_chips(leaving, width)
    arrived_other = core_swap(arrived, width)

    lower_heads = jnp.stack(
        [
            jnp.where(upper, arrived[:, heads_here:], arrived[:, :heads_here]),
            jnp.where(upper, arrived_other[:, heads_here:], arrived_other[:, :heads_here]),
        ],
        axis=1,
    )
    upper_heads = jnp.stack(
        [
            jnp.where(upper, arrived[:, :heads_here], arrived[:, heads_here:]),
            jnp.where(upper, arrived_other[:, :heads_here], arrived_other[:, heads_here:]),
        ],
        axis=1,
    )

    def project(part, weight):
        out = jnp.einsum("pohra,had->porhd", part, weight, preferred_element_type=jnp.float32)
        return out.astype(jnp.bfloat16).reshape(rows, heads_here * head)

    values_mine = project(lower_heads, value_weight)
    values_other = project(upper_heads, value_other)
    attended_part = jnp.dot(
        values_mine, output_mine, preferred_element_type=jnp.float32
    ) + jnp.dot(values_other, output_other, preferred_element_type=jnp.float32)
    attended_part = attended_part.astype(jnp.bfloat16).reshape(chips, chip_slots, half)
    attended = jnp.sum(between_chips(attended_part, width).astype(jnp.float32), axis=0)
    residual_mine = (input_mine.astype(jnp.float32) + attended[:slots]).astype(jnp.bfloat16)
    residual_other = (input_other.astype(jnp.float32) + attended[slots:]).astype(jnp.bfloat16)
    residual = jnp.where(
        upper,
        jnp.concatenate([residual_other, residual_mine], axis=0),
        jnp.concatenate([residual_mine, residual_other], axis=0),
    )

    gathered = between_chips(
        jnp.broadcast_to(residual[None], (chips, chip_slots, half)), width
    ).reshape(rows, half)
    gathered_other = core_swap(gathered, width)
    wide_mine = gathered.astype(jnp.float32)
    wide_other = gathered_other.astype(jnp.float32)
    square_mean = (
        jnp.sum(wide_mine * wide_mine, axis=1, keepdims=True)
        + jnp.sum(wide_other * wide_other, axis=1, keepdims=True)
    ) / model
    scale = lax.rsqrt(square_mean + norm_eps)
    wide = jnp.concatenate(
        [
            jnp.where(upper, wide_other, wide_mine),
            jnp.where(upper, wide_mine, wide_other),
        ],
        axis=1,
    )
    normed = (wide * scale * norm_gain[None, :]).astype(jnp.bfloat16)
    gate = jnp.dot(normed, gate_weight, preferred_element_type=jnp.float32)
    upward = jnp.dot(normed, up_weight, preferred_element_type=jnp.float32)
    inner = (jax.nn.silu(gate) * upward).astype(jnp.bfloat16)
    inner_other = core_swap(inner, width)

    cut = down_parts.shape[0] // 2
    down_mine = lax.dynamic_slice_in_dim(down_parts, core * cut, cut, 0)
    down_other = core_swap(
        lax.dynamic_slice_in_dim(down_parts, (1 - core) * cut, cut, 0), width
    )
    feed_part = jnp.concatenate(
        [
            jnp.dot(inner, down_mine[s], preferred_element_type=jnp.float32)
            + jnp.dot(inner_other, down_other[s], preferred_element_type=jnp.float32)
            for s in range(cut)
        ],
        axis=1,
    )
    feed_part = feed_part.astype(jnp.bfloat16).reshape(chips, chip_slots, half)
    feed = jnp.sum(between_chips(feed_part, width).astype(jnp.float32), axis=0)
    mixed = (residual.astype(jnp.float32) + feed).astype(jnp.bfloat16)
    kept = lax.dynamic_slice_in_dim(mixed, core * slots, slots, 0)
    got = core_swap(lax.dynamic_slice_in_dim(mixed, (1 - core) * slots, slots, 0), width)
    out = jnp.where(
        upper,
        jnp.concatenate([got, kept], axis=1),
        jnp.concatenate([kept, got], axis=1),
    )
    live = jnp.arange(slots, dtype=jnp.int32) < counts[0]
    return jnp.where(live[:, None], out, jnp.bfloat16(0.0))


def solution(mesh):
    placed = (
        P(("dp", "tp"), None),
        P(("dp", "tp"), None, None),
        P(("dp", "tp"), None, None),
        P(("dp", "tp")),
        P(("dp", "tp")),
        P("tp", None, None),
        P("tp", None),
        P(),
        P(None, "tp"),
        P(None, "tp"),
        P("tp", "dp"),
    )
    width = mesh.shape["tp"]
    return jax.shard_map(
        lambda *args: on_device(*args, width),
        mesh=mesh,
        in_specs=placed,
        out_specs=P(("dp", "tp"), None),
        check_vma=False,
    )
```

time: 343 us -> 129 us (0.38)
  waiting for transfers between devices: 271 us -> 31.4 us
  blocking collectives: 17.4 us -> 33.9 us
  starting transfers between devices: 0.12 us -> 14.5 us
  matrix products: 27.5 us -> 21.9 us
    psum x1 -> x0, waiting for transfers between devices: 108 us -> none  [on_device(): lax.psum(jnp.dot(flat, output_weight, preferred_element_type=jnp.float32)...]
    unnamed x5 -> x1, waiting for transfers between devices: 106 us -> 0.02 us
    all_gather x2 -> x1, waiting for transfers between devices: 57.5 us -> 0.01 us  [on_device(): down_parts = lax.all_gather(down_weight, 'dp', axis=0, tiled=False)]
    all_to_all x0 -> x2, waiting for transfers between devices: none -> 29.1 us  [between_chips(): return lax.all_to_all(x, 'tp', 0, 0, tiled=True, axis_index_groups=groups)]
    all_to_all x1 -> x2, blocking collectives: 17.4 us -> 33.9 us  [between_chips(): return lax.all_to_all(x, 'tp', 0, 0, tiled=True, axis_index_groups=groups)]
    all_to_all x0 -> x2, starting transfers between devices: none -> 7.27 us  [between_chips(): return lax.all_to_all(x, 'tp', 0, 0, tiled=True, axis_index_groups=groups)]
    ppermute x0 -> x8, starting transfers between devices: none -> 7.19 us  [core_swap(): return lax.ppermute(x, 'tp', [(i, i ^ 1) for i in range(width)])]
    dynamic_slice x0 -> x4, local copies, waits for them, and re-layouts: none -> 5.98 us  [the longest x1 3.02 us: on_device(): lax.dynamic_slice_in_dim(down_parts, (1 - core) * cut, cut, 0)]
  transfers between devices with their start and end apart: 4 -> 11, of which waited for: 4 -> 5; matrix products, arithmetic and copies ran while one was open for 8% -> 21% of each run, Pallas kernels for 0% -> 0%
where the time goes in v1:
time: 129 us
  blocking collectives  33.9 us (26%)
  waiting for transfers between devices  31.4 us (24%)
  matrix products  21.9 us (17%)
  starting transfers between devices  14.5 us (11%)
  between operations  14.3 us (11%)
  local copies, waits for them, and re-layouts  8.22 us (6%)
  other arithmetic  4.36 us (3%)
    all_to_all x2, blocking collectives, between_chips(): return lax.all_to_all(x, 'tp', 0, 0, tiled=True, axis_index_groups=groups)  33.9 us
    all_to_all x2, waiting for transfers between devices, between_chips(): return lax.all_to_all(x, 'tp', 0, 0, tiled=True, axis_index_groups=groups)  29.1 us
    all_to_all x2, starting transfers between devices, between_chips(): return lax.all_to_all(x, 'tp', 0, 0, tiled=True, axis_index_groups=groups)  7.27 us
    ppermute x8, starting transfers between devices, core_swap(): return lax.ppermute(x, 'tp', [(i, i ^ 1) for i in range(width)])  7.19 us
    dot_general x1, matrix products, attend(): jnp.einsum('rht,rta->rha', attention, cache[:, :, :latent_width], preferr...  6.11 us
    sub x1, matrix products, attend(): raised = jnp.where(visible, jnp.exp(scores - peak), jnp.float32(0.0))  6.06 us
    dynamic_slice x1, local copies, waits for them, and re-layouts, on_device(): lax.dynamic_slice_in_dim(down_parts, (1 - core) * cut, cut, 0)  3.02 us
    dot_general x1, matrix products, on_device(): jnp.dot(values_other, output_other, preferred_element_type=jnp.float32)  2.91 us
  transfers between devices with their start and end apart: 11, of which 5 were waited for; matrix products, arithmetic and copies ran while one was open for 21% of the time, Pallas kernels for 0%

profile of v1, /device:TPU:1, one launch (start us, length us, event | category | flops | bytes accessed | tf_op | source)
XLA Modules:
  0.0 128.6 jit_solution(2292338110702188146)
XLA Ops:
  6.5 2.9 %constant_dynamic-slice_fusion.3 = bf16[256,3584]{1,0:T(8,128)(2,1)} fusion(bf16[256,7168]{1,0:T(8,128)(2,1)} %param.17, s32[]{:T(128)S(6)} %select_n.93), kind=kLoop, calls=%fused_computation.73 | loop fusion | bytes 3670020 | tf_op jit(solution)/shard_map/dynamic_slice | solution.py:62
  9.4 1.4 %collective-permute-start.3 = (bf16[256,3584]{1,0:T(8,128)(2,1)}, bf16[256,3584]{1,0:T(8,128)(2,1)}, u32[]{:S(2)}, u32[]{:S(2)}) collective-permute-start(bf16[256,3584]{1,0:T(8,128)(2,1)} %constant_dynamic-slice_fusion.3), channel_id=1, source_target_pairs={{0,1},{1,0},{2,3},{3,2},{4,5},{5,4},{6,7},{7,6},{8,9},{9,8},{10,11... | collective-permute-start | bytes 5505032 | tf_op jit(solution)/shard_map/ppermute | solution.py:11
  11.0 6.1 %fusion.49 = (f32[4,64]{1,0:T(4,128)S(1)}, f32[4,64,2048]{2,1,0:T(8,128)S(1)}) fusion(pred[4,2048]{1,0:T(4,128)(4,1)S(1)} %iota_compare_fusion, bf16[4,64,576]{2,1,0:T(8,128)(2,1)S(1)} %copy-done, bf16[4,2048,576]{1,2,0:T(8,128)(2,1)} %param.13), kind=kOutput, calls=%fused_computation.81 | convolution fusion | flops 606603264 | bytes 11838464 | tf_op jit(solution)/shard_map/sub | solution.py:27
  17.1 6.1 %fusion.18 = bf16[4,64,512]{2,1,0:T(8,128)(2,1)S(1)} fusion(bf16[4,2048,576]{1,2,0:T(8,128)(2,1)} %param.13, f32[4,64,2048]{2,1,0:T(8,128)S(1)} %get-tuple-element.17, f32[4,64]{1,0:T(4,128)S(1)} %get-tuple-element.16), kind=kOutput, calls=%fused_computation.30 | convolution fusion | flops 538050560 | bytes 10748928 | tf_op jit(solution)/shard_map/rht,rta->rha/dot_general | solution.py:29
  23.4 15.2 %all_to_all.20 = bf16[16,4,4,512]{3,2,1,0:T(4,128)(2,1)S(1)} all-to-all(bf16[16,4,4,512]{3,2,1,0:T(4,128)(2,1)S(1)} %bitcast.74), channel_id=1, replica_groups={{0,2,4,6,8,10,12,14,16,18,20,22,24,26,28,30},{1,3,5,7,9,11,13,15,17,19,..., dimensions={0} | all-to-all | bytes 524288 | tf_op jit(solution)/shard_map/all_to_all | solution.py:16
  38.7 1.2 collective-permute-start.1
  40.0 1.0 collective-permute-done.1
  42.0 1.9 %fusion.16 = f32[128,3584]{1,0:T(8,128)S(1)} fusion(bf16[256,7168]{1,0:T(8,128)(2,1)} %param.17, s32[]{:T(128)S(6)} %select_n.99, bf16[16,8,2,128]{3,2,1,0:T(2,128)(2,1)S(1)} %bitcast.76), kind=kOutput, calls=%fused_computation.28 | convolution fusion | flops 234881024 | bytes 3735556 | tf_op jit(solution)/shard_map/dot_general | solution.py:95
  44.0 2.9 %fusion.4 = bf16[16,8,3584]{2,1,0:T(8,128)(2,1)} fusion(f32[128,3584]{1,0:T(8,128)S(1)} %fusion.16, bf16[256,3584]{1,0:T(8,128)(2,1)} %collective-permute-done.3, bf16[16,8,2,128]{3,2,1,0:T(2,128)(2,1)S(1)} %bitcast.75), kind=kOutput, calls=%fused_computation.5 | convolution fusion | flops 235798528 | bytes 4653056 | tf_op jit(solution)/shard_map/dot_general | solution.py:97
  46.9 3.6 %all-to-all-start.1 = ((bf16[16,8,3584]{2,1,0:T(8,128)(2,1)}), bf16[16,8,3584]{2,1,0:T(8,128)(2,1)S(1)}, u32[]{:S(2)}, u32[]{:S(2)}) async-start(bf16[16,8,3584]{2,1,0:T(8,128)(2,1)} %fusion.4), calls=%async_computation.1 | async-start | bytes 1835008 | tf_op jit(solution)/shard_map/all_to_all | solution.py:16
  51.0 14.8 %all-to-all-done.1 = bf16[16,8,3584]{2,1,0:T(8,128)(2,1)S(1)} async-done(((bf16[16,8,3584]{2,1,0:T(8,128)(2,1)}), bf16[16,8,3584]{2,1,0:T(8,128)(2,1)S(1)}, u32[]{:S(2)}, u32[]{:S(2)}) %all-to-all-start.1) | async-done | bytes 917536 | tf_op jit(solution)/shard_map/all_to_all | solution.py:16
  66.1 18.8 %all_to_all.21 = bf16[16,8,3584]{2,1,0:T(8,128)(2,1)S(1)} all-to-all(bf16[16,8,3584]{2,1,0:T(8,128)(2,1)S(1)} %broadcast_in_dim.48), channel_id=1, replica_groups={{0,2,4,6,8,10,12,14,16,18,20,22,24,26,28,30},{1,3,5,7,9,11,13,15,17,19,..., dimensions={0} | all-to-all | bytes 1835008 | tf_op jit(solution)/shard_map/all_to_all | solution.py:16
  84.9 1.7 %collective-permute-start.4 = (bf16[128,3584]{1,0:T(8,128)(2,1)S(1)}, bf16[128,3584]{1,0:T(8,128)(2,1)}, u32[]{:S(2)}, u32[]{:S(2)}) collective-permute-start(bf16[128,3584]{1,0:T(8,128)(2,1)S(1)} %bitcast.70), channel_id=1, source_target_pairs={{0,1},{1,0},{2,3},{3,2},{4,5},{5,4},{6,7},{7,6},{8,9},{9,8},{10,11... | collective-permute-start | bytes 2752520 | tf_op jit(solution)/shard_map/ppermute | solution.py:11
  86.6 3.0 %constant_dynamic-slice_fusion.2 = bf16[2,288,1792]{2,1,0:T(8,128)(2,1)} fusion(bf16[4,288,1792]{2,1,0:T(8,128)(2,1)} %bitcast.71, s32[]{:T(128)S(6)} %select_n.107), kind=kLoop, calls=%fused_computation.71 | loop fusion | bytes 4128772 | tf_op jit(solution)/shard_map/dynamic_slice | solution.py:135
  90.0 1.9 %convert_select_fusion.1 = (f32[128,3584]{1,0:T(8,128)S(1)}, f32[128,3584]{1,0:T(8,128)S(1)}, f32[128]{0:T(128)S(1)}) fusion(bf16[128,3584]{1,0:T(8,128)(2,1)} %collective-permute-done.4, pred[]{:T(512)S(6)} %eq.5, bf16[16,8,3584]{2,1,0:T(8,128)(2,1)S(1)} %all_to_all.21), kind=kLoop, calls=%fused_computation.12 | loop fusion | flops 2752384 | bytes 5505537 | tf_op jit(solution)/shard_map/jit(_where)/select_n | solution.py:121
  92.4 1.3 %fusion.45 = f32[128,288]{0,1:T(8,128)S(1)} fusion(bf16[7168,288]{0,1:T(8,128)(2,1)S(1)} %copy-done.4, f32[128,3584]{1,0:T(8,128)S(1)} %get-tuple-element.6, f32[128,3584]{1,0:T(8,128)S(1)} %get-tuple-element.5, f32[7168]{0:T(1024)S(1)} %copy-done.7, f32[128]{0:T(128)S(1)} %add_rsqrt_fusion), kind=kOutput, calls=%fused_computation.80 | convolution fusion | flops 532152320 | bytes 7975424 | tf_op jit(solution)/shard_map/dot_general | solution.py:127
  93.7 0.9 copy-done.5
  94.6 1.4 %multiply_convert_fusion = bf16[128,288]{0,1:T(8,128)(2,1)S(1)} fusion(f32[128,288]{0,1:T(8,128)S(1)} %fusion.45, bf16[7168,288]{0,1:T(8,128)(2,1)S(1)} %copy-done.5, f32[128,3584]{1,0:T(8,128)S(1)} %get-tuple-element.6, f32[128,3584]{1,0:T(8,128)S(1)} %get-tuple-element.5, f32[7168]{0:T(1024)S(1)} %copy-done.7, f32[128]{0:T(128)S(1)} %add_rsqrt_fusion), kind=kOutput, calls=%fused_computation.50 | convolution fusion | flops 532373504 | bytes 8049152 | tf_op jit(solution)/shard_map/dot_general | solution.py:128
  98.5 1.0 pad_maximum_fusion
  99.5 3.6 %all-to-all-start.3 = ((bf16[16,8,3584]{2,1,0:T(8,128)(2,1)}), bf16[16,8,3584]{2,1,0:T(8,128)(2,1)S(1)}, u32[]{:S(2)}, u32[]{:S(2)}) async-start(bf16[16,8,3584]{2,1,0:T(8,128)(2,1)} %pad_maximum_fusion), calls=%async_computation.3 | async-start | bytes 1835008 | tf_op jit(solution)/shard_map/all_to_all | solution.py:16
  103.8 14.4 %all-to-all-done.3 = bf16[16,8,3584]{2,1,0:T(8,128)(2,1)S(1)} async-done(((bf16[16,8,3584]{2,1,0:T(8,128)(2,1)}), bf16[16,8,3584]{2,1,0:T(8,128)(2,1)S(1)}, u32[]{:S(2)}, u32[]{:S(2)}) %all-to-all-start.3) | async-done | bytes 917536 | tf_op jit(solution)/shard_map/all_to_all | solution.py:16
  118.4 1.8 %collective-permute-start.7 = (bf16[4,3584]{1,0:T(4,128)(2,1)S(1)}, bf16[4,3584]{1,0:T(4,128)(2,1)S(1)}, u32[]{:S(2)}, u32[]{:S(2)}) collective-permute-start(bf16[4,3584]{1,0:T(4,128)(2,1)S(1)} %get-tuple-element.14), channel_id=1, source_target_pairs={{0,1},{1,0},{2,3},{3,2},{4,5},{5,4},{6,7},{7,6},{8,9},{9,8},{10,11... | collective-permute-start | bytes 86024 | tf_op jit(solution)/shard_map/ppermute | solution.py:11
  120.2 0.8 collective-permute-done.7
  121.0 0.7 fusion.38
  (53 shorter events, 5.9 us)
Async XLA Ops:
  6.5 4.4 %copy-start = (bf16[4,64,576]{2,1,0:T(8,128)(2,1)S(1)}, bf16[4,64,576]{2,1,0:T(8,128)(2,1)}, u32[]{:S(2)}) copy-start(bf16[4,64,576]{2,1,0:T(8,128)(2,1)} %param.12) | copy-start | bytes 884740
  6.5 80.0 %all-gather.3.cloned.1.call-start = ((), (), s32[]{:S(2)}) async-start(), calls=%async_computation.4 | async-start | bytes 5160960 | tf_op jit(solution)/shard_map/all_gather | solution.py:58
  6.5 4.3 %copy-start.3 = (s32[4]{0:T(128)S(1)}, s32[4]{0:T(128)}, u32[]{:S(2)}) copy-start(s32[4]{0:T(128)} %param.14) | copy-start | bytes 52
  9.4 34.6 %collective-permute-start.3 = (bf16[256,3584]{1,0:T(8,128)(2,1)}, bf16[256,3584]{1,0:T(8,128)(2,1)}, u32[]{:S(2)}, u32[]{:S(2)}) collective-permute-start(bf16[256,3584]{1,0:T(8,128)(2,1)} %constant_dynamic-slice_fusion.3), channel_id=1, source_target_pairs={{0,1},{1,0},{2,3},{3,2},{4,5},{5,4},{6,7},{7,6},{8,9},{9,8},{10,11... | collective-permute-start | bytes 5505032 | tf_op jit(solution)/shard_map/ppermute | solution.py:11
  17.1 22.8 %copy-start.6 = (bf16[2,512,128]{2,1,0:T(8,128)(2,1)S(1)}, bf16[2,512,128]{2,1,0:T(8,128)(2,1)}, u32[]{:S(2)}) copy-start(bf16[2,512,128]{2,1,0:T(8,128)(2,1)} %param.16) | copy-start | bytes 786436
  38.7 2.3 %collective-permute-start.1 = (bf16[16,4,4,512]{3,0,2,1:T(8,128)(2,1)S(1)}, bf16[16,4,4,512]{3,0,2,1:T(8,128)(2,1)S(1)}, u32[]{:S(2)}, u32[]{:S(2)}) collective-permute-start(bf16[16,4,4,512]{3,0,2,1:T(8,128)(2,1)S(1)} %copy.33), channel_id=1, source_target_pairs={{0,1},{1,0},{2,3},{3,2},{4,5},{5,4},{6,7},{7,6},{8,9},{9,8},{10,11... | collective-permute-start | bytes 786440 | tf_op jit(solution)/shard_map/ppermute | solution.py:11
  39.9 1.5 %collective-permute-start.2 = (bf16[2,512,128]{2,1,0:T(8,128)(2,1)S(1)}, bf16[2,512,128]{2,1,0:T(8,128)(2,1)S(1)}, u32[]{:S(2)}, u32[]{:S(2)}) collective-permute-start(bf16[2,512,128]{2,1,0:T(8,128)(2,1)S(1)} %copy-done.6), channel_id=1, source_target_pairs={{0,1},{1,0},{2,3},{3,2},{4,5},{5,4},{6,7},{7,6},{8,9},{9,8},{10,11... | collective-permute-start | bytes 786440 | tf_op jit(solution)/shard_map/ppermute | solution.py:11
  44.0 6.6 %copy-start.2 = (bf16[4,7168]{1,0:T(4,128)(2,1)S(1)}, bf16[4,7168]{1,0:T(4,128)(2,1)}, u32[]{:S(2)}) copy-start(bf16[4,7168]{1,0:T(4,128)(2,1)} %param.11) | copy-start | bytes 172036
  46.9 18.9 %all-to-all-start.1 = ((bf16[16,8,3584]{2,1,0:T(8,128)(2,1)}), bf16[16,8,3584]{2,1,0:T(8,128)(2,1)S(1)}, u32[]{:S(2)}, u32[]{:S(2)}) async-start(bf16[16,8,3584]{2,1,0:T(8,128)(2,1)} %fusion.4), calls=%async_computation.1 | async-start | bytes 1835008 | tf_op jit(solution)/shard_map/all_to_all | solution.py:16
  50.6 15.3 %collective-permute-start = (bf16[4,3584]{1,0:T(4,128)(2,1)S(1)}, bf16[4,3584]{1,0:T(4,128)(2,1)S(1)}, u32[]{:S(2)}, u32[]{:S(2)}) collective-permute-start(bf16[4,3584]{1,0:T(4,128)(2,1)S(1)} %constant_dynamic-slice_fusion.4), channel_id=1, source_target_pairs={{0,1},{1,0},{2,3},{3,2},{4,5},{5,4},{6,7},{7,6},{8,9},{9,8},{10,11... | collective-permute-start | bytes 86024 | tf_op jit(solution)/shard_map/ppermute | solution.py:11
  84.9 5.1 %collective-permute-start.4 = (bf16[128,3584]{1,0:T(8,128)(2,1)S(1)}, bf16[128,3584]{1,0:T(8,128)(2,1)}, u32[]{:S(2)}, u32[]{:S(2)}) collective-permute-start(bf16[128,3584]{1,0:T(8,128)(2,1)S(1)} %bitcast.70), channel_id=1, source_target_pairs={{0,1},{1,0},{2,3},{3,2},{4,5},{5,4},{6,7},{7,6},{8,9},{9,8},{10,11... | collective-permute-start | bytes 2752520 | tf_op jit(solution)/shard_map/ppermute | solution.py:11
  89.6 8.0 %collective-permute-start.6 = (bf16[2,288,1792]{2,1,0:T(8,128)(2,1)}, bf16[2,288,1792]{2,1,0:T(8,128)(2,1)S(1)}, u32[]{:S(2)}, u32[]{:S(2)}) collective-permute-start(bf16[2,288,1792]{2,1,0:T(8,128)(2,1)} %constant_dynamic-slice_fusion.2), channel_id=1, source_target_pairs={{0,1},{1,0},{2,3},{3,2},{4,5},{5,4},{6,7},{7,6},{8,9},{9,8},{10,11... | collective-permute-start | bytes 6193160 | tf_op jit(solution)/shard_map/ppermute | solution.py:11
  90.0 2.4 %copy-start.4 = (bf16[7168,288]{0,1:T(8,128)(2,1)S(1)}, bf16[7168,288]{0,1:T(8,128)(2,1)}, u32[]{:S(2)}) copy-start(bf16[7168,288]{0,1:T(8,128)(2,1)} %param.19) | copy-start | bytes 12386308
  90.0 2.4 %copy-start.7 = (f32[7168]{0:T(1024)S(1)}, f32[7168]{0:T(1024)}, u32[]{:S(2)}) copy-start(f32[7168]{0:T(1024)} %param.18) | copy-start | bytes 86020
  92.4 2.2 %copy-start.5 = (bf16[7168,288]{0,1:T(8,128)(2,1)S(1)}, bf16[7168,288]{0,1:T(8,128)(2,1)}, u32[]{:S(2)}) copy-start(bf16[7168,288]{0,1:T(8,128)(2,1)} %param.20) | copy-start | bytes 12386308
  94.6 2.2 %copy-start.1 = (bf16[1152,1792]{1,0:T(8,128)(2,1)S(1)}, bf16[1152,1792]{1,0:T(8,128)(2,1)}, u32[]{:S(2)}) copy-start(bf16[1152,1792]{1,0:T(8,128)(2,1)} %all-gather.3.cloned.1.call-done) | copy-start | bytes 12386308
  95.9 1.7 %collective-permute-start.5 = (bf16[128,288]{0,1:T(8,128)(2,1)S(1)}, bf16[128,288]{0,1:T(8,128)(2,1)S(1)}, u32[]{:S(2)}, u32[]{:S(2)}) collective-permute-start(bf16[128,288]{0,1:T(8,128)(2,1)S(1)} %multiply_convert_fusion), channel_id=1, source_target_pairs={{0,1},{1,0},{2,3},{3,2},{4,5},{5,4},{6,7},{7,6},{8,9},{9,8},{10,11... | collective-permute-start | bytes 221192 | tf_op jit(solution)/shard_map/ppermute | solution.py:11
  99.5 18.7 %all-to-all-start.3 = ((bf16[16,8,3584]{2,1,0:T(8,128)(2,1)}), bf16[16,8,3584]{2,1,0:T(8,128)(2,1)S(1)}, u32[]{:S(2)}, u32[]{:S(2)}) async-start(bf16[16,8,3584]{2,1,0:T(8,128)(2,1)} %pad_maximum_fusion), calls=%async_computation.3 | async-start | bytes 1835008 | tf_op jit(solution)/shard_map/all_to_all | solution.py:16
  118.4 2.7 %collective-permute-start.7 = (bf16[4,3584]{1,0:T(4,128)(2,1)S(1)}, bf16[4,3584]{1,0:T(4,128)(2,1)S(1)}, u32[]{:S(2)}, u32[]{:S(2)}) collective-permute-start(bf16[4,3584]{1,0:T(4,128)(2,1)S(1)} %get-tuple-element.14), channel_id=1, source_target_pairs={{0,1},{1,0},{2,3},{3,2},{4,5},{5,4},{6,7},{7,6},{8,9},{9,8},{10,11... | collective-permute-start | bytes 86024 | tf_op jit(solution)/shard_map/ppermute | solution.py:11
Sparse Core Ops, SparseCore 0:
  11.0 49.8 all-gather.2

commit v2 on v1

v2 whole, which is shorter than its diff:
```python
import math

import jax
import jax.numpy as jnp
from jax import lax
from jax.sharding import PartitionSpec as P

score_scale = 1.0 / 192.0**0.5
norm_eps = 1e-06


def core_swap(x, width):
    return lax.ppermute(x, "tp", [(i, i ^ 1) for i in range(width)])


def between_chips(x, width):
    groups = [[2 * chip + core for chip in range(width // 2)] for core in range(2)]
    return lax.all_to_all(x, "tp", 0, 0, tiled=True, axis_index_groups=groups)


def ring(parts, axis, side, sign):
    out = [parts[0]]
    for k in range(1, side):
        pairs = []
        for y in range(side):
            for x in range(side):
                at = ((y + sign * k) % side, x) if axis == 0 else (y, (x + sign * k) % side)
                for core in range(2):
                    pairs.append(((y * side + x) * 2 + core, (at[0] * side + at[1]) * 2 + core))
        out.append(lax.ppermute(parts[k], "tp", pairs))
    return out


def down_pieces(down_weight, width):
    out = []
    for k in range(4):
        pairs = []
        for layer in range(4):
            for place in range(width):
                chip, core = divmod(place, 2)
                cut, row_core = (layer >> 1) ^ (k >> 1), (layer & 1) ^ (k & 1)
                pairs.append(((2 * core + cut) * width + 2 * chip + row_core, layer * width + place))
        out.append(lax.ppermute(down_weight, ("dp", "tp"), pairs))
    return out


def total(parts):
    wide = parts[0].astype(jnp.float32)
    for part in parts[1:]:
        wide = wide + part.astype(jnp.float32)
    return wide


def attend(query, cache, lengths, latent_width):
    positions = jnp.arange(cache.shape[1], dtype=jnp.int32)
    visible = positions[None, None, :] < lengths[:, None, None]
    scores = (
        jnp.einsum("rhc,rtc->rht", query, cache, preferred_element_type=jnp.float32) * score_scale
    )
    scores = jnp.where(visible, scores, jnp.float32(-1e30))
    peak = jnp.max(scores, axis=2, keepdims=True)
    raised = jnp.where(visible, jnp.exp(scores - peak), jnp.float32(0.0))
    attention = (raised / jnp.sum(raised, axis=2, keepdims=True)).astype(jnp.bfloat16)
    return jnp.einsum(
        "rht,rta->rha", attention, cache[:, :, :latent_width], preferred_element_type=jnp.float32
    ).astype(jnp.bfloat16)


def on_device(
    layer_input,
    query,
    cache,
    lengths,
    counts,
    value_weight,
    output_weight,
    norm_gain,
    gate_weight,
    up_weight,
    down_weight,
    width,
):
    slots, model = layer_input.shape
    half = model // 2
    chips = width // 2
    side = math.isqrt(chips)
    heads_here, latent_width, head = value_weight.shape
    heads = 2 * heads_here
    chip_slots = 2 * slots
    rows = chips * chip_slots
    line = side * chip_slots
    place = lax.axis_index("tp")
    core = place % 2
    upper = core == 1
    at_y = place // (2 * side)
    at_x = (place // 2) % side
    layer = lax.axis_index("dp")

    pieces = down_pieces(down_weight, width)
    value_other = core_swap(value_weight, width)
    output_mine = lax.dynamic_slice_in_dim(output_weight, core * half, half, 1)
    output_other = core_swap(
        lax.dynamic_slice_in_dim(output_weight, (1 - core) * half, half, 1), width
    )
    input_mine = lax.dynamic_slice_in_dim(layer_input, core * half, half, 1)
    input_other = core_swap(
        lax.dynamic_slice_in_dim(layer_input, (1 - core) * half, half, 1), width
    )
    input_chip = jnp.where(
        upper,
        jnp.concatenate([input_other, input_mine], axis=0),
        jnp.concatenate([input_mine, input_other], axis=0),
    ).astype(jnp.float32)

    latent = attend(query, cache, lengths, latent_width)
    leaving = latent.reshape(slots, chips, heads, latent_width).transpose(1, 2, 0, 3)
    arrived = between_chips(leaving, width)
    arrived_other = core_swap(arrived, width)

    first = jnp.where(upper, arrived_other, arrived)
    second = jnp.where(upper, arrived, arrived_other)
    both = jnp.stack([first, second], axis=1)
    heads_mine = jnp.where(upper, both[:, :, heads_here:], both[:, :, :heads_here])
    heads_other = jnp.where(upper, both[:, :, :heads_here], both[:, :, heads_here:])

    def project(part, weight):
        out = jnp.einsum("pohra,had->porhd", part, weight, preferred_element_type=jnp.float32)
        flat = out.astype(jnp.bfloat16).reshape(rows, heads_here * head)
        return lax.dynamic_slice_in_dim(jnp.concatenate([flat, flat]), at_y * line, rows, 0)

    values_mine = project(heads_mine, value_weight)
    values_other = project(heads_other, value_other)
    attended_part = jnp.dot(
        values_mine, output_mine, preferred_element_type=jnp.float32
    ) + jnp.dot(values_other, output_other, preferred_element_type=jnp.float32)
    attended_part = attended_part.astype(jnp.bfloat16).reshape(side, line, half)

    summed = total(ring([attended_part[k] for k in range(side)], 0, side, 1))
    own_rows = (jnp.arange(side) == at_x)[:, None, None]
    summed = summed.reshape(side, chip_slots, half) + jnp.where(own_rows, input_chip[None], 0.0)
    summed = summed.astype(jnp.bfloat16).reshape(line, half)
    residual_line = total(ring([summed] * side, 1, side, 1)).astype(jnp.bfloat16)
    residual_mine = ring([residual_line] * side, 0, side, -1)
    residual_other = [core_swap(part, width) for part in residual_mine]
    wide_mine = jnp.concatenate(residual_mine, axis=0).astype(jnp.float32)
    wide_other = jnp.concatenate(residual_other, axis=0).astype(jnp.float32)
    square_mean = (
        jnp.sum(wide_mine * wide_mine, axis=1, keepdims=True)
        + jnp.sum(wide_other * wide_other, axis=1, keepdims=True)
    ) / model
    scale = lax.rsqrt(square_mean + norm_eps)
    wide = jnp.concatenate(
        [
            jnp.where(upper, wide_other, wide_mine),
            jnp.where(upper, wide_mine, wide_other),
        ],
        axis=1,
    )
    normed = (wide * scale * norm_gain[None, :]).astype(jnp.bfloat16)
    gate = jnp.dot(normed, gate_weight, preferred_element_type=jnp.float32)
    upward = jnp.dot(normed, up_weight, preferred_element_type=jnp.float32)
    inner = (jax.nn.silu(gate) * upward).astype(jnp.bfloat16)
    inner_other = core_swap(inner, width)

    same = core == layer % 2
    inner_even = jnp.where(same, inner, inner_other)
    inner_odd = jnp.where(same, inner_other, inner)
    feed_part = jnp.concatenate(
        [
            jnp.dot(inner_even, pieces[2 * s], preferred_element_type=jnp.float32)
            + jnp.dot(inner_odd, pieces[2 * s + 1], preferred_element_type=jnp.float32)
            for s in range(2)
        ],
        axis=1,
    )
    feed_part = feed_part.astype(jnp.bfloat16).reshape(side, line, half)
    feed_line = total(ring([feed_part[k] for k in range(side)], 0, side, 1)).astype(jnp.bfloat16)
    feed = total(
        ring(
            [
                lax.dynamic_slice_in_dim(
                    feed_line, (at_x + k) % side * chip_slots, chip_slots, 0
                )
                for k in range(side)
            ],
            1,
            side,
            1,
        )
    )
    cut = half // 2
    feed = jnp.where(
        layer // 2 == 1, jnp.concatenate([feed[:, cut:], feed[:, :cut]], axis=1), feed
    )
    residual = lax.dynamic_slice_in_dim(residual_line, at_x * chip_slots, chip_slots, 0)
    mixed = (residual.astype(jnp.float32) + feed).astype(jnp.bfloat16)
    kept = lax.dynamic_slice_in_dim(mixed, core * slots, slots, 0)
    got = core_swap(lax.dynamic_slice_in_dim(mixed, (1 - core) * slots, slots, 0), width)
    out = jnp.where(
        upper,
        jnp.concatenate([got, kept], axis=1),
        jnp.concatenate([kept, got], axis=1),
    )
    live = jnp.arange(slots, dtype=jnp.int32) < counts[0]
    return jnp.where(live[:, None], out, jnp.bfloat16(0.0))


def solution(mesh):
    placed = (
        P(("dp", "tp"), None),
        P(("dp", "tp"), None, None),
        P(("dp", "tp"), None, None),
        P(("dp", "tp")),
        P(("dp", "tp")),
        P("tp", None, None),
        P("tp", None),
        P(),
        P(None, "tp"),
        P(None, "tp"),
        P("tp", "dp"),
    )
    width = mesh.shape["tp"]
    return jax.shard_map(
        lambda *args: on_device(*args, width),
        mesh=mesh,
        in_specs=placed,
        out_specs=P(("dp", "tp"), None),
        check_vma=False,
    )
```

time: 129 us -> 167 us (1.29)
  waiting for transfers between devices: 31.4 us -> 80.4 us
  starting transfers between devices: 14.5 us -> 52 us
  blocking collectives: 33.9 us -> 0 us
  between operations: 14.3 us -> 1.04 us
    ppermute x0 -> x19, waiting for transfers between devices: none -> 70.5 us  [the longest x15 42.2 us: ring(): out.append(lax.ppermute(parts[k], 'tp', pairs))]
    all_to_all x2 -> x0, blocking collectives: 33.9 us -> none  [between_chips(): return lax.all_to_all(x, 'tp', 0, 0, tiled=True, axis_index_groups=groups)]
    ppermute x0 -> x19, starting transfers between devices: none -> 28 us  [the longest x15 16.8 us: ring(): out.append(lax.ppermute(parts[k], 'tp', pairs))]
    all_to_all x2 -> x1, waiting for transfers between devices: 29.1 us -> 8.17 us  [between_chips(): return lax.all_to_all(x, 'tp', 0, 0, tiled=True, axis_index_groups=groups)]
    ppermute x8 -> x10, starting transfers between devices: 7.19 us -> 17.1 us  [core_swap(): return lax.ppermute(x, 'tp', [(i, i ^ 1) for i in range(width)])]
    dot_general x4, matrix products: 1.73 us -> 5.4 us  [the longest x2 3.31 us: on_device(): jnp.dot(inner_even, pieces[2 * s], preferred_element_type=jnp.float32)]
    dynamic_slice x1, local copies, waits for them, and re-layouts: 3.02 us -> 0.02 us  [on_device(): lax.dynamic_slice_in_dim(feed_line, (at_x + k) % side * chip_slots, chip_...]
    all_to_all x2 -> x1, starting transfers between devices: 7.27 us -> 6.84 us  [between_chips(): return lax.all_to_all(x, 'tp', 0, 0, tiled=True, axis_index_groups=groups)]
  transfers between devices with their start and end apart: 11 -> 30, of which waited for: 5 -> 17; matrix products, arithmetic and copies ran while one was open for 21% -> 15% of each run, Pallas kernels for 0% -> 0%
where the time goes in v2:
time: 167 us; the launch traced here: 166 us
  waiting for transfers between devices  80.4 us (48%)
  starting transfers between devices  52 us (31%)
  matrix products  23.1 us (14%)
  local copies, waits for them, and re-layouts  6.9 us (4%)
  other arithmetic  2.93 us (2%)
    ppermute x15, waiting for transfers between devices, ring(): out.append(lax.ppermute(parts[k], 'tp', pairs))  42.2 us
    ppermute x4, waiting for transfers between devices, down_pieces(): out.append(lax.ppermute(down_weight, ('dp', 'tp'), pairs))  28.3 us
    ppermute x10, starting transfers between devices, core_swap(): return lax.ppermute(x, 'tp', [(i, i ^ 1) for i in range(width)])  17.1 us
    ppermute x15, starting transfers between devices, ring(): out.append(lax.ppermute(parts[k], 'tp', pairs))  16.8 us
    ppermute x4, starting transfers between devices, down_pieces(): out.append(lax.ppermute(down_weight, ('dp', 'tp'), pairs))  11.2 us
    all_to_all x1, waiting for transfers between devices, between_chips(): return lax.all_to_all(x, 'tp', 0, 0, tiled=True, axis_index_groups=groups)  8.17 us
    all_to_all x1, starting transfers between devices, between_chips(): return lax.all_to_all(x, 'tp', 0, 0, tiled=True, axis_index_groups=groups)  6.84 us
    dot_general x1, matrix products, attend(): jnp.einsum('rht,rta->rha', attention, cache[:, :, :latent_width], preferr...  6.11 us
  transfers between devices with their start and end apart: 30, of which 17 were waited for; matrix products, arithmetic and copies ran while one was open for 15% of the time, Pallas kernels for 0%

profile of v2, /device:TPU:1, one launch (start us, length us, event | category | flops | bytes accessed | tf_op | source)
XLA Modules:
  0.0 166.4 jit_solution(4384988297164466223)
XLA Ops:
  0.0 2.9 %constant_dynamic-slice_fusion.6 = bf16[256,3584]{1,0:T(8,128)(2,1)} fusion(bf16[256,7168]{1,0:T(8,128)(2,1)} %param.17, s32[]{:T(128)S(6)} %select_n.179), kind=kLoop, calls=%fused_computation.90 | loop fusion | bytes 3670020 | tf_op jit(solution)/shard_map/dynamic_slice | solution.py:103
  4.4 6.1 %fusion.52 = (f32[4,64]{1,0:T(4,128)S(1)}, f32[4,64,2048]{2,1,0:T(8,128)S(1)}) fusion(pred[4,2048]{1,0:T(4,128)(4,1)S(1)} %iota_compare_fusion, bf16[4,64,576]{2,1,0:T(8,128)(2,1)S(1)} %copy-done, bf16[4,2048,576]{1,2,0:T(8,128)(2,1)} %param.13), kind=kOutput, calls=%fused_computation.102 | convolution fusion | flops 606603264 | bytes 11838464 | tf_op jit(solution)/shard_map/sub | solution.py:62
  10.5 6.1 %fusion.16 = bf16[4,64,512]{2,1,0:T(8,128)(2,1)S(1)} fusion(bf16[4,2048,576]{1,2,0:T(8,128)(2,1)} %param.13, f32[4,64,2048]{2,1,0:T(8,128)S(1)} %get-tuple-element.27, f32[4,64]{1,0:T(4,128)S(1)} %get-tuple-element.26), kind=kOutput, calls=%fused_computation.26 | convolution fusion | flops 538050560 | bytes 10748928 | tf_op jit(solution)/shard_map/rht,rta->rha/dot_general | solution.py:64
  17.5 6.8 %all-to-all-start = ((bf16[16,4,4,512]{3,2,1,0:T(4,128)(2,1)}), bf16[16,4,4,512]{3,2,1,0:T(4,128)(2,1)S(1)}, u32[]{:S(2)}, u32[]{:S(2)}) async-start(bf16[16,4,4,512]{3,2,1,0:T(4,128)(2,1)} %bitcast.2), calls=%async_computation | async-start | bytes 524288 | tf_op jit(solution)/shard_map/all_to_all | solution.py:18
  24.7 8.2 %all-to-all-done = bf16[16,4,4,512]{3,2,1,0:T(4,128)(2,1)S(1)} async-done(((bf16[16,4,4,512]{3,2,1,0:T(4,128)(2,1)}), bf16[16,4,4,512]{3,2,1,0:T(4,128)(2,1)S(1)}, u32[]{:S(2)}, u32[]{:S(2)}) %all-to-all-start) | async-done | bytes 262176 | tf_op jit(solution)/shard_map/all_to_all | solution.py:18
  37.0 2.0 %fusion.3 = bf16[128,3584]{1,0:T(8,128)(2,1)S(1)} fusion(f32[128,3584]{1,0:T(8,128)S(1)} %fusion.14, bf16[256,3584]{1,0:T(8,128)(2,1)} %collective-permute-done.2, s32[]{:T(128)S(6)} %select_n.176, bf16[128,256]{1,0:T(8,128)(2,1)S(1)} %bitcast.49), kind=kOutput, calls=%fused_computation.4 | convolution fusion | flops 235929600 | bytes 4653060 | tf_op jit(solution)/shard_map/dot_general | solution.py:135
  41.9 10.2 %collective-permute-done.3 = bf16[32,3584]{1,0:T(8,128)(2,1)S(1)} collective-permute-done((bf16[32,3584]{1,0:T(8,128)(2,1)S(1)}, bf16[32,3584]{1,0:T(8,128)(2,1)S(1)}, u32[]{:S(2)}, u32[]{:S(2)}) %collective-permute-start.3) | collective-permute-done | bytes 229408 | tf_op jit(solution)/shard_map/ppermute | solution.py:30
  55.4 5.7 %collective-permute-done.7 = bf16[32,3584]{1,0:T(8,128)(2,1)S(1)} collective-permute-done((bf16[32,3584]{1,0:T(8,128)(2,1)S(1)}, bf16[32,3584]{1,0:T(8,128)(2,1)S(1)}, u32[]{:S(2)}, u32[]{:S(2)}) %collective-permute-start.7) | collective-permute-done | bytes 229408 | tf_op jit(solution)/shard_map/ppermute | solution.py:30
  61.2 1.9 %collective-permute-done.8 = bf16[32,3584]{1,0:T(8,128)(2,1)S(1)} collective-permute-done((bf16[32,3584]{1,0:T(8,128)(2,1)S(1)}, bf16[32,3584]{1,0:T(8,128)(2,1)S(1)}, u32[]{:S(2)}, u32[]{:S(2)}) %collective-permute-start.8) | collective-permute-done | bytes 229408 | tf_op jit(solution)/shard_map/ppermute | solution.py:30
  63.1 2.4 %collective-permute-done.9 = bf16[32,3584]{1,0:T(8,128)(2,1)S(1)} collective-permute-done((bf16[32,3584]{1,0:T(8,128)(2,1)S(1)}, bf16[32,3584]{1,0:T(8,128)(2,1)S(1)}, u32[]{:S(2)}, u32[]{:S(2)}) %collective-permute-start.9) | collective-permute-done | bytes 229408 | tf_op jit(solution)/shard_map/ppermute | solution.py:30
  65.6 3.2 %collective-permute-start.11 = (bf16[32,3584]{1,0:T(8,128)(2,1)S(1)}, bf16[32,3584]{1,0:T(8,128)(2,1)S(1)}, u32[]{:S(2)}, u32[]{:S(2)}) collective-permute-start(bf16[32,3584]{1,0:T(8,128)(2,1)S(1)} %add_convert_fusion.1), channel_id=1, source_target_pairs={{0,24},{1,25},{2,26},{3,27},{4,28},{5,29},{6,30},{7,31},{8,0},{9,1... | collective-permute-start | bytes 688136 | tf_op jit(solution)/shard_map/ppermute | solution.py:30
  69.4 2.1 %collective-permute-start.10 = (bf16[32,3584]{1,0:T(8,128)(2,1)S(1)}, bf16[32,3584]{1,0:T(8,128)(2,1)S(1)}, u32[]{:S(2)}, u32[]{:S(2)}) collective-permute-start(bf16[32,3584]{1,0:T(8,128)(2,1)S(1)} %add_convert_fusion.1), channel_id=1, source_target_pairs={{0,1},{1,0},{2,3},{3,2},{4,5},{5,4},{6,7},{7,6},{8,9},{9,8},{10,11... | collective-permute-start | bytes 688136 | tf_op jit(solution)/shard_map/ppermute | solution.py:13
  71.5 6.1 %collective-permute-done.11 = bf16[32,3584]{1,0:T(8,128)(2,1)S(1)} collective-permute-done((bf16[32,3584]{1,0:T(8,128)(2,1)S(1)}, bf16[32,3584]{1,0:T(8,128)(2,1)S(1)}, u32[]{:S(2)}, u32[]{:S(2)}) %collective-permute-start.11) | collective-permute-done | bytes 229408 | tf_op jit(solution)/shard_map/ppermute | solution.py:30
  77.6 1.9 %collective-permute-start.12 = (bf16[32,3584]{1,0:T(8,128)(2,1)S(1)}, bf16[32,3584]{1,0:T(8,128)(2,1)S(1)}, u32[]{:S(2)}, u32[]{:S(2)}) collective-permute-start(bf16[32,3584]{1,0:T(8,128)(2,1)S(1)} %collective-permute-done.11), channel_id=1, source_target_pairs={{0,1},{1,0},{2,3},{3,2},{4,5},{5,4},{6,7},{7,6},{8,9},{9,8},{10,11... | collective-permute-start | bytes 688136 | tf_op jit(solution)/shard_map/ppermute | solution.py:13
  82.9 5.4 %collective-permute-start.21 = (bf16[288,1792]{1,0:T(8,128)(2,1)}, bf16[288,1792]{1,0:T(8,128)(2,1)S(1)}, u32[]{:S(2)}, u32[]{:S(2)}) collective-permute-start(bf16[288,1792]{1,0:T(8,128)(2,1)} %param.21), channel_id=1, source_target_pairs={{33,0},{97,1},{35,2},{99,3},{37,4},{101,5},{39,6},{103,7},{41,8},{... | collective-permute-start | bytes 3096584 | tf_op jit(solution)/shard_map/ppermute | solution.py:43
  90.8 3.6 %collective-permute-start.18 = (bf16[288,1792]{1,0:T(8,128)(2,1)}, bf16[288,1792]{1,0:T(8,128)(2,1)}, u32[]{:S(2)}, u32[]{:S(2)}) collective-permute-start(bf16[288,1792]{1,0:T(8,128)(2,1)} %param.21), channel_id=1, source_target_pairs={{0,0},{64,1},{2,2},{66,3},{4,4},{68,5},{6,6},{70,7},{8,8},{72,9},{... | collective-permute-start | bytes 3096584 | tf_op jit(solution)/shard_map/ppermute | solution.py:43
  100.3 6.3 %collective-permute-start.17 = (bf16[128,288]{0,1:T(8,128)(2,1)S(1)}, bf16[128,288]{0,1:T(8,128)(2,1)S(1)}, u32[]{:S(2)}, u32[]{:S(2)}) collective-permute-start(bf16[128,288]{0,1:T(8,128)(2,1)S(1)} %fusion.19), channel_id=1, source_target_pairs={{0,1},{1,0},{2,3},{3,2},{4,5},{5,4},{6,7},{7,6},{8,9},{9,8},{10,11... | collective-permute-start | bytes 221192 | tf_op jit(solution)/shard_map/ppermute | solution.py:13
  106.7 1.9 %collective-permute-done.21 = bf16[288,1792]{1,0:T(8,128)(2,1)S(1)} collective-permute-done((bf16[288,1792]{1,0:T(8,128)(2,1)}, bf16[288,1792]{1,0:T(8,128)(2,1)S(1)}, u32[]{:S(2)}, u32[]{:S(2)}) %collective-permute-start.21) | collective-permute-done | bytes 1032224 | tf_op jit(solution)/shard_map/ppermute | solution.py:43
  109.0 26.4 %collective-permute-done.19 = bf16[288,1792]{1,0:T(8,128)(2,1)} collective-permute-done((bf16[288,1792]{1,0:T(8,128)(2,1)}, bf16[288,1792]{1,0:T(8,128)(2,1)}, u32[]{:S(2)}, u32[]{:S(2)}) %collective-permute-start.19) | collective-permute-done | bytes 1032224 | tf_op jit(solution)/shard_map/ppermute | solution.py:43
  143.2 10.4 %collective-permute-done.22 = bf16[32,3584]{1,0:T(8,128)(2,1)S(1)} collective-permute-done((bf16[32,3584]{1,0:T(8,128)(2,1)S(1)}, bf16[32,3584]{1,0:T(8,128)(2,1)S(1)}, u32[]{:S(2)}, u32[]{:S(2)}) %collective-permute-start.22) | collective-permute-done | bytes 229408 | tf_op jit(solution)/shard_map/ppermute | solution.py:30
  154.8 1.8 %collective-permute-start.25 = (bf16[8,3584]{1,0:T(8,128)(2,1)S(1)}, bf16[8,3584]{1,0:T(8,128)(2,1)S(1)}, u32[]{:S(2)}, u32[]{:S(2)}) collective-permute-start(bf16[8,3584]{1,0:T(8,128)(2,1)S(1)} %get-tuple-element.17), channel_id=1, source_target_pairs={{0,2},{1,3},{2,4},{3,5},{4,6},{5,7},{6,0},{7,1},{8,10},{9,11},{10,... | collective-permute-start | bytes 172040 | tf_op jit(solution)/shard_map/ppermute | solution.py:30
  156.6 2.9 %collective-permute-start.26 = (bf16[8,3584]{1,0:T(8,128)(2,1)S(1)}, bf16[8,3584]{1,0:T(8,128)(2,1)S(1)}, u32[]{:S(2)}, u32[]{:S(2)}) collective-permute-start(bf16[8,3584]{1,0:T(8,128)(2,1)S(1)} %get-tuple-element.19), channel_id=1, source_target_pairs={{0,4},{1,5},{2,6},{3,7},{4,0},{5,1},{6,2},{7,3},{8,12},{9,13},{10,... | collective-permute-start | bytes 172040 | tf_op jit(solution)/shard_map/ppermute | solution.py:30
  160.2 1.8 %collective-permute-done.26 = bf16[8,3584]{1,0:T(8,128)(2,1)S(1)} collective-permute-done((bf16[8,3584]{1,0:T(8,128)(2,1)S(1)}, bf16[8,3584]{1,0:T(8,128)(2,1)S(1)}, u32[]{:S(2)}, u32[]{:S(2)}) %collective-permute-start.26) | collective-permute-done | bytes 57376 | tf_op jit(solution)/shard_map/ppermute | solution.py:30
  162.9 1.9 %collective-permute-start.28 = (bf16[4,3584]{1,0:T(4,128)(2,1)S(1)}, bf16[4,3584]{1,0:T(4,128)(2,1)S(1)}, u32[]{:S(2)}, u32[]{:S(2)}) collective-permute-start(bf16[4,3584]{1,0:T(4,128)(2,1)S(1)} %get-tuple-element.22), channel_id=1, source_target_pairs={{0,1},{1,0},{2,3},{3,2},{4,5},{5,4},{6,7},{7,6},{8,9},{9,8},{10,11... | collective-permute-start | bytes 86024 | tf_op jit(solution)/shard_map/ppermute | solution.py:13
  (94 shorter events, 37.4 us)
Async XLA Ops:
  2.9 34.1 %collective-permute-start.2 = (bf16[256,3584]{1,0:T(8,128)(2,1)}, bf16[256,3584]{1,0:T(8,128)(2,1)}, u32[]{:S(2)}, u32[]{:S(2)}) collective-permute-start(bf16[256,3584]{1,0:T(8,128)(2,1)} %constant_dynamic-slice_fusion.6), channel_id=1, source_target_pairs={{0,1},{1,0},{2,3},{3,2},{4,5},{5,4},{6,7},{7,6},{8,9},{9,8},{10,11... | collective-permute-start | bytes 5505032 | tf_op jit(solution)/shard_map/ppermute | solution.py:13
  17.5 15.4 %all-to-all-start = ((bf16[16,4,4,512]{3,2,1,0:T(4,128)(2,1)}), bf16[16,4,4,512]{3,2,1,0:T(4,128)(2,1)S(1)}, u32[]{:S(2)}, u32[]{:S(2)}) async-start(bf16[16,4,4,512]{3,2,1,0:T(4,128)(2,1)} %bitcast.2), calls=%async_computation | async-start | bytes 524288 | tf_op jit(solution)/shard_map/all_to_all | solution.py:18
  24.4 11.7 %collective-permute-start.1 = (bf16[2,512,128]{2,1,0:T(8,128)(2,1)S(1)}, bf16[2,512,128]{2,1,0:T(8,128)(2,1)S(1)}, u32[]{:S(2)}, u32[]{:S(2)}) collective-permute-start(bf16[2,512,128]{2,1,0:T(8,128)(2,1)S(1)} %copy-done.6), channel_id=1, source_target_pairs={{0,1},{1,0},{2,3},{3,2},{4,5},{5,4},{6,7},{7,6},{8,9},{9,8},{10,11... | collective-permute-start | bytes 786440 | tf_op jit(solution)/shard_map/ppermute | solution.py:13
  39.1 13.0 %collective-permute-start.3 = (bf16[32,3584]{1,0:T(8,128)(2,1)S(1)}, bf16[32,3584]{1,0:T(8,128)(2,1)S(1)}, u32[]{:S(2)}, u32[]{:S(2)}) collective-permute-start(bf16[32,3584]{1,0:T(8,128)(2,1)S(1)} %get-tuple-element.10), channel_id=1, source_target_pairs={{0,8},{1,9},{2,10},{3,11},{4,12},{5,13},{6,14},{7,15},{8,16},{9,17... | collective-permute-start | bytes 688136 | tf_op jit(solution)/shard_map/ppermute | solution.py:30
  39.1 12.9 %collective-permute-start.4 = (bf16[32,3584]{1,0:T(8,128)(2,1)S(1)}, bf16[32,3584]{1,0:T(8,128)(2,1)S(1)}, u32[]{:S(2)}, u32[]{:S(2)}) collective-permute-start(bf16[32,3584]{1,0:T(8,128)(2,1)S(1)} %get-tuple-element.12), channel_id=1, source_target_pairs={{0,16},{1,17},{2,18},{3,19},{4,20},{5,21},{6,22},{7,23},{8,24},{9,... | collective-permute-start | bytes 688136 | tf_op jit(solution)/shard_map/ppermute | solution.py:30
  40.9 11.6 %collective-permute-start.5 = (bf16[32,3584]{1,0:T(8,128)(2,1)S(1)}, bf16[32,3584]{1,0:T(8,128)(2,1)S(1)}, u32[]{:S(2)}, u32[]{:S(2)}) collective-permute-start(bf16[32,3584]{1,0:T(8,128)(2,1)S(1)} %get-tuple-element.11), channel_id=1, source_target_pairs={{0,24},{1,25},{2,26},{3,27},{4,28},{5,29},{6,30},{7,31},{8,0},{9,1... | collective-permute-start | bytes 688136 | tf_op jit(solution)/shard_map/ppermute | solution.py:30
  52.6 8.6 %collective-permute-start.7 = (bf16[32,3584]{1,0:T(8,128)(2,1)S(1)}, bf16[32,3584]{1,0:T(8,128)(2,1)S(1)}, u32[]{:S(2)}, u32[]{:S(2)}) collective-permute-start(bf16[32,3584]{1,0:T(8,128)(2,1)S(1)} %fusion.24), channel_id=1, source_target_pairs={{0,2},{1,3},{2,4},{3,5},{4,6},{5,7},{6,0},{7,1},{8,10},{9,11},{10,... | collective-permute-start | bytes 688136 | tf_op jit(solution)/shard_map/ppermute | solution.py:30
  53.0 10.1 %collective-permute-start.8 = (bf16[32,3584]{1,0:T(8,128)(2,1)S(1)}, bf16[32,3584]{1,0:T(8,128)(2,1)S(1)}, u32[]{:S(2)}, u32[]{:S(2)}) collective-permute-start(bf16[32,3584]{1,0:T(8,128)(2,1)S(1)} %fusion.24), channel_id=1, source_target_pairs={{0,4},{1,5},{2,6},{3,7},{4,0},{5,1},{6,2},{7,3},{8,12},{9,13},{10,... | collective-permute-start | bytes 688136 | tf_op jit(solution)/shard_map/ppermute | solution.py:30
  54.1 11.4 %collective-permute-start.9 = (bf16[32,3584]{1,0:T(8,128)(2,1)S(1)}, bf16[32,3584]{1,0:T(8,128)(2,1)S(1)}, u32[]{:S(2)}, u32[]{:S(2)}) collective-permute-start(bf16[32,3584]{1,0:T(8,128)(2,1)S(1)} %fusion.24), channel_id=1, source_target_pairs={{0,6},{1,7},{2,0},{3,1},{4,2},{5,3},{6,4},{7,5},{8,14},{9,15},{10,... | collective-permute-start | bytes 688136 | tf_op jit(solution)/shard_map/ppermute | solution.py:30
  65.6 12.0 %collective-permute-start.11 = (bf16[32,3584]{1,0:T(8,128)(2,1)S(1)}, bf16[32,3584]{1,0:T(8,128)(2,1)S(1)}, u32[]{:S(2)}, u32[]{:S(2)}) collective-permute-start(bf16[32,3584]{1,0:T(8,128)(2,1)S(1)} %add_convert_fusion.1), channel_id=1, source_target_pairs={{0,24},{1,25},{2,26},{3,27},{4,28},{5,29},{6,30},{7,31},{8,0},{9,1... | collective-permute-start | bytes 688136 | tf_op jit(solution)/shard_map/ppermute | solution.py:30
  68.8 10.7 %collective-permute-start.13 = (bf16[32,3584]{1,0:T(8,128)(2,1)S(1)}, bf16[32,3584]{1,0:T(8,128)(2,1)S(1)}, u32[]{:S(2)}, u32[]{:S(2)}) collective-permute-start(bf16[32,3584]{1,0:T(8,128)(2,1)S(1)} %add_convert_fusion.1), channel_id=1, source_target_pairs={{0,16},{1,17},{2,18},{3,19},{4,20},{5,21},{6,22},{7,23},{8,24},{9,... | collective-permute-start | bytes 688136 | tf_op jit(solution)/shard_map/ppermute | solution.py:30
  68.8 13.3 %collective-permute-start.15 = (bf16[32,3584]{1,0:T(8,128)(2,1)S(1)}, bf16[32,3584]{1,0:T(8,128)(2,1)S(1)}, u32[]{:S(2)}, u32[]{:S(2)}) collective-permute-start(bf16[32,3584]{1,0:T(8,128)(2,1)S(1)} %add_convert_fusion.1), channel_id=1, source_target_pairs={{0,8},{1,9},{2,10},{3,11},{4,12},{5,13},{6,14},{7,15},{8,16},{9,17... | collective-permute-start | bytes 688136 | tf_op jit(solution)/shard_map/ppermute | solution.py:30
  69.4 19.2 %collective-permute-start.10 = (bf16[32,3584]{1,0:T(8,128)(2,1)S(1)}, bf16[32,3584]{1,0:T(8,128)(2,1)S(1)}, u32[]{:S(2)}, u32[]{:S(2)}) collective-permute-start(bf16[32,3584]{1,0:T(8,128)(2,1)S(1)} %add_convert_fusion.1), channel_id=1, source_target_pairs={{0,1},{1,0},{2,3},{3,2},{4,5},{5,4},{6,7},{7,6},{8,9},{9,8},{10,11... | collective-permute-start | bytes 688136 | tf_op jit(solution)/shard_map/ppermute | solution.py:13
  77.6 11.9 %collective-permute-start.12 = (bf16[32,3584]{1,0:T(8,128)(2,1)S(1)}, bf16[32,3584]{1,0:T(8,128)(2,1)S(1)}, u32[]{:S(2)}, u32[]{:S(2)}) collective-permute-start(bf16[32,3584]{1,0:T(8,128)(2,1)S(1)} %collective-permute-done.11), channel_id=1, source_target_pairs={{0,1},{1,0},{2,3},{3,2},{4,5},{5,4},{6,7},{7,6},{8,9},{9,8},{10,11... | collective-permute-start | bytes 688136 | tf_op jit(solution)/shard_map/ppermute | solution.py:13
  79.5 11.3 %collective-permute-start.14 = (bf16[32,3584]{1,0:T(8,128)(2,1)S(1)}, bf16[32,3584]{1,0:T(8,128)(2,1)S(1)}, u32[]{:S(2)}, u32[]{:S(2)}) collective-permute-start(bf16[32,3584]{1,0:T(8,128)(2,1)S(1)} %collective-permute-done.13), channel_id=1, source_target_pairs={{0,1},{1,0},{2,3},{3,2},{4,5},{5,4},{6,7},{7,6},{8,9},{9,8},{10,11... | collective-permute-start | bytes 688136 | tf_op jit(solution)/shard_map/ppermute | solution.py:13
  82.1 12.3 %collective-permute-start.16 = (bf16[32,3584]{1,0:T(8,128)(2,1)S(1)}, bf16[32,3584]{1,0:T(8,128)(2,1)S(1)}, u32[]{:S(2)}, u32[]{:S(2)}) collective-permute-start(bf16[32,3584]{1,0:T(8,128)(2,1)S(1)} %collective-permute-done.15), channel_id=1, source_target_pairs={{0,1},{1,0},{2,3},{3,2},{4,5},{5,4},{6,7},{7,6},{8,9},{9,8},{10,11... | collective-permute-start | bytes 688136 | tf_op jit(solution)/shard_map/ppermute | solution.py:13
  82.9 25.7 %collective-permute-start.21 = (bf16[288,1792]{1,0:T(8,128)(2,1)}, bf16[288,1792]{1,0:T(8,128)(2,1)S(1)}, u32[]{:S(2)}, u32[]{:S(2)}) collective-permute-start(bf16[288,1792]{1,0:T(8,128)(2,1)} %param.21), channel_id=1, source_target_pairs={{33,0},{97,1},{35,2},{99,3},{37,4},{101,5},{39,6},{103,7},{41,8},{... | collective-permute-start | bytes 3096584 | tf_op jit(solution)/shard_map/ppermute | solution.py:43
  88.6 48.5 %collective-permute-start.20 = (bf16[288,1792]{1,0:T(8,128)(2,1)}, bf16[288,1792]{1,0:T(8,128)(2,1)}, u32[]{:S(2)}, u32[]{:S(2)}) collective-permute-start(bf16[288,1792]{1,0:T(8,128)(2,1)} %param.21), channel_id=1, source_target_pairs={{32,0},{96,1},{34,2},{98,3},{36,4},{100,5},{38,6},{102,7},{40,8},{... | collective-permute-start | bytes 3096584 | tf_op jit(solution)/shard_map/ppermute | solution.py:43
  89.5 45.9 %collective-permute-start.19 = (bf16[288,1792]{1,0:T(8,128)(2,1)}, bf16[288,1792]{1,0:T(8,128)(2,1)}, u32[]{:S(2)}, u32[]{:S(2)}) collective-permute-start(bf16[288,1792]{1,0:T(8,128)(2,1)} %param.21), channel_id=1, source_target_pairs={{1,0},{65,1},{3,2},{67,3},{5,4},{69,5},{7,6},{71,7},{9,8},{73,9},{... | collective-permute-start | bytes 3096584 | tf_op jit(solution)/shard_map/ppermute | solution.py:43
  90.8 47.9 %collective-permute-start.18 = (bf16[288,1792]{1,0:T(8,128)(2,1)}, bf16[288,1792]{1,0:T(8,128)(2,1)}, u32[]{:S(2)}, u32[]{:S(2)}) collective-permute-start(bf16[288,1792]{1,0:T(8,128)(2,1)} %param.21), channel_id=1, source_target_pairs={{0,0},{64,1},{2,2},{66,3},{4,4},{68,5},{6,6},{70,7},{8,8},{72,9},{... | collective-permute-start | bytes 3096584 | tf_op jit(solution)/shard_map/ppermute | solution.py:43
  100.3 8.3 %collective-permute-start.17 = (bf16[128,288]{0,1:T(8,128)(2,1)S(1)}, bf16[128,288]{0,1:T(8,128)(2,1)S(1)}, u32[]{:S(2)}, u32[]{:S(2)}) collective-permute-start(bf16[128,288]{0,1:T(8,128)(2,1)S(1)} %fusion.19), channel_id=1, source_target_pairs={{0,1},{1,0},{2,3},{3,2},{4,5},{5,4},{6,7},{7,6},{8,9},{9,8},{10,11... | collective-permute-start | bytes 221192 | tf_op jit(solution)/shard_map/ppermute | solution.py:13
  140.5 13.1 %collective-permute-start.22 = (bf16[32,3584]{1,0:T(8,128)(2,1)S(1)}, bf16[32,3584]{1,0:T(8,128)(2,1)S(1)}, u32[]{:S(2)}, u32[]{:S(2)}) collective-permute-start(bf16[32,3584]{1,0:T(8,128)(2,1)S(1)} %get-tuple-element.7), channel_id=1, source_target_pairs={{0,8},{1,9},{2,10},{3,11},{4,12},{5,13},{6,14},{7,15},{8,16},{9,17... | collective-permute-start | bytes 688136 | tf_op jit(solution)/shard_map/ppermute | solution.py:30
  140.5 13.0 %collective-permute-start.23 = (bf16[32,3584]{1,0:T(8,128)(2,1)S(1)}, bf16[32,3584]{1,0:T(8,128)(2,1)S(1)}, u32[]{:S(2)}, u32[]{:S(2)}) collective-permute-start(bf16[32,3584]{1,0:T(8,128)(2,1)S(1)} %get-tuple-element.9), channel_id=1, source_target_pairs={{0,16},{1,17},{2,18},{3,19},{4,20},{5,21},{6,22},{7,23},{8,24},{9,... | collective-permute-start | bytes 688136 | tf_op jit(solution)/shard_map/ppermute | solution.py:30
  142.3 12.3 %collective-permute-start.24 = (bf16[32,3584]{1,0:T(8,128)(2,1)S(1)}, bf16[32,3584]{1,0:T(8,128)(2,1)S(1)}, u32[]{:S(2)}, u32[]{:S(2)}) collective-permute-start(bf16[32,3584]{1,0:T(8,128)(2,1)S(1)} %get-tuple-element.8), channel_id=1, source_target_pairs={{0,24},{1,25},{2,26},{3,27},{4,28},{5,29},{6,30},{7,31},{8,0},{9,1... | collective-permute-start | bytes 688136 | tf_op jit(solution)/shard_map/ppermute | solution.py:30
  (14 other events, 81.8 us)

commit v3 on v1

v3 whole, which is shorter than its diff:
```python
import jax
import jax.numpy as jnp
from jax import lax
from jax.experimental import pallas as pl
from jax.experimental.pallas import tpu as pltpu
from jax.sharding import PartitionSpec as P

score_scale = 1.0 / 192.0**0.5
norm_eps = 1e-06


def core_swap(x, width):
    return lax.ppermute(x, "tp", [(i, i ^ 1) for i in range(width)])


def between_chips(x, width):
    groups = [[2 * chip + core for chip in range(width // 2)] for core in range(2)]
    return lax.all_to_all(x, "tp", 0, 0, tiled=True, axis_index_groups=groups)


def down_pieces(down_weight, width):
    out = []
    for k in range(4):
        pairs = []
        for layer in range(4):
            for place in range(width):
                chip, core = divmod(place, 2)
                cut, row_core = (layer >> 1) ^ (k >> 1), (layer & 1) ^ (k & 1)
                pairs.append(((2 * core + cut) * width + 2 * chip + row_core, layer * width + place))
        out.append(lax.ppermute(down_weight, ("dp", "tp"), pairs))
    return out


def attend(query, cache, lengths, counts, latent_width, chips):
    slots, heads, wide = query.shape
    ctx = cache.shape[1]
    group = heads // chips
    rows = slots * heads

    def kernel(lengths_ref, counts_ref, q_ref, cache_ref, out_ref, latent_ref):
        slot = pl.program_id(0)
        at = pl.ds(pl.multiple_of(slot * heads, heads), heads)

        @pl.when(slot < counts_ref[0])
        def _():
            scores = jnp.dot(q_ref[0], cache_ref[0], preferred_element_type=jnp.float32)
            place = lax.broadcasted_iota(jnp.int32, scores.shape, 1)
            scores = jnp.where(place < lengths_ref[slot], scores * score_scale, -1e30)
            raised = jnp.exp(scores - jnp.max(scores, axis=1, keepdims=True))
            latent = lax.dot_general(
                raised.astype(jnp.bfloat16),
                cache_ref[0, :latent_width, :],
                (((1,), (1,)), ((), ())),
                preferred_element_type=jnp.float32,
            )
            latent = latent / jnp.sum(raised, axis=1, keepdims=True)
            latent_ref[at, :] = latent.astype(jnp.bfloat16)

        @pl.when(slot >= counts_ref[0])
        def _():
            latent_ref[at, :] = jnp.zeros((heads, latent_width), jnp.bfloat16)

        @pl.when(slot == slots - 1)
        def _():
            to = lax.broadcasted_iota(jnp.int32, (rows, rows), 0)
            source = to // group % slots * heads + to // (slots * group) * group + to % group
            pick = source == lax.broadcasted_iota(jnp.int32, (rows, rows), 1)
            out_ref[...] = jnp.dot(
                pick.astype(jnp.bfloat16), latent_ref[...], preferred_element_type=jnp.float32
            ).astype(jnp.bfloat16)

    def last(slot, lengths_ref, counts_ref):
        return (jnp.minimum(slot, counts_ref[0] - 1), 0, 0)

    out = pl.pallas_call(
        kernel,
        grid_spec=pltpu.PrefetchScalarGridSpec(
            num_scalar_prefetch=2,
            grid=(slots,),
            in_specs=[pl.BlockSpec((1, heads, wide), last), pl.BlockSpec((1, wide, ctx), last)],
            out_specs=pl.BlockSpec((rows, latent_width), lambda slot, *refs: (0, 0)),
            scratch_shapes=[pltpu.VMEM((rows, latent_width), jnp.bfloat16)],
        ),
        out_shape=jax.ShapeDtypeStruct((rows, latent_width), jnp.bfloat16),
        compiler_params=pltpu.CompilerParams(vmem_limit_bytes=32 * 2**20),
        cost_estimate=pl.CostEstimate(
            flops=2 * rows * ctx * (wide + latent_width),
            bytes_accessed=2 * cache.size,
            transcendentals=rows * ctx,
        ),
    )(lengths, counts, query, jnp.swapaxes(cache, 1, 2))
    return out.reshape(chips, slots * group, latent_width)


def project(mine, other, value_mine, value_other, output_mine, output_other, core, slots):
    chips, pairs, latent_width = mine.shape
    heads_here, _, head = value_mine.shape
    heads = 2 * heads_here
    depth, model = output_mine.shape
    half = model // 2
    block = 512
    rows = 2 * chips * slots
    lines = chips * pairs

    def kernel(core_ref, mine_ref, other_ref, vm_ref, vo_ref, om_ref, oo_ref, out_ref, value_ref):
        core = core_ref[0]

        @pl.when(pl.program_id(0) == 0)
        def _():
            to = lax.broadcasted_iota(jnp.int32, (rows, lines), 0)
            line = lax.broadcasted_iota(jnp.int32, (rows, lines), 1)
            chip, row_core, slot = to // (2 * slots), to // slots % 2, to % slots
            own = row_core == core
            source = chip * pairs + slot * heads
            for index in range(heads):
                side, weight_ref = (core, vm_ref) if index < heads_here else (1 - core, vo_ref)
                place = index % heads_here
                hit = line == source + side * heads_here + place
                rows_mine = jnp.where(hit & own, 1.0, 0.0).astype(jnp.bfloat16)
                rows_other = jnp.where(hit & ~own, 1.0, 0.0).astype(jnp.bfloat16)
                picked = jnp.dot(
                    rows_mine, mine_ref[...], preferred_element_type=jnp.float32
                ) + jnp.dot(rows_other, other_ref[...], preferred_element_type=jnp.float32)
                value_ref[:, index * head : (index + 1) * head] = jnp.dot(
                    picked.astype(jnp.bfloat16),
                    weight_ref[place],
                    preferred_element_type=jnp.float32,
                ).astype(jnp.bfloat16)

        out_ref[...] = (
            jnp.dot(value_ref[:, :depth], om_ref[...], preferred_element_type=jnp.float32)
            + jnp.dot(value_ref[:, depth:], oo_ref[...], preferred_element_type=jnp.float32)
        ).astype(jnp.bfloat16)

    steps = half // block
    whole = lambda *shape: pl.BlockSpec(shape, lambda j, core_ref: (0,) * len(shape))
    weight = pl.BlockSpec((depth, block), lambda j, core_ref: (0, core_ref[0] * steps + j))
    return pl.pallas_call(
        kernel,
        grid_spec=pltpu.PrefetchScalarGridSpec(
            num_scalar_prefetch=1,
            grid=(steps,),
            in_specs=[
                whole(lines, latent_width),
                whole(lines, latent_width),
                whole(heads_here, latent_width, head),
                whole(heads_here, latent_width, head),
                weight,
                weight,
            ],
            out_specs=pl.BlockSpec((rows, block), lambda j, core_ref: (0, j)),
            scratch_shapes=[pltpu.VMEM((rows, 2 * depth), jnp.bfloat16)],
        ),
        out_shape=jax.ShapeDtypeStruct((rows, half), jnp.bfloat16),
        compiler_params=pltpu.CompilerParams(vmem_limit_bytes=16 * 2**20),
        cost_estimate=pl.CostEstimate(
            flops=4 * rows * depth * half, bytes_accessed=4 * depth * half, transcendentals=0
        ),
    )(
        core.reshape(1),
        mine.reshape(lines, latent_width),
        other.reshape(lines, latent_width),
        value_mine,
        value_other,
        output_mine,
        output_other,
    )


def gated(residual, gain, gate_weight, up_weight, side, before):
    rows, half = residual.shape
    units = gate_weight.shape[1]
    block = 512
    steps = half // block
    finish = before is not None

    def kernel(side_ref, res_ref, gain_ref, gate_ref, up_ref, *refs):
        j = pl.program_id(0)
        if finish:
            gate_before, up_before, square_before, out_ref, gate_sum, up_sum, square_sum = refs
        else:
            gate_sum, up_sum, square_sum = refs

        @pl.when(j == 0)
        def _():
            if finish:
                gate_sum[...] = gate_before[...]
                up_sum[...] = up_before[...]
                square_sum[...] = square_before[...]
            else:
                gate_sum[...] = jnp.zeros_like(gate_sum)
                up_sum[...] = jnp.zeros_like(up_sum)
                square_sum[...] = jnp.zeros_like(square_sum)

        wide = res_ref[...].astype(jnp.float32)
        scaled = (wide * gain_ref[...]).astype(jnp.bfloat16)
        squares = wide * wide
        part = squares[:, :128]
        for k in range(1, block // 128):
            part = part + squares[:, k * 128 : (k + 1) * 128]
        square_sum[...] += part
        across = (((1,), (1,)), ((), ()))
        gate_sum[...] += lax.dot_general(
            scaled, gate_ref[...], across, preferred_element_type=jnp.float32
        )
        up_sum[...] += lax.dot_general(
            scaled, up_ref[...], across, preferred_element_type=jnp.float32
        )

        if finish:

            @pl.when(j == steps - 1)
            def _():
                mean = jnp.sum(square_sum[...], axis=1, keepdims=True) / (2 * half)
                scale = lax.rsqrt(mean + norm_eps)
                gate = gate_sum[...] * scale
                out_ref[...] = (gate / (1.0 + jnp.exp(-gate)) * (up_sum[...] * scale)).astype(
                    jnp.bfloat16
                )

    sums = [
        jax.ShapeDtypeStruct((rows, units), jnp.float32),
        jax.ShapeDtypeStruct((rows, units), jnp.float32),
        jax.ShapeDtypeStruct((rows, 128), jnp.float32),
    ]
    whole = [pl.BlockSpec(leaf.shape, lambda j, side_ref: (0, 0)) for leaf in sums]
    feature = lambda lines: pl.BlockSpec(
        (lines, block), lambda j, side_ref: (0, side_ref[0] * steps + j)
    )
    in_specs = [
        pl.BlockSpec((rows, block), lambda j, side_ref: (0, j)),
        feature(1),
        feature(units),
        feature(units),
    ]
    operands = [residual, gain[None, :], gate_weight.T, up_weight.T]
    return pl.pallas_call(
        kernel,
        grid_spec=pltpu.PrefetchScalarGridSpec(
            num_scalar_prefetch=1,
            grid=(steps,),
            in_specs=in_specs + (whole if finish else []),
            out_specs=whole[0] if finish else whole,
            scratch_shapes=[pltpu.VMEM(leaf.shape, leaf.dtype) for leaf in sums] if finish else [],
        ),
        out_shape=jax.ShapeDtypeStruct((rows, units), jnp.bfloat16) if finish else sums,
        compiler_params=pltpu.CompilerParams(vmem_limit_bytes=16 * 2**20),
        cost_estimate=pl.CostEstimate(
            flops=4 * rows * half * units, bytes_accessed=4 * half * units, transcendentals=0
        ),
    )(side.reshape(1), *operands, *(before or []))


def feed_forward(even, odd, pieces):
    rows, units = even.shape
    cut = pieces[0].shape[1]
    block = cut // 2

    def kernel(even_ref, odd_ref, a_ref, b_ref, c_ref, d_ref, out_ref):
        def write(first_ref, second_ref):
            out_ref[...] = (
                jnp.dot(even_ref[...], first_ref[...], preferred_element_type=jnp.float32)
                + jnp.dot(odd_ref[...], second_ref[...], preferred_element_type=jnp.float32)
            ).astype(jnp.bfloat16)

        @pl.when(pl.program_id(0) < 2)
        def _():
            write(a_ref, b_ref)

        @pl.when(pl.program_id(0) >= 2)
        def _():
            write(c_ref, d_ref)

    whole = pl.BlockSpec((rows, units), lambda j: (0, 0))
    early = pl.BlockSpec((units, block), lambda j: (0, jnp.minimum(j, 1)))
    late = pl.BlockSpec((units, block), lambda j: (0, jnp.maximum(j - 2, 0)))
    return pl.pallas_call(
        kernel,
        grid=(4,),
        in_specs=[whole, whole, early, early, late, late],
        out_specs=pl.BlockSpec((rows, block), lambda j: (0, j)),
        out_shape=jax.ShapeDtypeStruct((rows, 2 * cut), jnp.bfloat16),
        compiler_params=pltpu.CompilerParams(vmem_limit_bytes=16 * 2**20),
        cost_estimate=pl.CostEstimate(
            flops=8 * rows * units * cut, bytes_accessed=8 * units * cut, transcendentals=0
        ),
    )(even, odd, *pieces)


def on_device(
    layer_input,
    query,
    cache,
    lengths,
    counts,
    value_weight,
    output_weight,
    norm_gain,
    gate_weight,
    up_weight,
    down_weight,
    width,
):
    slots, model = layer_input.shape
    half = model // 2
    chips = width // 2

    heads_here, latent_width, head = value_weight.shape
    chip_slots = 2 * slots
    rows = chips * chip_slots
    place = lax.axis_index("tp")
    core = place % 2
    upper = core == 1
    layer = lax.axis_index("dp")

    pieces = down_pieces(down_weight, width)
    value_other = core_swap(value_weight, width)
    output_other = core_swap(output_weight, width)
    input_mine = lax.dynamic_slice_in_dim(layer_input, core * half, half, 1)
    input_other = core_swap(
        lax.dynamic_slice_in_dim(layer_input, (1 - core) * half, half, 1), width
    )
    input_chip = jnp.where(
        upper,
        jnp.concatenate([input_other, input_mine], axis=0),
        jnp.concatenate([input_mine, input_other], axis=0),
    ).astype(jnp.float32)

    latent = attend(query, cache, lengths, counts, latent_width, chips)
    arrived = between_chips(latent, width)
    arrived, pieces[0], pieces[1] = lax.optimization_barrier((arrived, pieces[0], pieces[1]))
    arrived_other = core_swap(arrived, width)
    attended_part = project(
        arrived, arrived_other, value_weight, value_other, output_weight, output_other, core, slots
    )
    attended_parts = between_chips(attended_part.reshape(chips, chip_slots, half), width)
    attended_parts, pieces[2], pieces[3] = lax.optimization_barrier(
        (attended_parts, pieces[2], pieces[3])
    )
    attended = jnp.sum(attended_parts.astype(jnp.float32), axis=0)
    residual = (input_chip + attended).astype(jnp.bfloat16)
    gathered = between_chips(
        jnp.broadcast_to(residual[None], (chips, chip_slots, half)), width
    ).reshape(rows, half)
    gathered_other = core_swap(gathered, width)
    sums = gated(gathered, norm_gain, gate_weight, up_weight, core, None)
    inner = gated(gathered_other, norm_gain, gate_weight, up_weight, 1 - core, sums)
    inner_other = core_swap(inner, width)

    same = core == layer % 2
    feed_part = feed_forward(
        jnp.where(same, inner, inner_other), jnp.where(same, inner_other, inner), pieces
    )
    feed_parts = between_chips(feed_part.reshape(chips, chip_slots, half), width)
    feed = jnp.sum(feed_parts.astype(jnp.float32), axis=0)
    cut = half // 2
    feed = jnp.where(
        layer // 2 == 1, jnp.concatenate([feed[:, cut:], feed[:, :cut]], axis=1), feed
    )
    mixed = (residual.astype(jnp.float32) + feed).astype(jnp.bfloat16)
    kept = lax.dynamic_slice_in_dim(mixed, core * slots, slots, 0)
    got = core_swap(lax.dynamic_slice_in_dim(mixed, (1 - core) * slots, slots, 0), width)
    out = jnp.where(
        upper,
        jnp.concatenate([got, kept], axis=1),
        jnp.concatenate([kept, got], axis=1),
    )
    live = jnp.arange(slots, dtype=jnp.int32) < counts[0]
    return jnp.where(live[:, None], out, jnp.bfloat16(0.0))


def solution(mesh):
    placed = (
        P(("dp", "tp"), None),
        P(("dp", "tp"), None, None),
        P(("dp", "tp"), None, None),
        P(("dp", "tp")),
        P(("dp", "tp")),
        P("tp", None, None),
        P("tp", None),
        P(),
        P(None, "tp"),
        P(None, "tp"),
        P("tp", "dp"),
    )
    width = mesh.shape["tp"]
    return jax.shard_map(
        lambda *args: on_device(*args, width),
        mesh=mesh,
        in_specs=placed,
        out_specs=P(("dp", "tp"), None),
        check_vma=False,
    )
```

time: 129 us -> 133 us (1.031)
  Pallas kernels: 0 us -> 24.7 us
  matrix products: 21.9 us -> 0 us
  starting transfers between devices: 14.5 us -> 32.4 us
  blocking collectives: 33.9 us -> 17.6 us
  between operations: 14.3 us -> 0.94 us
  waiting for transfers between devices: 31.4 us -> 41.8 us
  local copies, waits for them, and re-layouts: 8.22 us -> 12.2 us
  other arithmetic: 4.36 us -> 2.27 us
    pallas_call x0 -> x5, Pallas kernels: none -> 24.7 us  [the longest x1 6.96 us: attend(): pl.pallas_call(kernel, grid_spec=pltpu.PrefetchScalarGridSpec(num_scalar_...]
    all_to_all x2 -> x1, blocking collectives: 33.9 us -> 17.6 us  [between_chips(): return lax.all_to_all(x, 'tp', 0, 0, tiled=True, axis_index_groups=groups)]
    dot_general x11 -> x0, matrix products: 15.8 us -> none  [the longest x1 6.11 us: attend(): jnp.einsum('rht,rta->rha', attention, cache[:, :, :latent_width], preferr...]
    unnamed x16 -> x20, local copies, waits for them, and re-layouts: 1.61 us -> 12 us
    ppermute x0 -> x4, starting transfers between devices: none -> 9.81 us  [down_pieces(): out.append(lax.ppermute(down_weight, ('dp', 'tp'), pairs))]
    ppermute x0 -> x4, waiting for transfers between devices: none -> 7.56 us  [down_pieces(): out.append(lax.ppermute(down_weight, ('dp', 'tp'), pairs))]
    all_to_all x2 -> x3, starting transfers between devices: 7.27 us -> 14.8 us  [between_chips(): return lax.all_to_all(x, 'tp', 0, 0, tiled=True, axis_index_groups=groups)]
    sub x1 -> x0, matrix products: 6.06 us -> none  [attend(): raised = jnp.where(visible, jnp.exp(scores - peak), jnp.float32(0.0))]
  transfers between devices with their start and end apart: 11 -> 14, of which waited for: 5 -> 7; matrix products, arithmetic and copies ran while one was open for 21% -> 1% of each run, Pallas kernels for 0% -> 13%
where the time goes in v3:
time: 133 us; the launch traced here: 132 us
  waiting for transfers between devices  41.8 us (31%)
  starting transfers between devices  32.4 us (24%)
  Pallas kernels  24.7 us (19%)
  blocking collectives  17.6 us (13%)
  local copies, waits for them, and re-layouts  12.2 us (9%)
  other arithmetic  2.27 us (2%)
    all_to_all x3, waiting for transfers between devices, between_chips(): return lax.all_to_all(x, 'tp', 0, 0, tiled=True, axis_index_groups=groups)  32.1 us
    all_to_all x1, blocking collectives, between_chips(): return lax.all_to_all(x, 'tp', 0, 0, tiled=True, axis_index_groups=groups)  17.6 us
    all_to_all x3, starting transfers between devices, between_chips(): return lax.all_to_all(x, 'tp', 0, 0, tiled=True, axis_index_groups=groups)  14.8 us
    unnamed x20, local copies, waits for them, and re-layouts  12 us
    ppermute x4, starting transfers between devices, down_pieces(): out.append(lax.ppermute(down_weight, ('dp', 'tp'), pairs))  9.81 us
    ppermute x7, starting transfers between devices, core_swap(): return lax.ppermute(x, 'tp', [(i, i ^ 1) for i in range(width)])  7.73 us
    ppermute x4, waiting for transfers between devices, down_pieces(): out.append(lax.ppermute(down_weight, ('dp', 'tp'), pairs))  7.56 us
    pallas_call x1, Pallas kernels, attend(): pl.pallas_call(kernel, grid_spec=pltpu.PrefetchScalarGridSpec(num_scalar_...  6.96 us
  transfers between devices with their start and end apart: 14, of which 7 were waited for; matrix products, arithmetic and copies ran while one was open for 1% of the time, Pallas kernels for 13%

profile of v3, /device:TPU:1, one launch (start us, length us, event | category | flops | bytes accessed | tf_op | source)
XLA Modules:
  0.0 131.8 jit_solution(8102308931396073850)
XLA Ops:
  0.0 1.4 %collective-permute-start.5 = (bf16[256,7168]{1,0:T(8,128)(2,1)}, bf16[256,7168]{1,0:T(8,128)(2,1)}, u32[]{:S(2)}, u32[]{:S(2)}) collective-permute-start(bf16[256,7168]{1,0:T(8,128)(2,1)} %om_ref.1), channel_id=1, source_target_pairs={{0,1},{1,0},{2,3},{3,2},{4,5},{5,4},{6,7},{7,6},{8,9},{9,8},{10,11... | collective-permute-start | bytes 11010056 | tf_op jit(solution)/shard_map/ppermute | solution.py:13
  1.4 3.5 %collective-permute-start.1 = (bf16[288,1792]{1,0:T(8,128)(2,1)}, bf16[288,1792]{1,0:T(8,128)(2,1)S(1)}, u32[]{:S(2)}, u32[]{:S(2)}) collective-permute-start(bf16[288,1792]{1,0:T(8,128)(2,1)} %param.21), channel_id=1, source_target_pairs={{0,0},{64,1},{2,2},{66,3},{4,4},{68,5},{6,6},{70,7},{8,8},{72,9},{... | collective-permute-start | bytes 3096584 | tf_op jit(solution)/shard_map/ppermute | solution.py:30
  5.7 3.7 %copy-done.4 = bf16[4,2048,576]{1,2,0:T(8,128)(2,1)S(1)} copy-done((bf16[4,2048,576]{1,2,0:T(8,128)(2,1)S(1)}, bf16[4,2048,576]{1,2,0:T(8,128)(2,1)}, u32[]{:S(2)}) %copy-start.4) | copy-done | bytes 9437208
  11.0 7.0 %shard_map.109 = bf16[256,512]{1,0:T(8,128)(2,1)} custom-call(s32[4]{0:T(128)S(1)} %copy-done.8, s32[1]{0:T(128)} %copy.12.counts_ref, bf16[4,64,576]{2,1,0:T(8,128)(2,1)S(1)} %copy-done.6, bf16[4,576,2048]{2,1,0:T(8,128)(2,1)S(1)} %bitcast.18), custom_call_target="tpu_custom_call" | custom-call | flops 1140850688 | bytes 9437184 | tf_op jit(solution)/shard_map/pallas_call | solution.py:75
  17.9 6.8 %all-to-all-start = ((bf16[16,16,512]{2,1,0:T(8,128)(2,1)}), bf16[16,16,512]{2,1,0:T(8,128)(2,1)S(1)}, u32[]{:S(2)}, u32[]{:S(2)}) async-start(bf16[16,16,512]{2,1,0:T(8,128)(2,1)} %bitcast.3), calls=%async_computation | async-start | bytes 524288 | tf_op jit(solution)/shard_map/all_to_all | solution.py:18
  25.8 6.4 %all-to-all-done = bf16[16,16,512]{2,1,0:T(8,128)(2,1)S(1)} async-done(((bf16[16,16,512]{2,1,0:T(8,128)(2,1)}), bf16[16,16,512]{2,1,0:T(8,128)(2,1)S(1)}, u32[]{:S(2)}, u32[]{:S(2)}) %all-to-all-start) | async-done | bytes 262176 | tf_op jit(solution)/shard_map/all_to_all | solution.py:18
  32.3 2.2 %collective-permute-start.3 = (bf16[16,16,512]{2,1,0:T(8,128)(2,1)S(1)}, bf16[16,16,512]{2,1,0:T(8,128)(2,1)}, u32[]{:S(2)}, u32[]{:S(2)}) collective-permute-start(bf16[16,16,512]{2,1,0:T(8,128)(2,1)S(1)} %all-to-all-done), channel_id=1, source_target_pairs={{0,1},{1,0},{2,3},{3,2},{4,5},{5,4},{6,7},{7,6},{8,9},{9,8},{10,11... | collective-permute-start | bytes 786440 | tf_op jit(solution)/shard_map/ppermute | solution.py:13
  34.5 2.0 %collective-permute-start.6 = (bf16[288,1792]{1,0:T(8,128)(2,1)}, bf16[288,1792]{1,0:T(8,128)(2,1)S(1)}, u32[]{:S(2)}, u32[]{:S(2)}) collective-permute-start(bf16[288,1792]{1,0:T(8,128)(2,1)} %param.21), channel_id=1, source_target_pairs={{32,0},{96,1},{34,2},{98,3},{36,4},{100,5},{38,6},{102,7},{40,8},{... | collective-permute-start | bytes 3096584 | tf_op jit(solution)/shard_map/ppermute | solution.py:30
  36.5 4.2 %collective-permute-start.7 = (bf16[288,1792]{1,0:T(8,128)(2,1)}, bf16[288,1792]{1,0:T(8,128)(2,1)}, u32[]{:S(2)}, u32[]{:S(2)}) collective-permute-start(bf16[288,1792]{1,0:T(8,128)(2,1)} %param.21), channel_id=1, source_target_pairs={{33,0},{97,1},{35,2},{99,3},{37,4},{101,5},{39,6},{103,7},{41,8},{... | collective-permute-start | bytes 3096584 | tf_op jit(solution)/shard_map/ppermute | solution.py:30
  40.7 2.0 %copy-done.5 = bf16[256,7168]{1,0:T(8,128)(2,1)S(1)} copy-done((bf16[256,7168]{1,0:T(8,128)(2,1)S(1)}, bf16[256,7168]{1,0:T(8,128)(2,1)}, u32[]{:S(2)}) %copy-start.5) | copy-done | bytes 3670040
  42.8 6.9 %shard_map.110 = bf16[128,3584]{1,0:T(8,128)(2,1)} custom-call(s32[1]{0:T(128)} %bitcast.1.core_ref.side_ref, bf16[256,512]{1,0:T(8,128)(2,1)S(1)} %bitcast.21, bf16[256,512]{1,0:T(8,128)(2,1)} %bitcast.5.other_ref, bf16[2,512,128]{2,1,0:T(8,128)(2,1)} %vm_ref.1, bf16[2,512,128]{2,1,0:T(8,128)(2,1)} %collective-permute-done.4.vo_ref, ...), custom_call_target="tpu_custom_call" | custom-call | flops 469762048 | bytes 3670016 | tf_op jit(solution)/shard_map/pallas_call | solution.py:138
  49.7 4.4 %all-to-all-start.1 = ((bf16[16,8,3584]{2,1,0:T(8,128)(2,1)}), bf16[16,8,3584]{2,1,0:T(8,128)(2,1)}, u32[]{:S(2)}, u32[]{:S(2)}) async-start(bf16[16,8,3584]{2,1,0:T(8,128)(2,1)} %bitcast.6), calls=%async_computation.1 | async-start | bytes 1835008 | tf_op jit(solution)/shard_map/all_to_all | solution.py:18
  54.3 3.0 %collective-permute-done.6.c_ref = bf16[288,1792]{1,0:T(8,128)(2,1)S(1)} collective-permute-done((bf16[288,1792]{1,0:T(8,128)(2,1)}, bf16[288,1792]{1,0:T(8,128)(2,1)S(1)}, u32[]{:S(2)}, u32[]{:S(2)}) %collective-permute-start.6) | collective-permute-done | bytes 1032224 | tf_op jit(solution)/shard_map/ppermute | solution.py:30
  57.3 4.6 %collective-permute-done.7.d_ref = bf16[288,1792]{1,0:T(8,128)(2,1)} collective-permute-done((bf16[288,1792]{1,0:T(8,128)(2,1)}, bf16[288,1792]{1,0:T(8,128)(2,1)}, u32[]{:S(2)}, u32[]{:S(2)}) %collective-permute-start.7) | collective-permute-done | bytes 1032224 | tf_op jit(solution)/shard_map/ppermute | solution.py:30
  61.9 9.5 %all-to-all-done.1 = bf16[16,8,3584]{2,1,0:T(8,128)(2,1)} async-done(((bf16[16,8,3584]{2,1,0:T(8,128)(2,1)}), bf16[16,8,3584]{2,1,0:T(8,128)(2,1)}, u32[]{:S(2)}, u32[]{:S(2)}) %all-to-all-start.1) | async-done | bytes 917536 | tf_op jit(solution)/shard_map/all_to_all | solution.py:18
  72.8 17.6 %all_to_all.20 = bf16[16,8,3584]{2,1,0:T(8,128)(2,1)S(1)} all-to-all(bf16[16,8,3584]{2,1,0:T(8,128)(2,1)S(1)} %broadcast_in_dim.24), channel_id=1, replica_groups={{0,2,4,6,8,10,12,14,16,18,20,22,24,26,28,30},{1,3,5,7,9,11,13,15,17,19,..., dimensions={0} | all-to-all | bytes 1835008 | tf_op jit(solution)/shard_map/all_to_all | solution.py:18
  90.4 1.8 %collective-permute-start.8 = (bf16[128,3584]{1,0:T(8,128)(2,1)S(1)}, bf16[128,3584]{1,0:T(8,128)(2,1)S(1)}, u32[]{:S(2)}, u32[]{:S(2)}) collective-permute-start(bf16[128,3584]{1,0:T(8,128)(2,1)S(1)} %bitcast.19), channel_id=1, source_target_pairs={{0,1},{1,0},{2,3},{3,2},{4,5},{5,4},{6,7},{7,6},{8,9},{9,8},{10,11... | collective-permute-start | bytes 2752520 | tf_op jit(solution)/shard_map/ppermute | solution.py:13
  92.2 2.2 %copy-done = bf16[7168,288]{0,1:T(8,128)(2,1)S(1)} copy-done((bf16[7168,288]{0,1:T(8,128)(2,1)S(1)}, bf16[7168,288]{0,1:T(8,128)(2,1)}, u32[]{:S(2)}) %copy-start) | copy-done | bytes 4128792
  94.4 2.2 %copy-done.2 = bf16[7168,288]{0,1:T(8,128)(2,1)S(1)} copy-done((bf16[7168,288]{0,1:T(8,128)(2,1)S(1)}, bf16[7168,288]{0,1:T(8,128)(2,1)}, u32[]{:S(2)}) %copy-start.2) | copy-done | bytes 4128792
  96.5 3.0 %shard_map.111 = (f32[128,288]{1,0:T(8,128)S(1)}, f32[128,288]{1,0:T(8,128)S(1)}, f32[128,128]{1,0:T(8,128)S(1)}) custom-call(s32[1]{0:T(128)} %bitcast.1.core_ref.side_ref, bf16[128,3584]{1,0:T(8,128)(2,1)S(1)} %bitcast.20, f32[1,7168]{1,0:T(1,128)S(1)} %bitcast.22, bf16[288,7168]{1,0:T(8,128)(2,1)S(1)} %bitcast.14, bf16[288,7168]{1,0:T(8,128)(2,1)S(1)} %bitcast.16), custom_call_target="tpu_custom_call" | custom-call | flops 528482304 | bytes 4128768 | tf_op jit(solution)/shard_map/pallas_call | solution.py:237
  100.0 3.2 %shard_map.112 = bf16[128,288]{1,0:T(8,128)(2,1)S(1)} custom-call(s32[1]{0:T(128)} %bitcast.7.side_ref, bf16[128,3584]{1,0:T(8,128)(2,1)S(1)} %collective-permute-done.8.res_ref, f32[1,7168]{1,0:T(1,128)S(1)} %bitcast.23, bf16[288,7168]{1,0:T(8,128)(2,1)S(1)} %bitcast.15, bf16[288,7168]{1,0:T(8,128)(2,1)S(1)} %bitcast.17, ...), custom_call_target="tpu_custom_call" | custom-call | flops 528482304 | bytes 4128768 | tf_op jit(solution)/shard_map/pallas_call | solution.py:237
  104.6 4.5 %shard_map.113 = bf16[128,3584]{1,0:T(8,128)(2,1)} custom-call(bf16[128,288]{1,0:T(8,128)(2,1)S(1)} %get-tuple-element.24.even_ref, bf16[128,288]{1,0:T(8,128)(2,1)S(1)} %get-tuple-element.23.odd_ref, bf16[288,1792]{1,0:T(8,128)(2,1)S(1)} %collective-permute-done.1.a_ref, bf16[288,1792]{1,0:T(8,128)(2,1)S(1)} %collective-permute-done.2.b_ref, ...), custom_call_target="tpu_custom_call" | custom-call | flops 528482304 | bytes 4128768 | tf_op jit(solution)/shard_map/pallas_call | solution.py:277
  109.1 3.6 %all-to-all-start.3 = ((bf16[16,8,3584]{2,1,0:T(8,128)(2,1)}), bf16[16,8,3584]{2,1,0:T(8,128)(2,1)S(1)}, u32[]{:S(2)}, u32[]{:S(2)}) async-start(bf16[16,8,3584]{2,1,0:T(8,128)(2,1)} %bitcast.12), calls=%async_computation.3 | async-start | bytes 1835008 | tf_op jit(solution)/shard_map/all_to_all | solution.py:18
  112.8 16.2 %all-to-all-done.3 = bf16[16,8,3584]{2,1,0:T(8,128)(2,1)S(1)} async-done(((bf16[16,8,3584]{2,1,0:T(8,128)(2,1)}), bf16[16,8,3584]{2,1,0:T(8,128)(2,1)S(1)}, u32[]{:S(2)}, u32[]{:S(2)}) %all-to-all-start.3) | async-done | bytes 917536 | tf_op jit(solution)/shard_map/all_to_all | solution.py:18
  (41 shorter events, 9.0 us)
Async XLA Ops:
  0.0 40.7 %collective-permute-start.5 = (bf16[256,7168]{1,0:T(8,128)(2,1)}, bf16[256,7168]{1,0:T(8,128)(2,1)}, u32[]{:S(2)}, u32[]{:S(2)}) collective-permute-start(bf16[256,7168]{1,0:T(8,128)(2,1)} %om_ref.1), channel_id=1, source_target_pairs={{0,1},{1,0},{2,3},{3,2},{4,5},{5,4},{6,7},{7,6},{8,9},{9,8},{10,11... | collective-permute-start | bytes 11010056 | tf_op jit(solution)/shard_map/ppermute | solution.py:13
  1.4 30.8 %collective-permute-start.1 = (bf16[288,1792]{1,0:T(8,128)(2,1)}, bf16[288,1792]{1,0:T(8,128)(2,1)S(1)}, u32[]{:S(2)}, u32[]{:S(2)}) collective-permute-start(bf16[288,1792]{1,0:T(8,128)(2,1)} %param.21), channel_id=1, source_target_pairs={{0,0},{64,1},{2,2},{66,3},{4,4},{68,5},{6,6},{70,7},{8,8},{72,9},{... | collective-permute-start | bytes 3096584 | tf_op jit(solution)/shard_map/ppermute | solution.py:30
  4.9 27.3 %collective-permute-start.2 = (bf16[288,1792]{1,0:T(8,128)(2,1)}, bf16[288,1792]{1,0:T(8,128)(2,1)S(1)}, u32[]{:S(2)}, u32[]{:S(2)}) collective-permute-start(bf16[288,1792]{1,0:T(8,128)(2,1)} %param.21), channel_id=1, source_target_pairs={{1,0},{65,1},{3,2},{67,3},{5,4},{69,5},{7,6},{71,7},{9,8},{73,9},{... | collective-permute-start | bytes 3096584 | tf_op jit(solution)/shard_map/ppermute | solution.py:30
  5.7 3.7 %copy-start.4 = (bf16[4,2048,576]{1,2,0:T(8,128)(2,1)S(1)}, bf16[4,2048,576]{1,2,0:T(8,128)(2,1)}, u32[]{:S(2)}) copy-start(bf16[4,2048,576]{1,2,0:T(8,128)(2,1)} %param.13) | copy-start | bytes 28311556
  9.4 1.0 copy-start.6
  10.3 0.7 copy-start.8
  17.9 14.3 %all-to-all-start = ((bf16[16,16,512]{2,1,0:T(8,128)(2,1)}), bf16[16,16,512]{2,1,0:T(8,128)(2,1)S(1)}, u32[]{:S(2)}, u32[]{:S(2)}) async-start(bf16[16,16,512]{2,1,0:T(8,128)(2,1)} %bitcast.3), calls=%async_computation | async-start | bytes 524288 | tf_op jit(solution)/shard_map/all_to_all | solution.py:18
  24.7 16.0 %collective-permute-start.4 = (bf16[2,512,128]{2,1,0:T(8,128)(2,1)}, bf16[2,512,128]{2,1,0:T(8,128)(2,1)}, u32[]{:S(2)}, u32[]{:S(2)}) collective-permute-start(bf16[2,512,128]{2,1,0:T(8,128)(2,1)} %vm_ref.1), channel_id=1, source_target_pairs={{0,1},{1,0},{2,3},{3,2},{4,5},{5,4},{6,7},{7,6},{8,9},{9,8},{10,11... | collective-permute-start | bytes 786440 | tf_op jit(solution)/shard_map/ppermute | solution.py:13
  32.3 8.4 %collective-permute-start.3 = (bf16[16,16,512]{2,1,0:T(8,128)(2,1)S(1)}, bf16[16,16,512]{2,1,0:T(8,128)(2,1)}, u32[]{:S(2)}, u32[]{:S(2)}) collective-permute-start(bf16[16,16,512]{2,1,0:T(8,128)(2,1)S(1)} %all-to-all-done), channel_id=1, source_target_pairs={{0,1},{1,0},{2,3},{3,2},{4,5},{5,4},{6,7},{7,6},{8,9},{9,8},{10,11... | collective-permute-start | bytes 786440 | tf_op jit(solution)/shard_map/ppermute | solution.py:13
  34.5 22.8 %collective-permute-start.6 = (bf16[288,1792]{1,0:T(8,128)(2,1)}, bf16[288,1792]{1,0:T(8,128)(2,1)S(1)}, u32[]{:S(2)}, u32[]{:S(2)}) collective-permute-start(bf16[288,1792]{1,0:T(8,128)(2,1)} %param.21), channel_id=1, source_target_pairs={{32,0},{96,1},{34,2},{98,3},{36,4},{100,5},{38,6},{102,7},{40,8},{... | collective-permute-start | bytes 3096584 | tf_op jit(solution)/shard_map/ppermute | solution.py:30
  36.5 25.4 %collective-permute-start.7 = (bf16[288,1792]{1,0:T(8,128)(2,1)}, bf16[288,1792]{1,0:T(8,128)(2,1)}, u32[]{:S(2)}, u32[]{:S(2)}) collective-permute-start(bf16[288,1792]{1,0:T(8,128)(2,1)} %param.21), channel_id=1, source_target_pairs={{33,0},{97,1},{35,2},{99,3},{37,4},{101,5},{39,6},{103,7},{41,8},{... | collective-permute-start | bytes 3096584 | tf_op jit(solution)/shard_map/ppermute | solution.py:30
  40.7 2.0 %copy-start.5 = (bf16[256,7168]{1,0:T(8,128)(2,1)S(1)}, bf16[256,7168]{1,0:T(8,128)(2,1)}, u32[]{:S(2)}) copy-start(bf16[256,7168]{1,0:T(8,128)(2,1)} %om_ref.1) | copy-start | bytes 11010052
  42.8 11.4 %copy-start.9 = (bf16[4,7168]{1,0:T(4,128)(2,1)S(1)}, bf16[4,7168]{1,0:T(4,128)(2,1)}, u32[]{:S(2)}) copy-start(bf16[4,7168]{1,0:T(4,128)(2,1)} %param.11) | copy-start | bytes 172036
  49.7 42.5 %copy-start.7 = (f32[7168]{0:T(1024)S(1)}, f32[7168]{0:T(1024)}, u32[]{:S(2)}) copy-start(f32[7168]{0:T(1024)} %param.18) | copy-start | bytes 86020
  49.7 21.6 %all-to-all-start.1 = ((bf16[16,8,3584]{2,1,0:T(8,128)(2,1)}), bf16[16,8,3584]{2,1,0:T(8,128)(2,1)}, u32[]{:S(2)}, u32[]{:S(2)}) async-start(bf16[16,8,3584]{2,1,0:T(8,128)(2,1)} %bitcast.6), calls=%async_computation.1 | async-start | bytes 1835008 | tf_op jit(solution)/shard_map/all_to_all | solution.py:18
  54.2 18.4 %collective-permute-start = (bf16[4,3584]{1,0:T(4,128)(2,1)S(1)}, bf16[4,3584]{1,0:T(4,128)(2,1)S(1)}, u32[]{:S(2)}, u32[]{:S(2)}) collective-permute-start(bf16[4,3584]{1,0:T(4,128)(2,1)S(1)} %get-tuple-element.29), channel_id=1, source_target_pairs={{0,1},{1,0},{2,3},{3,2},{4,5},{5,4},{6,7},{7,6},{8,9},{9,8},{10,11... | collective-permute-start | bytes 86024 | tf_op jit(solution)/shard_map/ppermute | solution.py:13
  90.4 9.2 %collective-permute-start.8 = (bf16[128,3584]{1,0:T(8,128)(2,1)S(1)}, bf16[128,3584]{1,0:T(8,128)(2,1)S(1)}, u32[]{:S(2)}, u32[]{:S(2)}) collective-permute-start(bf16[128,3584]{1,0:T(8,128)(2,1)S(1)} %bitcast.19), channel_id=1, source_target_pairs={{0,1},{1,0},{2,3},{3,2},{4,5},{5,4},{6,7},{7,6},{8,9},{9,8},{10,11... | collective-permute-start | bytes 2752520 | tf_op jit(solution)/shard_map/ppermute | solution.py:13
  92.2 2.2 %copy-start = (bf16[7168,288]{0,1:T(8,128)(2,1)S(1)}, bf16[7168,288]{0,1:T(8,128)(2,1)}, u32[]{:S(2)}) copy-start(bf16[7168,288]{0,1:T(8,128)(2,1)} %param.19) | copy-start | bytes 12386308
  94.4 2.2 %copy-start.2 = (bf16[7168,288]{0,1:T(8,128)(2,1)S(1)}, bf16[7168,288]{0,1:T(8,128)(2,1)}, u32[]{:S(2)}) copy-start(bf16[7168,288]{0,1:T(8,128)(2,1)} %param.20) | copy-start | bytes 12386308
  96.5 3.1 %copy-start.1 = (bf16[7168,288]{0,1:T(8,128)(2,1)S(1)}, bf16[7168,288]{0,1:T(8,128)(2,1)}, u32[]{:S(2)}) copy-start(bf16[7168,288]{0,1:T(8,128)(2,1)} %param.19) | copy-start | bytes 12386308
  96.5 3.4 %copy-start.3 = (bf16[7168,288]{0,1:T(8,128)(2,1)S(1)}, bf16[7168,288]{0,1:T(8,128)(2,1)}, u32[]{:S(2)}) copy-start(bf16[7168,288]{0,1:T(8,128)(2,1)} %param.20) | copy-start | bytes 12386308
  103.2 1.4 %collective-permute-start.9 = (bf16[128,288]{1,0:T(8,128)(2,1)S(1)}, bf16[128,288]{1,0:T(8,128)(2,1)S(1)}, u32[]{:S(2)}, u32[]{:S(2)}) collective-permute-start(bf16[128,288]{1,0:T(8,128)(2,1)S(1)} %shard_map.112), channel_id=1, source_target_pairs={{0,1},{1,0},{2,3},{3,2},{4,5},{5,4},{6,7},{7,6},{8,9},{9,8},{10,11... | collective-permute-start | bytes 221192 | tf_op jit(solution)/shard_map/ppermute | solution.py:13
  109.1 19.9 %all-to-all-start.3 = ((bf16[16,8,3584]{2,1,0:T(8,128)(2,1)}), bf16[16,8,3584]{2,1,0:T(8,128)(2,1)S(1)}, u32[]{:S(2)}, u32[]{:S(2)}) async-start(bf16[16,8,3584]{2,1,0:T(8,128)(2,1)} %bitcast.12), calls=%async_computation.3 | async-start | bytes 1835008 | tf_op jit(solution)/shard_map/all_to_all | solution.py:18
  129.2 1.9 %collective-permute-start.10 = (bf16[4,3584]{1,0:T(4,128)(2,1)S(1)}, bf16[4,3584]{1,0:T(4,128)(2,1)S(1)}, u32[]{:S(2)}, u32[]{:S(2)}) collective-permute-start(bf16[4,3584]{1,0:T(4,128)(2,1)S(1)} %get-tuple-element.27), channel_id=1, source_target_pairs={{0,1},{1,0},{2,3},{3,2},{4,5},{5,4},{6,7},{7,6},{8,9},{9,8},{10,11... | collective-permute-start | bytes 86024 | tf_op jit(solution)/shard_map/ppermute | solution.py:13

commit v4 on v2

v4 whole, which is shorter than its diff:
```python
import math

import jax
import jax.numpy as jnp
from jax import lax
from jax.experimental import pallas as pl
from jax.experimental.pallas import tpu as pltpu
from jax.sharding import PartitionSpec as P

score_scale = 1.0 / 192.0**0.5
norm_eps = 1e-06


def core_swap(x, width):
    return lax.ppermute(x, "tp", [(i, i ^ 1) for i in range(width)])


def between_chips(x, width):
    groups = [[2 * chip + core for chip in range(width // 2)] for core in range(2)]
    return lax.all_to_all(x, "tp", 0, 0, tiled=True, axis_index_groups=groups)


def turn(parts, axis, side, sign):
    out = [parts[0]]
    for k in range(1, side):
        pairs = []
        for y in range(side):
            for x in range(side):
                for core in range(2):
                    if axis == core:
                        to = ((y + sign * k) % side) * side + x
                    else:
                        to = y * side + (x + sign * k) % side
                    pairs.append(((y * side + x) * 2 + core, to * 2 + core))
        out.append(lax.ppermute(parts[k], "tp", pairs))
    return out


def total(parts):
    wide = parts[0].astype(jnp.float32)
    for part in parts[1:]:
        wide = wide + part.astype(jnp.float32)
    return wide


def down_pieces(down_weight, width):
    out = []
    for k in range(4):
        pairs = []
        for layer in range(4):
            for place in range(width):
                chip, core = divmod(place, 2)
                cut, row_core = (layer >> 1) ^ (k >> 1), (layer & 1) ^ (k & 1)
                pairs.append(((2 * core + cut) * width + 2 * chip + row_core, layer * width + place))
        out.append(lax.ppermute(down_weight, ("dp", "tp"), pairs))
    return out


in_vmem = pl.BlockSpec(memory_space=pltpu.VMEM)
in_hbm = pl.BlockSpec(memory_space=pltpu.HBM)
in_smem = pl.BlockSpec(memory_space=pltpu.SMEM)
across = (((1,), (1,)), ((), ()))


def product(a, b):
    return jnp.dot(a, b, preferred_element_type=jnp.float32)


def one_hot(source, columns):
    hit = source == lax.broadcasted_iota(jnp.int32, (source.shape[0], columns), 1)
    return jnp.where(hit, 1.0, 0.0).astype(jnp.bfloat16)


def line_numbers(rows):
    return lax.broadcasted_iota(jnp.int32, (rows, 1), 0)


def budget(mib):
    return pltpu.CompilerParams(vmem_limit_bytes=mib * 2**20)


def attend(query, cache, lengths, counts, latent_width, chips):
    slots, heads, wide = query.shape
    ctx = cache.shape[1]
    group = heads // chips
    rows = slots * heads

    def kernel(lengths_ref, counts_ref, q_ref, cache_ref, out_ref, held_ref, sems):
        copies = [
            pltpu.make_async_copy(cache_ref.at[slot], held_ref.at[slot], sems.at[slot])
            for slot in range(slots)
        ]

        def score(slot):
            copies[slot].wait()
            place = lax.broadcasted_iota(jnp.int32, (heads, ctx), 1)
            found = product(q_ref[slot], held_ref[slot]) * score_scale
            return jnp.where(place < lengths_ref[slot], found, -1e30)

        def gather(slot, scores):
            raised = jnp.exp(scores - jnp.max(scores, axis=1, keepdims=True))
            latent = lax.dot_general(
                raised.astype(jnp.bfloat16),
                held_ref[slot, :latent_width],
                across,
                preferred_element_type=jnp.float32,
            )
            latent = latent / jnp.sum(raised, axis=1, keepdims=True)
            return jnp.where(slot < counts_ref[0], latent, 0.0).astype(jnp.bfloat16)

        copies[0].start()
        copies[1].start()
        latents = []
        scores = score(0)
        for slot in range(slots):
            if slot + 2 < slots:
                copies[slot + 2].start()
            following = score(slot + 1) if slot + 1 < slots else None
            latents.append(gather(slot, scores))
            scores = following
        to = line_numbers(rows)
        source = to // group % slots * heads + to // (slots * group) * group + to % group
        out_ref[...] = product(
            one_hot(source, rows), jnp.concatenate(latents, axis=0)
        ).astype(jnp.bfloat16)

    out = pl.pallas_call(
        kernel,
        in_specs=[in_smem, in_smem, in_vmem, in_hbm],
        out_specs=in_vmem,
        out_shape=jax.ShapeDtypeStruct((rows, latent_width), jnp.bfloat16),
        scratch_shapes=[
            pltpu.VMEM((slots, wide, ctx), jnp.bfloat16),
            pltpu.SemaphoreType.DMA((slots,)),
        ],
        compiler_params=budget(60),
        cost_estimate=pl.CostEstimate(
            flops=2 * rows * ctx * (wide + latent_width),
            bytes_accessed=2 * cache.size,
            transcendentals=rows * ctx,
        ),
    )(lengths, counts, query, jnp.swapaxes(cache, 1, 2))
    return out.reshape(chips, slots * group, latent_width)


def project(mine, other, value_mine, value_other, output_mine, output_other, spot, side, slots):
    chips, pairs, latent_width = mine.shape
    heads_here, _, head = value_mine.shape
    heads = 2 * heads_here
    depth, model = output_mine.shape
    half = model // 2
    rows = 2 * chips * slots
    line = rows // side
    lines = chips * pairs
    cuts = 4
    span = half // cuts

    def kernel(spot_ref, mine_ref, other_ref, vm_ref, vo_ref, om_ref, oo_ref, *refs):
        outs, (held_ref, sems) = refs[:side], refs[side:]
        core, first = spot_ref[0], spot_ref[1]
        copies = []
        for cut in range(cuts):
            for k, weight_ref in enumerate((om_ref, oo_ref)):
                start = pl.multiple_of(core * half + cut * span, 128)
                copies.append(
                    pltpu.make_async_copy(
                        weight_ref.at[:, pl.ds(start, span)],
                        held_ref.at[pl.ds(k * depth, depth), pl.ds(cut * span, span)],
                        sems.at[cut, k],
                    )
                )
                copies[-1].start()
        to = line_numbers(rows)
        along = (to // line + first) % side
        second = to // (2 * slots) % side
        chip = jnp.where(core == 0, along * side + second, second * side + along)
        from_other = (to // slots % 2 + core) % 2
        source = from_other * lines + chip * pairs + to % slots * heads
        latents = jnp.concatenate([mine_ref[...], other_ref[...]], axis=0)
        values = []
        for index in range(heads):
            owner, weight_ref = (core, vm_ref) if index < heads_here else (1 - core, vo_ref)
            place = index % heads_here
            pick = one_hot(source + owner * heads_here + place, 2 * lines)
            picked = product(pick, latents).astype(jnp.bfloat16)
            values.append(product(picked, weight_ref[place]).astype(jnp.bfloat16))
        values = jnp.concatenate(values, axis=1)
        for cut in range(cuts):
            copies[2 * cut].wait()
            copies[2 * cut + 1].wait()
            part = slice(cut * span, (cut + 1) * span)
            result = product(values, held_ref[:, part]).astype(jnp.bfloat16)
            for k in range(side):
                outs[k][:, part] = result[k * line : (k + 1) * line]

    return pl.pallas_call(
        kernel,
        in_specs=[in_smem] + [in_vmem] * 4 + [in_hbm] * 2,
        out_specs=[in_vmem] * side,
        out_shape=[jax.ShapeDtypeStruct((line, half), jnp.bfloat16)] * side,
        scratch_shapes=[
            pltpu.VMEM((2 * depth, half), jnp.bfloat16),
            pltpu.SemaphoreType.DMA((cuts, 2)),
        ],
        compiler_params=budget(24),
        cost_estimate=pl.CostEstimate(
            flops=4 * rows * depth * half, bytes_accessed=4 * depth * half, transcendentals=0
        ),
    )(
        spot,
        mine.reshape(lines, latent_width),
        other.reshape(lines, latent_width),
        value_mine,
        value_other,
        output_mine,
        output_other,
    )


def gated(parts, gain, gate_weight, up_weight, spot, before):
    side = len(parts)
    line, half = parts[0].shape
    rows = side * line
    units = gate_weight.shape[1]
    cuts = 4
    span = half // cuts
    finish = before is not None

    def kernel(spot_ref, *refs):
        part_refs, refs = refs[:side], refs[side:]
        gain_ref, gate_ref, up_ref, refs = refs[0], refs[1], refs[2], refs[3:]
        if finish:
            sum_before, square_before, out_ref, held_ref, sems = refs
        else:
            sum_ref, square_ref, held_ref, sems = refs
        core, first, second = spot_ref[0], spot_ref[1], spot_ref[2]
        owner = 1 - core if finish else core
        copies = []
        for cut in range(cuts):
            for k, weight_ref in enumerate((gate_ref, up_ref)):
                start = pl.multiple_of(owner * half + cut * span, 128)
                copies.append(
                    pltpu.make_async_copy(
                        weight_ref.at[:, pl.ds(start, span)],
                        held_ref.at[pl.ds(k * units, units), pl.ds(cut * span, span)],
                        sems.at[cut, k],
                    )
                )
                copies[-1].start()
        if finish:
            pick = one_hot(swapped_rows(rows, line, side, first, second), rows)
        total = jnp.zeros((rows, 2 * units), jnp.float32)
        squares = jnp.zeros((rows, 128), jnp.float32)
        for cut in range(cuts):
            part = slice(cut * span, (cut + 1) * span)
            block = jnp.concatenate([ref[:, part] for ref in part_refs], axis=0)
            wide = block.astype(jnp.float32)
            if finish:
                wide = product(pick, block)
            for k in range(span // 128):
                lanes = wide[:, k * 128 : (k + 1) * 128]
                squares = squares + lanes * lanes
            start = pl.multiple_of(owner * half + cut * span, 128)
            scaled = (wide * gain_ref[:, pl.ds(start, span)]).astype(jnp.bfloat16)
            copies[2 * cut].wait()
            copies[2 * cut + 1].wait()
            total = total + lax.dot_general(
                scaled, held_ref[:, part], across, preferred_element_type=jnp.float32
            )
        if finish:
            total = total + sum_before[...]
            mean = jnp.sum(squares + square_before[...], axis=1, keepdims=True) / (2 * half)
            total = total * lax.rsqrt(mean + norm_eps)
            gate = total[:, :units]
            out_ref[...] = (gate / (1.0 + jnp.exp(-gate)) * total[:, units:]).astype(jnp.bfloat16)
        else:
            sum_ref[...] = total
            square_ref[...] = squares

    sums = [
        jax.ShapeDtypeStruct((rows, 2 * units), jnp.float32),
        jax.ShapeDtypeStruct((rows, 128), jnp.float32),
    ]
    return pl.pallas_call(
        kernel,
        in_specs=[in_smem] + [in_vmem] * (side + 1) + [in_hbm] * 2 + [in_vmem] * (2 * finish),
        out_specs=in_vmem if finish else [in_vmem] * 2,
        out_shape=jax.ShapeDtypeStruct((rows, units), jnp.bfloat16) if finish else sums,
        scratch_shapes=[
            pltpu.VMEM((2 * units, half), jnp.bfloat16),
            pltpu.SemaphoreType.DMA((cuts, 2)),
        ],
        compiler_params=budget(24),
        cost_estimate=pl.CostEstimate(
            flops=4 * rows * half * units, bytes_accessed=4 * half * units, transcendentals=0
        ),
    )(spot, *parts, gain[None, :], gate_weight.T, up_weight.T, *(before or []))


def swapped_rows(rows, line, side, first, second):
    chip_slots = line // side
    to = line_numbers(rows)
    along = (to // line + first) % side
    beside = to // chip_slots % side
    return ((beside - second + side) % side) * line + along * chip_slots + to % chip_slots


def feed_forward(inner, inner_other, pieces, spot, side):
    rows, units = inner.shape
    cut = pieces[0].shape[1]
    line = rows // side

    def kernel(spot_ref, inner_ref, other_ref, a_ref, b_ref, c_ref, d_ref, *outs):
        core, first, second, layer = spot_ref[0], spot_ref[1], spot_ref[2], spot_ref[3]
        pick = one_hot(swapped_rows(rows, line, side, first, second), rows)
        other = product(pick, other_ref[...]).astype(jnp.bfloat16)
        mine = inner_ref[...]
        same = core == layer % 2
        even = jnp.where(same, mine, other)
        odd = jnp.where(same, other, mine)
        for start, first_ref, second_ref in ((0, a_ref, b_ref), (cut, c_ref, d_ref)):
            result = product(even, first_ref[...]) + product(odd, second_ref[...])
            result = result.astype(jnp.bfloat16)
            for k in range(side):
                outs[k][:, start : start + cut] = result[k * line : (k + 1) * line]

    return pl.pallas_call(
        kernel,
        in_specs=[in_smem] + [in_vmem] * 6,
        out_specs=[in_vmem] * side,
        out_shape=[jax.ShapeDtypeStruct((line, 2 * cut), jnp.bfloat16)] * side,
        compiler_params=budget(24),
        cost_estimate=pl.CostEstimate(
            flops=8 * rows * units * cut, bytes_accessed=8 * units * cut, transcendentals=0
        ),
    )(spot, inner, inner_other, *pieces)


def on_device(
    layer_input,
    query,
    cache,
    lengths,
    counts,
    value_weight,
    output_weight,
    norm_gain,
    gate_weight,
    up_weight,
    down_weight,
    width,
):
    slots, model = layer_input.shape
    half = model // 2
    chips = width // 2

    heads_here, latent_width, head = value_weight.shape
    side = math.isqrt(chips)
    chip_slots = 2 * slots
    line = side * chip_slots
    place = lax.axis_index("tp")
    core = place % 2
    upper = core == 1
    at_y, at_x = place // (2 * side), place // 2 % side
    first, second = jnp.where(upper, at_x, at_y), jnp.where(upper, at_y, at_x)
    layer = lax.axis_index("dp")
    spot = jnp.stack([core, first, second, layer])

    pieces = down_pieces(down_weight, width)
    value_other = core_swap(value_weight, width)
    output_other = core_swap(output_weight, width)
    input_mine = lax.dynamic_slice_in_dim(layer_input, core * half, half, 1)
    input_other = core_swap(
        lax.dynamic_slice_in_dim(layer_input, (1 - core) * half, half, 1), width
    )
    input_chip = jnp.where(
        upper,
        jnp.concatenate([input_other, input_mine], axis=0),
        jnp.concatenate([input_mine, input_other], axis=0),
    ).astype(jnp.float32)

    latent = attend(query, cache, lengths, counts, latent_width, chips)
    arrived = between_chips(latent, width)
    arrived, pieces[0], pieces[1] = lax.optimization_barrier((arrived, pieces[0], pieces[1]))
    arrived_other = core_swap(arrived, width)
    attended_parts = project(
        arrived,
        arrived_other,
        value_weight,
        value_other,
        output_weight,
        output_other,
        spot,
        side,
        slots,
    )

    summed = total(turn(attended_parts, 0, side, 1)).reshape(side, chip_slots, half)
    own_rows = (jnp.arange(side) == second)[:, None, None]
    summed = summed + jnp.where(own_rows, input_chip[None], 0.0)
    summed = summed.astype(jnp.bfloat16).reshape(line, half)
    summed, pieces[2], pieces[3] = lax.optimization_barrier((summed, pieces[2], pieces[3]))
    residual_line = total(turn([summed] * side, 1, side, 1)).astype(jnp.bfloat16)
    residual_mine = turn([residual_line] * side, 0, side, -1)
    residual_other = [core_swap(part, width) for part in residual_mine]
    sums = gated(residual_mine, norm_gain, gate_weight, up_weight, spot, None)
    inner = gated(residual_other, norm_gain, gate_weight, up_weight, spot, sums)
    inner_other = core_swap(inner, width)

    feed_parts = feed_forward(inner, inner_other, pieces, spot, side)
    feed_line = total(turn(feed_parts, 0, side, 1)).astype(jnp.bfloat16)
    feed = total(
        turn(
            [
                lax.dynamic_slice_in_dim(
                    feed_line, (second + k) % side * chip_slots, chip_slots, 0
                )
                for k in range(side)
            ],
            1,
            side,
            1,
        )
    )
    residual = lax.dynamic_slice_in_dim(residual_line, second * chip_slots, chip_slots, 0)
    cut = half // 2
    feed = jnp.where(
        layer // 2 == 1, jnp.concatenate([feed[:, cut:], feed[:, :cut]], axis=1), feed
    )
    mixed = (residual.astype(jnp.float32) + feed).astype(jnp.bfloat16)
    kept = lax.dynamic_slice_in_dim(mixed, core * slots, slots, 0)
    got = core_swap(lax.dynamic_slice_in_dim(mixed, (1 - core) * slots, slots, 0), width)
    out = jnp.where(
        upper,
        jnp.concatenate([got, kept], axis=1),
        jnp.concatenate([kept, got], axis=1),
    )
    live = jnp.arange(slots, dtype=jnp.int32) < counts[0]
    return jnp.where(live[:, None], out, jnp.bfloat16(0.0))


def solution(mesh):
    placed = (
        P(("dp", "tp"), None),
        P(("dp", "tp"), None, None),
        P(("dp", "tp"), None, None),
        P(("dp", "tp")),
        P(("dp", "tp")),
        P("tp", None, None),
        P("tp", None),
        P(),
        P(None, "tp"),
        P(None, "tp"),
        P("tp", "dp"),
    )
    width = mesh.shape["tp"]
    return jax.shard_map(
        lambda *args: on_device(*args, width),
        mesh=mesh,
        in_specs=placed,
        out_specs=P(("dp", "tp"), None),
        check_vma=False,
    )
```

time: 167 us -> 113 us (0.68)
  waiting for transfers between devices: 80.4 us -> 27.8 us
  Pallas kernels: 0 us -> 23.5 us
  matrix products: 23.1 us -> 0 us
  local copies, waits for them, and re-layouts: 6.9 us -> 3.96 us
  starting transfers between devices: 52 us -> 53.7 us
    ppermute x4, waiting for transfers between devices: 28.3 us -> 4.02 us  [down_pieces(): out.append(lax.ppermute(down_weight, ('dp', 'tp'), pairs))]
    pallas_call x0 -> x5, Pallas kernels: none -> 23.5 us  [the longest x1 9.02 us: attend(): pl.pallas_call(kernel, in_specs=[in_smem, in_smem, in_vmem, in_hbm], out_...]
    ppermute x15, waiting for transfers between devices: 42.2 us -> 20.7 us  [turn(): out.append(lax.ppermute(parts[k], 'tp', pairs))]
    dot_general x11 -> x0, matrix products: 17.1 us -> none  [the longest x1 6.11 us: attend(): jnp.einsum('rht,rta->rha', attention, cache[:, :, :latent_width], preferr...]
    all_to_all x1, waiting for transfers between devices: 8.17 us -> 0.01 us  [between_chips(): return lax.all_to_all(x, 'tp', 0, 0, tiled=True, axis_index_groups=groups)]
    sub x1 -> x0, matrix products: 6.06 us -> none  [attend(): raised = jnp.where(visible, jnp.exp(scores - peak), jnp.float32(0.0))]
    dynamic_slice x2 -> x1, local copies, waits for them, and re-layouts: 2.95 us -> 0.02 us  [on_device(): lax.dynamic_slice_in_dim(feed_line, (second + k) % side * chip_slots, chi...]
    ppermute x15, starting transfers between devices: 16.8 us -> 19 us  [turn(): out.append(lax.ppermute(parts[k], 'tp', pairs))]
  transfers between devices with their start and end apart: 30 -> 30, of which waited for: 17 -> 16; matrix products, arithmetic and copies ran while one was open for 15% -> 0% of each run, Pallas kernels for 0% -> 15%
where the time goes in v4:
time: 113 us; the launch traced here: 112 us
  starting transfers between devices  53.7 us (48%)
  waiting for transfers between devices  27.8 us (25%)
  Pallas kernels  23.5 us (21%)
  local copies, waits for them, and re-layouts  3.96 us (4%)
  other arithmetic  2.23 us (2%)
    ppermute x15, waiting for transfers between devices, turn(): out.append(lax.ppermute(parts[k], 'tp', pairs))  20.7 us
    ppermute x15, starting transfers between devices, turn(): out.append(lax.ppermute(parts[k], 'tp', pairs))  19 us
    ppermute x10, starting transfers between devices, core_swap(): return lax.ppermute(x, 'tp', [(i, i ^ 1) for i in range(width)])  17 us
    ppermute x4, starting transfers between devices, down_pieces(): out.append(lax.ppermute(down_weight, ('dp', 'tp'), pairs))  10.9 us
    pallas_call x1, Pallas kernels, attend(): pl.pallas_call(kernel, in_specs=[in_smem, in_smem, in_vmem, in_hbm], out_...  9.02 us
    pallas_call x2, Pallas kernels, gated(): pl.pallas_call(kernel, in_specs=[in_smem] + [in_vmem] * (side + 1) + [in_...  6.81 us
    all_to_all x1, starting transfers between devices, between_chips(): return lax.all_to_all(x, 'tp', 0, 0, tiled=True, axis_index_groups=groups)  6.76 us
    pallas_call x1, Pallas kernels, project(): pl.pallas_call(kernel, in_specs=[in_smem] + [in_vmem] * 4 + [in_hbm] * 2,...  4.36 us
  transfers between devices with their start and end apart: 30, of which 16 were waited for; matrix products, arithmetic and copies ran while one was open for 0% of the time, Pallas kernels for 15%

profile of v4, /device:TPU:1, one launch (start us, length us, event | category | flops | bytes accessed | tf_op | source)
XLA Modules:
  0.0 112.0 jit_solution(3171490452178653374)
XLA Ops:
  1.4 3.5 %collective-permute-start = (bf16[288,1792]{1,0:T(8,128)(2,1)}, bf16[288,1792]{1,0:T(8,128)(2,1)S(1)}, u32[]{:S(2)}, u32[]{:S(2)}) collective-permute-start(bf16[288,1792]{1,0:T(8,128)(2,1)} %param.21), channel_id=1, source_target_pairs={{0,0},{64,1},{2,2},{66,3},{4,4},{68,5},{6,6},{70,7},{8,8},{72,9},{... | collective-permute-start | bytes 3096584 | tf_op jit(solution)/shard_map/ppermute | solution.py:55
  5.7 9.0 %shard_map.109 = bf16[256,512]{1,0:T(8,128)(2,1)} custom-call(s32[4]{0:T(128)} %lengths_ref.1, s32[1]{0:T(128)} %copy.12.counts_ref, bf16[4,64,576]{2,1,0:T(8,128)(2,1)} %q_ref.1, bf16[4,576,2048]{2,1,0:T(8,128)(2,1)} %bitcast.26), custom_call_target="tpu_custom_call" | custom-call | flops 1140850688 | bytes 9437184 | tf_op jit(solution)/shard_map/pallas_call | solution.py:127
  14.7 6.8 %all-to-all-start = ((bf16[16,16,512]{2,1,0:T(8,128)(2,1)}), bf16[16,16,512]{2,1,0:T(8,128)(2,1)S(1)}, u32[]{:S(2)}, u32[]{:S(2)}) async-start(bf16[16,16,512]{2,1,0:T(8,128)(2,1)} %bitcast.27), calls=%async_computation | async-start | bytes 524288 | tf_op jit(solution)/shard_map/all_to_all | solution.py:20
  21.5 6.9 %collective-permute-start.10 = (bf16[288,1792]{1,0:T(8,128)(2,1)}, bf16[288,1792]{1,0:T(8,128)(2,1)S(1)}, u32[]{:S(2)}, u32[]{:S(2)}) collective-permute-start(bf16[288,1792]{1,0:T(8,128)(2,1)} %param.21), channel_id=1, source_target_pairs={{33,0},{97,1},{35,2},{99,3},{37,4},{101,5},{39,6},{103,7},{41,8},{... | collective-permute-start | bytes 3096584 | tf_op jit(solution)/shard_map/ppermute | solution.py:55
  34.0 2.0 %copy-done.2 = bf16[256,7168]{1,0:T(8,128)(2,1)S(1)} copy-done((bf16[256,7168]{1,0:T(8,128)(2,1)S(1)}, bf16[256,7168]{1,0:T(8,128)(2,1)}, u32[]{:S(2)}) %copy-start.2) | copy-done | bytes 3670040
  37.0 4.4 %shard_map.110 = (bf16[32,3584]{1,0:T(8,128)(2,1)S(1)}, bf16[32,3584]{1,0:T(8,128)(2,1)S(1)}, bf16[32,3584]{1,0:T(8,128)(2,1)S(1)}, bf16[32,3584]{1,0:T(8,128)(2,1)S(1)}) custom-call(s32[4]{0:T(128)S(1)} %pad_add_fusion.spot_ref, bf16[256,512]{1,0:T(8,128)(2,1)S(1)} %bitcast.23, bf16[256,512]{1,0:T(8,128)(2,1)} %bitcast.8.other_ref, ...), custom_call_target="tpu_custom_call" | custom-call | flops 469762048 | bytes 3670016 | tf_op jit(solution)/shard_map/pallas_call | solution.py:196
  41.7 1.7 %collective-permute-start.6 = (bf16[32,3584]{1,0:T(8,128)(2,1)S(1)}, bf16[32,3584]{1,0:T(8,128)(2,1)S(1)}, u32[]{:S(2)}, u32[]{:S(2)}) collective-permute-start(bf16[32,3584]{1,0:T(8,128)(2,1)S(1)} %get-tuple-element.24), channel_id=1, source_target_pairs={{0,16},{1,5},{2,18},{3,7},{4,20},{5,1},{6,22},{7,3},{8,24},{9,13},... | collective-permute-start | bytes 688136 | tf_op jit(solution)/shard_map/ppermute | solution.py:35
  44.6 5.7 %collective-permute-done.5 = bf16[32,3584]{1,0:T(8,128)(2,1)S(1)} collective-permute-done((bf16[32,3584]{1,0:T(8,128)(2,1)S(1)}, bf16[32,3584]{1,0:T(8,128)(2,1)S(1)}, u32[]{:S(2)}, u32[]{:S(2)}) %collective-permute-start.5) | collective-permute-done | bytes 229408 | tf_op jit(solution)/shard_map/ppermute | solution.py:35
  54.0 2.6 %collective-permute-start.12 = (bf16[32,3584]{1,0:T(8,128)(2,1)S(1)}, bf16[32,3584]{1,0:T(8,128)(2,1)S(1)}, u32[]{:S(2)}, u32[]{:S(2)}) collective-permute-start(bf16[32,3584]{1,0:T(8,128)(2,1)S(1)} %fusion.1), channel_id=1, source_target_pairs={{0,4},{1,17},{2,6},{3,19},{4,0},{5,21},{6,2},{7,23},{8,12},{9,25},... | collective-permute-start | bytes 688136 | tf_op jit(solution)/shard_map/ppermute | solution.py:35
  59.1 3.6 %collective-permute-done.12 = bf16[32,3584]{1,0:T(8,128)(2,1)S(1)} collective-permute-done((bf16[32,3584]{1,0:T(8,128)(2,1)S(1)}, bf16[32,3584]{1,0:T(8,128)(2,1)S(1)}, u32[]{:S(2)}, u32[]{:S(2)}) %collective-permute-start.12) | collective-permute-done | bytes 229408 | tf_op jit(solution)/shard_map/ppermute | solution.py:35
  62.9 2.3 %collective-permute-start.15 = (bf16[32,3584]{1,0:T(8,128)(2,1)S(1)}, bf16[32,3584]{1,0:T(8,128)(2,1)S(1)}, u32[]{:S(2)}, u32[]{:S(2)}) collective-permute-start(bf16[32,3584]{1,0:T(8,128)(2,1)S(1)} %add_convert_fusion.1.refs_0_), channel_id=1, source_target_pairs={{0,24},{1,7},{2,26},{3,1},{4,28},{5,3},{6,30},{7,5},{8,0},{9,15},{... | collective-permute-start | bytes 688136 | tf_op jit(solution)/shard_map/ppermute | solution.py:35
  66.3 3.0 %collective-permute-start.14 = (bf16[32,3584]{1,0:T(8,128)(2,1)S(1)}, bf16[32,3584]{1,0:T(8,128)(2,1)S(1)}, u32[]{:S(2)}, u32[]{:S(2)}) collective-permute-start(bf16[32,3584]{1,0:T(8,128)(2,1)S(1)} %add_convert_fusion.1.refs_0_), channel_id=1, source_target_pairs={{0,1},{1,0},{2,3},{3,2},{4,5},{5,4},{6,7},{7,6},{8,9},{9,8},{10,11... | collective-permute-start | bytes 688136 | tf_op jit(solution)/shard_map/ppermute | solution.py:15
  70.6 3.1 %collective-permute-start.16 = (bf16[32,3584]{1,0:T(8,128)(2,1)S(1)}, bf16[32,3584]{1,0:T(8,128)(2,1)S(1)}, u32[]{:S(2)}, u32[]{:S(2)}) collective-permute-start(bf16[32,3584]{1,0:T(8,128)(2,1)S(1)} %collective-permute-done.15.refs_1_), channel_id=1, source_target_pairs={{0,1},{1,0},{2,3},{3,2},{4,5},{5,4},{6,7},{7,6},{8,9},{9,8},{10,11... | collective-permute-start | bytes 688136 | tf_op jit(solution)/shard_map/ppermute | solution.py:15
  73.7 1.6 %collective-permute-start.18 = (bf16[32,3584]{1,0:T(8,128)(2,1)S(1)}, bf16[32,3584]{1,0:T(8,128)(2,1)S(1)}, u32[]{:S(2)}, u32[]{:S(2)}) collective-permute-start(bf16[32,3584]{1,0:T(8,128)(2,1)S(1)} %collective-permute-done.17.refs_2_), channel_id=1, source_target_pairs={{0,1},{1,0},{2,3},{3,2},{4,5},{5,4},{6,7},{7,6},{8,9},{9,8},{10,11... | collective-permute-start | bytes 688136 | tf_op jit(solution)/shard_map/ppermute | solution.py:15
  75.3 2.4 %collective-permute-start.20 = (bf16[32,3584]{1,0:T(8,128)(2,1)S(1)}, bf16[32,3584]{1,0:T(8,128)(2,1)S(1)}, u32[]{:S(2)}, u32[]{:S(2)}) collective-permute-start(bf16[32,3584]{1,0:T(8,128)(2,1)S(1)} %collective-permute-done.19.refs_3_), channel_id=1, source_target_pairs={{0,1},{1,0},{2,3},{3,2},{4,5},{5,4},{6,7},{7,6},{8,9},{9,8},{10,11... | collective-permute-start | bytes 688136 | tf_op jit(solution)/shard_map/ppermute | solution.py:15
  77.7 3.1 %shard_map.111 = (f32[128,576]{1,0:T(8,128)S(1)}, f32[128,128]{1,0:T(8,128)S(1)}) custom-call(s32[4]{0:T(128)S(1)} %pad_add_fusion.spot_ref, bf16[32,3584]{1,0:T(8,128)(2,1)S(1)} %add_convert_fusion.1.refs_0_, bf16[32,3584]{1,0:T(8,128)(2,1)S(1)} %collective-permute-done.15.refs_1_, bf16[32,3584]{1,0:T(8,128)(2,1)S(1)} %collective-permute-done.17.refs_2_, ...), custom_call_target="tpu_custom_call" | custom-call | flops 528482304 | bytes 4128768 | tf_op jit(solution)/shard_map/pallas_call | solution.py:284
  80.9 3.7 %shard_map.112.inner_ref = bf16[128,288]{1,0:T(8,128)(2,1)S(1)} custom-call(s32[4]{0:T(128)S(1)} %pad_add_fusion.spot_ref, bf16[32,3584]{1,0:T(8,128)(2,1)S(1)} %collective-permute-done.14.refs_0_, bf16[32,3584]{1,0:T(8,128)(2,1)S(1)} %collective-permute-done.16.refs_1_, bf16[32,3584]{1,0:T(8,128)(2,1)S(1)} %collective-permute-done.18.refs_2_, ...), custom_call_target="tpu_custom_call" | custom-call | flops 528482304 | bytes 4128768 | tf_op jit(solution)/shard_map/pallas_call | solution.py:284
  85.9 3.3 %shard_map.113 = (bf16[32,3584]{1,0:T(8,128)(2,1)S(1)}, bf16[32,3584]{1,0:T(8,128)(2,1)}, bf16[32,3584]{1,0:T(8,128)(2,1)}, bf16[32,3584]{1,0:T(8,128)(2,1)}) custom-call(s32[4]{0:T(128)S(1)} %pad_add_fusion.spot_ref, bf16[128,288]{1,0:T(8,128)(2,1)S(1)} %shard_map.112.inner_ref, bf16[128,288]{1,0:T(8,128)(2,1)S(1)} %collective-permute-done.21.other_ref, ...), custom_call_target="tpu_custom_call" | custom-call | flops 528482304 | bytes 4128768 | tf_op jit(solution)/shard_map/pallas_call | solution.py:327
  91.6 1.8 %collective-permute-start.23 = (bf16[32,3584]{1,0:T(8,128)(2,1)}, bf16[32,3584]{1,0:T(8,128)(2,1)S(1)}, u32[]{:S(2)}, u32[]{:S(2)}) collective-permute-start(bf16[32,3584]{1,0:T(8,128)(2,1)} %get-tuple-element.35), channel_id=1, source_target_pairs={{0,16},{1,5},{2,18},{3,7},{4,20},{5,1},{6,22},{7,3},{8,24},{9,13},... | collective-permute-start | bytes 688136 | tf_op jit(solution)/shard_map/ppermute | solution.py:35
  94.7 1.9 %collective-permute-done.22 = bf16[32,3584]{1,0:T(8,128)(2,1)S(1)} collective-permute-done((bf16[32,3584]{1,0:T(8,128)(2,1)}, bf16[32,3584]{1,0:T(8,128)(2,1)S(1)}, u32[]{:S(2)}, u32[]{:S(2)}) %collective-permute-start.22) | collective-permute-done | bytes 229408 | tf_op jit(solution)/shard_map/ppermute | solution.py:35
  96.5 2.9 %collective-permute-done.23 = bf16[32,3584]{1,0:T(8,128)(2,1)S(1)} collective-permute-done((bf16[32,3584]{1,0:T(8,128)(2,1)}, bf16[32,3584]{1,0:T(8,128)(2,1)S(1)}, u32[]{:S(2)}, u32[]{:S(2)}) %collective-permute-start.23) | collective-permute-done | bytes 229408 | tf_op jit(solution)/shard_map/ppermute | solution.py:35
  100.7 1.7 %collective-permute-start.26 = (bf16[8,3584]{1,0:T(8,128)(2,1)S(1)}, bf16[8,3584]{1,0:T(8,128)(2,1)S(1)}, u32[]{:S(2)}, u32[]{:S(2)}) collective-permute-start(bf16[8,3584]{1,0:T(8,128)(2,1)S(1)} %get-tuple-element.39), channel_id=1, source_target_pairs={{0,4},{1,17},{2,6},{3,19},{4,0},{5,21},{6,2},{7,23},{8,12},{9,25},... | collective-permute-start | bytes 172040 | tf_op jit(solution)/shard_map/ppermute | solution.py:35
  103.4 2.2 %collective-permute-done.25 = bf16[8,3584]{1,0:T(8,128)(2,1)S(1)} collective-permute-done((bf16[8,3584]{1,0:T(8,128)(2,1)S(1)}, bf16[8,3584]{1,0:T(8,128)(2,1)S(1)}, u32[]{:S(2)}, u32[]{:S(2)}) %collective-permute-start.25) | collective-permute-done | bytes 57376 | tf_op jit(solution)/shard_map/ppermute | solution.py:35
  106.6 3.9 %collective-permute-start.28 = (bf16[4,3584]{1,0:T(4,128)(2,1)S(1)}, bf16[4,3584]{1,0:T(4,128)(2,1)S(1)}, u32[]{:S(2)}, u32[]{:S(2)}) collective-permute-start(bf16[4,3584]{1,0:T(4,128)(2,1)S(1)} %get-tuple-element.42), channel_id=1, source_target_pairs={{0,1},{1,0},{2,3},{3,2},{4,5},{5,4},{6,7},{7,6},{8,9},{9,8},{10,11... | collective-permute-start | bytes 86024 | tf_op jit(solution)/shard_map/ppermute | solution.py:15
  (71 shorter events, 28.0 us)
Async XLA Ops:
  0.0 34.0 %collective-permute-start.4 = (bf16[256,7168]{1,0:T(8,128)(2,1)}, bf16[256,7168]{1,0:T(8,128)(2,1)}, u32[]{:S(2)}, u32[]{:S(2)}) collective-permute-start(bf16[256,7168]{1,0:T(8,128)(2,1)} %om_ref.1), channel_id=1, source_target_pairs={{0,1},{1,0},{2,3},{3,2},{4,5},{5,4},{6,7},{7,6},{8,9},{9,8},{10,11... | collective-permute-start | bytes 11010056 | tf_op jit(solution)/shard_map/ppermute | solution.py:15
  1.4 28.6 %collective-permute-start = (bf16[288,1792]{1,0:T(8,128)(2,1)}, bf16[288,1792]{1,0:T(8,128)(2,1)S(1)}, u32[]{:S(2)}, u32[]{:S(2)}) collective-permute-start(bf16[288,1792]{1,0:T(8,128)(2,1)} %param.21), channel_id=1, source_target_pairs={{0,0},{64,1},{2,2},{66,3},{4,4},{68,5},{6,6},{70,7},{8,8},{72,9},{... | collective-permute-start | bytes 3096584 | tf_op jit(solution)/shard_map/ppermute | solution.py:55
  4.9 26.4 %collective-permute-start.1 = (bf16[288,1792]{1,0:T(8,128)(2,1)}, bf16[288,1792]{1,0:T(8,128)(2,1)S(1)}, u32[]{:S(2)}, u32[]{:S(2)}) collective-permute-start(bf16[288,1792]{1,0:T(8,128)(2,1)} %param.21), channel_id=1, source_target_pairs={{1,0},{65,1},{3,2},{67,3},{5,4},{69,5},{7,6},{71,7},{9,8},{73,9},{... | collective-permute-start | bytes 3096584 | tf_op jit(solution)/shard_map/ppermute | solution.py:55
  14.7 15.3 %all-to-all-start = ((bf16[16,16,512]{2,1,0:T(8,128)(2,1)}), bf16[16,16,512]{2,1,0:T(8,128)(2,1)S(1)}, u32[]{:S(2)}, u32[]{:S(2)}) async-start(bf16[16,16,512]{2,1,0:T(8,128)(2,1)} %bitcast.27), calls=%async_computation | async-start | bytes 524288 | tf_op jit(solution)/shard_map/all_to_all | solution.py:20
  21.5 29.7 %collective-permute-start.10 = (bf16[288,1792]{1,0:T(8,128)(2,1)}, bf16[288,1792]{1,0:T(8,128)(2,1)S(1)}, u32[]{:S(2)}, u32[]{:S(2)}) collective-permute-start(bf16[288,1792]{1,0:T(8,128)(2,1)} %param.21), channel_id=1, source_target_pairs={{33,0},{97,1},{35,2},{99,3},{37,4},{101,5},{39,6},{103,7},{41,8},{... | collective-permute-start | bytes 3096584 | tf_op jit(solution)/shard_map/ppermute | solution.py:55
  28.4 24.3 %collective-permute-start.9 = (bf16[288,1792]{1,0:T(8,128)(2,1)}, bf16[288,1792]{1,0:T(8,128)(2,1)}, u32[]{:S(2)}, u32[]{:S(2)}) collective-permute-start(bf16[288,1792]{1,0:T(8,128)(2,1)} %param.21), channel_id=1, source_target_pairs={{32,0},{96,1},{34,2},{98,3},{36,4},{100,5},{38,6},{102,7},{40,8},{... | collective-permute-start | bytes 3096584 | tf_op jit(solution)/shard_map/ppermute | solution.py:55
  33.1 10.4 %collective-permute-start.8 = (bf16[4,3584]{1,0:T(4,128)(2,1)S(1)}, bf16[4,3584]{1,0:T(4,128)(2,1)S(1)}, u32[]{:S(2)}, u32[]{:S(2)}) collective-permute-start(bf16[4,3584]{1,0:T(4,128)(2,1)S(1)} %get-tuple-element.44), channel_id=1, source_target_pairs={{0,1},{1,0},{2,3},{3,2},{4,5},{5,4},{6,7},{7,6},{8,9},{9,8},{10,11... | collective-permute-start | bytes 86024 | tf_op jit(solution)/shard_map/ppermute | solution.py:15
  41.4 8.9 %collective-permute-start.5 = (bf16[32,3584]{1,0:T(8,128)(2,1)S(1)}, bf16[32,3584]{1,0:T(8,128)(2,1)S(1)}, u32[]{:S(2)}, u32[]{:S(2)}) collective-permute-start(bf16[32,3584]{1,0:T(8,128)(2,1)S(1)} %get-tuple-element.23), channel_id=1, source_target_pairs={{0,8},{1,3},{2,10},{3,5},{4,12},{5,7},{6,14},{7,1},{8,16},{9,11},{... | collective-permute-start | bytes 688136 | tf_op jit(solution)/shard_map/ppermute | solution.py:35
  41.7 8.6 %collective-permute-start.6 = (bf16[32,3584]{1,0:T(8,128)(2,1)S(1)}, bf16[32,3584]{1,0:T(8,128)(2,1)S(1)}, u32[]{:S(2)}, u32[]{:S(2)}) collective-permute-start(bf16[32,3584]{1,0:T(8,128)(2,1)S(1)} %get-tuple-element.24), channel_id=1, source_target_pairs={{0,16},{1,5},{2,18},{3,7},{4,20},{5,1},{6,22},{7,3},{8,24},{9,13},... | collective-permute-start | bytes 688136 | tf_op jit(solution)/shard_map/ppermute | solution.py:35
  43.5 7.6 %collective-permute-start.7 = (bf16[32,3584]{1,0:T(8,128)(2,1)S(1)}, bf16[32,3584]{1,0:T(8,128)(2,1)S(1)}, u32[]{:S(2)}, u32[]{:S(2)}) collective-permute-start(bf16[32,3584]{1,0:T(8,128)(2,1)S(1)} %get-tuple-element.25), channel_id=1, source_target_pairs={{0,24},{1,7},{2,26},{3,1},{4,28},{5,3},{6,30},{7,5},{8,0},{9,15},{... | collective-permute-start | bytes 688136 | tf_op jit(solution)/shard_map/ppermute | solution.py:35
  52.7 6.4 %collective-permute-start.11 = (bf16[32,3584]{1,0:T(8,128)(2,1)S(1)}, bf16[32,3584]{1,0:T(8,128)(2,1)S(1)}, u32[]{:S(2)}, u32[]{:S(2)}) collective-permute-start(bf16[32,3584]{1,0:T(8,128)(2,1)S(1)} %fusion.1), channel_id=1, source_target_pairs={{0,2},{1,9},{2,4},{3,11},{4,6},{5,13},{6,0},{7,15},{8,10},{9,17},{... | collective-permute-start | bytes 688136 | tf_op jit(solution)/shard_map/ppermute | solution.py:35
  54.0 8.8 %collective-permute-start.12 = (bf16[32,3584]{1,0:T(8,128)(2,1)S(1)}, bf16[32,3584]{1,0:T(8,128)(2,1)S(1)}, u32[]{:S(2)}, u32[]{:S(2)}) collective-permute-start(bf16[32,3584]{1,0:T(8,128)(2,1)S(1)} %fusion.1), channel_id=1, source_target_pairs={{0,4},{1,17},{2,6},{3,19},{4,0},{5,21},{6,2},{7,23},{8,12},{9,25},... | collective-permute-start | bytes 688136 | tf_op jit(solution)/shard_map/ppermute | solution.py:35
  56.6 6.2 %collective-permute-start.13 = (bf16[32,3584]{1,0:T(8,128)(2,1)S(1)}, bf16[32,3584]{1,0:T(8,128)(2,1)S(1)}, u32[]{:S(2)}, u32[]{:S(2)}) collective-permute-start(bf16[32,3584]{1,0:T(8,128)(2,1)S(1)} %fusion.1), channel_id=1, source_target_pairs={{0,6},{1,25},{2,0},{3,27},{4,2},{5,29},{6,4},{7,31},{8,14},{9,1},{... | collective-permute-start | bytes 688136 | tf_op jit(solution)/shard_map/ppermute | solution.py:35
  62.9 7.7 %collective-permute-start.15 = (bf16[32,3584]{1,0:T(8,128)(2,1)S(1)}, bf16[32,3584]{1,0:T(8,128)(2,1)S(1)}, u32[]{:S(2)}, u32[]{:S(2)}) collective-permute-start(bf16[32,3584]{1,0:T(8,128)(2,1)S(1)} %add_convert_fusion.1.refs_0_), channel_id=1, source_target_pairs={{0,24},{1,7},{2,26},{3,1},{4,28},{5,3},{6,30},{7,5},{8,0},{9,15},{... | collective-permute-start | bytes 688136 | tf_op jit(solution)/shard_map/ppermute | solution.py:35
  65.1 8.6 %collective-permute-start.17 = (bf16[32,3584]{1,0:T(8,128)(2,1)S(1)}, bf16[32,3584]{1,0:T(8,128)(2,1)S(1)}, u32[]{:S(2)}, u32[]{:S(2)}) collective-permute-start(bf16[32,3584]{1,0:T(8,128)(2,1)S(1)} %add_convert_fusion.1.refs_0_), channel_id=1, source_target_pairs={{0,16},{1,5},{2,18},{3,7},{4,20},{5,1},{6,22},{7,3},{8,24},{9,13},... | collective-permute-start | bytes 688136 | tf_op jit(solution)/shard_map/ppermute | solution.py:35
  65.7 9.7 %collective-permute-start.19 = (bf16[32,3584]{1,0:T(8,128)(2,1)S(1)}, bf16[32,3584]{1,0:T(8,128)(2,1)S(1)}, u32[]{:S(2)}, u32[]{:S(2)}) collective-permute-start(bf16[32,3584]{1,0:T(8,128)(2,1)S(1)} %add_convert_fusion.1.refs_0_), channel_id=1, source_target_pairs={{0,8},{1,3},{2,10},{3,5},{4,12},{5,7},{6,14},{7,1},{8,16},{9,11},{... | collective-permute-start | bytes 688136 | tf_op jit(solution)/shard_map/ppermute | solution.py:35
  66.3 14.6 %collective-permute-start.14 = (bf16[32,3584]{1,0:T(8,128)(2,1)S(1)}, bf16[32,3584]{1,0:T(8,128)(2,1)S(1)}, u32[]{:S(2)}, u32[]{:S(2)}) collective-permute-start(bf16[32,3584]{1,0:T(8,128)(2,1)S(1)} %add_convert_fusion.1.refs_0_), channel_id=1, source_target_pairs={{0,1},{1,0},{2,3},{3,2},{4,5},{5,4},{6,7},{7,6},{8,9},{9,8},{10,11... | collective-permute-start | bytes 688136 | tf_op jit(solution)/shard_map/ppermute | solution.py:15
  70.6 10.3 %collective-permute-start.16 = (bf16[32,3584]{1,0:T(8,128)(2,1)S(1)}, bf16[32,3584]{1,0:T(8,128)(2,1)S(1)}, u32[]{:S(2)}, u32[]{:S(2)}) collective-permute-start(bf16[32,3584]{1,0:T(8,128)(2,1)S(1)} %collective-permute-done.15.refs_1_), channel_id=1, source_target_pairs={{0,1},{1,0},{2,3},{3,2},{4,5},{5,4},{6,7},{7,6},{8,9},{9,8},{10,11... | collective-permute-start | bytes 688136 | tf_op jit(solution)/shard_map/ppermute | solution.py:15
  73.7 7.2 %collective-permute-start.18 = (bf16[32,3584]{1,0:T(8,128)(2,1)S(1)}, bf16[32,3584]{1,0:T(8,128)(2,1)S(1)}, u32[]{:S(2)}, u32[]{:S(2)}) collective-permute-start(bf16[32,3584]{1,0:T(8,128)(2,1)S(1)} %collective-permute-done.17.refs_2_), channel_id=1, source_target_pairs={{0,1},{1,0},{2,3},{3,2},{4,5},{5,4},{6,7},{7,6},{8,9},{9,8},{10,11... | collective-permute-start | bytes 688136 | tf_op jit(solution)/shard_map/ppermute | solution.py:15
  75.3 5.5 %collective-permute-start.20 = (bf16[32,3584]{1,0:T(8,128)(2,1)S(1)}, bf16[32,3584]{1,0:T(8,128)(2,1)S(1)}, u32[]{:S(2)}, u32[]{:S(2)}) collective-permute-start(bf16[32,3584]{1,0:T(8,128)(2,1)S(1)} %collective-permute-done.19.refs_3_), channel_id=1, source_target_pairs={{0,1},{1,0},{2,3},{3,2},{4,5},{5,4},{6,7},{7,6},{8,9},{9,8},{10,11... | collective-permute-start | bytes 688136 | tf_op jit(solution)/shard_map/ppermute | solution.py:15
  89.9 6.6 %collective-permute-start.22 = (bf16[32,3584]{1,0:T(8,128)(2,1)}, bf16[32,3584]{1,0:T(8,128)(2,1)S(1)}, u32[]{:S(2)}, u32[]{:S(2)}) collective-permute-start(bf16[32,3584]{1,0:T(8,128)(2,1)} %get-tuple-element.34), channel_id=1, source_target_pairs={{0,8},{1,3},{2,10},{3,5},{4,12},{5,7},{6,14},{7,1},{8,16},{9,11},{... | collective-permute-start | bytes 688136 | tf_op jit(solution)/shard_map/ppermute | solution.py:35
  91.6 7.9 %collective-permute-start.23 = (bf16[32,3584]{1,0:T(8,128)(2,1)}, bf16[32,3584]{1,0:T(8,128)(2,1)S(1)}, u32[]{:S(2)}, u32[]{:S(2)}) collective-permute-start(bf16[32,3584]{1,0:T(8,128)(2,1)} %get-tuple-element.35), channel_id=1, source_target_pairs={{0,16},{1,5},{2,18},{3,7},{4,20},{5,1},{6,22},{7,3},{8,24},{9,13},... | collective-permute-start | bytes 688136 | tf_op jit(solution)/shard_map/ppermute | solution.py:35
  93.4 6.2 %collective-permute-start.24 = (bf16[32,3584]{1,0:T(8,128)(2,1)}, bf16[32,3584]{1,0:T(8,128)(2,1)S(1)}, u32[]{:S(2)}, u32[]{:S(2)}) collective-permute-start(bf16[32,3584]{1,0:T(8,128)(2,1)} %get-tuple-element.36), channel_id=1, source_target_pairs={{0,24},{1,7},{2,26},{3,1},{4,28},{5,3},{6,30},{7,5},{8,0},{9,15},{... | collective-permute-start | bytes 688136 | tf_op jit(solution)/shard_map/ppermute | solution.py:35
  100.7 4.9 %collective-permute-start.25 = (bf16[8,3584]{1,0:T(8,128)(2,1)S(1)}, bf16[8,3584]{1,0:T(8,128)(2,1)S(1)}, u32[]{:S(2)}, u32[]{:S(2)}) collective-permute-start(bf16[8,3584]{1,0:T(8,128)(2,1)S(1)} %get-tuple-element.37), channel_id=1, source_target_pairs={{0,2},{1,9},{2,4},{3,11},{4,6},{5,13},{6,0},{7,15},{8,10},{9,17},{... | collective-permute-start | bytes 172040 | tf_op jit(solution)/shard_map/ppermute | solution.py:35
  (13 other events, 173.4 us)

commit v5 on v4

--- a/solution.py
+++ b/solution.py
@@ -133,7 +133,7 @@
             pltpu.VMEM((slots, wide, ctx), jnp.bfloat16),
             pltpu.SemaphoreType.DMA((slots,)),
         ],
-        compiler_params=budget(60),
+        compiler_params=budget(57),
         cost_estimate=pl.CostEstimate(
             flops=2 * rows * ctx * (wide + latent_width),
             bytes_accessed=2 * cache.size,
@@ -152,24 +152,9 @@
     rows = 2 * chips * slots
     line = rows // side
     lines = chips * pairs
-    cuts = 4
-    span = half // cuts
-
-    def kernel(spot_ref, mine_ref, other_ref, vm_ref, vo_ref, om_ref, oo_ref, *refs):
-        outs, (held_ref, sems) = refs[:side], refs[side:]
+
+    def kernel(spot_ref, mine_ref, other_ref, vm_ref, vo_ref, om_ref, oo_ref, *outs):
         core, first = spot_ref[0], spot_ref[1]
-        copies = []
-        for cut in range(cuts):
-            for k, weight_ref in enumerate((om_ref, oo_ref)):
-                start = pl.multiple_of(core * half + cut * span, 128)
-                copies.append(
-                    pltpu.make_async_copy(
-                        weight_ref.at[:, pl.ds(start, span)],
-                        held_ref.at[pl.ds(k * depth, depth), pl.ds(cut * span, span)],
-                        sems.at[cut, k],
-                    )
-                )
-                copies[-1].start()
         to = line_numbers(rows)
         along = (to // line + first) % side
         second = to // (2 * slots) % side
@@ -185,23 +170,17 @@
             picked = product(pick, latents).astype(jnp.bfloat16)
             values.append(product(picked, weight_ref[place]).astype(jnp.bfloat16))
         values = jnp.concatenate(values, axis=1)
-        for cut in range(cuts):
-            copies[2 * cut].wait()
-            copies[2 * cut + 1].wait()
-            part = slice(cut * span, (cut + 1) * span)
-            result = product(values, held_ref[:, part]).astype(jnp.bfloat16)
-            for k in range(side):
-                outs[k][:, part] = result[k * line : (k + 1) * line]
+        at = pl.ds(pl.multiple_of(core * half, 128), half)
+        result = product(values[:, :depth], om_ref[:, at]) + product(values[:, depth:], oo_ref[:, at])
+        result = result.astype(jnp.bfloat16)
+        for k in range(side):
+            outs[k][...] = result[k * line : (k + 1) * line]
 
     return pl.pallas_call(
         kernel,
-        in_specs=[in_smem] + [in_vmem] * 4 + [in_hbm] * 2,
+        in_specs=[in_smem] + [in_vmem] * 6,
         out_specs=[in_vmem] * side,
         out_shape=[jax.ShapeDtypeStruct((line, half), jnp.bfloat16)] * side,
-        scratch_shapes=[
-            pltpu.VMEM((2 * depth, half), jnp.bfloat16),
-            pltpu.SemaphoreType.DMA((cuts, 2)),
-        ],
         compiler_params=budget(24),
         cost_estimate=pl.CostEstimate(
             flops=4 * rows * depth * half, bytes_accessed=4 * depth * half, transcendentals=0
@@ -222,51 +201,31 @@
     line, half = parts[0].shape
     rows = side * line
     units = gate_weight.shape[1]
-    cuts = 4
-    span = half // cuts
     finish = before is not None
 
     def kernel(spot_ref, *refs):
         part_refs, refs = refs[:side], refs[side:]
         gain_ref, gate_ref, up_ref, refs = refs[0], refs[1], refs[2], refs[3:]
         if finish:
-            sum_before, square_before, out_ref, held_ref, sems = refs
+            sum_before, square_before, out_ref = refs
         else:
-            sum_ref, square_ref, held_ref, sems = refs
+            sum_ref, square_ref = refs
         core, first, second = spot_ref[0], spot_ref[1], spot_ref[2]
         owner = 1 - core if finish else core
-        copies = []
-        for cut in range(cuts):
-            for k, weight_ref in enumerate((gate_ref, up_ref)):
-                start = pl.multiple_of(owner * half + cut * span, 128)
-                copies.append(
-                    pltpu.make_async_copy(
-                        weight_ref.at[:, pl.ds(start, span)],
-                        held_ref.at[pl.ds(k * units, units), pl.ds(cut * span, span)],
-                        sems.at[cut, k],
-                    )
-                )
-                copies[-1].start()
+        at = pl.ds(pl.multiple_of(owner * half, 128), half)
+        block = jnp.concatenate([ref[...] for ref in part_refs], axis=0)
         if finish:
-            pick = one_hot(swapped_rows(rows, line, side, first, second), rows)
-        total = jnp.zeros((rows, 2 * units), jnp.float32)
+            wide = product(one_hot(swapped_rows(rows, line, side, first, second), rows), block)
+        else:
+            wide = block.astype(jnp.float32)
         squares = jnp.zeros((rows, 128), jnp.float32)
-        for cut in range(cuts):
-            part = slice(cut * span, (cut + 1) * span)
-            block = jnp.concatenate([ref[:, part] for ref in part_refs], axis=0)
-            wide = block.astype(jnp.float32)
-            if finish:
-                wide = product(pick, block)
-            for k in range(span // 128):
-                lanes = wide[:, k * 128 : (k + 1) * 128]
-                squares = squares + lanes * lanes
-            start = pl.multiple_of(owner * half + cut * span, 128)
-            scaled = (wide * gain_ref[:, pl.ds(start, span)]).astype(jnp.bfloat16)
-            copies[2 * cut].wait()
-            copies[2 * cut + 1].wait()
-            total = total + lax.dot_general(
-                scaled, held_ref[:, part], across, preferred_element_type=jnp.float32
-            )
+        for k in range(half // 128):
+            lanes = wide[:, k * 128 : (k + 1) * 128]
+            squares = squares + lanes * lanes
+        scaled = (wide * gain_ref[:, at]).astype(jnp.bfloat16).T
+        total = jnp.concatenate(
+            [product(gate_ref[:, at], scaled), product(up_ref[:, at], scaled)], axis=0
+        ).T
         if finish:
             total = total + sum_before[...]
             mean = jnp.sum(squares + square_before[...], axis=1, keepdims=True) / (2 * half)
@@ -283,13 +242,9 @@
     ]
     return pl.pallas_call(
         kernel,
-        in_specs=[in_smem] + [in_vmem] * (side + 1) + [in_hbm] * 2 + [in_vmem] * (2 * finish),
+        in_specs=[in_smem] + [in_vmem] * (side + 3 + 2 * finish),
         out_specs=in_vmem if finish else [in_vmem] * 2,
         out_shape=jax.ShapeDtypeStruct((rows, units), jnp.bfloat16) if finish else sums,
-        scratch_shapes=[
-            pltpu.VMEM((2 * units, half), jnp.bfloat16),
-            pltpu.SemaphoreType.DMA((cuts, 2)),
-        ],
         compiler_params=budget(24),
         cost_estimate=pl.CostEstimate(
             flops=4 * rows * half * units, bytes_accessed=4 * half * units, transcendentals=0

time: 113 us -> 110 us (0.973)
  Pallas kernels: 23.5 us -> 20.5 us
    pallas_call x3, Pallas kernels: 11.2 us -> 8.17 us  [the longest x2 4.18 us: gated(): pl.pallas_call(kernel, in_specs=[in_smem] + [in_vmem] * (side + 3 + 2 * f...]
  transfers between devices with their start and end apart: 30 -> 30, of which waited for: 16 -> 16; matrix products, arithmetic and copies ran while one was open for 0% -> 0% of each run, Pallas kernels for 15% -> 14%
where the time goes in v5:
time: 110 us; the launch traced here: 109 us
  starting transfers between devices  53.7 us (49%)
  waiting for transfers between devices  28.1 us (26%)
  Pallas kernels  20.5 us (19%)
  local copies, waits for them, and re-layouts  3.96 us (4%)
  other arithmetic  2.23 us (2%)
    ppermute x15, waiting for transfers between devices, turn(): out.append(lax.ppermute(parts[k], 'tp', pairs))  20.7 us
    ppermute x15, starting transfers between devices, turn(): out.append(lax.ppermute(parts[k], 'tp', pairs))  19 us
    ppermute x10, starting transfers between devices, core_swap(): return lax.ppermute(x, 'tp', [(i, i ^ 1) for i in range(width)])  16.9 us
    ppermute x4, starting transfers between devices, down_pieces(): out.append(lax.ppermute(down_weight, ('dp', 'tp'), pairs))  10.9 us
    pallas_call x1, Pallas kernels, attend(): pl.pallas_call(kernel, in_specs=[in_smem, in_smem, in_vmem, in_hbm], out_...  9.02 us
    all_to_all x1, starting transfers between devices, between_chips(): return lax.all_to_all(x, 'tp', 0, 0, tiled=True, axis_index_groups=groups)  6.76 us
    ppermute x4, waiting for transfers between devices, down_pieces(): out.append(lax.ppermute(down_weight, ('dp', 'tp'), pairs))  4.38 us
    pallas_call x2, Pallas kernels, gated(): pl.pallas_call(kernel, in_specs=[in_smem] + [in_vmem] * (side + 3 + 2 * f...  4.18 us
  transfers between devices with their start and end apart: 30, of which 16 were waited for; matrix products, arithmetic and copies ran while one was open for 0% of the time, Pallas kernels for 14%

profile of v5, /device:TPU:1, one launch (start us, length us, event | category | flops | bytes accessed | tf_op | source)
XLA Modules:
  0.0 109.4 jit_solution(14138701554842478331)
XLA Ops:
  1.4 3.5 %collective-permute-start = (bf16[288,1792]{1,0:T(8,128)(2,1)}, bf16[288,1792]{1,0:T(8,128)(2,1)S(1)}, u32[]{:S(2)}, u32[]{:S(2)}) collective-permute-start(bf16[288,1792]{1,0:T(8,128)(2,1)} %param.21), channel_id=1, source_target_pairs={{0,0},{64,1},{2,2},{66,3},{4,4},{68,5},{6,6},{70,7},{8,8},{72,9},{... | collective-permute-start | bytes 3096584 | tf_op jit(solution)/shard_map/ppermute | solution.py:55
  5.7 9.0 %shard_map.109 = bf16[256,512]{1,0:T(8,128)(2,1)} custom-call(s32[4]{0:T(128)} %lengths_ref.1, s32[1]{0:T(128)} %copy.12.counts_ref, bf16[4,64,576]{2,1,0:T(8,128)(2,1)} %q_ref.1, bf16[4,576,2048]{2,1,0:T(8,128)(2,1)} %bitcast.26), custom_call_target="tpu_custom_call" | custom-call | flops 1140850688 | bytes 9437184 | tf_op jit(solution)/shard_map/pallas_call | solution.py:127
  14.7 6.8 %all-to-all-start = ((bf16[16,16,512]{2,1,0:T(8,128)(2,1)}), bf16[16,16,512]{2,1,0:T(8,128)(2,1)S(1)}, u32[]{:S(2)}, u32[]{:S(2)}) async-start(bf16[16,16,512]{2,1,0:T(8,128)(2,1)} %bitcast.27), calls=%async_computation | async-start | bytes 524288 | tf_op jit(solution)/shard_map/all_to_all | solution.py:20
  21.5 6.9 %collective-permute-start.10 = (bf16[288,1792]{1,0:T(8,128)(2,1)}, bf16[288,1792]{1,0:T(8,128)(2,1)S(1)}, u32[]{:S(2)}, u32[]{:S(2)}) collective-permute-start(bf16[288,1792]{1,0:T(8,128)(2,1)} %param.21), channel_id=1, source_target_pairs={{33,0},{97,1},{35,2},{99,3},{37,4},{101,5},{39,6},{103,7},{41,8},{... | collective-permute-start | bytes 3096584 | tf_op jit(solution)/shard_map/ppermute | solution.py:55
  34.0 2.0 %copy-done.2 = bf16[256,7168]{1,0:T(8,128)(2,1)S(1)} copy-done((bf16[256,7168]{1,0:T(8,128)(2,1)S(1)}, bf16[256,7168]{1,0:T(8,128)(2,1)}, u32[]{:S(2)}) %copy-start.2) | copy-done | bytes 3670040
  37.0 4.0 %shard_map.110 = (bf16[32,3584]{1,0:T(8,128)(2,1)S(1)}, bf16[32,3584]{1,0:T(8,128)(2,1)S(1)}, bf16[32,3584]{1,0:T(8,128)(2,1)S(1)}, bf16[32,3584]{1,0:T(8,128)(2,1)S(1)}) custom-call(s32[4]{0:T(128)S(1)} %pad_add_fusion.spot_ref, bf16[256,512]{1,0:T(8,128)(2,1)S(1)} %bitcast.23, bf16[256,512]{1,0:T(8,128)(2,1)} %bitcast.8.other_ref, ...), custom_call_target="tpu_custom_call" | custom-call | flops 469762048 | bytes 3670016 | tf_op jit(solution)/shard_map/pallas_call | solution.py:179
  41.4 1.7 %collective-permute-start.6 = (bf16[32,3584]{1,0:T(8,128)(2,1)S(1)}, bf16[32,3584]{1,0:T(8,128)(2,1)S(1)}, u32[]{:S(2)}, u32[]{:S(2)}) collective-permute-start(bf16[32,3584]{1,0:T(8,128)(2,1)S(1)} %get-tuple-element.24), channel_id=1, source_target_pairs={{0,16},{1,5},{2,18},{3,7},{4,20},{5,1},{6,22},{7,3},{8,24},{9,13},... | collective-permute-start | bytes 688136 | tf_op jit(solution)/shard_map/ppermute | solution.py:35
  44.3 5.7 %collective-permute-done.5 = bf16[32,3584]{1,0:T(8,128)(2,1)S(1)} collective-permute-done((bf16[32,3584]{1,0:T(8,128)(2,1)S(1)}, bf16[32,3584]{1,0:T(8,128)(2,1)S(1)}, u32[]{:S(2)}, u32[]{:S(2)}) %collective-permute-start.5) | collective-permute-done | bytes 229408 | tf_op jit(solution)/shard_map/ppermute | solution.py:35
  50.8 1.9 %collective-permute-done.9.c_ref = bf16[288,1792]{1,0:T(8,128)(2,1)} collective-permute-done((bf16[288,1792]{1,0:T(8,128)(2,1)}, bf16[288,1792]{1,0:T(8,128)(2,1)}, u32[]{:S(2)}, u32[]{:S(2)}) %collective-permute-start.9) | collective-permute-done | bytes 1032224 | tf_op jit(solution)/shard_map/ppermute | solution.py:55
  54.0 2.6 %collective-permute-start.12 = (bf16[32,3584]{1,0:T(8,128)(2,1)S(1)}, bf16[32,3584]{1,0:T(8,128)(2,1)S(1)}, u32[]{:S(2)}, u32[]{:S(2)}) collective-permute-start(bf16[32,3584]{1,0:T(8,128)(2,1)S(1)} %fusion.1), channel_id=1, source_target_pairs={{0,4},{1,17},{2,6},{3,19},{4,0},{5,21},{6,2},{7,23},{8,12},{9,25},... | collective-permute-start | bytes 688136 | tf_op jit(solution)/shard_map/ppermute | solution.py:35
  59.1 3.6 %collective-permute-done.12 = bf16[32,3584]{1,0:T(8,128)(2,1)S(1)} collective-permute-done((bf16[32,3584]{1,0:T(8,128)(2,1)S(1)}, bf16[32,3584]{1,0:T(8,128)(2,1)S(1)}, u32[]{:S(2)}, u32[]{:S(2)}) %collective-permute-start.12) | collective-permute-done | bytes 229408 | tf_op jit(solution)/shard_map/ppermute | solution.py:35
  62.9 2.3 %collective-permute-start.15 = (bf16[32,3584]{1,0:T(8,128)(2,1)S(1)}, bf16[32,3584]{1,0:T(8,128)(2,1)S(1)}, u32[]{:S(2)}, u32[]{:S(2)}) collective-permute-start(bf16[32,3584]{1,0:T(8,128)(2,1)S(1)} %add_convert_fusion.1.refs_0_), channel_id=1, source_target_pairs={{0,24},{1,7},{2,26},{3,1},{4,28},{5,3},{6,30},{7,5},{8,0},{9,15},{... | collective-permute-start | bytes 688136 | tf_op jit(solution)/shard_map/ppermute | solution.py:35
  66.3 3.0 %collective-permute-start.14 = (bf16[32,3584]{1,0:T(8,128)(2,1)S(1)}, bf16[32,3584]{1,0:T(8,128)(2,1)S(1)}, u32[]{:S(2)}, u32[]{:S(2)}) collective-permute-start(bf16[32,3584]{1,0:T(8,128)(2,1)S(1)} %add_convert_fusion.1.refs_0_), channel_id=1, source_target_pairs={{0,1},{1,0},{2,3},{3,2},{4,5},{5,4},{6,7},{7,6},{8,9},{9,8},{10,11... | collective-permute-start | bytes 688136 | tf_op jit(solution)/shard_map/ppermute | solution.py:15
  70.6 3.1 %collective-permute-start.16 = (bf16[32,3584]{1,0:T(8,128)(2,1)S(1)}, bf16[32,3584]{1,0:T(8,128)(2,1)S(1)}, u32[]{:S(2)}, u32[]{:S(2)}) collective-permute-start(bf16[32,3584]{1,0:T(8,128)(2,1)S(1)} %collective-permute-done.15.refs_1_), channel_id=1, source_target_pairs={{0,1},{1,0},{2,3},{3,2},{4,5},{5,4},{6,7},{7,6},{8,9},{9,8},{10,11... | collective-permute-start | bytes 688136 | tf_op jit(solution)/shard_map/ppermute | solution.py:15
  75.3 2.4 %collective-permute-start.20 = (bf16[32,3584]{1,0:T(8,128)(2,1)S(1)}, bf16[32,3584]{1,0:T(8,128)(2,1)S(1)}, u32[]{:S(2)}, u32[]{:S(2)}) collective-permute-start(bf16[32,3584]{1,0:T(8,128)(2,1)S(1)} %collective-permute-done.19.refs_3_), channel_id=1, source_target_pairs={{0,1},{1,0},{2,3},{3,2},{4,5},{5,4},{6,7},{7,6},{8,9},{9,8},{10,11... | collective-permute-start | bytes 688136 | tf_op jit(solution)/shard_map/ppermute | solution.py:15
  77.7 1.9 %shard_map.111 = (f32[128,576]{1,0:T(8,128)S(1)}, f32[128,128]{1,0:T(8,128)S(1)}) custom-call(s32[4]{0:T(128)S(1)} %pad_add_fusion.spot_ref, bf16[32,3584]{1,0:T(8,128)(2,1)S(1)} %add_convert_fusion.1.refs_0_, bf16[32,3584]{1,0:T(8,128)(2,1)S(1)} %collective-permute-done.15.refs_1_, bf16[32,3584]{1,0:T(8,128)(2,1)S(1)} %collective-permute-done.17.refs_2_, ...), custom_call_target="tpu_custom_call" | custom-call | flops 528482304 | bytes 4128768 | tf_op jit(solution)/shard_map/pallas_call | solution.py:243
  79.6 2.3 %shard_map.112.inner_ref = bf16[128,288]{1,0:T(8,128)(2,1)S(1)} custom-call(s32[4]{0:T(128)S(1)} %pad_add_fusion.spot_ref, bf16[32,3584]{1,0:T(8,128)(2,1)S(1)} %collective-permute-done.14.refs_0_, bf16[32,3584]{1,0:T(8,128)(2,1)S(1)} %collective-permute-done.16.refs_1_, bf16[32,3584]{1,0:T(8,128)(2,1)S(1)} %collective-permute-done.18.refs_2_, ...), custom_call_target="tpu_custom_call" | custom-call | flops 528482304 | bytes 4128768 | tf_op jit(solution)/shard_map/pallas_call | solution.py:243
  83.3 3.3 %shard_map.113 = (bf16[32,3584]{1,0:T(8,128)(2,1)S(1)}, bf16[32,3584]{1,0:T(8,128)(2,1)}, bf16[32,3584]{1,0:T(8,128)(2,1)}, bf16[32,3584]{1,0:T(8,128)(2,1)}) custom-call(s32[4]{0:T(128)S(1)} %pad_add_fusion.spot_ref, bf16[128,288]{1,0:T(8,128)(2,1)S(1)} %shard_map.112.inner_ref, bf16[128,288]{1,0:T(8,128)(2,1)S(1)} %collective-permute-done.21.other_ref, ...), custom_call_target="tpu_custom_call" | custom-call | flops 528482304 | bytes 4128768 | tf_op jit(solution)/shard_map/pallas_call | solution.py:282
  88.9 1.8 %collective-permute-start.23 = (bf16[32,3584]{1,0:T(8,128)(2,1)}, bf16[32,3584]{1,0:T(8,128)(2,1)S(1)}, u32[]{:S(2)}, u32[]{:S(2)}) collective-permute-start(bf16[32,3584]{1,0:T(8,128)(2,1)} %get-tuple-element.35), channel_id=1, source_target_pairs={{0,16},{1,5},{2,18},{3,7},{4,20},{5,1},{6,22},{7,3},{8,24},{9,13},... | collective-permute-start | bytes 688136 | tf_op jit(solution)/shard_map/ppermute | solution.py:35
  92.1 1.8 %collective-permute-done.22 = bf16[32,3584]{1,0:T(8,128)(2,1)S(1)} collective-permute-done((bf16[32,3584]{1,0:T(8,128)(2,1)}, bf16[32,3584]{1,0:T(8,128)(2,1)S(1)}, u32[]{:S(2)}, u32[]{:S(2)}) %collective-permute-start.22) | collective-permute-done | bytes 229408 | tf_op jit(solution)/shard_map/ppermute | solution.py:35
  93.9 2.9 %collective-permute-done.23 = bf16[32,3584]{1,0:T(8,128)(2,1)S(1)} collective-permute-done((bf16[32,3584]{1,0:T(8,128)(2,1)}, bf16[32,3584]{1,0:T(8,128)(2,1)S(1)}, u32[]{:S(2)}, u32[]{:S(2)}) %collective-permute-start.23) | collective-permute-done | bytes 229408 | tf_op jit(solution)/shard_map/ppermute | solution.py:35
  98.1 1.7 %collective-permute-start.26 = (bf16[8,3584]{1,0:T(8,128)(2,1)S(1)}, bf16[8,3584]{1,0:T(8,128)(2,1)S(1)}, u32[]{:S(2)}, u32[]{:S(2)}) collective-permute-start(bf16[8,3584]{1,0:T(8,128)(2,1)S(1)} %get-tuple-element.39), channel_id=1, source_target_pairs={{0,4},{1,17},{2,6},{3,19},{4,0},{5,21},{6,2},{7,23},{8,12},{9,25},... | collective-permute-start | bytes 172040 | tf_op jit(solution)/shard_map/ppermute | solution.py:35
  100.8 2.2 %collective-permute-done.25 = bf16[8,3584]{1,0:T(8,128)(2,1)S(1)} collective-permute-done((bf16[8,3584]{1,0:T(8,128)(2,1)S(1)}, bf16[8,3584]{1,0:T(8,128)(2,1)S(1)}, u32[]{:S(2)}, u32[]{:S(2)}) %collective-permute-start.25) | collective-permute-done | bytes 57376 | tf_op jit(solution)/shard_map/ppermute | solution.py:35
  103.9 3.9 %collective-permute-start.28 = (bf16[4,3584]{1,0:T(4,128)(2,1)S(1)}, bf16[4,3584]{1,0:T(4,128)(2,1)S(1)}, u32[]{:S(2)}, u32[]{:S(2)}) collective-permute-start(bf16[4,3584]{1,0:T(4,128)(2,1)S(1)} %get-tuple-element.42), channel_id=1, source_target_pairs={{0,1},{1,0},{2,3},{3,2},{4,5},{5,4},{6,7},{7,6},{8,9},{9,8},{10,11... | collective-permute-start | bytes 86024 | tf_op jit(solution)/shard_map/ppermute | solution.py:15
  (71 shorter events, 28.2 us)
Async XLA Ops:
  0.0 34.0 %collective-permute-start.4 = (bf16[256,7168]{1,0:T(8,128)(2,1)}, bf16[256,7168]{1,0:T(8,128)(2,1)}, u32[]{:S(2)}, u32[]{:S(2)}) collective-permute-start(bf16[256,7168]{1,0:T(8,128)(2,1)} %om_ref.1), channel_id=1, source_target_pairs={{0,1},{1,0},{2,3},{3,2},{4,5},{5,4},{6,7},{7,6},{8,9},{9,8},{10,11... | collective-permute-start | bytes 11010056 | tf_op jit(solution)/shard_map/ppermute | solution.py:15
  1.4 28.6 %collective-permute-start = (bf16[288,1792]{1,0:T(8,128)(2,1)}, bf16[288,1792]{1,0:T(8,128)(2,1)S(1)}, u32[]{:S(2)}, u32[]{:S(2)}) collective-permute-start(bf16[288,1792]{1,0:T(8,128)(2,1)} %param.21), channel_id=1, source_target_pairs={{0,0},{64,1},{2,2},{66,3},{4,4},{68,5},{6,6},{70,7},{8,8},{72,9},{... | collective-permute-start | bytes 3096584 | tf_op jit(solution)/shard_map/ppermute | solution.py:55
  4.9 26.4 %collective-permute-start.1 = (bf16[288,1792]{1,0:T(8,128)(2,1)}, bf16[288,1792]{1,0:T(8,128)(2,1)S(1)}, u32[]{:S(2)}, u32[]{:S(2)}) collective-permute-start(bf16[288,1792]{1,0:T(8,128)(2,1)} %param.21), channel_id=1, source_target_pairs={{1,0},{65,1},{3,2},{67,3},{5,4},{69,5},{7,6},{71,7},{9,8},{73,9},{... | collective-permute-start | bytes 3096584 | tf_op jit(solution)/shard_map/ppermute | solution.py:55
  14.7 15.3 %all-to-all-start = ((bf16[16,16,512]{2,1,0:T(8,128)(2,1)}), bf16[16,16,512]{2,1,0:T(8,128)(2,1)S(1)}, u32[]{:S(2)}, u32[]{:S(2)}) async-start(bf16[16,16,512]{2,1,0:T(8,128)(2,1)} %bitcast.27), calls=%async_computation | async-start | bytes 524288 | tf_op jit(solution)/shard_map/all_to_all | solution.py:20
  21.5 29.3 %collective-permute-start.10 = (bf16[288,1792]{1,0:T(8,128)(2,1)}, bf16[288,1792]{1,0:T(8,128)(2,1)S(1)}, u32[]{:S(2)}, u32[]{:S(2)}) collective-permute-start(bf16[288,1792]{1,0:T(8,128)(2,1)} %param.21), channel_id=1, source_target_pairs={{33,0},{97,1},{35,2},{99,3},{37,4},{101,5},{39,6},{103,7},{41,8},{... | collective-permute-start | bytes 3096584 | tf_op jit(solution)/shard_map/ppermute | solution.py:55
  28.4 24.3 %collective-permute-start.9 = (bf16[288,1792]{1,0:T(8,128)(2,1)}, bf16[288,1792]{1,0:T(8,128)(2,1)}, u32[]{:S(2)}, u32[]{:S(2)}) collective-permute-start(bf16[288,1792]{1,0:T(8,128)(2,1)} %param.21), channel_id=1, source_target_pairs={{32,0},{96,1},{34,2},{98,3},{36,4},{100,5},{38,6},{102,7},{40,8},{... | collective-permute-start | bytes 3096584 | tf_op jit(solution)/shard_map/ppermute | solution.py:55
  33.1 10.0 %collective-permute-start.8 = (bf16[4,3584]{1,0:T(4,128)(2,1)S(1)}, bf16[4,3584]{1,0:T(4,128)(2,1)S(1)}, u32[]{:S(2)}, u32[]{:S(2)}) collective-permute-start(bf16[4,3584]{1,0:T(4,128)(2,1)S(1)} %get-tuple-element.44), channel_id=1, source_target_pairs={{0,1},{1,0},{2,3},{3,2},{4,5},{5,4},{6,7},{7,6},{8,9},{9,8},{10,11... | collective-permute-start | bytes 86024 | tf_op jit(solution)/shard_map/ppermute | solution.py:15
  41.0 8.9 %collective-permute-start.5 = (bf16[32,3584]{1,0:T(8,128)(2,1)S(1)}, bf16[32,3584]{1,0:T(8,128)(2,1)S(1)}, u32[]{:S(2)}, u32[]{:S(2)}) collective-permute-start(bf16[32,3584]{1,0:T(8,128)(2,1)S(1)} %get-tuple-element.23), channel_id=1, source_target_pairs={{0,8},{1,3},{2,10},{3,5},{4,12},{5,7},{6,14},{7,1},{8,16},{9,11},{... | collective-permute-start | bytes 688136 | tf_op jit(solution)/shard_map/ppermute | solution.py:35
  41.4 8.6 %collective-permute-start.6 = (bf16[32,3584]{1,0:T(8,128)(2,1)S(1)}, bf16[32,3584]{1,0:T(8,128)(2,1)S(1)}, u32[]{:S(2)}, u32[]{:S(2)}) collective-permute-start(bf16[32,3584]{1,0:T(8,128)(2,1)S(1)} %get-tuple-element.24), channel_id=1, source_target_pairs={{0,16},{1,5},{2,18},{3,7},{4,20},{5,1},{6,22},{7,3},{8,24},{9,13},... | collective-permute-start | bytes 688136 | tf_op jit(solution)/shard_map/ppermute | solution.py:35
  43.1 7.6 %collective-permute-start.7 = (bf16[32,3584]{1,0:T(8,128)(2,1)S(1)}, bf16[32,3584]{1,0:T(8,128)(2,1)S(1)}, u32[]{:S(2)}, u32[]{:S(2)}) collective-permute-start(bf16[32,3584]{1,0:T(8,128)(2,1)S(1)} %get-tuple-element.25), channel_id=1, source_target_pairs={{0,24},{1,7},{2,26},{3,1},{4,28},{5,3},{6,30},{7,5},{8,0},{9,15},{... | collective-permute-start | bytes 688136 | tf_op jit(solution)/shard_map/ppermute | solution.py:35
  52.7 6.4 %collective-permute-start.11 = (bf16[32,3584]{1,0:T(8,128)(2,1)S(1)}, bf16[32,3584]{1,0:T(8,128)(2,1)S(1)}, u32[]{:S(2)}, u32[]{:S(2)}) collective-permute-start(bf16[32,3584]{1,0:T(8,128)(2,1)S(1)} %fusion.1), channel_id=1, source_target_pairs={{0,2},{1,9},{2,4},{3,11},{4,6},{5,13},{6,0},{7,15},{8,10},{9,17},{... | collective-permute-start | bytes 688136 | tf_op jit(solution)/shard_map/ppermute | solution.py:35
  54.0 8.8 %collective-permute-start.12 = (bf16[32,3584]{1,0:T(8,128)(2,1)S(1)}, bf16[32,3584]{1,0:T(8,128)(2,1)S(1)}, u32[]{:S(2)}, u32[]{:S(2)}) collective-permute-start(bf16[32,3584]{1,0:T(8,128)(2,1)S(1)} %fusion.1), channel_id=1, source_target_pairs={{0,4},{1,17},{2,6},{3,19},{4,0},{5,21},{6,2},{7,23},{8,12},{9,25},... | collective-permute-start | bytes 688136 | tf_op jit(solution)/shard_map/ppermute | solution.py:35
  56.6 6.2 %collective-permute-start.13 = (bf16[32,3584]{1,0:T(8,128)(2,1)S(1)}, bf16[32,3584]{1,0:T(8,128)(2,1)S(1)}, u32[]{:S(2)}, u32[]{:S(2)}) collective-permute-start(bf16[32,3584]{1,0:T(8,128)(2,1)S(1)} %fusion.1), channel_id=1, source_target_pairs={{0,6},{1,25},{2,0},{3,27},{4,2},{5,29},{6,4},{7,31},{8,14},{9,1},{... | collective-permute-start | bytes 688136 | tf_op jit(solution)/shard_map/ppermute | solution.py:35
  62.9 7.7 %collective-permute-start.15 = (bf16[32,3584]{1,0:T(8,128)(2,1)S(1)}, bf16[32,3584]{1,0:T(8,128)(2,1)S(1)}, u32[]{:S(2)}, u32[]{:S(2)}) collective-permute-start(bf16[32,3584]{1,0:T(8,128)(2,1)S(1)} %add_convert_fusion.1.refs_0_), channel_id=1, source_target_pairs={{0,24},{1,7},{2,26},{3,1},{4,28},{5,3},{6,30},{7,5},{8,0},{9,15},{... | collective-permute-start | bytes 688136 | tf_op jit(solution)/shard_map/ppermute | solution.py:35
  65.1 8.6 %collective-permute-start.17 = (bf16[32,3584]{1,0:T(8,128)(2,1)S(1)}, bf16[32,3584]{1,0:T(8,128)(2,1)S(1)}, u32[]{:S(2)}, u32[]{:S(2)}) collective-permute-start(bf16[32,3584]{1,0:T(8,128)(2,1)S(1)} %add_convert_fusion.1.refs_0_), channel_id=1, source_target_pairs={{0,16},{1,5},{2,18},{3,7},{4,20},{5,1},{6,22},{7,3},{8,24},{9,13},... | collective-permute-start | bytes 688136 | tf_op jit(solution)/shard_map/ppermute | solution.py:35
  65.7 9.7 %collective-permute-start.19 = (bf16[32,3584]{1,0:T(8,128)(2,1)S(1)}, bf16[32,3584]{1,0:T(8,128)(2,1)S(1)}, u32[]{:S(2)}, u32[]{:S(2)}) collective-permute-start(bf16[32,3584]{1,0:T(8,128)(2,1)S(1)} %add_convert_fusion.1.refs_0_), channel_id=1, source_target_pairs={{0,8},{1,3},{2,10},{3,5},{4,12},{5,7},{6,14},{7,1},{8,16},{9,11},{... | collective-permute-start | bytes 688136 | tf_op jit(solution)/shard_map/ppermute | solution.py:35
  66.3 13.3 %collective-permute-start.14 = (bf16[32,3584]{1,0:T(8,128)(2,1)S(1)}, bf16[32,3584]{1,0:T(8,128)(2,1)S(1)}, u32[]{:S(2)}, u32[]{:S(2)}) collective-permute-start(bf16[32,3584]{1,0:T(8,128)(2,1)S(1)} %add_convert_fusion.1.refs_0_), channel_id=1, source_target_pairs={{0,1},{1,0},{2,3},{3,2},{4,5},{5,4},{6,7},{7,6},{8,9},{9,8},{10,11... | collective-permute-start | bytes 688136 | tf_op jit(solution)/shard_map/ppermute | solution.py:15
  70.6 9.0 %collective-permute-start.16 = (bf16[32,3584]{1,0:T(8,128)(2,1)S(1)}, bf16[32,3584]{1,0:T(8,128)(2,1)S(1)}, u32[]{:S(2)}, u32[]{:S(2)}) collective-permute-start(bf16[32,3584]{1,0:T(8,128)(2,1)S(1)} %collective-permute-done.15.refs_1_), channel_id=1, source_target_pairs={{0,1},{1,0},{2,3},{3,2},{4,5},{5,4},{6,7},{7,6},{8,9},{9,8},{10,11... | collective-permute-start | bytes 688136 | tf_op jit(solution)/shard_map/ppermute | solution.py:15
  73.7 5.9 %collective-permute-start.18 = (bf16[32,3584]{1,0:T(8,128)(2,1)S(1)}, bf16[32,3584]{1,0:T(8,128)(2,1)S(1)}, u32[]{:S(2)}, u32[]{:S(2)}) collective-permute-start(bf16[32,3584]{1,0:T(8,128)(2,1)S(1)} %collective-permute-done.17.refs_2_), channel_id=1, source_target_pairs={{0,1},{1,0},{2,3},{3,2},{4,5},{5,4},{6,7},{7,6},{8,9},{9,8},{10,11... | collective-permute-start | bytes 688136 | tf_op jit(solution)/shard_map/ppermute | solution.py:15
  87.3 6.6 %collective-permute-start.22 = (bf16[32,3584]{1,0:T(8,128)(2,1)}, bf16[32,3584]{1,0:T(8,128)(2,1)S(1)}, u32[]{:S(2)}, u32[]{:S(2)}) collective-permute-start(bf16[32,3584]{1,0:T(8,128)(2,1)} %get-tuple-element.34), channel_id=1, source_target_pairs={{0,8},{1,3},{2,10},{3,5},{4,12},{5,7},{6,14},{7,1},{8,16},{9,11},{... | collective-permute-start | bytes 688136 | tf_op jit(solution)/shard_map/ppermute | solution.py:35
  88.9 7.9 %collective-permute-start.23 = (bf16[32,3584]{1,0:T(8,128)(2,1)}, bf16[32,3584]{1,0:T(8,128)(2,1)S(1)}, u32[]{:S(2)}, u32[]{:S(2)}) collective-permute-start(bf16[32,3584]{1,0:T(8,128)(2,1)} %get-tuple-element.35), channel_id=1, source_target_pairs={{0,16},{1,5},{2,18},{3,7},{4,20},{5,1},{6,22},{7,3},{8,24},{9,13},... | collective-permute-start | bytes 688136 | tf_op jit(solution)/shard_map/ppermute | solution.py:35
  90.7 6.2 %collective-permute-start.24 = (bf16[32,3584]{1,0:T(8,128)(2,1)}, bf16[32,3584]{1,0:T(8,128)(2,1)S(1)}, u32[]{:S(2)}, u32[]{:S(2)}) collective-permute-start(bf16[32,3584]{1,0:T(8,128)(2,1)} %get-tuple-element.36), channel_id=1, source_target_pairs={{0,24},{1,7},{2,26},{3,1},{4,28},{5,3},{6,30},{7,5},{8,0},{9,15},{... | collective-permute-start | bytes 688136 | tf_op jit(solution)/shard_map/ppermute | solution.py:35
  98.0 4.9 %collective-permute-start.25 = (bf16[8,3584]{1,0:T(8,128)(2,1)S(1)}, bf16[8,3584]{1,0:T(8,128)(2,1)S(1)}, u32[]{:S(2)}, u32[]{:S(2)}) collective-permute-start(bf16[8,3584]{1,0:T(8,128)(2,1)S(1)} %get-tuple-element.37), channel_id=1, source_target_pairs={{0,2},{1,9},{2,4},{3,11},{4,6},{5,13},{6,0},{7,15},{8,10},{9,17},{... | collective-permute-start | bytes 172040 | tf_op jit(solution)/shard_map/ppermute | solution.py:35
  98.1 4.8 %collective-permute-start.26 = (bf16[8,3584]{1,0:T(8,128)(2,1)S(1)}, bf16[8,3584]{1,0:T(8,128)(2,1)S(1)}, u32[]{:S(2)}, u32[]{:S(2)}) collective-permute-start(bf16[8,3584]{1,0:T(8,128)(2,1)S(1)} %get-tuple-element.39), channel_id=1, source_target_pairs={{0,4},{1,17},{2,6},{3,19},{4,0},{5,21},{6,2},{7,23},{8,12},{9,25},... | collective-permute-start | bytes 172040 | tf_op jit(solution)/shard_map/ppermute | solution.py:35
  (13 other events, 172.8 us)

commit v6 on v5

--- a/solution.py
+++ b/solution.py
@@ -133,7 +133,7 @@
             pltpu.VMEM((slots, wide, ctx), jnp.bfloat16),
             pltpu.SemaphoreType.DMA((slots,)),
         ],
-        compiler_params=budget(57),
+        compiler_params=budget(55),
         cost_estimate=pl.CostEstimate(
             flops=2 * rows * ctx * (wide + latent_width),
             bytes_accessed=2 * cache.size,
@@ -328,13 +328,13 @@
     input_other = core_swap(
         lax.dynamic_slice_in_dim(layer_input, (1 - core) * half, half, 1), width
     )
+    latent = attend(query, cache, lengths, counts, latent_width, chips)
+    latent, value_other, input_other = lax.optimization_barrier((latent, value_other, input_other))
     input_chip = jnp.where(
         upper,
         jnp.concatenate([input_other, input_mine], axis=0),
         jnp.concatenate([input_mine, input_other], axis=0),
     ).astype(jnp.float32)
-
-    latent = attend(query, cache, lengths, counts, latent_width, chips)
     arrived = between_chips(latent, width)
     arrived, pieces[0], pieces[1] = lax.optimization_barrier((arrived, pieces[0], pieces[1]))
     arrived_other = core_swap(arrived, width)
@@ -357,6 +357,7 @@
     summed, pieces[2], pieces[3] = lax.optimization_barrier((summed, pieces[2], pieces[3]))
     residual_line = total(turn([summed] * side, 1, side, 1)).astype(jnp.bfloat16)
     residual_mine = turn([residual_line] * side, 0, side, -1)
+    residual_mine = lax.optimization_barrier(residual_mine)
     residual_other = [core_swap(part, width) for part in residual_mine]
     sums = gated(residual_mine, norm_gain, gate_weight, up_weight, spot, None)
     inner = gated(residual_other, norm_gain, gate_weight, up_weight, spot, sums)

time: 110 us -> 118 us (1.073)
  starting transfers between devices: 53.7 us -> 36.9 us
  blocking collectives: 0 us -> 14.7 us
  waiting for transfers between devices: 28.1 us -> 35.5 us
  local copies, waits for them, and re-layouts: 3.96 us -> 6.38 us
    all_to_all x0 -> x1, blocking collectives: none -> 14.7 us  [between_chips(): return lax.all_to_all(x, 'tp', 0, 0, tiled=True, axis_index_groups=groups)]
    ppermute x15, waiting for transfers between devices: 20.7 us -> 29.6 us  [turn(): out.append(lax.ppermute(parts[k], 'tp', pairs))]
    all_to_all x1 -> x0, starting transfers between devices: 6.76 us -> none  [between_chips(): return lax.all_to_all(x, 'tp', 0, 0, tiled=True, axis_index_groups=groups)]
    ppermute x15, starting transfers between devices: 19 us -> 14.3 us  [turn(): out.append(lax.ppermute(parts[k], 'tp', pairs))]
    ppermute x10, starting transfers between devices: 16.9 us -> 13 us  [core_swap(): return lax.ppermute(x, 'tp', [(i, i ^ 1) for i in range(width)])]
    unnamed x14 -> x16, local copies, waits for them, and re-layouts: 3.7 us -> 5.36 us
    ppermute x4, starting transfers between devices: 10.9 us -> 9.53 us  [down_pieces(): out.append(lax.ppermute(down_weight, ('dp', 'tp'), pairs))]
    ppermute x10, waiting for transfers between devices: 3.07 us -> 1.81 us  [core_swap(): return lax.ppermute(x, 'tp', [(i, i ^ 1) for i in range(width)])]
  transfers between devices with their start and end apart: 30 -> 29, of which waited for: 16 -> 16; matrix products, arithmetic and copies ran while one was open for 0% -> 1% of each run, Pallas kernels for 14% -> 13%
where the time goes in v6:
time: 118 us; the launch traced here: 117 us
  starting transfers between devices  36.9 us (31%)
  waiting for transfers between devices  35.5 us (30%)
  Pallas kernels  20.4 us (17%)
  blocking collectives  14.7 us (12%)
  local copies, waits for them, and re-layouts  6.38 us (5%)
  other arithmetic  2.23 us (2%)
    ppermute x15, waiting for transfers between devices, turn(): out.append(lax.ppermute(parts[k], 'tp', pairs))  29.6 us
    all_to_all x1, blocking collectives, between_chips(): return lax.all_to_all(x, 'tp', 0, 0, tiled=True, axis_index_groups=groups)  14.7 us
    ppermute x15, starting transfers between devices, turn(): out.append(lax.ppermute(parts[k], 'tp', pairs))  14.3 us
    ppermute x10, starting transfers between devices, core_swap(): return lax.ppermute(x, 'tp', [(i, i ^ 1) for i in range(width)])  13 us
    ppermute x4, starting transfers between devices, down_pieces(): out.append(lax.ppermute(down_weight, ('dp', 'tp'), pairs))  9.53 us
    pallas_call x1, Pallas kernels, attend(): pl.pallas_call(kernel, in_specs=[in_smem, in_smem, in_vmem, in_hbm], out_...  8.99 us
    unnamed x16, local copies, waits for them, and re-layouts  5.36 us
    pallas_call x2, Pallas kernels, gated(): pl.pallas_call(kernel, in_specs=[in_smem] + [in_vmem] * (side + 3 + 2 * f...  4.2 us
  transfers between devices with their start and end apart: 29, of which 16 were waited for; matrix products, arithmetic and copies ran while one was open for 1% of the time, Pallas kernels for 13%

profile of v6, /device:TPU:1, one launch (start us, length us, event | category | flops | bytes accessed | tf_op | source)
XLA Modules:
  0.0 117.0 jit_solution(16451711111231090777)
XLA Ops:
  1.4 3.5 %collective-permute-start.2 = (bf16[288,1792]{1,0:T(8,128)(2,1)}, bf16[288,1792]{1,0:T(8,128)(2,1)S(1)}, u32[]{:S(2)}, u32[]{:S(2)}) collective-permute-start(bf16[288,1792]{1,0:T(8,128)(2,1)} %param.21), channel_id=1, source_target_pairs={{0,0},{64,1},{2,2},{66,3},{4,4},{68,5},{6,6},{70,7},{8,8},{72,9},{... | collective-permute-start | bytes 3096584 | tf_op jit(solution)/shard_map/ppermute | solution.py:55
  5.0 2.3 %collective-permute-start = (bf16[2,512,128]{2,1,0:T(8,128)(2,1)}, bf16[2,512,128]{2,1,0:T(8,128)(2,1)S(1)}, u32[]{:S(2)}, u32[]{:S(2)}) collective-permute-start(bf16[2,512,128]{2,1,0:T(8,128)(2,1)} %vm_ref.1), channel_id=1, source_target_pairs={{0,1},{1,0},{2,3},{3,2},{4,5},{5,4},{6,7},{7,6},{8,9},{9,8},{10,11... | collective-permute-start | bytes 786440 | tf_op jit(solution)/shard_map/ppermute | solution.py:15
  8.8 9.0 %shard_map.109 = bf16[256,512]{1,0:T(8,128)(2,1)} custom-call(s32[4]{0:T(128)} %lengths_ref.1, s32[1]{0:T(128)} %copy.12.counts_ref, bf16[4,64,576]{2,1,0:T(8,128)(2,1)} %q_ref.1, bf16[4,576,2048]{2,1,0:T(8,128)(2,1)} %bitcast.26), custom_call_target="tpu_custom_call" | custom-call | flops 1140850688 | bytes 9437184 | tf_op jit(solution)/shard_map/pallas_call | solution.py:127
  18.6 14.7 %all_to_all.5 = bf16[16,16,512]{2,1,0:T(8,128)(2,1)S(1)} all-to-all(bf16[16,16,512]{2,1,0:T(8,128)(2,1)} %bitcast.27), channel_id=1, replica_groups={{0,2,4,6,8,10,12,14,16,18,20,22,24,26,28,30},{1,3,5,7,9,11,13,15,17,19,..., dimensions={0} | all-to-all | bytes 524288 | tf_op jit(solution)/shard_map/all_to_all | solution.py:20
  35.0 4.4 %collective-permute-start.10 = (bf16[288,1792]{1,0:T(8,128)(2,1)}, bf16[288,1792]{1,0:T(8,128)(2,1)S(1)}, u32[]{:S(2)}, u32[]{:S(2)}) collective-permute-start(bf16[288,1792]{1,0:T(8,128)(2,1)} %param.21), channel_id=1, source_target_pairs={{33,0},{97,1},{35,2},{99,3},{37,4},{101,5},{39,6},{103,7},{41,8},{... | collective-permute-start | bytes 3096584 | tf_op jit(solution)/shard_map/ppermute | solution.py:55
  41.2 2.0 %copy-done.2 = bf16[256,7168]{1,0:T(8,128)(2,1)S(1)} copy-done((bf16[256,7168]{1,0:T(8,128)(2,1)S(1)}, bf16[256,7168]{1,0:T(8,128)(2,1)}, u32[]{:S(2)}) %copy-start.2) | copy-done | bytes 3670040
  45.1 3.9 %shard_map.110 = (bf16[32,3584]{1,0:T(8,128)(2,1)S(1)}, bf16[32,3584]{1,0:T(8,128)(2,1)S(1)}, bf16[32,3584]{1,0:T(8,128)(2,1)S(1)}, bf16[32,3584]{1,0:T(8,128)(2,1)S(1)}) custom-call(s32[4]{0:T(128)S(1)} %pad_add_fusion.spot_ref, bf16[256,512]{1,0:T(8,128)(2,1)S(1)} %bitcast.23, bf16[256,512]{1,0:T(8,128)(2,1)} %bitcast.8.other_ref, ...), custom_call_target="tpu_custom_call" | custom-call | flops 469762048 | bytes 3670016 | tf_op jit(solution)/shard_map/pallas_call | solution.py:179
  52.0 5.7 %collective-permute-done.6 = bf16[32,3584]{1,0:T(8,128)(2,1)S(1)} collective-permute-done((bf16[32,3584]{1,0:T(8,128)(2,1)S(1)}, bf16[32,3584]{1,0:T(8,128)(2,1)S(1)}, u32[]{:S(2)}, u32[]{:S(2)}) %collective-permute-start.6) | collective-permute-done | bytes 229408 | tf_op jit(solution)/shard_map/ppermute | solution.py:35
  58.9 2.8 %collective-permute-done.10.d_ref = bf16[288,1792]{1,0:T(8,128)(2,1)S(1)} collective-permute-done((bf16[288,1792]{1,0:T(8,128)(2,1)}, bf16[288,1792]{1,0:T(8,128)(2,1)S(1)}, u32[]{:S(2)}, u32[]{:S(2)}) %collective-permute-start.10) | collective-permute-done | bytes 1032224 | tf_op jit(solution)/shard_map/ppermute | solution.py:55
  62.9 1.8 %collective-permute-start.12 = (bf16[32,3584]{1,0:T(8,128)(2,1)S(1)}, bf16[32,3584]{1,0:T(8,128)(2,1)S(1)}, u32[]{:S(2)}, u32[]{:S(2)}) collective-permute-start(bf16[32,3584]{1,0:T(8,128)(2,1)S(1)} %fusion.1), channel_id=1, source_target_pairs={{0,4},{1,17},{2,6},{3,19},{4,0},{5,21},{6,2},{7,23},{8,12},{9,25},... | collective-permute-start | bytes 688136 | tf_op jit(solution)/shard_map/ppermute | solution.py:35
  65.6 6.2 %collective-permute-done.11 = bf16[32,3584]{1,0:T(8,128)(2,1)S(1)} collective-permute-done((bf16[32,3584]{1,0:T(8,128)(2,1)S(1)}, bf16[32,3584]{1,0:T(8,128)(2,1)S(1)}, u32[]{:S(2)}, u32[]{:S(2)}) %collective-permute-start.11) | collective-permute-done | bytes 229408 | tf_op jit(solution)/shard_map/ppermute | solution.py:35
  74.7 3.1 %collective-permute-done.14.refs_1_ = bf16[32,3584]{1,0:T(8,128)(2,1)S(1)} collective-permute-done((bf16[32,3584]{1,0:T(8,128)(2,1)S(1)}, bf16[32,3584]{1,0:T(8,128)(2,1)S(1)}, u32[]{:S(2)}, u32[]{:S(2)}) %collective-permute-start.14) | collective-permute-done | bytes 229408 | tf_op jit(solution)/shard_map/ppermute | solution.py:35
  77.7 2.0 %collective-permute-done.15.refs_2_ = bf16[32,3584]{1,0:T(8,128)(2,1)S(1)} collective-permute-done((bf16[32,3584]{1,0:T(8,128)(2,1)S(1)}, bf16[32,3584]{1,0:T(8,128)(2,1)S(1)}, u32[]{:S(2)}, u32[]{:S(2)}) %collective-permute-start.15) | collective-permute-done | bytes 229408 | tf_op jit(solution)/shard_map/ppermute | solution.py:35
  79.7 2.5 %collective-permute-done.16.refs_3_ = bf16[32,3584]{1,0:T(8,128)(2,1)S(1)} collective-permute-done((bf16[32,3584]{1,0:T(8,128)(2,1)S(1)}, bf16[32,3584]{1,0:T(8,128)(2,1)S(1)}, u32[]{:S(2)}, u32[]{:S(2)}) %collective-permute-start.16) | collective-permute-done | bytes 229408 | tf_op jit(solution)/shard_map/ppermute | solution.py:35
  82.2 2.1 %collective-permute-start.17 = (bf16[32,3584]{1,0:T(8,128)(2,1)S(1)}, bf16[32,3584]{1,0:T(8,128)(2,1)S(1)}, u32[]{:S(2)}, u32[]{:S(2)}) collective-permute-start(bf16[32,3584]{1,0:T(8,128)(2,1)S(1)} %add_convert_fusion.1.refs_0_), channel_id=1, source_target_pairs={{0,1},{1,0},{2,3},{3,2},{4,5},{5,4},{6,7},{7,6},{8,9},{9,8},{10,11... | collective-permute-start | bytes 688136 | tf_op jit(solution)/shard_map/ppermute | solution.py:15
  84.8 1.9 %shard_map.111 = (f32[128,576]{1,0:T(8,128)S(1)}, f32[128,128]{1,0:T(8,128)S(1)}) custom-call(s32[4]{0:T(128)S(1)} %pad_add_fusion.spot_ref, bf16[32,3584]{1,0:T(8,128)(2,1)S(1)} %add_convert_fusion.1.refs_0_, bf16[32,3584]{1,0:T(8,128)(2,1)S(1)} %collective-permute-done.14.refs_1_, bf16[32,3584]{1,0:T(8,128)(2,1)S(1)} %collective-permute-done.15.refs_2_, ...), custom_call_target="tpu_custom_call" | custom-call | flops 528482304 | bytes 4128768 | tf_op jit(solution)/shard_map/pallas_call | solution.py:243
  86.8 2.3 %shard_map.112.inner_ref = bf16[128,288]{1,0:T(8,128)(2,1)S(1)} custom-call(s32[4]{0:T(128)S(1)} %pad_add_fusion.spot_ref, bf16[32,3584]{1,0:T(8,128)(2,1)S(1)} %collective-permute-done.17.refs_0_, bf16[32,3584]{1,0:T(8,128)(2,1)S(1)} %collective-permute-done.18.refs_1_, bf16[32,3584]{1,0:T(8,128)(2,1)S(1)} %collective-permute-done.19.refs_2_, ...), custom_call_target="tpu_custom_call" | custom-call | flops 528482304 | bytes 4128768 | tf_op jit(solution)/shard_map/pallas_call | solution.py:243
  90.6 3.3 %shard_map.113 = (bf16[32,3584]{1,0:T(8,128)(2,1)S(1)}, bf16[32,3584]{1,0:T(8,128)(2,1)}, bf16[32,3584]{1,0:T(8,128)(2,1)}, bf16[32,3584]{1,0:T(8,128)(2,1)}) custom-call(s32[4]{0:T(128)S(1)} %pad_add_fusion.spot_ref, bf16[128,288]{1,0:T(8,128)(2,1)S(1)} %shard_map.112.inner_ref, bf16[128,288]{1,0:T(8,128)(2,1)S(1)} %collective-permute-done.21.other_ref, ...), custom_call_target="tpu_custom_call" | custom-call | flops 528482304 | bytes 4128768 | tf_op jit(solution)/shard_map/pallas_call | solution.py:282
  95.2 2.9 %collective-permute-start.23 = (bf16[32,3584]{1,0:T(8,128)(2,1)}, bf16[32,3584]{1,0:T(8,128)(2,1)S(1)}, u32[]{:S(2)}, u32[]{:S(2)}) collective-permute-start(bf16[32,3584]{1,0:T(8,128)(2,1)} %get-tuple-element.49), channel_id=1, source_target_pairs={{0,16},{1,5},{2,18},{3,7},{4,20},{5,1},{6,22},{7,3},{8,24},{9,13},... | collective-permute-start | bytes 688136 | tf_op jit(solution)/shard_map/ppermute | solution.py:35
  98.1 3.1 %collective-permute-done.22 = bf16[32,3584]{1,0:T(8,128)(2,1)S(1)} collective-permute-done((bf16[32,3584]{1,0:T(8,128)(2,1)}, bf16[32,3584]{1,0:T(8,128)(2,1)S(1)}, u32[]{:S(2)}, u32[]{:S(2)}) %collective-permute-start.22) | collective-permute-done | bytes 229408 | tf_op jit(solution)/shard_map/ppermute | solution.py:35
  101.2 3.0 %collective-permute-done.23 = bf16[32,3584]{1,0:T(8,128)(2,1)S(1)} collective-permute-done((bf16[32,3584]{1,0:T(8,128)(2,1)}, bf16[32,3584]{1,0:T(8,128)(2,1)S(1)}, u32[]{:S(2)}, u32[]{:S(2)}) %collective-permute-start.23) | collective-permute-done | bytes 229408 | tf_op jit(solution)/shard_map/ppermute | solution.py:35
  105.4 1.7 %collective-permute-start.26 = (bf16[8,3584]{1,0:T(8,128)(2,1)S(1)}, bf16[8,3584]{1,0:T(8,128)(2,1)S(1)}, u32[]{:S(2)}, u32[]{:S(2)}) collective-permute-start(bf16[8,3584]{1,0:T(8,128)(2,1)S(1)} %get-tuple-element.53), channel_id=1, source_target_pairs={{0,4},{1,17},{2,6},{3,19},{4,0},{5,21},{6,2},{7,23},{8,12},{9,25},... | collective-permute-start | bytes 172040 | tf_op jit(solution)/shard_map/ppermute | solution.py:35
  108.5 1.8 %collective-permute-done.25 = bf16[8,3584]{1,0:T(8,128)(2,1)S(1)} collective-permute-done((bf16[8,3584]{1,0:T(8,128)(2,1)S(1)}, bf16[8,3584]{1,0:T(8,128)(2,1)S(1)}, u32[]{:S(2)}, u32[]{:S(2)}) %collective-permute-start.25) | collective-permute-done | bytes 57376 | tf_op jit(solution)/shard_map/ppermute | solution.py:35
  111.0 4.4 %collective-permute-start.28 = (bf16[4,3584]{1,0:T(4,128)(2,1)S(1)}, bf16[4,3584]{1,0:T(4,128)(2,1)S(1)}, u32[]{:S(2)}, u32[]{:S(2)}) collective-permute-start(bf16[4,3584]{1,0:T(4,128)(2,1)S(1)} %get-tuple-element.56), channel_id=1, source_target_pairs={{0,1},{1,0},{2,3},{3,2},{4,5},{5,4},{6,7},{7,6},{8,9},{9,8},{10,11... | collective-permute-start | bytes 86024 | tf_op jit(solution)/shard_map/ppermute | solution.py:15
  (72 shorter events, 25.8 us)
Async XLA Ops:
  0.0 41.2 %collective-permute-start.5 = (bf16[256,7168]{1,0:T(8,128)(2,1)}, bf16[256,7168]{1,0:T(8,128)(2,1)}, u32[]{:S(2)}, u32[]{:S(2)}) collective-permute-start(bf16[256,7168]{1,0:T(8,128)(2,1)} %om_ref.1), channel_id=1, source_target_pairs={{0,1},{1,0},{2,3},{3,2},{4,5},{5,4},{6,7},{7,6},{8,9},{9,8},{10,11... | collective-permute-start | bytes 11010056 | tf_op jit(solution)/shard_map/ppermute | solution.py:15
  1.4 31.9 %collective-permute-start.2 = (bf16[288,1792]{1,0:T(8,128)(2,1)}, bf16[288,1792]{1,0:T(8,128)(2,1)S(1)}, u32[]{:S(2)}, u32[]{:S(2)}) collective-permute-start(bf16[288,1792]{1,0:T(8,128)(2,1)} %param.21), channel_id=1, source_target_pairs={{0,0},{64,1},{2,2},{66,3},{4,4},{68,5},{6,6},{70,7},{8,8},{72,9},{... | collective-permute-start | bytes 3096584 | tf_op jit(solution)/shard_map/ppermute | solution.py:55
  4.9 28.4 %collective-permute-start.3 = (bf16[288,1792]{1,0:T(8,128)(2,1)}, bf16[288,1792]{1,0:T(8,128)(2,1)S(1)}, u32[]{:S(2)}, u32[]{:S(2)}) collective-permute-start(bf16[288,1792]{1,0:T(8,128)(2,1)} %param.21), channel_id=1, source_target_pairs={{1,0},{65,1},{3,2},{67,3},{5,4},{69,5},{7,6},{71,7},{9,8},{73,9},{... | collective-permute-start | bytes 3096584 | tf_op jit(solution)/shard_map/ppermute | solution.py:55
  5.0 12.8 %collective-permute-start = (bf16[2,512,128]{2,1,0:T(8,128)(2,1)}, bf16[2,512,128]{2,1,0:T(8,128)(2,1)S(1)}, u32[]{:S(2)}, u32[]{:S(2)}) collective-permute-start(bf16[2,512,128]{2,1,0:T(8,128)(2,1)} %vm_ref.1), channel_id=1, source_target_pairs={{0,1},{1,0},{2,3},{3,2},{4,5},{5,4},{6,7},{7,6},{8,9},{9,8},{10,11... | collective-permute-start | bytes 786440 | tf_op jit(solution)/shard_map/ppermute | solution.py:15
  8.1 9.7 %collective-permute-start.1 = (bf16[4,3584]{1,0:T(4,128)(2,1)S(1)}, bf16[4,3584]{1,0:T(4,128)(2,1)S(1)}, u32[]{:S(2)}, u32[]{:S(2)}) collective-permute-start(bf16[4,3584]{1,0:T(4,128)(2,1)S(1)} %get-tuple-element.59), channel_id=1, source_target_pairs={{0,1},{1,0},{2,3},{3,2},{4,5},{5,4},{6,7},{7,6},{8,9},{9,8},{10,11... | collective-permute-start | bytes 86024 | tf_op jit(solution)/shard_map/ppermute | solution.py:15
  33.3 7.8 %collective-permute-start.4 = (bf16[16,16,512]{2,1,0:T(8,128)(2,1)S(1)}, bf16[16,16,512]{2,1,0:T(8,128)(2,1)}, u32[]{:S(2)}, u32[]{:S(2)}) collective-permute-start(bf16[16,16,512]{2,1,0:T(8,128)(2,1)S(1)} %all_to_all.5), channel_id=1, source_target_pairs={{0,1},{1,0},{2,3},{3,2},{4,5},{5,4},{6,7},{7,6},{8,9},{9,8},{10,11... | collective-permute-start | bytes 786440 | tf_op jit(solution)/shard_map/ppermute | solution.py:15
  35.0 26.6 %collective-permute-start.10 = (bf16[288,1792]{1,0:T(8,128)(2,1)}, bf16[288,1792]{1,0:T(8,128)(2,1)S(1)}, u32[]{:S(2)}, u32[]{:S(2)}) collective-permute-start(bf16[288,1792]{1,0:T(8,128)(2,1)} %param.21), channel_id=1, source_target_pairs={{33,0},{97,1},{35,2},{99,3},{37,4},{101,5},{39,6},{103,7},{41,8},{... | collective-permute-start | bytes 3096584 | tf_op jit(solution)/shard_map/ppermute | solution.py:55
  39.4 23.6 %collective-permute-start.9 = (bf16[288,1792]{1,0:T(8,128)(2,1)}, bf16[288,1792]{1,0:T(8,128)(2,1)}, u32[]{:S(2)}, u32[]{:S(2)}) collective-permute-start(bf16[288,1792]{1,0:T(8,128)(2,1)} %param.21), channel_id=1, source_target_pairs={{32,0},{96,1},{34,2},{98,3},{36,4},{100,5},{38,6},{102,7},{40,8},{... | collective-permute-start | bytes 3096584 | tf_op jit(solution)/shard_map/ppermute | solution.py:55
  49.1 8.6 %collective-permute-start.6 = (bf16[32,3584]{1,0:T(8,128)(2,1)S(1)}, bf16[32,3584]{1,0:T(8,128)(2,1)S(1)}, u32[]{:S(2)}, u32[]{:S(2)}) collective-permute-start(bf16[32,3584]{1,0:T(8,128)(2,1)S(1)} %get-tuple-element.32), channel_id=1, source_target_pairs={{0,8},{1,3},{2,10},{3,5},{4,12},{5,7},{6,14},{7,1},{8,16},{9,11},{... | collective-permute-start | bytes 688136 | tf_op jit(solution)/shard_map/ppermute | solution.py:35
  49.4 8.3 %collective-permute-start.7 = (bf16[32,3584]{1,0:T(8,128)(2,1)S(1)}, bf16[32,3584]{1,0:T(8,128)(2,1)S(1)}, u32[]{:S(2)}, u32[]{:S(2)}) collective-permute-start(bf16[32,3584]{1,0:T(8,128)(2,1)S(1)} %get-tuple-element.33), channel_id=1, source_target_pairs={{0,16},{1,5},{2,18},{3,7},{4,20},{5,1},{6,22},{7,3},{8,24},{9,13},... | collective-permute-start | bytes 688136 | tf_op jit(solution)/shard_map/ppermute | solution.py:35
  50.8 7.9 %collective-permute-start.8 = (bf16[32,3584]{1,0:T(8,128)(2,1)S(1)}, bf16[32,3584]{1,0:T(8,128)(2,1)S(1)}, u32[]{:S(2)}, u32[]{:S(2)}) collective-permute-start(bf16[32,3584]{1,0:T(8,128)(2,1)S(1)} %get-tuple-element.34), channel_id=1, source_target_pairs={{0,24},{1,7},{2,26},{3,1},{4,28},{5,3},{6,30},{7,5},{8,0},{9,15},{... | collective-permute-start | bytes 688136 | tf_op jit(solution)/shard_map/ppermute | solution.py:35
  62.9 8.8 %collective-permute-start.11 = (bf16[32,3584]{1,0:T(8,128)(2,1)S(1)}, bf16[32,3584]{1,0:T(8,128)(2,1)S(1)}, u32[]{:S(2)}, u32[]{:S(2)}) collective-permute-start(bf16[32,3584]{1,0:T(8,128)(2,1)S(1)} %fusion.1), channel_id=1, source_target_pairs={{0,2},{1,9},{2,4},{3,11},{4,6},{5,13},{6,0},{7,15},{8,10},{9,17},{... | collective-permute-start | bytes 688136 | tf_op jit(solution)/shard_map/ppermute | solution.py:35
  62.9 8.8 %collective-permute-start.12 = (bf16[32,3584]{1,0:T(8,128)(2,1)S(1)}, bf16[32,3584]{1,0:T(8,128)(2,1)S(1)}, u32[]{:S(2)}, u32[]{:S(2)}) collective-permute-start(bf16[32,3584]{1,0:T(8,128)(2,1)S(1)} %fusion.1), channel_id=1, source_target_pairs={{0,4},{1,17},{2,6},{3,19},{4,0},{5,21},{6,2},{7,23},{8,12},{9,25},... | collective-permute-start | bytes 688136 | tf_op jit(solution)/shard_map/ppermute | solution.py:35
  64.7 7.7 %collective-permute-start.13 = (bf16[32,3584]{1,0:T(8,128)(2,1)S(1)}, bf16[32,3584]{1,0:T(8,128)(2,1)S(1)}, u32[]{:S(2)}, u32[]{:S(2)}) collective-permute-start(bf16[32,3584]{1,0:T(8,128)(2,1)S(1)} %fusion.1), channel_id=1, source_target_pairs={{0,6},{1,25},{2,0},{3,27},{4,2},{5,29},{6,4},{7,31},{8,14},{9,1},{... | collective-permute-start | bytes 688136 | tf_op jit(solution)/shard_map/ppermute | solution.py:35
  72.5 5.2 %collective-permute-start.14 = (bf16[32,3584]{1,0:T(8,128)(2,1)S(1)}, bf16[32,3584]{1,0:T(8,128)(2,1)S(1)}, u32[]{:S(2)}, u32[]{:S(2)}) collective-permute-start(bf16[32,3584]{1,0:T(8,128)(2,1)S(1)} %add_convert_fusion.1.refs_0_), channel_id=1, source_target_pairs={{0,24},{1,7},{2,26},{3,1},{4,28},{5,3},{6,30},{7,5},{8,0},{9,15},{... | collective-permute-start | bytes 688136 | tf_op jit(solution)/shard_map/ppermute | solution.py:35
  73.1 6.7 %collective-permute-start.15 = (bf16[32,3584]{1,0:T(8,128)(2,1)S(1)}, bf16[32,3584]{1,0:T(8,128)(2,1)S(1)}, u32[]{:S(2)}, u32[]{:S(2)}) collective-permute-start(bf16[32,3584]{1,0:T(8,128)(2,1)S(1)} %add_convert_fusion.1.refs_0_), channel_id=1, source_target_pairs={{0,16},{1,5},{2,18},{3,7},{4,20},{5,1},{6,22},{7,3},{8,24},{9,13},... | collective-permute-start | bytes 688136 | tf_op jit(solution)/shard_map/ppermute | solution.py:35
  74.7 7.5 %collective-permute-start.16 = (bf16[32,3584]{1,0:T(8,128)(2,1)S(1)}, bf16[32,3584]{1,0:T(8,128)(2,1)S(1)}, u32[]{:S(2)}, u32[]{:S(2)}) collective-permute-start(bf16[32,3584]{1,0:T(8,128)(2,1)S(1)} %add_convert_fusion.1.refs_0_), channel_id=1, source_target_pairs={{0,8},{1,3},{2,10},{3,5},{4,12},{5,7},{6,14},{7,1},{8,16},{9,11},{... | collective-permute-start | bytes 688136 | tf_op jit(solution)/shard_map/ppermute | solution.py:35
  82.2 4.5 %collective-permute-start.17 = (bf16[32,3584]{1,0:T(8,128)(2,1)S(1)}, bf16[32,3584]{1,0:T(8,128)(2,1)S(1)}, u32[]{:S(2)}, u32[]{:S(2)}) collective-permute-start(bf16[32,3584]{1,0:T(8,128)(2,1)S(1)} %add_convert_fusion.1.refs_0_), channel_id=1, source_target_pairs={{0,1},{1,0},{2,3},{3,2},{4,5},{5,4},{6,7},{7,6},{8,9},{9,8},{10,11... | collective-permute-start | bytes 688136 | tf_op jit(solution)/shard_map/ppermute | solution.py:15
  94.6 6.6 %collective-permute-start.22 = (bf16[32,3584]{1,0:T(8,128)(2,1)}, bf16[32,3584]{1,0:T(8,128)(2,1)S(1)}, u32[]{:S(2)}, u32[]{:S(2)}) collective-permute-start(bf16[32,3584]{1,0:T(8,128)(2,1)} %get-tuple-element.48), channel_id=1, source_target_pairs={{0,8},{1,3},{2,10},{3,5},{4,12},{5,7},{6,14},{7,1},{8,16},{9,11},{... | collective-permute-start | bytes 688136 | tf_op jit(solution)/shard_map/ppermute | solution.py:35
  95.2 9.0 %collective-permute-start.23 = (bf16[32,3584]{1,0:T(8,128)(2,1)}, bf16[32,3584]{1,0:T(8,128)(2,1)S(1)}, u32[]{:S(2)}, u32[]{:S(2)}) collective-permute-start(bf16[32,3584]{1,0:T(8,128)(2,1)} %get-tuple-element.49), channel_id=1, source_target_pairs={{0,16},{1,5},{2,18},{3,7},{4,20},{5,1},{6,22},{7,3},{8,24},{9,13},... | collective-permute-start | bytes 688136 | tf_op jit(solution)/shard_map/ppermute | solution.py:35
  98.1 6.1 %collective-permute-start.24 = (bf16[32,3584]{1,0:T(8,128)(2,1)}, bf16[32,3584]{1,0:T(8,128)(2,1)S(1)}, u32[]{:S(2)}, u32[]{:S(2)}) collective-permute-start(bf16[32,3584]{1,0:T(8,128)(2,1)} %get-tuple-element.50), channel_id=1, source_target_pairs={{0,24},{1,7},{2,26},{3,1},{4,28},{5,3},{6,30},{7,5},{8,0},{9,15},{... | collective-permute-start | bytes 688136 | tf_op jit(solution)/shard_map/ppermute | solution.py:35
  105.4 4.9 %collective-permute-start.25 = (bf16[8,3584]{1,0:T(8,128)(2,1)S(1)}, bf16[8,3584]{1,0:T(8,128)(2,1)S(1)}, u32[]{:S(2)}, u32[]{:S(2)}) collective-permute-start(bf16[8,3584]{1,0:T(8,128)(2,1)S(1)} %get-tuple-element.51), channel_id=1, source_target_pairs={{0,2},{1,9},{2,4},{3,11},{4,6},{5,13},{6,0},{7,15},{8,10},{9,17},{... | collective-permute-start | bytes 172040 | tf_op jit(solution)/shard_map/ppermute | solution.py:35
  105.4 4.8 %collective-permute-start.26 = (bf16[8,3584]{1,0:T(8,128)(2,1)S(1)}, bf16[8,3584]{1,0:T(8,128)(2,1)S(1)}, u32[]{:S(2)}, u32[]{:S(2)}) collective-permute-start(bf16[8,3584]{1,0:T(8,128)(2,1)S(1)} %get-tuple-element.53), channel_id=1, source_target_pairs={{0,4},{1,17},{2,6},{3,19},{4,0},{5,21},{6,2},{7,23},{8,12},{9,25},... | collective-permute-start | bytes 172040 | tf_op jit(solution)/shard_map/ppermute | solution.py:35
  111.0 5.3 %collective-permute-start.28 = (bf16[4,3584]{1,0:T(4,128)(2,1)S(1)}, bf16[4,3584]{1,0:T(4,128)(2,1)S(1)}, u32[]{:S(2)}, u32[]{:S(2)}) collective-permute-start(bf16[4,3584]{1,0:T(4,128)(2,1)S(1)} %get-tuple-element.56), channel_id=1, source_target_pairs={{0,1},{1,0},{2,3},{3,2},{4,5},{5,4},{6,7},{7,6},{8,9},{9,8},{10,11... | collective-permute-start | bytes 86024 | tf_op jit(solution)/shard_map/ppermute | solution.py:15
  (13 other events, 136.5 us)

commit v7 on v5

--- a/solution.py
+++ b/solution.py
@@ -152,9 +152,29 @@
     rows = 2 * chips * slots
     line = rows // side
     lines = chips * pairs
-
-    def kernel(spot_ref, mine_ref, other_ref, vm_ref, vo_ref, om_ref, oo_ref, *outs):
+    cuts = 4
+    span = half // cuts
+
+    def kernel(spot_ref, mine_ref, other_ref, vm_ref, vo_ref, om_ref, oo_ref, *refs):
+        outs, (value_ref, held_ref, value_sems, sems) = refs[:side], refs[side:]
         core, first = spot_ref[0], spot_ref[1]
+        value_copies, copies = [], []
+        for k, weight_ref in enumerate((vm_ref, vo_ref)):
+            value_copies.append(
+                pltpu.make_async_copy(weight_ref, value_ref.at[k], value_sems.at[k])
+            )
+            value_copies[-1].start()
+        for cut in range(cuts):
+            for k, weight_ref in enumerate((om_ref, oo_ref)):
+                start = pl.multiple_of(core * half + cut * span, 128)
+                copies.append(
+                    pltpu.make_async_copy(
+                        weight_ref.at[:, pl.ds(start, span)],
+                        held_ref.at[pl.ds(k * depth, depth), pl.ds(cut * span, span)],
+                        sems.at[cut, k],
+                    )
+                )
+                copies[-1].start()
         to = line_numbers(rows)
         along = (to // line + first) % side
         second = to // (2 * slots) % side
@@ -164,24 +184,34 @@
         latents = jnp.concatenate([mine_ref[...], other_ref[...]], axis=0)
         values = []
         for index in range(heads):
-            owner, weight_ref = (core, vm_ref) if index < heads_here else (1 - core, vo_ref)
-            place = index % heads_here
+            whose, place = divmod(index, heads_here)
+            owner = (core + whose) % 2
+            if place == 0:
+                value_copies[whose].wait()
             pick = one_hot(source + owner * heads_here + place, 2 * lines)
             picked = product(pick, latents).astype(jnp.bfloat16)
-            values.append(product(picked, weight_ref[place]).astype(jnp.bfloat16))
+            values.append(product(picked, value_ref[whose, place]).astype(jnp.bfloat16))
         values = jnp.concatenate(values, axis=1)
-        at = pl.ds(pl.multiple_of(core * half, 128), half)
-        result = product(values[:, :depth], om_ref[:, at]) + product(values[:, depth:], oo_ref[:, at])
-        result = result.astype(jnp.bfloat16)
-        for k in range(side):
-            outs[k][...] = result[k * line : (k + 1) * line]
+        for cut in range(cuts):
+            copies[2 * cut].wait()
+            copies[2 * cut + 1].wait()
+            part = slice(cut * span, (cut + 1) * span)
+            result = product(values, held_ref[:, part]).astype(jnp.bfloat16)
+            for k in range(side):
+                outs[k][:, part] = result[k * line : (k + 1) * line]
 
     return pl.pallas_call(
         kernel,
-        in_specs=[in_smem] + [in_vmem] * 6,
+        in_specs=[in_smem] + [in_vmem] * 2 + [in_hbm] * 4,
         out_specs=[in_vmem] * side,
         out_shape=[jax.ShapeDtypeStruct((line, half), jnp.bfloat16)] * side,
-        compiler_params=budget(24),
+        scratch_shapes=[
+            pltpu.VMEM((2, heads_here, latent_width, head), jnp.bfloat16),
+            pltpu.VMEM((2 * depth, half), jnp.bfloat16),
+            pltpu.SemaphoreType.DMA((2,)),
+            pltpu.SemaphoreType.DMA((cuts, 2)),
+        ],
+        compiler_params=budget(59),
         cost_estimate=pl.CostEstimate(
             flops=4 * rows * depth * half, bytes_accessed=4 * depth * half, transcendentals=0
         ),
@@ -357,6 +387,7 @@
     summed, pieces[2], pieces[3] = lax.optimization_barrier((summed, pieces[2], pieces[3]))
     residual_line = total(turn([summed] * side, 1, side, 1)).astype(jnp.bfloat16)
     residual_mine = turn([residual_line] * side, 0, side, -1)
+    residual_mine = lax.optimization_barrier(residual_mine)
     residual_other = [core_swap(part, width) for part in residual_mine]
     sums = gated(residual_mine, norm_gain, gate_weight, up_weight, spot, None)
     inner = gated(residual_other, norm_gain, gate_weight, up_weight, spot, sums)

time: 110 us -> 113 us (1.027)
  starting transfers between devices: 53.7 us -> 46.8 us
  local copies, waits for them, and re-layouts: 3.96 us -> 7.59 us
  waiting for transfers between devices: 28.1 us -> 31.3 us
  Pallas kernels: 20.5 us -> 22.3 us
  other arithmetic: 2.23 us -> 3.65 us
    ppermute x15, waiting for transfers between devices: 20.7 us -> 27.9 us  [turn(): out.append(lax.ppermute(parts[k], 'tp', pairs))]
    ppermute x10, starting transfers between devices: 16.9 us -> 12.2 us  [core_swap(): return lax.ppermute(x, 'tp', [(i, i ^ 1) for i in range(width)])]
    unnamed x14 -> x28, local copies, waits for them, and re-layouts: 3.7 us -> 6.7 us
    ppermute x4, waiting for transfers between devices: 4.38 us -> 1.53 us  [down_pieces(): out.append(lax.ppermute(down_weight, ('dp', 'tp'), pairs))]
    pallas_call x1, Pallas kernels: 3.99 us -> 6.66 us  [project(): pl.pallas_call(kernel, in_specs=[in_smem] + [in_vmem] * 2 + [in_hbm] * 4,...]
    ppermute x15, starting transfers between devices: 19 us -> 16.9 us  [turn(): out.append(lax.ppermute(parts[k], 'tp', pairs))]
    ppermute x10, waiting for transfers between devices: 3.07 us -> 1.81 us  [core_swap(): return lax.ppermute(x, 'tp', [(i, i ^ 1) for i in range(width)])]
  transfers between devices with their start and end apart: 30 -> 30, of which waited for: 16 -> 16; matrix products, arithmetic and copies ran while one was open for 0% -> 3% of each run, Pallas kernels for 14% -> 16%
where the time goes in v7:
time: 113 us
  starting transfers between devices  46.8 us (41%)
  waiting for transfers between devices  31.3 us (28%)
  Pallas kernels  22.3 us (20%)
  local copies, waits for them, and re-layouts  7.59 us (7%)
  other arithmetic  3.65 us (3%)
    ppermute x15, waiting for transfers between devices, turn(): out.append(lax.ppermute(parts[k], 'tp', pairs))  27.9 us
    ppermute x15, starting transfers between devices, turn(): out.append(lax.ppermute(parts[k], 'tp', pairs))  16.9 us
    ppermute x10, starting transfers between devices, core_swap(): return lax.ppermute(x, 'tp', [(i, i ^ 1) for i in range(width)])  12.2 us
    ppermute x4, starting transfers between devices, down_pieces(): out.append(lax.ppermute(down_weight, ('dp', 'tp'), pairs))  10.9 us
    pallas_call x1, Pallas kernels, attend(): pl.pallas_call(kernel, in_specs=[in_smem, in_smem, in_vmem, in_hbm], out_...  9.01 us
    all_to_all x1, starting transfers between devices, between_chips(): return lax.all_to_all(x, 'tp', 0, 0, tiled=True, axis_index_groups=groups)  6.76 us
    unnamed x28, local copies, waits for them, and re-layouts  6.7 us
    pallas_call x1, Pallas kernels, project(): pl.pallas_call(kernel, in_specs=[in_smem] + [in_vmem] * 2 + [in_hbm] * 4,...  6.66 us
  transfers between devices with their start and end apart: 30, of which 16 were waited for; matrix products, arithmetic and copies ran while one was open for 3% of the time, Pallas kernels for 16%

profile of v7, /device:TPU:1, one launch (start us, length us, event | category | flops | bytes accessed | tf_op | source)
XLA Modules:
  0.0 112.5 jit_solution(137228767792202662)
XLA Ops:
  1.4 3.5 %collective-permute-start = (bf16[288,1792]{1,0:T(8,128)(2,1)}, bf16[288,1792]{1,0:T(8,128)(2,1)S(1)}, u32[]{:S(2)}, u32[]{:S(2)}) collective-permute-start(bf16[288,1792]{1,0:T(8,128)(2,1)} %param.21), channel_id=1, source_target_pairs={{0,0},{64,1},{2,2},{66,3},{4,4},{68,5},{6,6},{70,7},{8,8},{72,9},{... | collective-permute-start | bytes 3096584 | tf_op jit(solution)/shard_map/ppermute | solution.py:55
  5.7 9.0 %shard_map.109 = bf16[256,512]{1,0:T(8,128)(2,1)} custom-call(s32[4]{0:T(128)} %lengths_ref.1, s32[1]{0:T(128)} %copy.12.counts_ref, bf16[4,64,576]{2,1,0:T(8,128)(2,1)} %q_ref.1, bf16[4,576,2048]{2,1,0:T(8,128)(2,1)} %bitcast.25), custom_call_target="tpu_custom_call" | custom-call | flops 1140850688 | bytes 9437184 | tf_op jit(solution)/shard_map/pallas_call | solution.py:127
  14.7 6.8 %all-to-all-start = ((bf16[16,16,512]{2,1,0:T(8,128)(2,1)}), bf16[16,16,512]{2,1,0:T(8,128)(2,1)S(1)}, u32[]{:S(2)}, u32[]{:S(2)}) async-start(bf16[16,16,512]{2,1,0:T(8,128)(2,1)} %bitcast.27), calls=%async_computation | async-start | bytes 524288 | tf_op jit(solution)/shard_map/all_to_all | solution.py:20
  21.5 6.9 %collective-permute-start.10 = (bf16[288,1792]{1,0:T(8,128)(2,1)}, bf16[288,1792]{1,0:T(8,128)(2,1)S(1)}, u32[]{:S(2)}, u32[]{:S(2)}) collective-permute-start(bf16[288,1792]{1,0:T(8,128)(2,1)} %param.21), channel_id=1, source_target_pairs={{33,0},{97,1},{35,2},{99,3},{37,4},{101,5},{39,6},{103,7},{41,8},{... | collective-permute-start | bytes 3096584 | tf_op jit(solution)/shard_map/ppermute | solution.py:55
  36.1 6.7 %shard_map.110 = (bf16[32,3584]{1,0:T(8,128)(2,1)}, bf16[32,3584]{1,0:T(8,128)(2,1)}, bf16[32,3584]{1,0:T(8,128)(2,1)}, bf16[32,3584]{1,0:T(8,128)(2,1)}) custom-call(s32[4]{0:T(128)} %pad_add_fusion.spot_ref, bf16[256,512]{1,0:T(8,128)(2,1)} %bitcast.26, bf16[256,512]{1,0:T(8,128)(2,1)} %bitcast.28, bf16[2,512,128]{2,1,0:T(8,128)(2,1)} %vm_ref.1, ...), custom_call_target="tpu_custom_call" | custom-call | flops 469762048 | bytes 3670016 | tf_op jit(solution)/shard_map/pallas_call | solution.py:203
  43.1 2.2 %collective-permute-start.6 = (bf16[32,3584]{1,0:T(8,128)(2,1)}, bf16[32,3584]{1,0:T(8,128)(2,1)S(1)}, u32[]{:S(2)}, u32[]{:S(2)}) collective-permute-start(bf16[32,3584]{1,0:T(8,128)(2,1)} %get-tuple-element.28), channel_id=1, source_target_pairs={{0,16},{1,5},{2,18},{3,7},{4,20},{5,1},{6,22},{7,3},{8,24},{9,13},... | collective-permute-start | bytes 688136 | tf_op jit(solution)/shard_map/ppermute | solution.py:35
  47.3 4.5 %collective-permute-done.5 = bf16[32,3584]{1,0:T(8,128)(2,1)S(1)} collective-permute-done((bf16[32,3584]{1,0:T(8,128)(2,1)}, bf16[32,3584]{1,0:T(8,128)(2,1)S(1)}, u32[]{:S(2)}, u32[]{:S(2)}) %collective-permute-start.5) | collective-permute-done | bytes 229408 | tf_op jit(solution)/shard_map/ppermute | solution.py:35
  54.7 2.6 %collective-permute-start.12 = (bf16[32,3584]{1,0:T(8,128)(2,1)S(1)}, bf16[32,3584]{1,0:T(8,128)(2,1)S(1)}, u32[]{:S(2)}, u32[]{:S(2)}) collective-permute-start(bf16[32,3584]{1,0:T(8,128)(2,1)S(1)} %fusion.1), channel_id=1, source_target_pairs={{0,4},{1,17},{2,6},{3,19},{4,0},{5,21},{6,2},{7,23},{8,12},{9,25},... | collective-permute-start | bytes 688136 | tf_op jit(solution)/shard_map/ppermute | solution.py:35
  58.4 2.6 %collective-permute-done.11 = bf16[32,3584]{1,0:T(8,128)(2,1)S(1)} collective-permute-done((bf16[32,3584]{1,0:T(8,128)(2,1)S(1)}, bf16[32,3584]{1,0:T(8,128)(2,1)S(1)}, u32[]{:S(2)}, u32[]{:S(2)}) %collective-permute-start.11) | collective-permute-done | bytes 229408 | tf_op jit(solution)/shard_map/ppermute | solution.py:35
  61.0 2.5 %collective-permute-done.12 = bf16[32,3584]{1,0:T(8,128)(2,1)S(1)} collective-permute-done((bf16[32,3584]{1,0:T(8,128)(2,1)S(1)}, bf16[32,3584]{1,0:T(8,128)(2,1)S(1)}, u32[]{:S(2)}, u32[]{:S(2)}) %collective-permute-start.12) | collective-permute-done | bytes 229408 | tf_op jit(solution)/shard_map/ppermute | solution.py:35
  64.2 2.3 %collective-permute-start.14 = (bf16[32,3584]{1,0:T(8,128)(2,1)S(1)}, bf16[32,3584]{1,0:T(8,128)(2,1)S(1)}, u32[]{:S(2)}, u32[]{:S(2)}) collective-permute-start(bf16[32,3584]{1,0:T(8,128)(2,1)S(1)} %add_convert_fusion.1.refs_0_), channel_id=1, source_target_pairs={{0,24},{1,7},{2,26},{3,1},{4,28},{5,3},{6,30},{7,5},{8,0},{9,15},{... | collective-permute-start | bytes 688136 | tf_op jit(solution)/shard_map/ppermute | solution.py:35
  67.2 4.8 %collective-permute-done.14.refs_1_ = bf16[32,3584]{1,0:T(8,128)(2,1)S(1)} collective-permute-done((bf16[32,3584]{1,0:T(8,128)(2,1)S(1)}, bf16[32,3584]{1,0:T(8,128)(2,1)S(1)}, u32[]{:S(2)}, u32[]{:S(2)}) %collective-permute-start.14) | collective-permute-done | bytes 229408 | tf_op jit(solution)/shard_map/ppermute | solution.py:35
  73.0 2.6 %collective-permute-done.16.refs_3_ = bf16[32,3584]{1,0:T(8,128)(2,1)S(1)} collective-permute-done((bf16[32,3584]{1,0:T(8,128)(2,1)S(1)}, bf16[32,3584]{1,0:T(8,128)(2,1)S(1)}, u32[]{:S(2)}, u32[]{:S(2)}) %collective-permute-start.16) | collective-permute-done | bytes 229408 | tf_op jit(solution)/shard_map/ppermute | solution.py:35
  75.7 3.8 %collective-permute-start.17 = (bf16[32,3584]{1,0:T(8,128)(2,1)S(1)}, bf16[32,3584]{1,0:T(8,128)(2,1)S(1)}, u32[]{:S(2)}, u32[]{:S(2)}) collective-permute-start(bf16[32,3584]{1,0:T(8,128)(2,1)S(1)} %add_convert_fusion.1.refs_0_), channel_id=1, source_target_pairs={{0,1},{1,0},{2,3},{3,2},{4,5},{5,4},{6,7},{7,6},{8,9},{9,8},{10,11... | collective-permute-start | bytes 688136 | tf_op jit(solution)/shard_map/ppermute | solution.py:15
  80.0 2.2 %copy-done.1 = bf16[7168,288]{0,1:T(8,128)(2,1)S(1)} copy-done((bf16[7168,288]{0,1:T(8,128)(2,1)S(1)}, bf16[7168,288]{0,1:T(8,128)(2,1)}, u32[]{:S(2)}) %copy-start.1) | copy-done | bytes 4128792
  82.9 1.9 %shard_map.111 = (f32[128,576]{1,0:T(8,128)S(1)}, f32[128,128]{1,0:T(8,128)S(1)}) custom-call(s32[4]{0:T(128)S(1)} %copy-done.9, bf16[32,3584]{1,0:T(8,128)(2,1)S(1)} %add_convert_fusion.1.refs_0_, bf16[32,3584]{1,0:T(8,128)(2,1)S(1)} %collective-permute-done.14.refs_1_, bf16[32,3584]{1,0:T(8,128)(2,1)S(1)} %collective-permute-done.15.refs_2_, ...), custom_call_target="tpu_custom_call" | custom-call | flops 528482304 | bytes 4128768 | tf_op jit(solution)/shard_map/pallas_call | solution.py:273
  84.9 2.3 %shard_map.112.inner_ref = bf16[128,288]{1,0:T(8,128)(2,1)S(1)} custom-call(s32[4]{0:T(128)S(1)} %copy-done.9, bf16[32,3584]{1,0:T(8,128)(2,1)S(1)} %collective-permute-done.17.refs_0_, bf16[32,3584]{1,0:T(8,128)(2,1)S(1)} %collective-permute-done.18.refs_1_, bf16[32,3584]{1,0:T(8,128)(2,1)S(1)} %collective-permute-done.19.refs_2_, ...), custom_call_target="tpu_custom_call" | custom-call | flops 528482304 | bytes 4128768 | tf_op jit(solution)/shard_map/pallas_call | solution.py:273
  88.7 2.5 %shard_map.113 = (bf16[32,3584]{1,0:T(8,128)(2,1)S(1)}, bf16[32,3584]{1,0:T(8,128)(2,1)S(1)}, bf16[32,3584]{1,0:T(8,128)(2,1)S(1)}, bf16[32,3584]{1,0:T(8,128)(2,1)S(1)}) custom-call(s32[4]{0:T(128)S(1)} %copy-done.9, bf16[128,288]{1,0:T(8,128)(2,1)S(1)} %shard_map.112.inner_ref, bf16[128,288]{1,0:T(8,128)(2,1)S(1)} %collective-permute-done.21.other_ref, ...), custom_call_target="tpu_custom_call" | custom-call | flops 528482304 | bytes 4128768 | tf_op jit(solution)/shard_map/pallas_call | solution.py:312
  92.2 2.6 %collective-permute-start.23 = (bf16[32,3584]{1,0:T(8,128)(2,1)S(1)}, bf16[32,3584]{1,0:T(8,128)(2,1)S(1)}, u32[]{:S(2)}, u32[]{:S(2)}) collective-permute-start(bf16[32,3584]{1,0:T(8,128)(2,1)S(1)} %get-tuple-element.43), channel_id=1, source_target_pairs={{0,16},{1,5},{2,18},{3,7},{4,20},{5,1},{6,22},{7,3},{8,24},{9,13},... | collective-permute-start | bytes 688136 | tf_op jit(solution)/shard_map/ppermute | solution.py:35
  94.9 2.7 %collective-permute-done.22 = bf16[32,3584]{1,0:T(8,128)(2,1)S(1)} collective-permute-done((bf16[32,3584]{1,0:T(8,128)(2,1)S(1)}, bf16[32,3584]{1,0:T(8,128)(2,1)S(1)}, u32[]{:S(2)}, u32[]{:S(2)}) %collective-permute-start.22) | collective-permute-done | bytes 229408 | tf_op jit(solution)/shard_map/ppermute | solution.py:35
  97.6 3.1 %collective-permute-done.23 = bf16[32,3584]{1,0:T(8,128)(2,1)S(1)} collective-permute-done((bf16[32,3584]{1,0:T(8,128)(2,1)S(1)}, bf16[32,3584]{1,0:T(8,128)(2,1)S(1)}, u32[]{:S(2)}, u32[]{:S(2)}) %collective-permute-start.23) | collective-permute-done | bytes 229408 | tf_op jit(solution)/shard_map/ppermute | solution.py:35
  100.9 1.8 %collective-permute-start.26 = (bf16[8,3584]{1,0:T(8,128)(2,1)S(1)}, bf16[8,3584]{1,0:T(8,128)(2,1)S(1)}, u32[]{:S(2)}, u32[]{:S(2)}) collective-permute-start(bf16[8,3584]{1,0:T(8,128)(2,1)S(1)} %get-tuple-element.47), channel_id=1, source_target_pairs={{0,4},{1,17},{2,6},{3,19},{4,0},{5,21},{6,2},{7,23},{8,12},{9,25},... | collective-permute-start | bytes 172040 | tf_op jit(solution)/shard_map/ppermute | solution.py:35
  103.6 2.2 %collective-permute-done.25 = bf16[8,3584]{1,0:T(8,128)(2,1)S(1)} collective-permute-done((bf16[8,3584]{1,0:T(8,128)(2,1)S(1)}, bf16[8,3584]{1,0:T(8,128)(2,1)S(1)}, u32[]{:S(2)}, u32[]{:S(2)}) %collective-permute-start.25) | collective-permute-done | bytes 57376 | tf_op jit(solution)/shard_map/ppermute | solution.py:35
  106.5 4.5 %collective-permute-start.28 = (bf16[4,3584]{1,0:T(4,128)(2,1)S(1)}, bf16[4,3584]{1,0:T(4,128)(2,1)S(1)}, u32[]{:S(2)}, u32[]{:S(2)}) collective-permute-start(bf16[4,3584]{1,0:T(4,128)(2,1)S(1)} %get-tuple-element.50), channel_id=1, source_target_pairs={{0,1},{1,0},{2,3},{3,2},{4,5},{5,4},{6,7},{7,6},{8,9},{9,8},{10,11... | collective-permute-start | bytes 86024 | tf_op jit(solution)/shard_map/ppermute | solution.py:15
  (85 shorter events, 25.1 us)
Async XLA Ops:
  0.0 35.3 %collective-permute-start.4 = (bf16[256,7168]{1,0:T(8,128)(2,1)}, bf16[256,7168]{1,0:T(8,128)(2,1)}, u32[]{:S(2)}, u32[]{:S(2)}) collective-permute-start(bf16[256,7168]{1,0:T(8,128)(2,1)} %om_ref.1), channel_id=1, source_target_pairs={{0,1},{1,0},{2,3},{3,2},{4,5},{5,4},{6,7},{7,6},{8,9},{9,8},{10,11... | collective-permute-start | bytes 11010056 | tf_op jit(solution)/shard_map/ppermute | solution.py:15
  1.4 28.6 %collective-permute-start = (bf16[288,1792]{1,0:T(8,128)(2,1)}, bf16[288,1792]{1,0:T(8,128)(2,1)S(1)}, u32[]{:S(2)}, u32[]{:S(2)}) collective-permute-start(bf16[288,1792]{1,0:T(8,128)(2,1)} %param.21), channel_id=1, source_target_pairs={{0,0},{64,1},{2,2},{66,3},{4,4},{68,5},{6,6},{70,7},{8,8},{72,9},{... | collective-permute-start | bytes 3096584 | tf_op jit(solution)/shard_map/ppermute | solution.py:55
  4.9 26.4 %collective-permute-start.1 = (bf16[288,1792]{1,0:T(8,128)(2,1)}, bf16[288,1792]{1,0:T(8,128)(2,1)S(1)}, u32[]{:S(2)}, u32[]{:S(2)}) collective-permute-start(bf16[288,1792]{1,0:T(8,128)(2,1)} %param.21), channel_id=1, source_target_pairs={{1,0},{65,1},{3,2},{67,3},{5,4},{69,5},{7,6},{71,7},{9,8},{73,9},{... | collective-permute-start | bytes 3096584 | tf_op jit(solution)/shard_map/ppermute | solution.py:55
  14.7 16.3 %all-to-all-start = ((bf16[16,16,512]{2,1,0:T(8,128)(2,1)}), bf16[16,16,512]{2,1,0:T(8,128)(2,1)S(1)}, u32[]{:S(2)}, u32[]{:S(2)}) async-start(bf16[16,16,512]{2,1,0:T(8,128)(2,1)} %bitcast.27), calls=%async_computation | async-start | bytes 524288 | tf_op jit(solution)/shard_map/all_to_all | solution.py:20
  21.5 32.2 %collective-permute-start.10 = (bf16[288,1792]{1,0:T(8,128)(2,1)}, bf16[288,1792]{1,0:T(8,128)(2,1)S(1)}, u32[]{:S(2)}, u32[]{:S(2)}) collective-permute-start(bf16[288,1792]{1,0:T(8,128)(2,1)} %param.21), channel_id=1, source_target_pairs={{33,0},{97,1},{35,2},{99,3},{37,4},{101,5},{39,6},{103,7},{41,8},{... | collective-permute-start | bytes 3096584 | tf_op jit(solution)/shard_map/ppermute | solution.py:55
  28.4 26.2 %collective-permute-start.9 = (bf16[288,1792]{1,0:T(8,128)(2,1)}, bf16[288,1792]{1,0:T(8,128)(2,1)}, u32[]{:S(2)}, u32[]{:S(2)}) collective-permute-start(bf16[288,1792]{1,0:T(8,128)(2,1)} %param.21), channel_id=1, source_target_pairs={{32,0},{96,1},{34,2},{98,3},{36,4},{100,5},{38,6},{102,7},{40,8},{... | collective-permute-start | bytes 3096584 | tf_op jit(solution)/shard_map/ppermute | solution.py:55
  35.2 10.0 %collective-permute-start.8 = (bf16[4,3584]{1,0:T(4,128)(2,1)}, bf16[4,3584]{1,0:T(4,128)(2,1)}, u32[]{:S(2)}, u32[]{:S(2)}) collective-permute-start(bf16[4,3584]{1,0:T(4,128)(2,1)} %get-tuple-element.52), channel_id=1, source_target_pairs={{0,1},{1,0},{2,3},{3,2},{4,5},{5,4},{6,7},{7,6},{8,9},{9,8},{10,11... | collective-permute-start | bytes 86024 | tf_op jit(solution)/shard_map/ppermute | solution.py:15
  42.7 9.1 %collective-permute-start.5 = (bf16[32,3584]{1,0:T(8,128)(2,1)}, bf16[32,3584]{1,0:T(8,128)(2,1)S(1)}, u32[]{:S(2)}, u32[]{:S(2)}) collective-permute-start(bf16[32,3584]{1,0:T(8,128)(2,1)} %get-tuple-element.27), channel_id=1, source_target_pairs={{0,8},{1,3},{2,10},{3,5},{4,12},{5,7},{6,14},{7,1},{8,16},{9,11},{... | collective-permute-start | bytes 688136 | tf_op jit(solution)/shard_map/ppermute | solution.py:35
  43.1 8.8 %collective-permute-start.6 = (bf16[32,3584]{1,0:T(8,128)(2,1)}, bf16[32,3584]{1,0:T(8,128)(2,1)S(1)}, u32[]{:S(2)}, u32[]{:S(2)}) collective-permute-start(bf16[32,3584]{1,0:T(8,128)(2,1)} %get-tuple-element.28), channel_id=1, source_target_pairs={{0,16},{1,5},{2,18},{3,7},{4,20},{5,1},{6,22},{7,3},{8,24},{9,13},... | collective-permute-start | bytes 688136 | tf_op jit(solution)/shard_map/ppermute | solution.py:35
  45.3 7.3 %collective-permute-start.7 = (bf16[32,3584]{1,0:T(8,128)(2,1)}, bf16[32,3584]{1,0:T(8,128)(2,1)S(1)}, u32[]{:S(2)}, u32[]{:S(2)}) collective-permute-start(bf16[32,3584]{1,0:T(8,128)(2,1)} %get-tuple-element.29), channel_id=1, source_target_pairs={{0,24},{1,7},{2,26},{3,1},{4,28},{5,3},{6,30},{7,5},{8,0},{9,15},{... | collective-permute-start | bytes 688136 | tf_op jit(solution)/shard_map/ppermute | solution.py:35
  54.7 6.4 %collective-permute-start.11 = (bf16[32,3584]{1,0:T(8,128)(2,1)S(1)}, bf16[32,3584]{1,0:T(8,128)(2,1)S(1)}, u32[]{:S(2)}, u32[]{:S(2)}) collective-permute-start(bf16[32,3584]{1,0:T(8,128)(2,1)S(1)} %fusion.1), channel_id=1, source_target_pairs={{0,2},{1,9},{2,4},{3,11},{4,6},{5,13},{6,0},{7,15},{8,10},{9,17},{... | collective-permute-start | bytes 688136 | tf_op jit(solution)/shard_map/ppermute | solution.py:35
  54.7 8.8 %collective-permute-start.12 = (bf16[32,3584]{1,0:T(8,128)(2,1)S(1)}, bf16[32,3584]{1,0:T(8,128)(2,1)S(1)}, u32[]{:S(2)}, u32[]{:S(2)}) collective-permute-start(bf16[32,3584]{1,0:T(8,128)(2,1)S(1)} %fusion.1), channel_id=1, source_target_pairs={{0,4},{1,17},{2,6},{3,19},{4,0},{5,21},{6,2},{7,23},{8,12},{9,25},... | collective-permute-start | bytes 688136 | tf_op jit(solution)/shard_map/ppermute | solution.py:35
  57.4 6.7 %collective-permute-start.13 = (bf16[32,3584]{1,0:T(8,128)(2,1)S(1)}, bf16[32,3584]{1,0:T(8,128)(2,1)S(1)}, u32[]{:S(2)}, u32[]{:S(2)}) collective-permute-start(bf16[32,3584]{1,0:T(8,128)(2,1)S(1)} %fusion.1), channel_id=1, source_target_pairs={{0,6},{1,25},{2,0},{3,27},{4,2},{5,29},{6,4},{7,31},{8,14},{9,1},{... | collective-permute-start | bytes 688136 | tf_op jit(solution)/shard_map/ppermute | solution.py:35
  64.2 7.8 %collective-permute-start.14 = (bf16[32,3584]{1,0:T(8,128)(2,1)S(1)}, bf16[32,3584]{1,0:T(8,128)(2,1)S(1)}, u32[]{:S(2)}, u32[]{:S(2)}) collective-permute-start(bf16[32,3584]{1,0:T(8,128)(2,1)S(1)} %add_convert_fusion.1.refs_0_), channel_id=1, source_target_pairs={{0,24},{1,7},{2,26},{3,1},{4,28},{5,3},{6,30},{7,5},{8,0},{9,15},{... | collective-permute-start | bytes 688136 | tf_op jit(solution)/shard_map/ppermute | solution.py:35
  66.6 6.5 %collective-permute-start.15 = (bf16[32,3584]{1,0:T(8,128)(2,1)S(1)}, bf16[32,3584]{1,0:T(8,128)(2,1)S(1)}, u32[]{:S(2)}, u32[]{:S(2)}) collective-permute-start(bf16[32,3584]{1,0:T(8,128)(2,1)S(1)} %add_convert_fusion.1.refs_0_), channel_id=1, source_target_pairs={{0,16},{1,5},{2,18},{3,7},{4,20},{5,1},{6,22},{7,3},{8,24},{9,13},... | collective-permute-start | bytes 688136 | tf_op jit(solution)/shard_map/ppermute | solution.py:35
  67.0 8.7 %collective-permute-start.16 = (bf16[32,3584]{1,0:T(8,128)(2,1)S(1)}, bf16[32,3584]{1,0:T(8,128)(2,1)S(1)}, u32[]{:S(2)}, u32[]{:S(2)}) collective-permute-start(bf16[32,3584]{1,0:T(8,128)(2,1)S(1)} %add_convert_fusion.1.refs_0_), channel_id=1, source_target_pairs={{0,8},{1,3},{2,10},{3,5},{4,12},{5,7},{6,14},{7,1},{8,16},{9,11},{... | collective-permute-start | bytes 688136 | tf_op jit(solution)/shard_map/ppermute | solution.py:35
  75.7 9.2 %collective-permute-start.17 = (bf16[32,3584]{1,0:T(8,128)(2,1)S(1)}, bf16[32,3584]{1,0:T(8,128)(2,1)S(1)}, u32[]{:S(2)}, u32[]{:S(2)}) collective-permute-start(bf16[32,3584]{1,0:T(8,128)(2,1)S(1)} %add_convert_fusion.1.refs_0_), channel_id=1, source_target_pairs={{0,1},{1,0},{2,3},{3,2},{4,5},{5,4},{6,7},{7,6},{8,9},{9,8},{10,11... | collective-permute-start | bytes 688136 | tf_op jit(solution)/shard_map/ppermute | solution.py:15
  79.5 5.4 %collective-permute-start.18 = (bf16[32,3584]{1,0:T(8,128)(2,1)S(1)}, bf16[32,3584]{1,0:T(8,128)(2,1)S(1)}, u32[]{:S(2)}, u32[]{:S(2)}) collective-permute-start(bf16[32,3584]{1,0:T(8,128)(2,1)S(1)} %collective-permute-done.14.refs_1_), channel_id=1, source_target_pairs={{0,1},{1,0},{2,3},{3,2},{4,5},{5,4},{6,7},{7,6},{8,9},{9,8},{10,11... | collective-permute-start | bytes 688136 | tf_op jit(solution)/shard_map/ppermute | solution.py:15
  79.5 5.4 %collective-permute-start.19 = (bf16[32,3584]{1,0:T(8,128)(2,1)S(1)}, bf16[32,3584]{1,0:T(8,128)(2,1)S(1)}, u32[]{:S(2)}, u32[]{:S(2)}) collective-permute-start(bf16[32,3584]{1,0:T(8,128)(2,1)S(1)} %collective-permute-done.15.refs_2_), channel_id=1, source_target_pairs={{0,1},{1,0},{2,3},{3,2},{4,5},{5,4},{6,7},{7,6},{8,9},{9,8},{10,11... | collective-permute-start | bytes 688136 | tf_op jit(solution)/shard_map/ppermute | solution.py:15
  91.2 6.4 %collective-permute-start.22 = (bf16[32,3584]{1,0:T(8,128)(2,1)S(1)}, bf16[32,3584]{1,0:T(8,128)(2,1)S(1)}, u32[]{:S(2)}, u32[]{:S(2)}) collective-permute-start(bf16[32,3584]{1,0:T(8,128)(2,1)S(1)} %get-tuple-element.42), channel_id=1, source_target_pairs={{0,8},{1,3},{2,10},{3,5},{4,12},{5,7},{6,14},{7,1},{8,16},{9,11},{... | collective-permute-start | bytes 688136 | tf_op jit(solution)/shard_map/ppermute | solution.py:35
  92.2 8.5 %collective-permute-start.23 = (bf16[32,3584]{1,0:T(8,128)(2,1)S(1)}, bf16[32,3584]{1,0:T(8,128)(2,1)S(1)}, u32[]{:S(2)}, u32[]{:S(2)}) collective-permute-start(bf16[32,3584]{1,0:T(8,128)(2,1)S(1)} %get-tuple-element.43), channel_id=1, source_target_pairs={{0,16},{1,5},{2,18},{3,7},{4,20},{5,1},{6,22},{7,3},{8,24},{9,13},... | collective-permute-start | bytes 688136 | tf_op jit(solution)/shard_map/ppermute | solution.py:35
  94.8 5.9 %collective-permute-start.24 = (bf16[32,3584]{1,0:T(8,128)(2,1)S(1)}, bf16[32,3584]{1,0:T(8,128)(2,1)S(1)}, u32[]{:S(2)}, u32[]{:S(2)}) collective-permute-start(bf16[32,3584]{1,0:T(8,128)(2,1)S(1)} %get-tuple-element.44), channel_id=1, source_target_pairs={{0,24},{1,7},{2,26},{3,1},{4,28},{5,3},{6,30},{7,5},{8,0},{9,15},{... | collective-permute-start | bytes 688136 | tf_op jit(solution)/shard_map/ppermute | solution.py:35
  100.9 4.9 %collective-permute-start.25 = (bf16[8,3584]{1,0:T(8,128)(2,1)S(1)}, bf16[8,3584]{1,0:T(8,128)(2,1)S(1)}, u32[]{:S(2)}, u32[]{:S(2)}) collective-permute-start(bf16[8,3584]{1,0:T(8,128)(2,1)S(1)} %get-tuple-element.45), channel_id=1, source_target_pairs={{0,2},{1,9},{2,4},{3,11},{4,6},{5,13},{6,0},{7,15},{8,10},{9,17},{... | collective-permute-start | bytes 172040 | tf_op jit(solution)/shard_map/ppermute | solution.py:35
  106.5 5.3 %collective-permute-start.28 = (bf16[4,3584]{1,0:T(4,128)(2,1)S(1)}, bf16[4,3584]{1,0:T(4,128)(2,1)S(1)}, u32[]{:S(2)}, u32[]{:S(2)}) collective-permute-start(bf16[4,3584]{1,0:T(4,128)(2,1)S(1)} %get-tuple-element.50), channel_id=1, source_target_pairs={{0,1},{1,0},{2,3},{3,2},{4,5},{5,4},{6,7},{7,6},{8,9},{9,8},{10,11... | collective-permute-start | bytes 86024 | tf_op jit(solution)/shard_map/ppermute | solution.py:15
  (20 other events, 161.1 us)

commit v8 on v5

--- a/solution.py
+++ b/solution.py
@@ -43,17 +43,14 @@
     return wide
 
 
-def down_pieces(down_weight, width):
-    out = []
-    for k in range(4):
-        pairs = []
-        for layer in range(4):
-            for place in range(width):
-                chip, core = divmod(place, 2)
-                cut, row_core = (layer >> 1) ^ (k >> 1), (layer & 1) ^ (k & 1)
-                pairs.append(((2 * core + cut) * width + 2 * chip + row_core, layer * width + place))
-        out.append(lax.ppermute(down_weight, ("dp", "tp"), pairs))
-    return out
+def down_piece(down_weight, width, k):
+    pairs = []
+    for layer in range(4):
+        for place in range(width):
+            chip, core = divmod(place, 2)
+            cut, row_core = (layer >> 1) ^ (k >> 1), (layer & 1) ^ (k & 1)
+            pairs.append(((2 * core + cut) * width + 2 * chip + row_core, layer * width + place))
+    return lax.ppermute(down_weight, ("dp", "tp"), pairs)
 
 
 in_vmem = pl.BlockSpec(memory_space=pltpu.VMEM)
@@ -321,7 +318,7 @@
     layer = lax.axis_index("dp")
     spot = jnp.stack([core, first, second, layer])
 
-    pieces = down_pieces(down_weight, width)
+    pieces = [down_piece(down_weight, width, k) for k in range(2)]
     value_other = core_swap(value_weight, width)
     output_other = core_swap(output_weight, width)
     input_mine = lax.dynamic_slice_in_dim(layer_input, core * half, half, 1)
@@ -350,13 +347,20 @@
         slots,
     )
 
+    later, attended_parts = lax.optimization_barrier((down_weight, attended_parts))
+    pieces.append(down_piece(later, width, 2))
+    later, pieces[2] = lax.optimization_barrier((down_weight, pieces[2]))
+    pieces.append(down_piece(later, width, 3))
+
     summed = total(turn(attended_parts, 0, side, 1)).reshape(side, chip_slots, half)
     own_rows = (jnp.arange(side) == second)[:, None, None]
     summed = summed + jnp.where(own_rows, input_chip[None], 0.0)
     summed = summed.astype(jnp.bfloat16).reshape(line, half)
-    summed, pieces[2], pieces[3] = lax.optimization_barrier((summed, pieces[2], pieces[3]))
     residual_line = total(turn([summed] * side, 1, side, 1)).astype(jnp.bfloat16)
     residual_mine = turn([residual_line] * side, 0, side, -1)
+    residual_mine, pieces[2], pieces[3] = lax.optimization_barrier(
+        (residual_mine, pieces[2], pieces[3])
+    )
     residual_other = [core_swap(part, width) for part in residual_mine]
     sums = gated(residual_mine, norm_gain, gate_weight, up_weight, spot, None)
     inner = gated(residual_other, norm_gain, gate_weight, up_weight, spot, sums)

time: 110 us -> 107 us (0.973)
  waiting for transfers between devices: 28.1 us -> 34 us
  starting transfers between devices: 53.7 us -> 49.3 us
  Pallas kernels: 20.5 us -> 18.8 us
  local copies, waits for them, and re-layouts: 3.96 us -> 2.32 us
    ppermute x4, waiting for transfers between devices: 4.38 us -> 10.4 us  [down_piece(): return lax.ppermute(down_weight, ('dp', 'tp'), pairs)]
    all_to_all x1, waiting for transfers between devices: 0.01 us -> 4.92 us  [between_chips(): return lax.all_to_all(x, 'tp', 0, 0, tiled=True, axis_index_groups=groups)]
    ppermute x10, starting transfers between devices: 16.9 us -> 12.3 us  [core_swap(): return lax.ppermute(x, 'tp', [(i, i ^ 1) for i in range(width)])]
    ppermute x15, waiting for transfers between devices: 20.7 us -> 16.2 us  [turn(): out.append(lax.ppermute(parts[k], 'tp', pairs))]
    unnamed x14, local copies, waits for them, and re-layouts: 3.7 us -> 2.06 us
    ppermute x4, starting transfers between devices: 10.9 us -> 12.5 us  [down_piece(): return lax.ppermute(down_weight, ('dp', 'tp'), pairs)]
    pallas_call x1, Pallas kernels: 3.31 us -> 1.78 us  [feed_forward(): pl.pallas_call(kernel, in_specs=[in_smem] + [in_vmem] * 6, out_specs=[in_...]
    ppermute x15, starting transfers between devices: 19 us -> 17.7 us  [turn(): out.append(lax.ppermute(parts[k], 'tp', pairs))]
  transfers between devices with their start and end apart: 30 -> 30, of which waited for: 16 -> 18; matrix products, arithmetic and copies ran while one was open for 0% -> 1% of each run, Pallas kernels for 14% -> 14%
where the time goes in v8:
time: 107 us
  starting transfers between devices  49.3 us (46%)
  waiting for transfers between devices  34 us (32%)
  Pallas kernels  18.8 us (18%)
  local copies, waits for them, and re-layouts  2.32 us (2%)
  other arithmetic  1.3 us (1%)
    ppermute x15, starting transfers between devices, turn(): out.append(lax.ppermute(parts[k], 'tp', pairs))  17.7 us
    ppermute x15, waiting for transfers between devices, turn(): out.append(lax.ppermute(parts[k], 'tp', pairs))  16.2 us
    ppermute x4, starting transfers between devices, down_piece(): return lax.ppermute(down_weight, ('dp', 'tp'), pairs)  12.5 us
    ppermute x10, starting transfers between devices, core_swap(): return lax.ppermute(x, 'tp', [(i, i ^ 1) for i in range(width)])  12.3 us
    ppermute x4, waiting for transfers between devices, down_piece(): return lax.ppermute(down_weight, ('dp', 'tp'), pairs)  10.4 us
    pallas_call x1, Pallas kernels, attend(): pl.pallas_call(kernel, in_specs=[in_smem, in_smem, in_vmem, in_hbm], out_...  9.03 us
    all_to_all x1, starting transfers between devices, between_chips(): return lax.all_to_all(x, 'tp', 0, 0, tiled=True, axis_index_groups=groups)  6.76 us
    all_to_all x1, waiting for transfers between devices, between_chips(): return lax.all_to_all(x, 'tp', 0, 0, tiled=True, axis_index_groups=groups)  4.92 us
  transfers between devices with their start and end apart: 30, of which 18 were waited for; matrix products, arithmetic and copies ran while one was open for 1% of the time, Pallas kernels for 14%

profile of v8, /device:TPU:1, one launch (start us, length us, event | category | flops | bytes accessed | tf_op | source)
XLA Modules:
  0.0 106.7 jit_solution(6518296132052278252)
XLA Ops:
  1.4 3.5 %collective-permute-start = (bf16[288,1792]{1,0:T(8,128)(2,1)}, bf16[288,1792]{1,0:T(8,128)(2,1)S(1)}, u32[]{:S(2)}, u32[]{:S(2)}) collective-permute-start(bf16[288,1792]{1,0:T(8,128)(2,1)} %param.21), channel_id=1, source_target_pairs={{0,0},{64,1},{2,2},{66,3},{4,4},{68,5},{6,6},{70,7},{8,8},{72,9},{... | collective-permute-start | bytes 3096584 | tf_op jit(solution)/shard_map/ppermute | solution.py:53
  5.7 9.0 %shard_map.109 = bf16[256,512]{1,0:T(8,128)(2,1)} custom-call(s32[4]{0:T(128)} %lengths_ref.1, s32[1]{0:T(128)} %copy.12.counts_ref, bf16[4,64,576]{2,1,0:T(8,128)(2,1)} %q_ref.1, bf16[4,576,2048]{2,1,0:T(8,128)(2,1)} %bitcast.27), custom_call_target="tpu_custom_call" | custom-call | flops 1140850688 | bytes 9437184 | tf_op jit(solution)/shard_map/pallas_call | solution.py:124
  14.7 6.8 %all-to-all-start = ((bf16[16,16,512]{2,1,0:T(8,128)(2,1)}), bf16[16,16,512]{2,1,0:T(8,128)(2,1)S(1)}, u32[]{:S(2)}, u32[]{:S(2)}) async-start(bf16[16,16,512]{2,1,0:T(8,128)(2,1)} %bitcast.28), calls=%async_computation | async-start | bytes 524288 | tf_op jit(solution)/shard_map/all_to_all | solution.py:20
  21.5 2.7 %collective-permute-start.3 = (bf16[2,512,128]{2,1,0:T(8,128)(2,1)S(1)}, bf16[2,512,128]{2,1,0:T(8,128)(2,1)S(1)}, u32[]{:S(2)}, u32[]{:S(2)}) collective-permute-start(bf16[2,512,128]{2,1,0:T(8,128)(2,1)S(1)} %copy-done.3), channel_id=1, source_target_pairs={{0,1},{1,0},{2,3},{3,2},{4,5},{5,4},{6,7},{7,6},{8,9},{9,8},{10,11... | collective-permute-start | bytes 786440 | tf_op jit(solution)/shard_map/ppermute | solution.py:15
  24.2 4.9 %all-to-all-done = bf16[16,16,512]{2,1,0:T(8,128)(2,1)S(1)} async-done(((bf16[16,16,512]{2,1,0:T(8,128)(2,1)}), bf16[16,16,512]{2,1,0:T(8,128)(2,1)S(1)}, u32[]{:S(2)}, u32[]{:S(2)}) %all-to-all-start) | async-done | bytes 262176 | tf_op jit(solution)/shard_map/all_to_all | solution.py:20
  30.8 2.0 %collective-permute-start.2 = (bf16[16,16,512]{2,1,0:T(8,128)(2,1)S(1)}, bf16[16,16,512]{2,1,0:T(8,128)(2,1)S(1)}, u32[]{:S(2)}, u32[]{:S(2)}) collective-permute-start(bf16[16,16,512]{2,1,0:T(8,128)(2,1)S(1)} %all-to-all-done), channel_id=1, source_target_pairs={{0,1},{1,0},{2,3},{3,2},{4,5},{5,4},{6,7},{7,6},{8,9},{9,8},{10,11... | collective-permute-start | bytes 786440 | tf_op jit(solution)/shard_map/ppermute | solution.py:15
  33.9 2.0 %copy-done.2 = bf16[256,7168]{1,0:T(8,128)(2,1)S(1)} copy-done((bf16[256,7168]{1,0:T(8,128)(2,1)S(1)}, bf16[256,7168]{1,0:T(8,128)(2,1)}, u32[]{:S(2)}) %copy-start.2) | copy-done | bytes 3670040
  36.0 3.8 %shard_map.110 = (bf16[32,3584]{1,0:T(8,128)(2,1)S(1)}, bf16[32,3584]{1,0:T(8,128)(2,1)S(1)}, bf16[32,3584]{1,0:T(8,128)(2,1)S(1)}, bf16[32,3584]{1,0:T(8,128)(2,1)S(1)}) custom-call(s32[4]{0:T(128)S(1)} %pad_add_fusion.spot_ref, bf16[256,512]{1,0:T(8,128)(2,1)S(1)} %bitcast.23, bf16[256,512]{1,0:T(8,128)(2,1)S(1)} %bitcast.24, ...), custom_call_target="tpu_custom_call" | custom-call | flops 469762048 | bytes 3670016 | tf_op jit(solution)/shard_map/pallas_call | solution.py:176
  40.2 1.4 %collective-permute-start.6 = (bf16[32,3584]{1,0:T(8,128)(2,1)S(1)}, bf16[32,3584]{1,0:T(8,128)(2,1)S(1)}, u32[]{:S(2)}, u32[]{:S(2)}) collective-permute-start(bf16[32,3584]{1,0:T(8,128)(2,1)S(1)} %get-tuple-element.38), channel_id=1, source_target_pairs={{0,16},{1,5},{2,18},{3,7},{4,20},{5,1},{6,22},{7,3},{8,24},{9,13},... | collective-permute-start | bytes 688136 | tf_op jit(solution)/shard_map/ppermute | solution.py:35
  42.8 4.5 %collective-permute-start.15 = (bf16[288,1792]{1,0:T(8,128)(2,1)}, bf16[288,1792]{1,0:T(8,128)(2,1)S(1)}, u32[]{:S(2)}, u32[]{:S(2)}) collective-permute-start(bf16[288,1792]{1,0:T(8,128)(2,1)} %param.21), channel_id=1, source_target_pairs={{32,0},{96,1},{34,2},{98,3},{36,4},{100,5},{38,6},{102,7},{40,8},{... | collective-permute-start | bytes 3096584 | tf_op jit(solution)/shard_map/ppermute | solution.py:53
  52.1 8.0 %collective-permute-done.15.c_ref = bf16[288,1792]{1,0:T(8,128)(2,1)S(1)} collective-permute-done((bf16[288,1792]{1,0:T(8,128)(2,1)}, bf16[288,1792]{1,0:T(8,128)(2,1)S(1)}, u32[]{:S(2)}, u32[]{:S(2)}) %collective-permute-start.15) | collective-permute-done | bytes 1032224 | tf_op jit(solution)/shard_map/ppermute | solution.py:53
  60.1 4.5 %collective-permute-start.16 = (bf16[288,1792]{1,0:T(8,128)(2,1)S(1)}, bf16[288,1792]{1,0:T(8,128)(2,1)S(1)}, u32[]{:S(2)}, u32[]{:S(2)}) collective-permute-start(bf16[288,1792]{1,0:T(8,128)(2,1)S(1)} %copy-done.6), channel_id=1, source_target_pairs={{33,0},{97,1},{35,2},{99,3},{37,4},{101,5},{39,6},{103,7},{41,8},{... | collective-permute-start | bytes 3096584 | tf_op jit(solution)/shard_map/ppermute | solution.py:53
  64.8 2.4 %collective-permute-start.12 = (bf16[32,3584]{1,0:T(8,128)(2,1)S(1)}, bf16[32,3584]{1,0:T(8,128)(2,1)S(1)}, u32[]{:S(2)}, u32[]{:S(2)}) collective-permute-start(bf16[32,3584]{1,0:T(8,128)(2,1)S(1)} %add_convert_fusion.1.refs_0_), channel_id=1, source_target_pairs={{0,24},{1,7},{2,26},{3,1},{4,28},{5,3},{6,30},{7,5},{8,0},{9,15},{... | collective-permute-start | bytes 688136 | tf_op jit(solution)/shard_map/ppermute | solution.py:35
  68.3 4.3 %collective-permute-done.12.refs_1_ = bf16[32,3584]{1,0:T(8,128)(2,1)S(1)} collective-permute-done((bf16[32,3584]{1,0:T(8,128)(2,1)S(1)}, bf16[32,3584]{1,0:T(8,128)(2,1)S(1)}, u32[]{:S(2)}, u32[]{:S(2)}) %collective-permute-start.12) | collective-permute-done | bytes 229408 | tf_op jit(solution)/shard_map/ppermute | solution.py:35
  73.7 2.4 %collective-permute-done.14.refs_3_ = bf16[32,3584]{1,0:T(8,128)(2,1)S(1)} collective-permute-done((bf16[32,3584]{1,0:T(8,128)(2,1)S(1)}, bf16[32,3584]{1,0:T(8,128)(2,1)S(1)}, u32[]{:S(2)}, u32[]{:S(2)}) %collective-permute-start.14) | collective-permute-done | bytes 229408 | tf_op jit(solution)/shard_map/ppermute | solution.py:35
  77.7 1.9 %shard_map.111 = (f32[128,576]{1,0:T(8,128)S(1)}, f32[128,128]{1,0:T(8,128)S(1)}) custom-call(s32[4]{0:T(128)S(1)} %pad_add_fusion.spot_ref, bf16[32,3584]{1,0:T(8,128)(2,1)S(1)} %add_convert_fusion.1.refs_0_, bf16[32,3584]{1,0:T(8,128)(2,1)S(1)} %collective-permute-done.12.refs_1_, bf16[32,3584]{1,0:T(8,128)(2,1)S(1)} %collective-permute-done.13.refs_2_, ...), custom_call_target="tpu_custom_call" | custom-call | flops 528482304 | bytes 4128768 | tf_op jit(solution)/shard_map/pallas_call | solution.py:240
  79.7 2.3 %shard_map.112.inner_ref = bf16[128,288]{1,0:T(8,128)(2,1)S(1)} custom-call(s32[4]{0:T(128)S(1)} %pad_add_fusion.spot_ref, bf16[32,3584]{1,0:T(8,128)(2,1)S(1)} %collective-permute-done.17.refs_0_, bf16[32,3584]{1,0:T(8,128)(2,1)S(1)} %collective-permute-done.18.refs_1_, bf16[32,3584]{1,0:T(8,128)(2,1)S(1)} %collective-permute-done.19.refs_2_, ...), custom_call_target="tpu_custom_call" | custom-call | flops 528482304 | bytes 4128768 | tf_op jit(solution)/shard_map/pallas_call | solution.py:240
  83.5 1.8 %shard_map.113 = (bf16[32,3584]{1,0:T(8,128)(2,1)S(1)}, bf16[32,3584]{1,0:T(8,128)(2,1)S(1)}, bf16[32,3584]{1,0:T(8,128)(2,1)S(1)}, bf16[32,3584]{1,0:T(8,128)(2,1)S(1)}) custom-call(s32[4]{0:T(128)S(1)} %pad_add_fusion.spot_ref, bf16[128,288]{1,0:T(8,128)(2,1)S(1)} %shard_map.112.inner_ref, bf16[128,288]{1,0:T(8,128)(2,1)S(1)} %collective-permute-done.21.other_ref, ...), custom_call_target="tpu_custom_call" | custom-call | flops 528482304 | bytes 4128768 | tf_op jit(solution)/shard_map/pallas_call | solution.py:279
  86.6 2.5 %collective-permute-start.23 = (bf16[32,3584]{1,0:T(8,128)(2,1)S(1)}, bf16[32,3584]{1,0:T(8,128)(2,1)S(1)}, u32[]{:S(2)}, u32[]{:S(2)}) collective-permute-start(bf16[32,3584]{1,0:T(8,128)(2,1)S(1)} %get-tuple-element.55), channel_id=1, source_target_pairs={{0,16},{1,5},{2,18},{3,7},{4,20},{5,1},{6,22},{7,3},{8,24},{9,13},... | collective-permute-start | bytes 688136 | tf_op jit(solution)/shard_map/ppermute | solution.py:35
  90.2 1.6 %collective-permute-done.22 = bf16[32,3584]{1,0:T(8,128)(2,1)S(1)} collective-permute-done((bf16[32,3584]{1,0:T(8,128)(2,1)S(1)}, bf16[32,3584]{1,0:T(8,128)(2,1)S(1)}, u32[]{:S(2)}, u32[]{:S(2)}) %collective-permute-start.22) | collective-permute-done | bytes 229408 | tf_op jit(solution)/shard_map/ppermute | solution.py:35
  91.8 3.1 %collective-permute-done.23 = bf16[32,3584]{1,0:T(8,128)(2,1)S(1)} collective-permute-done((bf16[32,3584]{1,0:T(8,128)(2,1)S(1)}, bf16[32,3584]{1,0:T(8,128)(2,1)S(1)}, u32[]{:S(2)}, u32[]{:S(2)}) %collective-permute-start.23) | collective-permute-done | bytes 229408 | tf_op jit(solution)/shard_map/ppermute | solution.py:35
  95.5 1.8 %collective-permute-start.26 = (bf16[8,3584]{1,0:T(8,128)(2,1)S(1)}, bf16[8,3584]{1,0:T(8,128)(2,1)S(1)}, u32[]{:S(2)}, u32[]{:S(2)}) collective-permute-start(bf16[8,3584]{1,0:T(8,128)(2,1)S(1)} %get-tuple-element.59), channel_id=1, source_target_pairs={{0,4},{1,17},{2,6},{3,19},{4,0},{5,21},{6,2},{7,23},{8,12},{9,25},... | collective-permute-start | bytes 172040 | tf_op jit(solution)/shard_map/ppermute | solution.py:35
  97.3 1.5 %collective-permute-start.27 = (bf16[8,3584]{1,0:T(8,128)(2,1)S(1)}, bf16[8,3584]{1,0:T(8,128)(2,1)S(1)}, u32[]{:S(2)}, u32[]{:S(2)}) collective-permute-start(bf16[8,3584]{1,0:T(8,128)(2,1)S(1)} %get-tuple-element.58), channel_id=1, source_target_pairs={{0,6},{1,25},{2,0},{3,27},{4,2},{5,29},{6,4},{7,31},{8,14},{9,1},{... | collective-permute-start | bytes 172040 | tf_op jit(solution)/shard_map/ppermute | solution.py:35
  100.7 4.5 %collective-permute-start.28 = (bf16[4,3584]{1,0:T(4,128)(2,1)S(1)}, bf16[4,3584]{1,0:T(4,128)(2,1)S(1)}, u32[]{:S(2)}, u32[]{:S(2)}) collective-permute-start(bf16[4,3584]{1,0:T(4,128)(2,1)S(1)} %get-tuple-element.62), channel_id=1, source_target_pairs={{0,1},{1,0},{2,3},{3,2},{4,5},{5,4},{6,7},{7,6},{8,9},{9,8},{10,11... | collective-permute-start | bytes 86024 | tf_op jit(solution)/shard_map/ppermute | solution.py:15
  (71 shorter events, 22.7 us)
Async XLA Ops:
  0.0 33.9 %collective-permute-start.4 = (bf16[256,7168]{1,0:T(8,128)(2,1)}, bf16[256,7168]{1,0:T(8,128)(2,1)}, u32[]{:S(2)}, u32[]{:S(2)}) collective-permute-start(bf16[256,7168]{1,0:T(8,128)(2,1)} %om_ref.1), channel_id=1, source_target_pairs={{0,1},{1,0},{2,3},{3,2},{4,5},{5,4},{6,7},{7,6},{8,9},{9,8},{10,11... | collective-permute-start | bytes 11010056 | tf_op jit(solution)/shard_map/ppermute | solution.py:15
  1.4 28.6 %collective-permute-start = (bf16[288,1792]{1,0:T(8,128)(2,1)}, bf16[288,1792]{1,0:T(8,128)(2,1)S(1)}, u32[]{:S(2)}, u32[]{:S(2)}) collective-permute-start(bf16[288,1792]{1,0:T(8,128)(2,1)} %param.21), channel_id=1, source_target_pairs={{0,0},{64,1},{2,2},{66,3},{4,4},{68,5},{6,6},{70,7},{8,8},{72,9},{... | collective-permute-start | bytes 3096584 | tf_op jit(solution)/shard_map/ppermute | solution.py:53
  4.9 25.8 %collective-permute-start.1 = (bf16[288,1792]{1,0:T(8,128)(2,1)}, bf16[288,1792]{1,0:T(8,128)(2,1)S(1)}, u32[]{:S(2)}, u32[]{:S(2)}) collective-permute-start(bf16[288,1792]{1,0:T(8,128)(2,1)} %param.21), channel_id=1, source_target_pairs={{1,0},{65,1},{3,2},{67,3},{5,4},{69,5},{7,6},{71,7},{9,8},{73,9},{... | collective-permute-start | bytes 3096584 | tf_op jit(solution)/shard_map/ppermute | solution.py:53
  14.7 14.3 %all-to-all-start = ((bf16[16,16,512]{2,1,0:T(8,128)(2,1)}), bf16[16,16,512]{2,1,0:T(8,128)(2,1)S(1)}, u32[]{:S(2)}, u32[]{:S(2)}) async-start(bf16[16,16,512]{2,1,0:T(8,128)(2,1)} %bitcast.28), calls=%async_computation | async-start | bytes 524288 | tf_op jit(solution)/shard_map/all_to_all | solution.py:20
  21.5 11.7 %collective-permute-start.3 = (bf16[2,512,128]{2,1,0:T(8,128)(2,1)S(1)}, bf16[2,512,128]{2,1,0:T(8,128)(2,1)S(1)}, u32[]{:S(2)}, u32[]{:S(2)}) collective-permute-start(bf16[2,512,128]{2,1,0:T(8,128)(2,1)S(1)} %copy-done.3), channel_id=1, source_target_pairs={{0,1},{1,0},{2,3},{3,2},{4,5},{5,4},{6,7},{7,6},{8,9},{9,8},{10,11... | collective-permute-start | bytes 786440 | tf_op jit(solution)/shard_map/ppermute | solution.py:15
  32.8 10.0 %collective-permute-start.8 = (bf16[4,3584]{1,0:T(4,128)(2,1)S(1)}, bf16[4,3584]{1,0:T(4,128)(2,1)S(1)}, u32[]{:S(2)}, u32[]{:S(2)}) collective-permute-start(bf16[4,3584]{1,0:T(4,128)(2,1)S(1)} %get-tuple-element.64), channel_id=1, source_target_pairs={{0,1},{1,0},{2,3},{3,2},{4,5},{5,4},{6,7},{7,6},{8,9},{9,8},{10,11... | collective-permute-start | bytes 86024 | tf_op jit(solution)/shard_map/ppermute | solution.py:15
  39.8 8.9 %collective-permute-start.5 = (bf16[32,3584]{1,0:T(8,128)(2,1)S(1)}, bf16[32,3584]{1,0:T(8,128)(2,1)S(1)}, u32[]{:S(2)}, u32[]{:S(2)}) collective-permute-start(bf16[32,3584]{1,0:T(8,128)(2,1)S(1)} %get-tuple-element.37), channel_id=1, source_target_pairs={{0,8},{1,3},{2,10},{3,5},{4,12},{5,7},{6,14},{7,1},{8,16},{9,11},{... | collective-permute-start | bytes 688136 | tf_op jit(solution)/shard_map/ppermute | solution.py:35
  40.2 8.5 %collective-permute-start.6 = (bf16[32,3584]{1,0:T(8,128)(2,1)S(1)}, bf16[32,3584]{1,0:T(8,128)(2,1)S(1)}, u32[]{:S(2)}, u32[]{:S(2)}) collective-permute-start(bf16[32,3584]{1,0:T(8,128)(2,1)S(1)} %get-tuple-element.38), channel_id=1, source_target_pairs={{0,16},{1,5},{2,18},{3,7},{4,20},{5,1},{6,22},{7,3},{8,24},{9,13},... | collective-permute-start | bytes 688136 | tf_op jit(solution)/shard_map/ppermute | solution.py:35
  41.6 7.7 %collective-permute-start.7 = (bf16[32,3584]{1,0:T(8,128)(2,1)S(1)}, bf16[32,3584]{1,0:T(8,128)(2,1)S(1)}, u32[]{:S(2)}, u32[]{:S(2)}) collective-permute-start(bf16[32,3584]{1,0:T(8,128)(2,1)S(1)} %get-tuple-element.39), channel_id=1, source_target_pairs={{0,24},{1,7},{2,26},{3,1},{4,28},{5,3},{6,30},{7,5},{8,0},{9,15},{... | collective-permute-start | bytes 688136 | tf_op jit(solution)/shard_map/ppermute | solution.py:35
  42.8 17.3 %collective-permute-start.15 = (bf16[288,1792]{1,0:T(8,128)(2,1)}, bf16[288,1792]{1,0:T(8,128)(2,1)S(1)}, u32[]{:S(2)}, u32[]{:S(2)}) collective-permute-start(bf16[288,1792]{1,0:T(8,128)(2,1)} %param.21), channel_id=1, source_target_pairs={{32,0},{96,1},{34,2},{98,3},{36,4},{100,5},{38,6},{102,7},{40,8},{... | collective-permute-start | bytes 3096584 | tf_op jit(solution)/shard_map/ppermute | solution.py:53
  49.5 15.1 %collective-permute-start.10 = (bf16[32,3584]{1,0:T(8,128)(2,1)S(1)}, bf16[32,3584]{1,0:T(8,128)(2,1)S(1)}, u32[]{:S(2)}, u32[]{:S(2)}) collective-permute-start(bf16[32,3584]{1,0:T(8,128)(2,1)S(1)} %fusion.1), channel_id=1, source_target_pairs={{0,4},{1,17},{2,6},{3,19},{4,0},{5,21},{6,2},{7,23},{8,12},{9,25},... | collective-permute-start | bytes 688136 | tf_op jit(solution)/shard_map/ppermute | solution.py:35
  50.6 14.0 %collective-permute-start.11 = (bf16[32,3584]{1,0:T(8,128)(2,1)S(1)}, bf16[32,3584]{1,0:T(8,128)(2,1)S(1)}, u32[]{:S(2)}, u32[]{:S(2)}) collective-permute-start(bf16[32,3584]{1,0:T(8,128)(2,1)S(1)} %fusion.1), channel_id=1, source_target_pairs={{0,6},{1,25},{2,0},{3,27},{4,2},{5,29},{6,4},{7,31},{8,14},{9,1},{... | collective-permute-start | bytes 688136 | tf_op jit(solution)/shard_map/ppermute | solution.py:35
  51.5 13.1 %collective-permute-start.9 = (bf16[32,3584]{1,0:T(8,128)(2,1)S(1)}, bf16[32,3584]{1,0:T(8,128)(2,1)S(1)}, u32[]{:S(2)}, u32[]{:S(2)}) collective-permute-start(bf16[32,3584]{1,0:T(8,128)(2,1)S(1)} %fusion.1), channel_id=1, source_target_pairs={{0,2},{1,9},{2,4},{3,11},{4,6},{5,13},{6,0},{7,15},{8,10},{9,17},{... | collective-permute-start | bytes 688136 | tf_op jit(solution)/shard_map/ppermute | solution.py:35
  60.1 16.6 %collective-permute-start.16 = (bf16[288,1792]{1,0:T(8,128)(2,1)S(1)}, bf16[288,1792]{1,0:T(8,128)(2,1)S(1)}, u32[]{:S(2)}, u32[]{:S(2)}) collective-permute-start(bf16[288,1792]{1,0:T(8,128)(2,1)S(1)} %copy-done.6), channel_id=1, source_target_pairs={{33,0},{97,1},{35,2},{99,3},{37,4},{101,5},{39,6},{103,7},{41,8},{... | collective-permute-start | bytes 3096584 | tf_op jit(solution)/shard_map/ppermute | solution.py:53
  64.8 7.9 %collective-permute-start.12 = (bf16[32,3584]{1,0:T(8,128)(2,1)S(1)}, bf16[32,3584]{1,0:T(8,128)(2,1)S(1)}, u32[]{:S(2)}, u32[]{:S(2)}) collective-permute-start(bf16[32,3584]{1,0:T(8,128)(2,1)S(1)} %add_convert_fusion.1.refs_0_), channel_id=1, source_target_pairs={{0,24},{1,7},{2,26},{3,1},{4,28},{5,3},{6,30},{7,5},{8,0},{9,15},{... | collective-permute-start | bytes 688136 | tf_op jit(solution)/shard_map/ppermute | solution.py:35
  67.2 6.5 %collective-permute-start.13 = (bf16[32,3584]{1,0:T(8,128)(2,1)S(1)}, bf16[32,3584]{1,0:T(8,128)(2,1)S(1)}, u32[]{:S(2)}, u32[]{:S(2)}) collective-permute-start(bf16[32,3584]{1,0:T(8,128)(2,1)S(1)} %add_convert_fusion.1.refs_0_), channel_id=1, source_target_pairs={{0,16},{1,5},{2,18},{3,7},{4,20},{5,1},{6,22},{7,3},{8,24},{9,13},... | collective-permute-start | bytes 688136 | tf_op jit(solution)/shard_map/ppermute | solution.py:35
  67.7 8.3 %collective-permute-start.14 = (bf16[32,3584]{1,0:T(8,128)(2,1)S(1)}, bf16[32,3584]{1,0:T(8,128)(2,1)S(1)}, u32[]{:S(2)}, u32[]{:S(2)}) collective-permute-start(bf16[32,3584]{1,0:T(8,128)(2,1)S(1)} %add_convert_fusion.1.refs_0_), channel_id=1, source_target_pairs={{0,8},{1,3},{2,10},{3,5},{4,12},{5,7},{6,14},{7,1},{8,16},{9,11},{... | collective-permute-start | bytes 688136 | tf_op jit(solution)/shard_map/ppermute | solution.py:35
  85.3 6.4 %collective-permute-start.22 = (bf16[32,3584]{1,0:T(8,128)(2,1)S(1)}, bf16[32,3584]{1,0:T(8,128)(2,1)S(1)}, u32[]{:S(2)}, u32[]{:S(2)}) collective-permute-start(bf16[32,3584]{1,0:T(8,128)(2,1)S(1)} %get-tuple-element.54), channel_id=1, source_target_pairs={{0,8},{1,3},{2,10},{3,5},{4,12},{5,7},{6,14},{7,1},{8,16},{9,11},{... | collective-permute-start | bytes 688136 | tf_op jit(solution)/shard_map/ppermute | solution.py:35
  86.6 8.3 %collective-permute-start.23 = (bf16[32,3584]{1,0:T(8,128)(2,1)S(1)}, bf16[32,3584]{1,0:T(8,128)(2,1)S(1)}, u32[]{:S(2)}, u32[]{:S(2)}) collective-permute-start(bf16[32,3584]{1,0:T(8,128)(2,1)S(1)} %get-tuple-element.55), channel_id=1, source_target_pairs={{0,16},{1,5},{2,18},{3,7},{4,20},{5,1},{6,22},{7,3},{8,24},{9,13},... | collective-permute-start | bytes 688136 | tf_op jit(solution)/shard_map/ppermute | solution.py:35
  89.0 5.9 %collective-permute-start.24 = (bf16[32,3584]{1,0:T(8,128)(2,1)S(1)}, bf16[32,3584]{1,0:T(8,128)(2,1)S(1)}, u32[]{:S(2)}, u32[]{:S(2)}) collective-permute-start(bf16[32,3584]{1,0:T(8,128)(2,1)S(1)} %get-tuple-element.56), channel_id=1, source_target_pairs={{0,24},{1,7},{2,26},{3,1},{4,28},{5,3},{6,30},{7,5},{8,0},{9,15},{... | collective-permute-start | bytes 688136 | tf_op jit(solution)/shard_map/ppermute | solution.py:35
  95.1 4.3 %collective-permute-start.25 = (bf16[8,3584]{1,0:T(8,128)(2,1)S(1)}, bf16[8,3584]{1,0:T(8,128)(2,1)S(1)}, u32[]{:S(2)}, u32[]{:S(2)}) collective-permute-start(bf16[8,3584]{1,0:T(8,128)(2,1)S(1)} %get-tuple-element.57), channel_id=1, source_target_pairs={{0,2},{1,9},{2,4},{3,11},{4,6},{5,13},{6,0},{7,15},{8,10},{9,17},{... | collective-permute-start | bytes 172040 | tf_op jit(solution)/shard_map/ppermute | solution.py:35
  95.5 4.5 %collective-permute-start.26 = (bf16[8,3584]{1,0:T(8,128)(2,1)S(1)}, bf16[8,3584]{1,0:T(8,128)(2,1)S(1)}, u32[]{:S(2)}, u32[]{:S(2)}) collective-permute-start(bf16[8,3584]{1,0:T(8,128)(2,1)S(1)} %get-tuple-element.59), channel_id=1, source_target_pairs={{0,4},{1,17},{2,6},{3,19},{4,0},{5,21},{6,2},{7,23},{8,12},{9,25},... | collective-permute-start | bytes 172040 | tf_op jit(solution)/shard_map/ppermute | solution.py:35
  97.3 3.2 %collective-permute-start.27 = (bf16[8,3584]{1,0:T(8,128)(2,1)S(1)}, bf16[8,3584]{1,0:T(8,128)(2,1)S(1)}, u32[]{:S(2)}, u32[]{:S(2)}) collective-permute-start(bf16[8,3584]{1,0:T(8,128)(2,1)S(1)} %get-tuple-element.58), channel_id=1, source_target_pairs={{0,6},{1,25},{2,0},{3,27},{4,2},{5,29},{6,4},{7,31},{8,14},{9,1},{... | collective-permute-start | bytes 172040 | tf_op jit(solution)/shard_map/ppermute | solution.py:35
  100.7 5.3 %collective-permute-start.28 = (bf16[4,3584]{1,0:T(4,128)(2,1)S(1)}, bf16[4,3584]{1,0:T(4,128)(2,1)S(1)}, u32[]{:S(2)}, u32[]{:S(2)}) collective-permute-start(bf16[4,3584]{1,0:T(4,128)(2,1)S(1)} %get-tuple-element.62), channel_id=1, source_target_pairs={{0,1},{1,0},{2,3},{3,2},{4,5},{5,4},{6,7},{7,6},{8,9},{9,8},{10,11... | collective-permute-start | bytes 86024 | tf_op jit(solution)/shard_map/ppermute | solution.py:15
  (13 other events, 208.9 us)

commit v9 on v8

--- a/solution.py
+++ b/solution.py
@@ -140,17 +140,15 @@
     return out.reshape(chips, slots * group, latent_width)
 
 
-def project(mine, other, value_mine, value_other, output_mine, output_other, spot, side, slots):
+def project(mine, other, value_mine, value_other, spot, side, slots):
     chips, pairs, latent_width = mine.shape
     heads_here, _, head = value_mine.shape
     heads = 2 * heads_here
-    depth, model = output_mine.shape
-    half = model // 2
     rows = 2 * chips * slots
     line = rows // side
     lines = chips * pairs
 
-    def kernel(spot_ref, mine_ref, other_ref, vm_ref, vo_ref, om_ref, oo_ref, *outs):
+    def kernel(spot_ref, mine_ref, other_ref, vm_ref, vo_ref, out_ref):
         core, first = spot_ref[0], spot_ref[1]
         to = line_numbers(rows)
         along = (to // line + first) % side
@@ -159,28 +157,23 @@
         from_other = (to // slots % 2 + core) % 2
         source = from_other * lines + chip * pairs + to % slots * heads
         latents = jnp.concatenate([mine_ref[...], other_ref[...]], axis=0)
-        values = []
         for index in range(heads):
             owner, weight_ref = (core, vm_ref) if index < heads_here else (1 - core, vo_ref)
             place = index % heads_here
             pick = one_hot(source + owner * heads_here + place, 2 * lines)
             picked = product(pick, latents).astype(jnp.bfloat16)
-            values.append(product(picked, weight_ref[place]).astype(jnp.bfloat16))
-        values = jnp.concatenate(values, axis=1)
-        at = pl.ds(pl.multiple_of(core * half, 128), half)
-        result = product(values[:, :depth], om_ref[:, at]) + product(values[:, depth:], oo_ref[:, at])
-        result = result.astype(jnp.bfloat16)
-        for k in range(side):
-            outs[k][...] = result[k * line : (k + 1) * line]
+            out_ref[:, index * head : (index + 1) * head] = product(
+                picked, weight_ref[place]
+            ).astype(jnp.bfloat16)
 
     return pl.pallas_call(
         kernel,
-        in_specs=[in_smem] + [in_vmem] * 6,
-        out_specs=[in_vmem] * side,
-        out_shape=[jax.ShapeDtypeStruct((line, half), jnp.bfloat16)] * side,
-        compiler_params=budget(24),
+        in_specs=[in_smem] + [in_vmem] * 4,
+        out_specs=in_vmem,
+        out_shape=jax.ShapeDtypeStruct((rows, heads * head), jnp.bfloat16),
+        compiler_params=budget(16),
         cost_estimate=pl.CostEstimate(
-            flops=4 * rows * depth * half, bytes_accessed=4 * depth * half, transcendentals=0
+            flops=64 * rows * latent_width * (lines + head), bytes_accessed=4 * mine.size, transcendentals=0
         ),
     )(
         spot,
@@ -188,9 +181,38 @@
         other.reshape(lines, latent_width),
         value_mine,
         value_other,
-        output_mine,
-        output_other,
-    )
+    )
+
+
+def sum_heads(values, output_mine, output_other, spot, side):
+    rows = values.shape[0]
+    depth, model = output_mine.shape
+    half = model // 2
+    line = rows // side
+
+    def kernel(spot_ref, value_ref, om_ref, oo_ref, *refs):
+        outs, (held_ref, sem) = refs[:side], refs[side:]
+        at = pl.ds(pl.multiple_of(spot_ref[0] * half, 128), half)
+        copy = pltpu.make_async_copy(oo_ref.at[:, at], held_ref, sem)
+        copy.start()
+        result = product(value_ref[:, :depth], om_ref[:, at])
+        copy.wait()
+        result = result + product(value_ref[:, depth:], held_ref[...])
+        result = result.astype(jnp.bfloat16)
+        for k in range(side):
+            outs[k][...] = result[k * line : (k + 1) * line]
+
+    return pl.pallas_call(
+        kernel,
+        in_specs=[in_smem] + [in_vmem] * 2 + [in_hbm],
+        out_specs=[in_vmem] * side,
+        out_shape=[jax.ShapeDtypeStruct((line, half), jnp.bfloat16)] * side,
+        scratch_shapes=[pltpu.VMEM((depth, half), jnp.bfloat16), pltpu.SemaphoreType.DMA],
+        compiler_params=budget(24),
+        cost_estimate=pl.CostEstimate(
+            flops=4 * rows * depth * half, bytes_accessed=4 * depth * half, transcendentals=0
+        ),
+    )(spot, values, output_mine, output_other)
 
 
 def gated(parts, gain, gate_weight, up_weight, spot, before):
@@ -333,21 +355,13 @@
 
     latent = attend(query, cache, lengths, counts, latent_width, chips)
     arrived = between_chips(latent, width)
-    arrived, pieces[0], pieces[1] = lax.optimization_barrier((arrived, pieces[0], pieces[1]))
     arrived_other = core_swap(arrived, width)
-    attended_parts = project(
-        arrived,
-        arrived_other,
-        value_weight,
-        value_other,
-        output_weight,
-        output_other,
-        spot,
-        side,
-        slots,
-    )
-
-    later, attended_parts = lax.optimization_barrier((down_weight, attended_parts))
+    values = project(arrived, arrived_other, value_weight, value_other, spot, side, slots)
+    attended_parts = sum_heads(values, output_weight, output_other, spot, side)
+
+    attended_parts, pieces[0], pieces[1], later = lax.optimization_barrier(
+        (attended_parts, pieces[0], pieces[1], down_weight)
+    )
     pieces.append(down_piece(later, width, 2))
     later, pieces[2] = lax.optimization_barrier((down_weight, pieces[2]))
     pieces.append(down_piece(later, width, 3))

time: 107 us -> 117 us (1.093)
  waiting for transfers between devices: 34 us -> 42.6 us
  starting transfers between devices: 49.3 us -> 51.7 us
  local copies, waits for them, and re-layouts: 2.32 us -> 0.28 us
    ppermute x4, waiting for transfers between devices: 10.4 us -> 22.3 us  [down_piece(): return lax.ppermute(down_weight, ('dp', 'tp'), pairs)]
    ppermute x15, starting transfers between devices: 17.7 us -> 20.8 us  [turn(): out.append(lax.ppermute(parts[k], 'tp', pairs))]
    all_to_all x1, waiting for transfers between devices: 4.92 us -> 2.43 us  [between_chips(): return lax.all_to_all(x, 'tp', 0, 0, tiled=True, axis_index_groups=groups)]
    unnamed x14 -> x12, local copies, waits for them, and re-layouts: 2.06 us -> 0.03 us
    pallas_call x1 -> x2, Pallas kernels: 3.83 us -> 4.58 us  [the longest x1 2.99 us: sum_heads(): pl.pallas_call(kernel, in_specs=[in_smem] + [in_vmem] * 2 + [in_hbm], out...]
  transfers between devices with their start and end apart: 30 -> 30, of which waited for: 18 -> 17; matrix products, arithmetic and copies ran while one was open for 1% -> 1% of each run, Pallas kernels for 14% -> 13%
where the time goes in v9:
time: 117 us; the launch traced here: 116 us
  starting transfers between devices  51.7 us (44%)
  waiting for transfers between devices  42.6 us (36%)
  Pallas kernels  19.6 us (17%)
  other arithmetic  1.3 us (1%)
    ppermute x4, waiting for transfers between devices, down_piece(): return lax.ppermute(down_weight, ('dp', 'tp'), pairs)  22.3 us
    ppermute x15, starting transfers between devices, turn(): out.append(lax.ppermute(parts[k], 'tp', pairs))  20.8 us
    ppermute x15, waiting for transfers between devices, turn(): out.append(lax.ppermute(parts[k], 'tp', pairs))  15.2 us
    ppermute x4, starting transfers between devices, down_piece(): return lax.ppermute(down_weight, ('dp', 'tp'), pairs)  12.8 us
    ppermute x10, starting transfers between devices, core_swap(): return lax.ppermute(x, 'tp', [(i, i ^ 1) for i in range(width)])  11.3 us
    pallas_call x1, Pallas kernels, attend(): pl.pallas_call(kernel, in_specs=[in_smem, in_smem, in_vmem, in_hbm], out_...  9.03 us
    all_to_all x1, starting transfers between devices, between_chips(): return lax.all_to_all(x, 'tp', 0, 0, tiled=True, axis_index_groups=groups)  6.85 us
    pallas_call x2, Pallas kernels, gated(): pl.pallas_call(kernel, in_specs=[in_smem] + [in_vmem] * (side + 3 + 2 * f...  4.2 us
  transfers between devices with their start and end apart: 30, of which 17 were waited for; matrix products, arithmetic and copies ran while one was open for 1% of the time, Pallas kernels for 13%

profile of v9, /device:TPU:1, one launch (start us, length us, event | category | flops | bytes accessed | tf_op | source)
XLA Modules:
  0.0 116.4 jit_solution(5541203596613020564)
XLA Ops:
  2.1 9.0 %shard_map.109 = bf16[256,512]{1,0:T(8,128)(2,1)} custom-call(s32[4]{0:T(128)} %lengths_ref.1, s32[1]{0:T(128)} %copy.12.counts_ref, bf16[4,64,576]{2,1,0:T(8,128)(2,1)} %q_ref.1, bf16[4,576,2048]{2,1,0:T(8,128)(2,1)} %bitcast.27), custom_call_target="tpu_custom_call" | custom-call | flops 1140850688 | bytes 9437184 | tf_op jit(solution)/shard_map/pallas_call | solution.py:124
  11.1 6.8 %all-to-all-start = ((bf16[16,16,512]{2,1,0:T(8,128)(2,1)}), bf16[16,16,512]{2,1,0:T(8,128)(2,1)S(1)}, u32[]{:S(2)}, u32[]{:S(2)}) async-start(bf16[16,16,512]{2,1,0:T(8,128)(2,1)} %bitcast.28), calls=%async_computation | async-start | bytes 524288 | tf_op jit(solution)/shard_map/all_to_all | solution.py:20
  18.0 3.7 %collective-permute-start.3 = (bf16[288,1792]{1,0:T(8,128)(2,1)}, bf16[288,1792]{1,0:T(8,128)(2,1)S(1)}, u32[]{:S(2)}, u32[]{:S(2)}) collective-permute-start(bf16[288,1792]{1,0:T(8,128)(2,1)} %param.21), channel_id=1, source_target_pairs={{0,0},{64,1},{2,2},{66,3},{4,4},{68,5},{6,6},{70,7},{8,8},{72,9},{... | collective-permute-start | bytes 3096584 | tf_op jit(solution)/shard_map/ppermute | solution.py:53
  21.8 2.3 %collective-permute-start.1 = (bf16[2,512,128]{2,1,0:T(8,128)(2,1)S(1)}, bf16[2,512,128]{2,1,0:T(8,128)(2,1)S(1)}, u32[]{:S(2)}, u32[]{:S(2)}) collective-permute-start(bf16[2,512,128]{2,1,0:T(8,128)(2,1)S(1)} %copy-done.4), channel_id=1, source_target_pairs={{0,1},{1,0},{2,3},{3,2},{4,5},{5,4},{6,7},{7,6},{8,9},{9,8},{10,11... | collective-permute-start | bytes 786440 | tf_op jit(solution)/shard_map/ppermute | solution.py:15
  24.1 2.4 %all-to-all-done = bf16[16,16,512]{2,1,0:T(8,128)(2,1)S(1)} async-done(((bf16[16,16,512]{2,1,0:T(8,128)(2,1)}), bf16[16,16,512]{2,1,0:T(8,128)(2,1)S(1)}, u32[]{:S(2)}, u32[]{:S(2)}) %all-to-all-start) | async-done | bytes 262176 | tf_op jit(solution)/shard_map/all_to_all | solution.py:20
  28.8 1.6 %shard_map.110.value_ref = bf16[128,512]{1,0:T(8,128)(2,1)S(1)} custom-call(s32[4]{0:T(128)S(1)} %pad_add_fusion.spot_ref, bf16[256,512]{1,0:T(8,128)(2,1)S(1)} %bitcast.23, bf16[256,512]{1,0:T(8,128)(2,1)S(1)} %bitcast.26, bf16[2,512,128]{2,1,0:T(8,128)(2,1)S(1)} %copy-done.4, bf16[2,512,128]{2,1,0:T(8,128)(2,1)S(1)} %collective-permute-done.1.vo_ref), custom_call_target="tpu_custom_call" | custom-call | flops 1610612736 | bytes 524288 | tf_op jit(solution)/shard_map/pallas_call | solution.py:169
  30.4 3.0 %shard_map.111 = (bf16[32,3584]{1,0:T(8,128)(2,1)S(1)}, bf16[32,3584]{1,0:T(8,128)(2,1)S(1)}, bf16[32,3584]{1,0:T(8,128)(2,1)S(1)}, bf16[32,3584]{1,0:T(8,128)(2,1)S(1)}) custom-call(s32[4]{0:T(128)S(1)} %pad_add_fusion.spot_ref, bf16[128,512]{1,0:T(8,128)(2,1)S(1)} %shard_map.110.value_ref, bf16[256,7168]{1,0:T(8,128)(2,1)S(1)} %copy-done.2, ...), custom_call_target="tpu_custom_call" | custom-call | flops 469762048 | bytes 3670016 | tf_op jit(solution)/shard_map/pallas_call | solution.py:205
  33.4 13.0 %collective-permute-done.3.a_ref = bf16[288,1792]{1,0:T(8,128)(2,1)S(1)} collective-permute-done((bf16[288,1792]{1,0:T(8,128)(2,1)}, bf16[288,1792]{1,0:T(8,128)(2,1)S(1)}, u32[]{:S(2)}, u32[]{:S(2)}) %collective-permute-start.3) | collective-permute-done | bytes 1032224 | tf_op jit(solution)/shard_map/ppermute | solution.py:53
  47.2 1.6 %collective-permute-start.5 = (bf16[32,3584]{1,0:T(8,128)(2,1)S(1)}, bf16[32,3584]{1,0:T(8,128)(2,1)S(1)}, u32[]{:S(2)}, u32[]{:S(2)}) collective-permute-start(bf16[32,3584]{1,0:T(8,128)(2,1)S(1)} %get-tuple-element.35), channel_id=1, source_target_pairs={{0,8},{1,3},{2,10},{3,5},{4,12},{5,7},{6,14},{7,1},{8,16},{9,11},{... | collective-permute-start | bytes 688136 | tf_op jit(solution)/shard_map/ppermute | solution.py:35
  48.9 2.4 %collective-permute-start.6 = (bf16[32,3584]{1,0:T(8,128)(2,1)S(1)}, bf16[32,3584]{1,0:T(8,128)(2,1)S(1)}, u32[]{:S(2)}, u32[]{:S(2)}) collective-permute-start(bf16[32,3584]{1,0:T(8,128)(2,1)S(1)} %get-tuple-element.36), channel_id=1, source_target_pairs={{0,16},{1,5},{2,18},{3,7},{4,20},{5,1},{6,22},{7,3},{8,24},{9,13},... | collective-permute-start | bytes 688136 | tf_op jit(solution)/shard_map/ppermute | solution.py:35
  52.5 4.3 %collective-permute-start.15 = (bf16[288,1792]{1,0:T(8,128)(2,1)}, bf16[288,1792]{1,0:T(8,128)(2,1)S(1)}, u32[]{:S(2)}, u32[]{:S(2)}) collective-permute-start(bf16[288,1792]{1,0:T(8,128)(2,1)} %param.21), channel_id=1, source_target_pairs={{32,0},{96,1},{34,2},{98,3},{36,4},{100,5},{38,6},{102,7},{40,8},{... | collective-permute-start | bytes 3096584 | tf_op jit(solution)/shard_map/ppermute | solution.py:53
  57.3 2.8 %collective-permute-start.10 = (bf16[32,3584]{1,0:T(8,128)(2,1)S(1)}, bf16[32,3584]{1,0:T(8,128)(2,1)S(1)}, u32[]{:S(2)}, u32[]{:S(2)}) collective-permute-start(bf16[32,3584]{1,0:T(8,128)(2,1)S(1)} %fusion.1), channel_id=1, source_target_pairs={{0,4},{1,17},{2,6},{3,19},{4,0},{5,21},{6,2},{7,23},{8,12},{9,25},... | collective-permute-start | bytes 688136 | tf_op jit(solution)/shard_map/ppermute | solution.py:35
  61.5 7.8 %collective-permute-done.15.c_ref = bf16[288,1792]{1,0:T(8,128)(2,1)S(1)} collective-permute-done((bf16[288,1792]{1,0:T(8,128)(2,1)}, bf16[288,1792]{1,0:T(8,128)(2,1)S(1)}, u32[]{:S(2)}, u32[]{:S(2)}) %collective-permute-start.15) | collective-permute-done | bytes 1032224 | tf_op jit(solution)/shard_map/ppermute | solution.py:53
  69.3 4.6 %collective-permute-start.16 = (bf16[288,1792]{1,0:T(8,128)(2,1)}, bf16[288,1792]{1,0:T(8,128)(2,1)S(1)}, u32[]{:S(2)}, u32[]{:S(2)}) collective-permute-start(bf16[288,1792]{1,0:T(8,128)(2,1)} %param.21), channel_id=1, source_target_pairs={{33,0},{97,1},{35,2},{99,3},{37,4},{101,5},{39,6},{103,7},{41,8},{... | collective-permute-start | bytes 3096584 | tf_op jit(solution)/shard_map/ppermute | solution.py:53
  74.1 2.5 %collective-permute-start.12 = (bf16[32,3584]{1,0:T(8,128)(2,1)S(1)}, bf16[32,3584]{1,0:T(8,128)(2,1)S(1)}, u32[]{:S(2)}, u32[]{:S(2)}) collective-permute-start(bf16[32,3584]{1,0:T(8,128)(2,1)S(1)} %add_convert_fusion.1.refs_0_), channel_id=1, source_target_pairs={{0,24},{1,7},{2,26},{3,1},{4,28},{5,3},{6,30},{7,5},{8,0},{9,15},{... | collective-permute-start | bytes 688136 | tf_op jit(solution)/shard_map/ppermute | solution.py:35
  77.8 4.3 %collective-permute-done.12.refs_1_ = bf16[32,3584]{1,0:T(8,128)(2,1)S(1)} collective-permute-done((bf16[32,3584]{1,0:T(8,128)(2,1)S(1)}, bf16[32,3584]{1,0:T(8,128)(2,1)S(1)}, u32[]{:S(2)}, u32[]{:S(2)}) %collective-permute-start.12) | collective-permute-done | bytes 229408 | tf_op jit(solution)/shard_map/ppermute | solution.py:35
  83.1 2.4 %collective-permute-done.14.refs_3_ = bf16[32,3584]{1,0:T(8,128)(2,1)S(1)} collective-permute-done((bf16[32,3584]{1,0:T(8,128)(2,1)S(1)}, bf16[32,3584]{1,0:T(8,128)(2,1)S(1)}, u32[]{:S(2)}, u32[]{:S(2)}) %collective-permute-start.14) | collective-permute-done | bytes 229408 | tf_op jit(solution)/shard_map/ppermute | solution.py:35
  87.6 1.9 %shard_map.112 = (f32[128,576]{1,0:T(8,128)S(1)}, f32[128,128]{1,0:T(8,128)S(1)}) custom-call(s32[4]{0:T(128)S(1)} %pad_add_fusion.spot_ref, bf16[32,3584]{1,0:T(8,128)(2,1)S(1)} %add_convert_fusion.1.refs_0_, bf16[32,3584]{1,0:T(8,128)(2,1)S(1)} %collective-permute-done.12.refs_1_, bf16[32,3584]{1,0:T(8,128)(2,1)S(1)} %collective-permute-done.13.refs_2_, ...), custom_call_target="tpu_custom_call" | custom-call | flops 528482304 | bytes 4128768 | tf_op jit(solution)/shard_map/pallas_call | solution.py:262
  89.5 2.3 %shard_map.113.inner_ref = bf16[128,288]{1,0:T(8,128)(2,1)S(1)} custom-call(s32[4]{0:T(128)S(1)} %pad_add_fusion.spot_ref, bf16[32,3584]{1,0:T(8,128)(2,1)S(1)} %collective-permute-done.17.refs_0_, bf16[32,3584]{1,0:T(8,128)(2,1)S(1)} %collective-permute-done.18.refs_1_, bf16[32,3584]{1,0:T(8,128)(2,1)S(1)} %collective-permute-done.19.refs_2_, ...), custom_call_target="tpu_custom_call" | custom-call | flops 528482304 | bytes 4128768 | tf_op jit(solution)/shard_map/pallas_call | solution.py:262
  93.3 1.8 %shard_map.114 = (bf16[32,3584]{1,0:T(8,128)(2,1)S(1)}, bf16[32,3584]{1,0:T(8,128)(2,1)S(1)}, bf16[32,3584]{1,0:T(8,128)(2,1)S(1)}, bf16[32,3584]{1,0:T(8,128)(2,1)S(1)}) custom-call(s32[4]{0:T(128)S(1)} %pad_add_fusion.spot_ref, bf16[128,288]{1,0:T(8,128)(2,1)S(1)} %shard_map.113.inner_ref, bf16[128,288]{1,0:T(8,128)(2,1)S(1)} %collective-permute-done.21.other_ref, ...), custom_call_target="tpu_custom_call" | custom-call | flops 528482304 | bytes 4128768 | tf_op jit(solution)/shard_map/pallas_call | solution.py:301
  96.4 2.4 %collective-permute-start.23 = (bf16[32,3584]{1,0:T(8,128)(2,1)S(1)}, bf16[32,3584]{1,0:T(8,128)(2,1)S(1)}, u32[]{:S(2)}, u32[]{:S(2)}) collective-permute-start(bf16[32,3584]{1,0:T(8,128)(2,1)S(1)} %get-tuple-element.53), channel_id=1, source_target_pairs={{0,16},{1,5},{2,18},{3,7},{4,20},{5,1},{6,22},{7,3},{8,24},{9,13},... | collective-permute-start | bytes 688136 | tf_op jit(solution)/shard_map/ppermute | solution.py:35
  99.9 1.6 %collective-permute-done.22 = bf16[32,3584]{1,0:T(8,128)(2,1)S(1)} collective-permute-done((bf16[32,3584]{1,0:T(8,128)(2,1)S(1)}, bf16[32,3584]{1,0:T(8,128)(2,1)S(1)}, u32[]{:S(2)}, u32[]{:S(2)}) %collective-permute-start.22) | collective-permute-done | bytes 229408 | tf_op jit(solution)/shard_map/ppermute | solution.py:35
  101.6 3.0 %collective-permute-done.23 = bf16[32,3584]{1,0:T(8,128)(2,1)S(1)} collective-permute-done((bf16[32,3584]{1,0:T(8,128)(2,1)S(1)}, bf16[32,3584]{1,0:T(8,128)(2,1)S(1)}, u32[]{:S(2)}, u32[]{:S(2)}) %collective-permute-start.23) | collective-permute-done | bytes 229408 | tf_op jit(solution)/shard_map/ppermute | solution.py:35
  110.4 4.5 %collective-permute-start.28 = (bf16[4,3584]{1,0:T(4,128)(2,1)S(1)}, bf16[4,3584]{1,0:T(4,128)(2,1)S(1)}, u32[]{:S(2)}, u32[]{:S(2)}) collective-permute-start(bf16[4,3584]{1,0:T(4,128)(2,1)S(1)} %get-tuple-element.60), channel_id=1, source_target_pairs={{0,1},{1,0},{2,3},{3,2},{4,5},{5,4},{6,7},{7,6},{8,9},{9,8},{10,11... | collective-permute-start | bytes 86024 | tf_op jit(solution)/shard_map/ppermute | solution.py:15
  (70 shorter events, 23.4 us)
Async XLA Ops:
  0.0 30.4 %collective-permute-start.2 = (bf16[256,7168]{1,0:T(8,128)(2,1)}, bf16[256,7168]{1,0:T(8,128)(2,1)}, u32[]{:S(2)}, u32[]{:S(2)}) collective-permute-start(bf16[256,7168]{1,0:T(8,128)(2,1)} %om_ref.1), channel_id=1, source_target_pairs={{0,1},{1,0},{2,3},{3,2},{4,5},{5,4},{6,7},{7,6},{8,9},{9,8},{10,11... | collective-permute-start | bytes 11010056 | tf_op jit(solution)/shard_map/ppermute | solution.py:15
  11.1 15.4 %all-to-all-start = ((bf16[16,16,512]{2,1,0:T(8,128)(2,1)}), bf16[16,16,512]{2,1,0:T(8,128)(2,1)S(1)}, u32[]{:S(2)}, u32[]{:S(2)}) async-start(bf16[16,16,512]{2,1,0:T(8,128)(2,1)} %bitcast.28), calls=%async_computation | async-start | bytes 524288 | tf_op jit(solution)/shard_map/all_to_all | solution.py:20
  18.0 28.4 %collective-permute-start.3 = (bf16[288,1792]{1,0:T(8,128)(2,1)}, bf16[288,1792]{1,0:T(8,128)(2,1)S(1)}, u32[]{:S(2)}, u32[]{:S(2)}) collective-permute-start(bf16[288,1792]{1,0:T(8,128)(2,1)} %param.21), channel_id=1, source_target_pairs={{0,0},{64,1},{2,2},{66,3},{4,4},{68,5},{6,6},{70,7},{8,8},{72,9},{... | collective-permute-start | bytes 3096584 | tf_op jit(solution)/shard_map/ppermute | solution.py:53
  21.7 25.5 %collective-permute-start.4 = (bf16[288,1792]{1,0:T(8,128)(2,1)}, bf16[288,1792]{1,0:T(8,128)(2,1)S(1)}, u32[]{:S(2)}, u32[]{:S(2)}) collective-permute-start(bf16[288,1792]{1,0:T(8,128)(2,1)} %param.21), channel_id=1, source_target_pairs={{1,0},{65,1},{3,2},{67,3},{5,4},{69,5},{7,6},{71,7},{9,8},{73,9},{... | collective-permute-start | bytes 3096584 | tf_op jit(solution)/shard_map/ppermute | solution.py:53
  21.8 6.1 %collective-permute-start.1 = (bf16[2,512,128]{2,1,0:T(8,128)(2,1)S(1)}, bf16[2,512,128]{2,1,0:T(8,128)(2,1)S(1)}, u32[]{:S(2)}, u32[]{:S(2)}) collective-permute-start(bf16[2,512,128]{2,1,0:T(8,128)(2,1)S(1)} %copy-done.4), channel_id=1, source_target_pairs={{0,1},{1,0},{2,3},{3,2},{4,5},{5,4},{6,7},{7,6},{8,9},{9,8},{10,11... | collective-permute-start | bytes 786440 | tf_op jit(solution)/shard_map/ppermute | solution.py:15
  28.0 24.5 %collective-permute-start.8 = (bf16[4,3584]{1,0:T(4,128)(2,1)S(1)}, bf16[4,3584]{1,0:T(4,128)(2,1)S(1)}, u32[]{:S(2)}, u32[]{:S(2)}) collective-permute-start(bf16[4,3584]{1,0:T(4,128)(2,1)S(1)} %get-tuple-element.62), channel_id=1, source_target_pairs={{0,1},{1,0},{2,3},{3,2},{4,5},{5,4},{6,7},{7,6},{8,9},{9,8},{10,11... | collective-permute-start | bytes 86024 | tf_op jit(solution)/shard_map/ppermute | solution.py:15
  47.2 9.6 %collective-permute-start.5 = (bf16[32,3584]{1,0:T(8,128)(2,1)S(1)}, bf16[32,3584]{1,0:T(8,128)(2,1)S(1)}, u32[]{:S(2)}, u32[]{:S(2)}) collective-permute-start(bf16[32,3584]{1,0:T(8,128)(2,1)S(1)} %get-tuple-element.35), channel_id=1, source_target_pairs={{0,8},{1,3},{2,10},{3,5},{4,12},{5,7},{6,14},{7,1},{8,16},{9,11},{... | collective-permute-start | bytes 688136 | tf_op jit(solution)/shard_map/ppermute | solution.py:35
  48.9 8.3 %collective-permute-start.6 = (bf16[32,3584]{1,0:T(8,128)(2,1)S(1)}, bf16[32,3584]{1,0:T(8,128)(2,1)S(1)}, u32[]{:S(2)}, u32[]{:S(2)}) collective-permute-start(bf16[32,3584]{1,0:T(8,128)(2,1)S(1)} %get-tuple-element.36), channel_id=1, source_target_pairs={{0,16},{1,5},{2,18},{3,7},{4,20},{5,1},{6,22},{7,3},{8,24},{9,13},... | collective-permute-start | bytes 688136 | tf_op jit(solution)/shard_map/ppermute | solution.py:35
  51.3 5.9 %collective-permute-start.7 = (bf16[32,3584]{1,0:T(8,128)(2,1)S(1)}, bf16[32,3584]{1,0:T(8,128)(2,1)S(1)}, u32[]{:S(2)}, u32[]{:S(2)}) collective-permute-start(bf16[32,3584]{1,0:T(8,128)(2,1)S(1)} %get-tuple-element.37), channel_id=1, source_target_pairs={{0,24},{1,7},{2,26},{3,1},{4,28},{5,3},{6,30},{7,5},{8,0},{9,15},{... | collective-permute-start | bytes 688136 | tf_op jit(solution)/shard_map/ppermute | solution.py:35
  52.5 16.8 %collective-permute-start.15 = (bf16[288,1792]{1,0:T(8,128)(2,1)}, bf16[288,1792]{1,0:T(8,128)(2,1)S(1)}, u32[]{:S(2)}, u32[]{:S(2)}) collective-permute-start(bf16[288,1792]{1,0:T(8,128)(2,1)} %param.21), channel_id=1, source_target_pairs={{32,0},{96,1},{34,2},{98,3},{36,4},{100,5},{38,6},{102,7},{40,8},{... | collective-permute-start | bytes 3096584 | tf_op jit(solution)/shard_map/ppermute | solution.py:53
  57.3 16.7 %collective-permute-start.10 = (bf16[32,3584]{1,0:T(8,128)(2,1)S(1)}, bf16[32,3584]{1,0:T(8,128)(2,1)S(1)}, u32[]{:S(2)}, u32[]{:S(2)}) collective-permute-start(bf16[32,3584]{1,0:T(8,128)(2,1)S(1)} %fusion.1), channel_id=1, source_target_pairs={{0,4},{1,17},{2,6},{3,19},{4,0},{5,21},{6,2},{7,23},{8,12},{9,25},... | collective-permute-start | bytes 688136 | tf_op jit(solution)/shard_map/ppermute | solution.py:35
  60.1 13.9 %collective-permute-start.11 = (bf16[32,3584]{1,0:T(8,128)(2,1)S(1)}, bf16[32,3584]{1,0:T(8,128)(2,1)S(1)}, u32[]{:S(2)}, u32[]{:S(2)}) collective-permute-start(bf16[32,3584]{1,0:T(8,128)(2,1)S(1)} %fusion.1), channel_id=1, source_target_pairs={{0,6},{1,25},{2,0},{3,27},{4,2},{5,29},{6,4},{7,31},{8,14},{9,1},{... | collective-permute-start | bytes 688136 | tf_op jit(solution)/shard_map/ppermute | solution.py:35
  60.9 13.1 %collective-permute-start.9 = (bf16[32,3584]{1,0:T(8,128)(2,1)S(1)}, bf16[32,3584]{1,0:T(8,128)(2,1)S(1)}, u32[]{:S(2)}, u32[]{:S(2)}) collective-permute-start(bf16[32,3584]{1,0:T(8,128)(2,1)S(1)} %fusion.1), channel_id=1, source_target_pairs={{0,2},{1,9},{2,4},{3,11},{4,6},{5,13},{6,0},{7,15},{8,10},{9,17},{... | collective-permute-start | bytes 688136 | tf_op jit(solution)/shard_map/ppermute | solution.py:35
  69.3 16.8 %collective-permute-start.16 = (bf16[288,1792]{1,0:T(8,128)(2,1)}, bf16[288,1792]{1,0:T(8,128)(2,1)S(1)}, u32[]{:S(2)}, u32[]{:S(2)}) collective-permute-start(bf16[288,1792]{1,0:T(8,128)(2,1)} %param.21), channel_id=1, source_target_pairs={{33,0},{97,1},{35,2},{99,3},{37,4},{101,5},{39,6},{103,7},{41,8},{... | collective-permute-start | bytes 3096584 | tf_op jit(solution)/shard_map/ppermute | solution.py:53
  74.1 7.9 %collective-permute-start.12 = (bf16[32,3584]{1,0:T(8,128)(2,1)S(1)}, bf16[32,3584]{1,0:T(8,128)(2,1)S(1)}, u32[]{:S(2)}, u32[]{:S(2)}) collective-permute-start(bf16[32,3584]{1,0:T(8,128)(2,1)S(1)} %add_convert_fusion.1.refs_0_), channel_id=1, source_target_pairs={{0,24},{1,7},{2,26},{3,1},{4,28},{5,3},{6,30},{7,5},{8,0},{9,15},{... | collective-permute-start | bytes 688136 | tf_op jit(solution)/shard_map/ppermute | solution.py:35
  76.6 6.5 %collective-permute-start.13 = (bf16[32,3584]{1,0:T(8,128)(2,1)S(1)}, bf16[32,3584]{1,0:T(8,128)(2,1)S(1)}, u32[]{:S(2)}, u32[]{:S(2)}) collective-permute-start(bf16[32,3584]{1,0:T(8,128)(2,1)S(1)} %add_convert_fusion.1.refs_0_), channel_id=1, source_target_pairs={{0,16},{1,5},{2,18},{3,7},{4,20},{5,1},{6,22},{7,3},{8,24},{9,13},... | collective-permute-start | bytes 688136 | tf_op jit(solution)/shard_map/ppermute | solution.py:35
  77.2 8.3 %collective-permute-start.14 = (bf16[32,3584]{1,0:T(8,128)(2,1)S(1)}, bf16[32,3584]{1,0:T(8,128)(2,1)S(1)}, u32[]{:S(2)}, u32[]{:S(2)}) collective-permute-start(bf16[32,3584]{1,0:T(8,128)(2,1)S(1)} %add_convert_fusion.1.refs_0_), channel_id=1, source_target_pairs={{0,8},{1,3},{2,10},{3,5},{4,12},{5,7},{6,14},{7,1},{8,16},{9,11},{... | collective-permute-start | bytes 688136 | tf_op jit(solution)/shard_map/ppermute | solution.py:35
  95.1 6.4 %collective-permute-start.22 = (bf16[32,3584]{1,0:T(8,128)(2,1)S(1)}, bf16[32,3584]{1,0:T(8,128)(2,1)S(1)}, u32[]{:S(2)}, u32[]{:S(2)}) collective-permute-start(bf16[32,3584]{1,0:T(8,128)(2,1)S(1)} %get-tuple-element.52), channel_id=1, source_target_pairs={{0,8},{1,3},{2,10},{3,5},{4,12},{5,7},{6,14},{7,1},{8,16},{9,11},{... | collective-permute-start | bytes 688136 | tf_op jit(solution)/shard_map/ppermute | solution.py:35
  96.4 8.3 %collective-permute-start.23 = (bf16[32,3584]{1,0:T(8,128)(2,1)S(1)}, bf16[32,3584]{1,0:T(8,128)(2,1)S(1)}, u32[]{:S(2)}, u32[]{:S(2)}) collective-permute-start(bf16[32,3584]{1,0:T(8,128)(2,1)S(1)} %get-tuple-element.53), channel_id=1, source_target_pairs={{0,16},{1,5},{2,18},{3,7},{4,20},{5,1},{6,22},{7,3},{8,24},{9,13},... | collective-permute-start | bytes 688136 | tf_op jit(solution)/shard_map/ppermute | solution.py:35
  98.8 5.9 %collective-permute-start.24 = (bf16[32,3584]{1,0:T(8,128)(2,1)S(1)}, bf16[32,3584]{1,0:T(8,128)(2,1)S(1)}, u32[]{:S(2)}, u32[]{:S(2)}) collective-permute-start(bf16[32,3584]{1,0:T(8,128)(2,1)S(1)} %get-tuple-element.54), channel_id=1, source_target_pairs={{0,24},{1,7},{2,26},{3,1},{4,28},{5,3},{6,30},{7,5},{8,0},{9,15},{... | collective-permute-start | bytes 688136 | tf_op jit(solution)/shard_map/ppermute | solution.py:35
  104.8 4.3 %collective-permute-start.25 = (bf16[8,3584]{1,0:T(8,128)(2,1)S(1)}, bf16[8,3584]{1,0:T(8,128)(2,1)S(1)}, u32[]{:S(2)}, u32[]{:S(2)}) collective-permute-start(bf16[8,3584]{1,0:T(8,128)(2,1)S(1)} %get-tuple-element.55), channel_id=1, source_target_pairs={{0,2},{1,9},{2,4},{3,11},{4,6},{5,13},{6,0},{7,15},{8,10},{9,17},{... | collective-permute-start | bytes 172040 | tf_op jit(solution)/shard_map/ppermute | solution.py:35
  105.1 4.6 %collective-permute-start.26 = (bf16[8,3584]{1,0:T(8,128)(2,1)S(1)}, bf16[8,3584]{1,0:T(8,128)(2,1)S(1)}, u32[]{:S(2)}, u32[]{:S(2)}) collective-permute-start(bf16[8,3584]{1,0:T(8,128)(2,1)S(1)} %get-tuple-element.57), channel_id=1, source_target_pairs={{0,4},{1,17},{2,6},{3,19},{4,0},{5,21},{6,2},{7,23},{8,12},{9,25},... | collective-permute-start | bytes 172040 | tf_op jit(solution)/shard_map/ppermute | solution.py:35
  106.6 3.7 %collective-permute-start.27 = (bf16[8,3584]{1,0:T(8,128)(2,1)S(1)}, bf16[8,3584]{1,0:T(8,128)(2,1)S(1)}, u32[]{:S(2)}, u32[]{:S(2)}) collective-permute-start(bf16[8,3584]{1,0:T(8,128)(2,1)S(1)} %get-tuple-element.56), channel_id=1, source_target_pairs={{0,6},{1,25},{2,0},{3,27},{4,2},{5,29},{6,4},{7,31},{8,14},{9,1},{... | collective-permute-start | bytes 172040 | tf_op jit(solution)/shard_map/ppermute | solution.py:35
  110.4 5.3 %collective-permute-start.28 = (bf16[4,3584]{1,0:T(4,128)(2,1)S(1)}, bf16[4,3584]{1,0:T(4,128)(2,1)S(1)}, u32[]{:S(2)}, u32[]{:S(2)}) collective-permute-start(bf16[4,3584]{1,0:T(4,128)(2,1)S(1)} %get-tuple-element.60), channel_id=1, source_target_pairs={{0,1},{1,0},{2,3},{3,2},{4,5},{5,4},{6,7},{7,6},{8,9},{9,8},{10,11... | collective-permute-start | bytes 86024 | tf_op jit(solution)/shard_map/ppermute | solution.py:15
  (12 other events, 233.3 us)

commit v10 on v9

--- a/solution.py
+++ b/solution.py
@@ -356,12 +356,11 @@
     latent = attend(query, cache, lengths, counts, latent_width, chips)
     arrived = between_chips(latent, width)
     arrived_other = core_swap(arrived, width)
+    arrived_other, pieces[0] = lax.optimization_barrier((arrived_other, pieces[0]))
     values = project(arrived, arrived_other, value_weight, value_other, spot, side, slots)
     attended_parts = sum_heads(values, output_weight, output_other, spot, side)
 
-    attended_parts, pieces[0], pieces[1], later = lax.optimization_barrier(
-        (attended_parts, pieces[0], pieces[1], down_weight)
-    )
+    attended_parts, later = lax.optimization_barrier((attended_parts, down_weight))
     pieces.append(down_piece(later, width, 2))
     later, pieces[2] = lax.optimization_barrier((down_weight, pieces[2]))
     pieces.append(down_piece(later, width, 3))
@@ -370,6 +369,7 @@
     own_rows = (jnp.arange(side) == second)[:, None, None]
     summed = summed + jnp.where(own_rows, input_chip[None], 0.0)
     summed = summed.astype(jnp.bfloat16).reshape(line, half)
+    summed, pieces[1] = lax.optimization_barrier((summed, pieces[1]))
     residual_line = total(turn([summed] * side, 1, side, 1)).astype(jnp.bfloat16)
     residual_mine = turn([residual_line] * side, 0, side, -1)
     residual_mine, pieces[2], pieces[3] = lax.optimization_barrier(

time: 117 us -> 102 us (0.87)
  starting transfers between devices: 51.7 us -> 43.7 us
  waiting for transfers between devices: 42.6 us -> 34.9 us
    ppermute x4, waiting for transfers between devices: 22.3 us -> 9.41 us  [down_piece(): return lax.ppermute(down_weight, ('dp', 'tp'), pairs)]
    ppermute x15, starting transfers between devices: 20.8 us -> 15.8 us  [turn(): out.append(lax.ppermute(parts[k], 'tp', pairs))]
    ppermute x10, starting transfers between devices: 11.3 us -> 7.85 us  [core_swap(): return lax.ppermute(x, 'tp', [(i, i ^ 1) for i in range(width)])]
    all_to_all x1, waiting for transfers between devices: 2.43 us -> 5.47 us  [between_chips(): return lax.all_to_all(x, 'tp', 0, 0, tiled=True, axis_index_groups=groups)]
    ppermute x15, waiting for transfers between devices: 15.2 us -> 16.9 us  [turn(): out.append(lax.ppermute(parts[k], 'tp', pairs))]
  transfers between devices with their start and end apart: 30 -> 30, of which waited for: 17 -> 15; matrix products, arithmetic and copies ran while one was open for 1% -> 1% of each run, Pallas kernels for 13% -> 15%
where the time goes in v10:
time: 102 us; the launch traced here: 101 us
  starting transfers between devices  43.7 us (43%)
  waiting for transfers between devices  34.9 us (34%)
  Pallas kernels  19.6 us (19%)
  other arithmetic  1.29 us (1%)
    ppermute x15, waiting for transfers between devices, turn(): out.append(lax.ppermute(parts[k], 'tp', pairs))  16.9 us
    ppermute x15, starting transfers between devices, turn(): out.append(lax.ppermute(parts[k], 'tp', pairs))  15.8 us
    ppermute x4, starting transfers between devices, down_piece(): return lax.ppermute(down_weight, ('dp', 'tp'), pairs)  13.3 us
    ppermute x4, waiting for transfers between devices, down_piece(): return lax.ppermute(down_weight, ('dp', 'tp'), pairs)  9.41 us
    pallas_call x1, Pallas kernels, attend(): pl.pallas_call(kernel, in_specs=[in_smem, in_smem, in_vmem, in_hbm], out_...  9.02 us
    ppermute x10, starting transfers between devices, core_swap(): return lax.ppermute(x, 'tp', [(i, i ^ 1) for i in range(width)])  7.85 us
    all_to_all x1, starting transfers between devices, between_chips(): return lax.all_to_all(x, 'tp', 0, 0, tiled=True, axis_index_groups=groups)  6.78 us
    all_to_all x1, waiting for transfers between devices, between_chips(): return lax.all_to_all(x, 'tp', 0, 0, tiled=True, axis_index_groups=groups)  5.47 us
  transfers between devices with their start and end apart: 30, of which 15 were waited for; matrix products, arithmetic and copies ran while one was open for 1% of the time, Pallas kernels for 15%

profile of v10, /device:TPU:1, one launch (start us, length us, event | category | flops | bytes accessed | tf_op | source)
XLA Modules:
  0.0 100.8 jit_solution(9829873980715473187)
XLA Ops:
  1.4 3.5 %collective-permute-start.1 = (bf16[288,1792]{1,0:T(8,128)(2,1)}, bf16[288,1792]{1,0:T(8,128)(2,1)S(1)}, u32[]{:S(2)}, u32[]{:S(2)}) collective-permute-start(bf16[288,1792]{1,0:T(8,128)(2,1)} %param.21), channel_id=1, source_target_pairs={{0,0},{64,1},{2,2},{66,3},{4,4},{68,5},{6,6},{70,7},{8,8},{72,9},{... | collective-permute-start | bytes 3096584 | tf_op jit(solution)/shard_map/ppermute | solution.py:53
  5.6 9.0 %shard_map.109 = bf16[256,512]{1,0:T(8,128)(2,1)} custom-call(s32[4]{0:T(128)} %lengths_ref.1, s32[1]{0:T(128)} %copy.12.counts_ref, bf16[4,64,576]{2,1,0:T(8,128)(2,1)} %q_ref.1, bf16[4,576,2048]{2,1,0:T(8,128)(2,1)} %bitcast.27), custom_call_target="tpu_custom_call" | custom-call | flops 1140850688 | bytes 9437184 | tf_op jit(solution)/shard_map/pallas_call | solution.py:124
  14.6 6.8 %all-to-all-start = ((bf16[16,16,512]{2,1,0:T(8,128)(2,1)}), bf16[16,16,512]{2,1,0:T(8,128)(2,1)S(1)}, u32[]{:S(2)}, u32[]{:S(2)}) async-start(bf16[16,16,512]{2,1,0:T(8,128)(2,1)} %bitcast.28), calls=%async_computation | async-start | bytes 524288 | tf_op jit(solution)/shard_map/all_to_all | solution.py:20
  21.5 2.5 %collective-permute-start.2 = (bf16[2,512,128]{2,1,0:T(8,128)(2,1)S(1)}, bf16[2,512,128]{2,1,0:T(8,128)(2,1)S(1)}, u32[]{:S(2)}, u32[]{:S(2)}) collective-permute-start(bf16[2,512,128]{2,1,0:T(8,128)(2,1)S(1)} %copy-done.4), channel_id=1, source_target_pairs={{0,1},{1,0},{2,3},{3,2},{4,5},{5,4},{6,7},{7,6},{8,9},{9,8},{10,11... | collective-permute-start | bytes 786440 | tf_op jit(solution)/shard_map/ppermute | solution.py:15
  24.1 5.5 %all-to-all-done = bf16[16,16,512]{2,1,0:T(8,128)(2,1)S(1)} async-done(((bf16[16,16,512]{2,1,0:T(8,128)(2,1)}), bf16[16,16,512]{2,1,0:T(8,128)(2,1)S(1)}, u32[]{:S(2)}, u32[]{:S(2)}) %all-to-all-start) | async-done | bytes 262176 | tf_op jit(solution)/shard_map/all_to_all | solution.py:20
  31.2 1.6 %shard_map.110.value_ref = bf16[128,512]{1,0:T(8,128)(2,1)S(1)} custom-call(s32[4]{0:T(128)S(1)} %pad_add_fusion.spot_ref, bf16[256,512]{1,0:T(8,128)(2,1)S(1)} %bitcast.23, bf16[256,512]{1,0:T(8,128)(2,1)S(1)} %bitcast.26, bf16[2,512,128]{2,1,0:T(8,128)(2,1)S(1)} %copy-done.4, bf16[2,512,128]{2,1,0:T(8,128)(2,1)S(1)} %collective-permute-done.2.vo_ref), custom_call_target="tpu_custom_call" | custom-call | flops 1610612736 | bytes 524288 | tf_op jit(solution)/shard_map/pallas_call | solution.py:169
  32.9 3.0 %shard_map.111 = (bf16[32,3584]{1,0:T(8,128)(2,1)S(1)}, bf16[32,3584]{1,0:T(8,128)(2,1)S(1)}, bf16[32,3584]{1,0:T(8,128)(2,1)S(1)}, bf16[32,3584]{1,0:T(8,128)(2,1)S(1)}) custom-call(s32[4]{0:T(128)S(1)} %pad_add_fusion.spot_ref, bf16[128,512]{1,0:T(8,128)(2,1)S(1)} %shard_map.110.value_ref, bf16[256,7168]{1,0:T(8,128)(2,1)S(1)} %copy-done.2, ...), custom_call_target="tpu_custom_call" | custom-call | flops 469762048 | bytes 3670016 | tf_op jit(solution)/shard_map/pallas_call | solution.py:205
  38.8 4.4 %collective-permute-start.15 = (bf16[288,1792]{1,0:T(8,128)(2,1)S(1)}, bf16[288,1792]{1,0:T(8,128)(2,1)S(1)}, u32[]{:S(2)}, u32[]{:S(2)}) collective-permute-start(bf16[288,1792]{1,0:T(8,128)(2,1)S(1)} %copy-done.6), channel_id=1, source_target_pairs={{32,0},{96,1},{34,2},{98,3},{36,4},{100,5},{38,6},{102,7},{40,8},{... | collective-permute-start | bytes 3096584 | tf_op jit(solution)/shard_map/ppermute | solution.py:53
  43.2 1.6 %collective-permute-done.4 = bf16[32,3584]{1,0:T(8,128)(2,1)S(1)} collective-permute-done((bf16[32,3584]{1,0:T(8,128)(2,1)S(1)}, bf16[32,3584]{1,0:T(8,128)(2,1)S(1)}, u32[]{:S(2)}, u32[]{:S(2)}) %collective-permute-start.4) | collective-permute-done | bytes 229408 | tf_op jit(solution)/shard_map/ppermute | solution.py:35
  46.2 1.6 %collective-permute-start.11 = (bf16[32,3584]{1,0:T(8,128)(2,1)S(1)}, bf16[32,3584]{1,0:T(8,128)(2,1)S(1)}, u32[]{:S(2)}, u32[]{:S(2)}) collective-permute-start(bf16[32,3584]{1,0:T(8,128)(2,1)S(1)} %fusion.1), channel_id=1, source_target_pairs={{0,6},{1,25},{2,0},{3,27},{4,2},{5,29},{6,4},{7,31},{8,14},{9,1},{... | collective-permute-start | bytes 688136 | tf_op jit(solution)/shard_map/ppermute | solution.py:35
  47.8 8.0 %collective-permute-done.15.c_ref = bf16[288,1792]{1,0:T(8,128)(2,1)S(1)} collective-permute-done((bf16[288,1792]{1,0:T(8,128)(2,1)S(1)}, bf16[288,1792]{1,0:T(8,128)(2,1)S(1)}, u32[]{:S(2)}, u32[]{:S(2)}) %collective-permute-start.15) | collective-permute-done | bytes 1032224 | tf_op jit(solution)/shard_map/ppermute | solution.py:53
  55.8 5.3 %collective-permute-start.16 = (bf16[288,1792]{1,0:T(8,128)(2,1)S(1)}, bf16[288,1792]{1,0:T(8,128)(2,1)S(1)}, u32[]{:S(2)}, u32[]{:S(2)}) collective-permute-start(bf16[288,1792]{1,0:T(8,128)(2,1)S(1)} %copy-done.6), channel_id=1, source_target_pairs={{33,0},{97,1},{35,2},{99,3},{37,4},{101,5},{39,6},{103,7},{41,8},{... | collective-permute-start | bytes 3096584 | tf_op jit(solution)/shard_map/ppermute | solution.py:53
  63.4 3.1 %collective-permute-done.12.refs_1_ = bf16[32,3584]{1,0:T(8,128)(2,1)S(1)} collective-permute-done((bf16[32,3584]{1,0:T(8,128)(2,1)S(1)}, bf16[32,3584]{1,0:T(8,128)(2,1)S(1)}, u32[]{:S(2)}, u32[]{:S(2)}) %collective-permute-start.12) | collective-permute-done | bytes 229408 | tf_op jit(solution)/shard_map/ppermute | solution.py:35
  66.5 2.3 %collective-permute-done.13.refs_2_ = bf16[32,3584]{1,0:T(8,128)(2,1)S(1)} collective-permute-done((bf16[32,3584]{1,0:T(8,128)(2,1)S(1)}, bf16[32,3584]{1,0:T(8,128)(2,1)S(1)}, u32[]{:S(2)}, u32[]{:S(2)}) %collective-permute-start.13) | collective-permute-done | bytes 229408 | tf_op jit(solution)/shard_map/ppermute | solution.py:35
  68.8 2.5 %collective-permute-done.14.refs_3_ = bf16[32,3584]{1,0:T(8,128)(2,1)S(1)} collective-permute-done((bf16[32,3584]{1,0:T(8,128)(2,1)S(1)}, bf16[32,3584]{1,0:T(8,128)(2,1)S(1)}, u32[]{:S(2)}, u32[]{:S(2)}) %collective-permute-start.14) | collective-permute-done | bytes 229408 | tf_op jit(solution)/shard_map/ppermute | solution.py:35
  73.7 1.9 %shard_map.112 = (f32[128,576]{1,0:T(8,128)S(1)}, f32[128,128]{1,0:T(8,128)S(1)}) custom-call(s32[4]{0:T(128)S(1)} %pad_add_fusion.spot_ref, bf16[32,3584]{1,0:T(8,128)(2,1)S(1)} %add_convert_fusion.1.refs_0_, bf16[32,3584]{1,0:T(8,128)(2,1)S(1)} %collective-permute-done.12.refs_1_, bf16[32,3584]{1,0:T(8,128)(2,1)S(1)} %collective-permute-done.13.refs_2_, ...), custom_call_target="tpu_custom_call" | custom-call | flops 528482304 | bytes 4128768 | tf_op jit(solution)/shard_map/pallas_call | solution.py:262
  75.6 2.3 %shard_map.113.inner_ref = bf16[128,288]{1,0:T(8,128)(2,1)S(1)} custom-call(s32[4]{0:T(128)S(1)} %pad_add_fusion.spot_ref, bf16[32,3584]{1,0:T(8,128)(2,1)S(1)} %collective-permute-done.17.refs_0_, bf16[32,3584]{1,0:T(8,128)(2,1)S(1)} %collective-permute-done.18.refs_1_, bf16[32,3584]{1,0:T(8,128)(2,1)S(1)} %collective-permute-done.19.refs_2_, ...), custom_call_target="tpu_custom_call" | custom-call | flops 528482304 | bytes 4128768 | tf_op jit(solution)/shard_map/pallas_call | solution.py:262
  79.3 1.8 %shard_map.114 = (bf16[32,3584]{1,0:T(8,128)(2,1)S(1)}, bf16[32,3584]{1,0:T(8,128)(2,1)S(1)}, bf16[32,3584]{1,0:T(8,128)(2,1)S(1)}, bf16[32,3584]{1,0:T(8,128)(2,1)S(1)}) custom-call(s32[4]{0:T(128)S(1)} %pad_add_fusion.spot_ref, bf16[128,288]{1,0:T(8,128)(2,1)S(1)} %shard_map.113.inner_ref, bf16[128,288]{1,0:T(8,128)(2,1)S(1)} %collective-permute-done.21.other_ref, ...), custom_call_target="tpu_custom_call" | custom-call | flops 528482304 | bytes 4128768 | tf_op jit(solution)/shard_map/pallas_call | solution.py:301
  81.4 1.8 %collective-permute-start.23 = (bf16[32,3584]{1,0:T(8,128)(2,1)S(1)}, bf16[32,3584]{1,0:T(8,128)(2,1)S(1)}, u32[]{:S(2)}, u32[]{:S(2)}) collective-permute-start(bf16[32,3584]{1,0:T(8,128)(2,1)S(1)} %get-tuple-element.57), channel_id=1, source_target_pairs={{0,16},{1,5},{2,18},{3,7},{4,20},{5,1},{6,22},{7,3},{8,24},{9,13},... | collective-permute-start | bytes 688136 | tf_op jit(solution)/shard_map/ppermute | solution.py:35
  83.2 1.8 %collective-permute-start.24 = (bf16[32,3584]{1,0:T(8,128)(2,1)S(1)}, bf16[32,3584]{1,0:T(8,128)(2,1)S(1)}, u32[]{:S(2)}, u32[]{:S(2)}) collective-permute-start(bf16[32,3584]{1,0:T(8,128)(2,1)S(1)} %get-tuple-element.58), channel_id=1, source_target_pairs={{0,24},{1,7},{2,26},{3,1},{4,28},{5,3},{6,30},{7,5},{8,0},{9,15},{... | collective-permute-start | bytes 688136 | tf_op jit(solution)/shard_map/ppermute | solution.py:35
  85.0 4.9 %collective-permute-done.22 = bf16[32,3584]{1,0:T(8,128)(2,1)S(1)} collective-permute-done((bf16[32,3584]{1,0:T(8,128)(2,1)S(1)}, bf16[32,3584]{1,0:T(8,128)(2,1)S(1)}, u32[]{:S(2)}, u32[]{:S(2)}) %collective-permute-start.22) | collective-permute-done | bytes 229408 | tf_op jit(solution)/shard_map/ppermute | solution.py:35
  91.4 1.9 %collective-permute-start.26 = (bf16[8,3584]{1,0:T(8,128)(2,1)S(1)}, bf16[8,3584]{1,0:T(8,128)(2,1)S(1)}, u32[]{:S(2)}, u32[]{:S(2)}) collective-permute-start(bf16[8,3584]{1,0:T(8,128)(2,1)S(1)} %get-tuple-element.61), channel_id=1, source_target_pairs={{0,4},{1,17},{2,6},{3,19},{4,0},{5,21},{6,2},{7,23},{8,12},{9,25},... | collective-permute-start | bytes 172040 | tf_op jit(solution)/shard_map/ppermute | solution.py:35
  93.3 2.0 %collective-permute-start.27 = (bf16[8,3584]{1,0:T(8,128)(2,1)S(1)}, bf16[8,3584]{1,0:T(8,128)(2,1)S(1)}, u32[]{:S(2)}, u32[]{:S(2)}) collective-permute-start(bf16[8,3584]{1,0:T(8,128)(2,1)S(1)} %get-tuple-element.60), channel_id=1, source_target_pairs={{0,6},{1,25},{2,0},{3,27},{4,2},{5,29},{6,4},{7,31},{8,14},{9,1},{... | collective-permute-start | bytes 172040 | tf_op jit(solution)/shard_map/ppermute | solution.py:35
  96.8 2.4 %collective-permute-start.28 = (bf16[4,3584]{1,0:T(4,128)(2,1)S(1)}, bf16[4,3584]{1,0:T(4,128)(2,1)S(1)}, u32[]{:S(2)}, u32[]{:S(2)}) collective-permute-start(bf16[4,3584]{1,0:T(4,128)(2,1)S(1)} %get-tuple-element.64), channel_id=1, source_target_pairs={{0,1},{1,0},{2,3},{3,2},{4,5},{5,4},{6,7},{7,6},{8,9},{9,8},{10,11... | collective-permute-start | bytes 86024 | tf_op jit(solution)/shard_map/ppermute | solution.py:15
  (72 shorter events, 18.3 us)
Async XLA Ops:
  0.0 32.8 %collective-permute-start.3 = (bf16[256,7168]{1,0:T(8,128)(2,1)}, bf16[256,7168]{1,0:T(8,128)(2,1)}, u32[]{:S(2)}, u32[]{:S(2)}) collective-permute-start(bf16[256,7168]{1,0:T(8,128)(2,1)} %om_ref.1), channel_id=1, source_target_pairs={{0,1},{1,0},{2,3},{3,2},{4,5},{5,4},{6,7},{7,6},{8,9},{9,8},{10,11... | collective-permute-start | bytes 11010056 | tf_op jit(solution)/shard_map/ppermute | solution.py:15
  1.4 29.8 %collective-permute-start.1 = (bf16[288,1792]{1,0:T(8,128)(2,1)}, bf16[288,1792]{1,0:T(8,128)(2,1)S(1)}, u32[]{:S(2)}, u32[]{:S(2)}) collective-permute-start(bf16[288,1792]{1,0:T(8,128)(2,1)} %param.21), channel_id=1, source_target_pairs={{0,0},{64,1},{2,2},{66,3},{4,4},{68,5},{6,6},{70,7},{8,8},{72,9},{... | collective-permute-start | bytes 3096584 | tf_op jit(solution)/shard_map/ppermute | solution.py:53
  14.6 14.9 %all-to-all-start = ((bf16[16,16,512]{2,1,0:T(8,128)(2,1)}), bf16[16,16,512]{2,1,0:T(8,128)(2,1)S(1)}, u32[]{:S(2)}, u32[]{:S(2)}) async-start(bf16[16,16,512]{2,1,0:T(8,128)(2,1)} %bitcast.28), calls=%async_computation | async-start | bytes 524288 | tf_op jit(solution)/shard_map/all_to_all | solution.py:20
  21.4 24.1 %collective-permute-start.8 = (bf16[288,1792]{1,0:T(8,128)(2,1)}, bf16[288,1792]{1,0:T(8,128)(2,1)S(1)}, u32[]{:S(2)}, u32[]{:S(2)}) collective-permute-start(bf16[288,1792]{1,0:T(8,128)(2,1)} %param.21), channel_id=1, source_target_pairs={{1,0},{65,1},{3,2},{67,3},{5,4},{69,5},{7,6},{71,7},{9,8},{73,9},{... | collective-permute-start | bytes 3096584 | tf_op jit(solution)/shard_map/ppermute | solution.py:53
  21.5 9.7 %collective-permute-start.2 = (bf16[2,512,128]{2,1,0:T(8,128)(2,1)S(1)}, bf16[2,512,128]{2,1,0:T(8,128)(2,1)S(1)}, u32[]{:S(2)}, u32[]{:S(2)}) collective-permute-start(bf16[2,512,128]{2,1,0:T(8,128)(2,1)S(1)} %copy-done.4), channel_id=1, source_target_pairs={{0,1},{1,0},{2,3},{3,2},{4,5},{5,4},{6,7},{7,6},{8,9},{9,8},{10,11... | collective-permute-start | bytes 786440 | tf_op jit(solution)/shard_map/ppermute | solution.py:15
  31.1 7.6 %collective-permute-start.7 = (bf16[4,3584]{1,0:T(4,128)(2,1)S(1)}, bf16[4,3584]{1,0:T(4,128)(2,1)S(1)}, u32[]{:S(2)}, u32[]{:S(2)}) collective-permute-start(bf16[4,3584]{1,0:T(4,128)(2,1)S(1)} %get-tuple-element.66), channel_id=1, source_target_pairs={{0,1},{1,0},{2,3},{3,2},{4,5},{5,4},{6,7},{7,6},{8,9},{9,8},{10,11... | collective-permute-start | bytes 86024 | tf_op jit(solution)/shard_map/ppermute | solution.py:15
  35.9 8.9 %collective-permute-start.4 = (bf16[32,3584]{1,0:T(8,128)(2,1)S(1)}, bf16[32,3584]{1,0:T(8,128)(2,1)S(1)}, u32[]{:S(2)}, u32[]{:S(2)}) collective-permute-start(bf16[32,3584]{1,0:T(8,128)(2,1)S(1)} %get-tuple-element.38), channel_id=1, source_target_pairs={{0,8},{1,3},{2,10},{3,5},{4,12},{5,7},{6,14},{7,1},{8,16},{9,11},{... | collective-permute-start | bytes 688136 | tf_op jit(solution)/shard_map/ppermute | solution.py:35
  36.2 8.6 %collective-permute-start.5 = (bf16[32,3584]{1,0:T(8,128)(2,1)S(1)}, bf16[32,3584]{1,0:T(8,128)(2,1)S(1)}, u32[]{:S(2)}, u32[]{:S(2)}) collective-permute-start(bf16[32,3584]{1,0:T(8,128)(2,1)S(1)} %get-tuple-element.39), channel_id=1, source_target_pairs={{0,16},{1,5},{2,18},{3,7},{4,20},{5,1},{6,22},{7,3},{8,24},{9,13},... | collective-permute-start | bytes 688136 | tf_op jit(solution)/shard_map/ppermute | solution.py:35
  37.5 7.9 %collective-permute-start.6 = (bf16[32,3584]{1,0:T(8,128)(2,1)S(1)}, bf16[32,3584]{1,0:T(8,128)(2,1)S(1)}, u32[]{:S(2)}, u32[]{:S(2)}) collective-permute-start(bf16[32,3584]{1,0:T(8,128)(2,1)S(1)} %get-tuple-element.40), channel_id=1, source_target_pairs={{0,24},{1,7},{2,26},{3,1},{4,28},{5,3},{6,30},{7,5},{8,0},{9,15},{... | collective-permute-start | bytes 688136 | tf_op jit(solution)/shard_map/ppermute | solution.py:35
  38.8 17.0 %collective-permute-start.15 = (bf16[288,1792]{1,0:T(8,128)(2,1)S(1)}, bf16[288,1792]{1,0:T(8,128)(2,1)S(1)}, u32[]{:S(2)}, u32[]{:S(2)}) collective-permute-start(bf16[288,1792]{1,0:T(8,128)(2,1)S(1)} %copy-done.6), channel_id=1, source_target_pairs={{32,0},{96,1},{34,2},{98,3},{36,4},{100,5},{38,6},{102,7},{40,8},{... | collective-permute-start | bytes 3096584 | tf_op jit(solution)/shard_map/ppermute | solution.py:53
  45.6 15.5 %collective-permute-start.10 = (bf16[32,3584]{1,0:T(8,128)(2,1)S(1)}, bf16[32,3584]{1,0:T(8,128)(2,1)S(1)}, u32[]{:S(2)}, u32[]{:S(2)}) collective-permute-start(bf16[32,3584]{1,0:T(8,128)(2,1)S(1)} %fusion.1), channel_id=1, source_target_pairs={{0,4},{1,17},{2,6},{3,19},{4,0},{5,21},{6,2},{7,23},{8,12},{9,25},... | collective-permute-start | bytes 688136 | tf_op jit(solution)/shard_map/ppermute | solution.py:35
  46.2 14.9 %collective-permute-start.11 = (bf16[32,3584]{1,0:T(8,128)(2,1)S(1)}, bf16[32,3584]{1,0:T(8,128)(2,1)S(1)}, u32[]{:S(2)}, u32[]{:S(2)}) collective-permute-start(bf16[32,3584]{1,0:T(8,128)(2,1)S(1)} %fusion.1), channel_id=1, source_target_pairs={{0,6},{1,25},{2,0},{3,27},{4,2},{5,29},{6,4},{7,31},{8,14},{9,1},{... | collective-permute-start | bytes 688136 | tf_op jit(solution)/shard_map/ppermute | solution.py:35
  47.8 13.3 %collective-permute-start.9 = (bf16[32,3584]{1,0:T(8,128)(2,1)S(1)}, bf16[32,3584]{1,0:T(8,128)(2,1)S(1)}, u32[]{:S(2)}, u32[]{:S(2)}) collective-permute-start(bf16[32,3584]{1,0:T(8,128)(2,1)S(1)} %fusion.1), channel_id=1, source_target_pairs={{0,2},{1,9},{2,4},{3,11},{4,6},{5,13},{6,0},{7,15},{8,10},{9,17},{... | collective-permute-start | bytes 688136 | tf_op jit(solution)/shard_map/ppermute | solution.py:35
  55.8 16.9 %collective-permute-start.16 = (bf16[288,1792]{1,0:T(8,128)(2,1)S(1)}, bf16[288,1792]{1,0:T(8,128)(2,1)S(1)}, u32[]{:S(2)}, u32[]{:S(2)}) collective-permute-start(bf16[288,1792]{1,0:T(8,128)(2,1)S(1)} %copy-done.6), channel_id=1, source_target_pairs={{33,0},{97,1},{35,2},{99,3},{37,4},{101,5},{39,6},{103,7},{41,8},{... | collective-permute-start | bytes 3096584 | tf_op jit(solution)/shard_map/ppermute | solution.py:53
  61.2 5.2 %collective-permute-start.12 = (bf16[32,3584]{1,0:T(8,128)(2,1)S(1)}, bf16[32,3584]{1,0:T(8,128)(2,1)S(1)}, u32[]{:S(2)}, u32[]{:S(2)}) collective-permute-start(bf16[32,3584]{1,0:T(8,128)(2,1)S(1)} %add_convert_fusion.1.refs_0_), channel_id=1, source_target_pairs={{0,24},{1,7},{2,26},{3,1},{4,28},{5,3},{6,30},{7,5},{8,0},{9,15},{... | collective-permute-start | bytes 688136 | tf_op jit(solution)/shard_map/ppermute | solution.py:35
  62.2 6.6 %collective-permute-start.13 = (bf16[32,3584]{1,0:T(8,128)(2,1)S(1)}, bf16[32,3584]{1,0:T(8,128)(2,1)S(1)}, u32[]{:S(2)}, u32[]{:S(2)}) collective-permute-start(bf16[32,3584]{1,0:T(8,128)(2,1)S(1)} %add_convert_fusion.1.refs_0_), channel_id=1, source_target_pairs={{0,16},{1,5},{2,18},{3,7},{4,20},{5,1},{6,22},{7,3},{8,24},{9,13},... | collective-permute-start | bytes 688136 | tf_op jit(solution)/shard_map/ppermute | solution.py:35
  63.4 7.8 %collective-permute-start.14 = (bf16[32,3584]{1,0:T(8,128)(2,1)S(1)}, bf16[32,3584]{1,0:T(8,128)(2,1)S(1)}, u32[]{:S(2)}, u32[]{:S(2)}) collective-permute-start(bf16[32,3584]{1,0:T(8,128)(2,1)S(1)} %add_convert_fusion.1.refs_0_), channel_id=1, source_target_pairs={{0,8},{1,3},{2,10},{3,5},{4,12},{5,7},{6,14},{7,1},{8,16},{9,11},{... | collective-permute-start | bytes 688136 | tf_op jit(solution)/shard_map/ppermute | solution.py:35
  81.1 8.9 %collective-permute-start.22 = (bf16[32,3584]{1,0:T(8,128)(2,1)S(1)}, bf16[32,3584]{1,0:T(8,128)(2,1)S(1)}, u32[]{:S(2)}, u32[]{:S(2)}) collective-permute-start(bf16[32,3584]{1,0:T(8,128)(2,1)S(1)} %get-tuple-element.56), channel_id=1, source_target_pairs={{0,8},{1,3},{2,10},{3,5},{4,12},{5,7},{6,14},{7,1},{8,16},{9,11},{... | collective-permute-start | bytes 688136 | tf_op jit(solution)/shard_map/ppermute | solution.py:35
  81.4 8.5 %collective-permute-start.23 = (bf16[32,3584]{1,0:T(8,128)(2,1)S(1)}, bf16[32,3584]{1,0:T(8,128)(2,1)S(1)}, u32[]{:S(2)}, u32[]{:S(2)}) collective-permute-start(bf16[32,3584]{1,0:T(8,128)(2,1)S(1)} %get-tuple-element.57), channel_id=1, source_target_pairs={{0,16},{1,5},{2,18},{3,7},{4,20},{5,1},{6,22},{7,3},{8,24},{9,13},... | collective-permute-start | bytes 688136 | tf_op jit(solution)/shard_map/ppermute | solution.py:35
  83.2 7.3 %collective-permute-start.24 = (bf16[32,3584]{1,0:T(8,128)(2,1)S(1)}, bf16[32,3584]{1,0:T(8,128)(2,1)S(1)}, u32[]{:S(2)}, u32[]{:S(2)}) collective-permute-start(bf16[32,3584]{1,0:T(8,128)(2,1)S(1)} %get-tuple-element.58), channel_id=1, source_target_pairs={{0,24},{1,7},{2,26},{3,1},{4,28},{5,3},{6,30},{7,5},{8,0},{9,15},{... | collective-permute-start | bytes 688136 | tf_op jit(solution)/shard_map/ppermute | solution.py:35
  90.7 4.6 %collective-permute-start.25 = (bf16[8,3584]{1,0:T(8,128)(2,1)S(1)}, bf16[8,3584]{1,0:T(8,128)(2,1)S(1)}, u32[]{:S(2)}, u32[]{:S(2)}) collective-permute-start(bf16[8,3584]{1,0:T(8,128)(2,1)S(1)} %get-tuple-element.59), channel_id=1, source_target_pairs={{0,2},{1,9},{2,4},{3,11},{4,6},{5,13},{6,0},{7,15},{8,10},{9,17},{... | collective-permute-start | bytes 172040 | tf_op jit(solution)/shard_map/ppermute | solution.py:35
  91.4 4.5 %collective-permute-start.26 = (bf16[8,3584]{1,0:T(8,128)(2,1)S(1)}, bf16[8,3584]{1,0:T(8,128)(2,1)S(1)}, u32[]{:S(2)}, u32[]{:S(2)}) collective-permute-start(bf16[8,3584]{1,0:T(8,128)(2,1)S(1)} %get-tuple-element.61), channel_id=1, source_target_pairs={{0,4},{1,17},{2,6},{3,19},{4,0},{5,21},{6,2},{7,23},{8,12},{9,25},... | collective-permute-start | bytes 172040 | tf_op jit(solution)/shard_map/ppermute | solution.py:35
  93.3 3.3 %collective-permute-start.27 = (bf16[8,3584]{1,0:T(8,128)(2,1)S(1)}, bf16[8,3584]{1,0:T(8,128)(2,1)S(1)}, u32[]{:S(2)}, u32[]{:S(2)}) collective-permute-start(bf16[8,3584]{1,0:T(8,128)(2,1)S(1)} %get-tuple-element.60), channel_id=1, source_target_pairs={{0,6},{1,25},{2,0},{3,27},{4,2},{5,29},{6,4},{7,31},{8,14},{9,1},{... | collective-permute-start | bytes 172040 | tf_op jit(solution)/shard_map/ppermute | solution.py:35
  96.8 3.3 %collective-permute-start.28 = (bf16[4,3584]{1,0:T(4,128)(2,1)S(1)}, bf16[4,3584]{1,0:T(4,128)(2,1)S(1)}, u32[]{:S(2)}, u32[]{:S(2)}) collective-permute-start(bf16[4,3584]{1,0:T(4,128)(2,1)S(1)} %get-tuple-element.64), channel_id=1, source_target_pairs={{0,1},{1,0},{2,3},{3,2},{4,5},{5,4},{6,7},{7,6},{8,9},{9,8},{10,11... | collective-permute-start | bytes 86024 | tf_op jit(solution)/shard_map/ppermute | solution.py:15
  (13 other events, 186.3 us)

commit v11 on v10

--- a/solution.py
+++ b/solution.py
@@ -105,13 +105,11 @@
             latent = latent / jnp.sum(raised, axis=1, keepdims=True)
             return jnp.where(slot < counts_ref[0], latent, 0.0).astype(jnp.bfloat16)
 
-        copies[0].start()
-        copies[1].start()
+        for copy in copies:
+            copy.start()
         latents = []
         scores = score(0)
         for slot in range(slots):
-            if slot + 2 < slots:
-                copies[slot + 2].start()
             following = score(slot + 1) if slot + 1 < slots else None
             latents.append(gather(slot, scores))
             scores = following
@@ -353,6 +351,7 @@
         jnp.concatenate([input_mine, input_other], axis=0),
     ).astype(jnp.float32)
 
+    query, spot = lax.optimization_barrier((query, spot))
     latent = attend(query, cache, lengths, counts, latent_width, chips)
     arrived = between_chips(latent, width)
     arrived_other = core_swap(arrived, width)
@@ -372,12 +371,11 @@
     summed, pieces[1] = lax.optimization_barrier((summed, pieces[1]))
     residual_line = total(turn([summed] * side, 1, side, 1)).astype(jnp.bfloat16)
     residual_mine = turn([residual_line] * side, 0, side, -1)
-    residual_mine, pieces[2], pieces[3] = lax.optimization_barrier(
-        (residual_mine, pieces[2], pieces[3])
-    )
+    residual_mine = lax.optimization_barrier(residual_mine)
     residual_other = [core_swap(part, width) for part in residual_mine]
     sums = gated(residual_mine, norm_gain, gate_weight, up_weight, spot, None)
     inner = gated(residual_other, norm_gain, gate_weight, up_weight, spot, sums)
+    inner, pieces[3] = lax.optimization_barrier((inner, pieces[3]))
     inner_other = core_swap(inner, width)
 
     feed_parts = feed_forward(inner, inner_other, pieces, spot, side)

time: 102 us -> 99.7 us (0.977)
    ppermute x4, waiting for transfers between devices: 9.41 us -> 8.06 us  [down_piece(): return lax.ppermute(down_weight, ('dp', 'tp'), pairs)]
    ppermute x15, starting transfers between devices: 15.8 us -> 14.4 us  [turn(): out.append(lax.ppermute(parts[k], 'tp', pairs))]
  transfers between devices with their start and end apart: 30 -> 30, of which waited for: 15 -> 15; matrix products, arithmetic and copies ran while one was open for 1% -> 1% of each run, Pallas kernels for 15% -> 18%
where the time goes in v11:
time: 99.7 us; the launch traced here: 99.4 us
  starting transfers between devices  43.1 us (43%)
  waiting for transfers between devices  34.4 us (35%)
  Pallas kernels  19.2 us (19%)
  other arithmetic  1.31 us (1%)
  between operations  1 us (1%)
    ppermute x15, waiting for transfers between devices, turn(): out.append(lax.ppermute(parts[k], 'tp', pairs))  17.8 us
    ppermute x15, starting transfers between devices, turn(): out.append(lax.ppermute(parts[k], 'tp', pairs))  14.4 us
    ppermute x4, starting transfers between devices, down_piece(): return lax.ppermute(down_weight, ('dp', 'tp'), pairs)  13.3 us
    pallas_call x1, Pallas kernels, attend(): pl.pallas_call(kernel, in_specs=[in_smem, in_smem, in_vmem, in_hbm], out_...  8.65 us
    ppermute x10, starting transfers between devices, core_swap(): return lax.ppermute(x, 'tp', [(i, i ^ 1) for i in range(width)])  8.59 us
    ppermute x4, waiting for transfers between devices, down_piece(): return lax.ppermute(down_weight, ('dp', 'tp'), pairs)  8.06 us
    all_to_all x1, starting transfers between devices, between_chips(): return lax.all_to_all(x, 'tp', 0, 0, tiled=True, axis_index_groups=groups)  6.77 us
    all_to_all x1, waiting for transfers between devices, between_chips(): return lax.all_to_all(x, 'tp', 0, 0, tiled=True, axis_index_groups=groups)  5.23 us
  transfers between devices with their start and end apart: 30, of which 15 were waited for; matrix products, arithmetic and copies ran while one was open for 1% of the time, Pallas kernels for 18%

profile of v11, /device:TPU:1, one launch (start us, length us, event | category | flops | bytes accessed | tf_op | source)
XLA Modules:
  0.0 99.4 jit_solution(14412155978200179435)
XLA Ops:
  1.4 3.5 %collective-permute-start.1 = (bf16[288,1792]{1,0:T(8,128)(2,1)}, bf16[288,1792]{1,0:T(8,128)(2,1)S(1)}, u32[]{:S(2)}, u32[]{:S(2)}) collective-permute-start(bf16[288,1792]{1,0:T(8,128)(2,1)} %param.21), channel_id=1, source_target_pairs={{0,0},{64,1},{2,2},{66,3},{4,4},{68,5},{6,6},{70,7},{8,8},{72,9},{... | collective-permute-start | bytes 3096584 | tf_op jit(solution)/shard_map/ppermute | solution.py:53
  5.7 8.6 %shard_map.109 = bf16[256,512]{1,0:T(8,128)(2,1)} custom-call(s32[4]{0:T(128)} %lengths_ref.1, s32[1]{0:T(128)} %copy.12.counts_ref, bf16[4,64,576]{2,1,0:T(8,128)(2,1)} %q_ref, bf16[4,576,2048]{2,1,0:T(8,128)(2,1)} %bitcast.27), custom_call_target="tpu_custom_call" | custom-call | flops 1140850688 | bytes 9437184 | tf_op jit(solution)/shard_map/pallas_call | solution.py:122
  14.4 6.8 %all-to-all-start = ((bf16[16,16,512]{2,1,0:T(8,128)(2,1)}), bf16[16,16,512]{2,1,0:T(8,128)(2,1)S(1)}, u32[]{:S(2)}, u32[]{:S(2)}) async-start(bf16[16,16,512]{2,1,0:T(8,128)(2,1)} %bitcast.28), calls=%async_computation | async-start | bytes 524288 | tf_op jit(solution)/shard_map/all_to_all | solution.py:20
  21.3 2.6 %collective-permute-start.2 = (bf16[2,512,128]{2,1,0:T(8,128)(2,1)S(1)}, bf16[2,512,128]{2,1,0:T(8,128)(2,1)S(1)}, u32[]{:S(2)}, u32[]{:S(2)}) collective-permute-start(bf16[2,512,128]{2,1,0:T(8,128)(2,1)S(1)} %copy-done.4), channel_id=1, source_target_pairs={{0,1},{1,0},{2,3},{3,2},{4,5},{5,4},{6,7},{7,6},{8,9},{9,8},{10,11... | collective-permute-start | bytes 786440 | tf_op jit(solution)/shard_map/ppermute | solution.py:15
  24.0 5.2 %all-to-all-done = bf16[16,16,512]{2,1,0:T(8,128)(2,1)S(1)} async-done(((bf16[16,16,512]{2,1,0:T(8,128)(2,1)}), bf16[16,16,512]{2,1,0:T(8,128)(2,1)S(1)}, u32[]{:S(2)}, u32[]{:S(2)}) %all-to-all-start) | async-done | bytes 262176 | tf_op jit(solution)/shard_map/all_to_all | solution.py:20
  29.3 1.5 %collective-permute-done = bf16[16,16,512]{2,1,0:T(8,128)(2,1)S(1)} collective-permute-done((bf16[16,16,512]{2,1,0:T(8,128)(2,1)S(1)}, bf16[16,16,512]{2,1,0:T(8,128)(2,1)S(1)}, u32[]{:S(2)}, u32[]{:S(2)}) %collective-permute-start) | collective-permute-done | bytes 262176 | tf_op jit(solution)/shard_map/ppermute | solution.py:15
  30.9 1.6 %shard_map.110.value_ref = bf16[128,512]{1,0:T(8,128)(2,1)S(1)} custom-call(s32[4]{0:T(128)S(1)} %pad_add_fusion.spot_ref, bf16[256,512]{1,0:T(8,128)(2,1)S(1)} %bitcast.23, bf16[256,512]{1,0:T(8,128)(2,1)S(1)} %bitcast.26, bf16[2,512,128]{2,1,0:T(8,128)(2,1)S(1)} %copy-done.4, bf16[2,512,128]{2,1,0:T(8,128)(2,1)S(1)} %collective-permute-done.2.vo_ref), custom_call_target="tpu_custom_call" | custom-call | flops 1610612736 | bytes 524288 | tf_op jit(solution)/shard_map/pallas_call | solution.py:167
  32.6 3.0 %shard_map.111 = (bf16[32,3584]{1,0:T(8,128)(2,1)S(1)}, bf16[32,3584]{1,0:T(8,128)(2,1)S(1)}, bf16[32,3584]{1,0:T(8,128)(2,1)S(1)}, bf16[32,3584]{1,0:T(8,128)(2,1)S(1)}) custom-call(s32[4]{0:T(128)S(1)} %pad_add_fusion.spot_ref, bf16[128,512]{1,0:T(8,128)(2,1)S(1)} %shard_map.110.value_ref, bf16[256,7168]{1,0:T(8,128)(2,1)S(1)} %copy-done.2, ...), custom_call_target="tpu_custom_call" | custom-call | flops 469762048 | bytes 3670016 | tf_op jit(solution)/shard_map/pallas_call | solution.py:203
  38.5 4.5 %collective-permute-start.19 = (bf16[288,1792]{1,0:T(8,128)(2,1)S(1)}, bf16[288,1792]{1,0:T(8,128)(2,1)S(1)}, u32[]{:S(2)}, u32[]{:S(2)}) collective-permute-start(bf16[288,1792]{1,0:T(8,128)(2,1)S(1)} %copy-done.6), channel_id=1, source_target_pairs={{32,0},{96,1},{34,2},{98,3},{36,4},{100,5},{38,6},{102,7},{40,8},{... | collective-permute-start | bytes 3096584 | tf_op jit(solution)/shard_map/ppermute | solution.py:53
  43.0 1.5 %collective-permute-done.4 = bf16[32,3584]{1,0:T(8,128)(2,1)S(1)} collective-permute-done((bf16[32,3584]{1,0:T(8,128)(2,1)S(1)}, bf16[32,3584]{1,0:T(8,128)(2,1)S(1)}, u32[]{:S(2)}, u32[]{:S(2)}) %collective-permute-start.4) | collective-permute-done | bytes 229408 | tf_op jit(solution)/shard_map/ppermute | solution.py:35
  45.9 1.6 %collective-permute-start.11 = (bf16[32,3584]{1,0:T(8,128)(2,1)S(1)}, bf16[32,3584]{1,0:T(8,128)(2,1)S(1)}, u32[]{:S(2)}, u32[]{:S(2)}) collective-permute-start(bf16[32,3584]{1,0:T(8,128)(2,1)S(1)} %fusion.1), channel_id=1, source_target_pairs={{0,6},{1,25},{2,0},{3,27},{4,2},{5,29},{6,4},{7,31},{8,14},{9,1},{... | collective-permute-start | bytes 688136 | tf_op jit(solution)/shard_map/ppermute | solution.py:35
  47.5 8.1 %collective-permute-done.19.c_ref = bf16[288,1792]{1,0:T(8,128)(2,1)S(1)} collective-permute-done((bf16[288,1792]{1,0:T(8,128)(2,1)S(1)}, bf16[288,1792]{1,0:T(8,128)(2,1)S(1)}, u32[]{:S(2)}, u32[]{:S(2)}) %collective-permute-start.19) | collective-permute-done | bytes 1032224 | tf_op jit(solution)/shard_map/ppermute | solution.py:53
  55.6 5.3 %collective-permute-start.20 = (bf16[288,1792]{1,0:T(8,128)(2,1)S(1)}, bf16[288,1792]{1,0:T(8,128)(2,1)S(1)}, u32[]{:S(2)}, u32[]{:S(2)}) collective-permute-start(bf16[288,1792]{1,0:T(8,128)(2,1)S(1)} %copy-done.6), channel_id=1, source_target_pairs={{33,0},{97,1},{35,2},{99,3},{37,4},{101,5},{39,6},{103,7},{41,8},{... | collective-permute-start | bytes 3096584 | tf_op jit(solution)/shard_map/ppermute | solution.py:53
  63.2 3.1 %collective-permute-done.12.refs_1_ = bf16[32,3584]{1,0:T(8,128)(2,1)S(1)} collective-permute-done((bf16[32,3584]{1,0:T(8,128)(2,1)S(1)}, bf16[32,3584]{1,0:T(8,128)(2,1)S(1)}, u32[]{:S(2)}, u32[]{:S(2)}) %collective-permute-start.12) | collective-permute-done | bytes 229408 | tf_op jit(solution)/shard_map/ppermute | solution.py:35
  66.2 2.3 %collective-permute-done.13.refs_2_ = bf16[32,3584]{1,0:T(8,128)(2,1)S(1)} collective-permute-done((bf16[32,3584]{1,0:T(8,128)(2,1)S(1)}, bf16[32,3584]{1,0:T(8,128)(2,1)S(1)}, u32[]{:S(2)}, u32[]{:S(2)}) %collective-permute-start.13) | collective-permute-done | bytes 229408 | tf_op jit(solution)/shard_map/ppermute | solution.py:35
  68.6 2.5 %collective-permute-done.14.refs_3_ = bf16[32,3584]{1,0:T(8,128)(2,1)S(1)} collective-permute-done((bf16[32,3584]{1,0:T(8,128)(2,1)S(1)}, bf16[32,3584]{1,0:T(8,128)(2,1)S(1)}, u32[]{:S(2)}, u32[]{:S(2)}) %collective-permute-start.14) | collective-permute-done | bytes 229408 | tf_op jit(solution)/shard_map/ppermute | solution.py:35
  72.0 1.9 %shard_map.112 = (f32[128,576]{1,0:T(8,128)S(1)}, f32[128,128]{1,0:T(8,128)S(1)}) custom-call(s32[4]{0:T(128)S(1)} %pad_add_fusion.spot_ref, bf16[32,3584]{1,0:T(8,128)(2,1)S(1)} %add_convert_fusion.1.refs_0_, bf16[32,3584]{1,0:T(8,128)(2,1)S(1)} %collective-permute-done.12.refs_1_, bf16[32,3584]{1,0:T(8,128)(2,1)S(1)} %collective-permute-done.13.refs_2_, ...), custom_call_target="tpu_custom_call" | custom-call | flops 528482304 | bytes 4128768 | tf_op jit(solution)/shard_map/pallas_call | solution.py:260
  74.0 2.3 %shard_map.113.inner_ref = bf16[128,288]{1,0:T(8,128)(2,1)S(1)} custom-call(s32[4]{0:T(128)S(1)} %pad_add_fusion.spot_ref, bf16[32,3584]{1,0:T(8,128)(2,1)S(1)} %collective-permute-done.15.refs_0_, bf16[32,3584]{1,0:T(8,128)(2,1)S(1)} %collective-permute-done.16.refs_1_, bf16[32,3584]{1,0:T(8,128)(2,1)S(1)} %collective-permute-done.17.refs_2_, ...), custom_call_target="tpu_custom_call" | custom-call | flops 528482304 | bytes 4128768 | tf_op jit(solution)/shard_map/pallas_call | solution.py:260
  77.7 1.8 %shard_map.114 = (bf16[32,3584]{1,0:T(8,128)(2,1)S(1)}, bf16[32,3584]{1,0:T(8,128)(2,1)S(1)}, bf16[32,3584]{1,0:T(8,128)(2,1)S(1)}, bf16[32,3584]{1,0:T(8,128)(2,1)S(1)}) custom-call(s32[4]{0:T(128)S(1)} %pad_add_fusion.spot_ref, bf16[128,288]{1,0:T(8,128)(2,1)S(1)} %shard_map.113.inner_ref, bf16[128,288]{1,0:T(8,128)(2,1)S(1)} %collective-permute-done.21.other_ref, ...), custom_call_target="tpu_custom_call" | custom-call | flops 528482304 | bytes 4128768 | tf_op jit(solution)/shard_map/pallas_call | solution.py:299
  79.8 1.8 %collective-permute-start.23 = (bf16[32,3584]{1,0:T(8,128)(2,1)S(1)}, bf16[32,3584]{1,0:T(8,128)(2,1)S(1)}, u32[]{:S(2)}, u32[]{:S(2)}) collective-permute-start(bf16[32,3584]{1,0:T(8,128)(2,1)S(1)} %get-tuple-element.61), channel_id=1, source_target_pairs={{0,16},{1,5},{2,18},{3,7},{4,20},{5,1},{6,22},{7,3},{8,24},{9,13},... | collective-permute-start | bytes 688136 | tf_op jit(solution)/shard_map/ppermute | solution.py:35
  82.9 5.5 %collective-permute-done.22 = bf16[32,3584]{1,0:T(8,128)(2,1)S(1)} collective-permute-done((bf16[32,3584]{1,0:T(8,128)(2,1)S(1)}, bf16[32,3584]{1,0:T(8,128)(2,1)S(1)}, u32[]{:S(2)}, u32[]{:S(2)}) %collective-permute-start.22) | collective-permute-done | bytes 229408 | tf_op jit(solution)/shard_map/ppermute | solution.py:35
  89.7 1.4 %collective-permute-start.26 = (bf16[8,3584]{1,0:T(8,128)(2,1)S(1)}, bf16[8,3584]{1,0:T(8,128)(2,1)S(1)}, u32[]{:S(2)}, u32[]{:S(2)}) collective-permute-start(bf16[8,3584]{1,0:T(8,128)(2,1)S(1)} %get-tuple-element.65), channel_id=1, source_target_pairs={{0,4},{1,17},{2,6},{3,19},{4,0},{5,21},{6,2},{7,23},{8,12},{9,25},... | collective-permute-start | bytes 172040 | tf_op jit(solution)/shard_map/ppermute | solution.py:35
  91.1 2.0 %collective-permute-start.27 = (bf16[8,3584]{1,0:T(8,128)(2,1)S(1)}, bf16[8,3584]{1,0:T(8,128)(2,1)S(1)}, u32[]{:S(2)}, u32[]{:S(2)}) collective-permute-start(bf16[8,3584]{1,0:T(8,128)(2,1)S(1)} %get-tuple-element.64), channel_id=1, source_target_pairs={{0,6},{1,25},{2,0},{3,27},{4,2},{5,29},{6,4},{7,31},{8,14},{9,1},{... | collective-permute-start | bytes 172040 | tf_op jit(solution)/shard_map/ppermute | solution.py:35
  94.8 3.0 %collective-permute-start.28 = (bf16[4,3584]{1,0:T(4,128)(2,1)S(1)}, bf16[4,3584]{1,0:T(4,128)(2,1)S(1)}, u32[]{:S(2)}, u32[]{:S(2)}) collective-permute-start(bf16[4,3584]{1,0:T(4,128)(2,1)S(1)} %get-tuple-element.68), channel_id=1, source_target_pairs={{0,1},{1,0},{2,3},{3,2},{4,5},{5,4},{6,7},{7,6},{8,9},{9,8},{10,11... | collective-permute-start | bytes 86024 | tf_op jit(solution)/shard_map/ppermute | solution.py:15
  (72 shorter events, 17.1 us)
Async XLA Ops:
  0.0 32.6 %collective-permute-start.3 = (bf16[256,7168]{1,0:T(8,128)(2,1)}, bf16[256,7168]{1,0:T(8,128)(2,1)}, u32[]{:S(2)}, u32[]{:S(2)}) collective-permute-start(bf16[256,7168]{1,0:T(8,128)(2,1)} %om_ref.1), channel_id=1, source_target_pairs={{0,1},{1,0},{2,3},{3,2},{4,5},{5,4},{6,7},{7,6},{8,9},{9,8},{10,11... | collective-permute-start | bytes 11010056 | tf_op jit(solution)/shard_map/ppermute | solution.py:15
  1.4 29.5 %collective-permute-start.1 = (bf16[288,1792]{1,0:T(8,128)(2,1)}, bf16[288,1792]{1,0:T(8,128)(2,1)S(1)}, u32[]{:S(2)}, u32[]{:S(2)}) collective-permute-start(bf16[288,1792]{1,0:T(8,128)(2,1)} %param.21), channel_id=1, source_target_pairs={{0,0},{64,1},{2,2},{66,3},{4,4},{68,5},{6,6},{70,7},{8,8},{72,9},{... | collective-permute-start | bytes 3096584 | tf_op jit(solution)/shard_map/ppermute | solution.py:53
  14.4 14.9 %all-to-all-start = ((bf16[16,16,512]{2,1,0:T(8,128)(2,1)}), bf16[16,16,512]{2,1,0:T(8,128)(2,1)S(1)}, u32[]{:S(2)}, u32[]{:S(2)}) async-start(bf16[16,16,512]{2,1,0:T(8,128)(2,1)} %bitcast.28), calls=%async_computation | async-start | bytes 524288 | tf_op jit(solution)/shard_map/all_to_all | solution.py:20
  21.2 24.1 %collective-permute-start.8 = (bf16[288,1792]{1,0:T(8,128)(2,1)}, bf16[288,1792]{1,0:T(8,128)(2,1)S(1)}, u32[]{:S(2)}, u32[]{:S(2)}) collective-permute-start(bf16[288,1792]{1,0:T(8,128)(2,1)} %param.21), channel_id=1, source_target_pairs={{1,0},{65,1},{3,2},{67,3},{5,4},{69,5},{7,6},{71,7},{9,8},{73,9},{... | collective-permute-start | bytes 3096584 | tf_op jit(solution)/shard_map/ppermute | solution.py:53
  21.3 9.6 %collective-permute-start.2 = (bf16[2,512,128]{2,1,0:T(8,128)(2,1)S(1)}, bf16[2,512,128]{2,1,0:T(8,128)(2,1)S(1)}, u32[]{:S(2)}, u32[]{:S(2)}) collective-permute-start(bf16[2,512,128]{2,1,0:T(8,128)(2,1)S(1)} %copy-done.4), channel_id=1, source_target_pairs={{0,1},{1,0},{2,3},{3,2},{4,5},{5,4},{6,7},{7,6},{8,9},{9,8},{10,11... | collective-permute-start | bytes 786440 | tf_op jit(solution)/shard_map/ppermute | solution.py:15
  30.8 7.6 %collective-permute-start.7 = (bf16[4,3584]{1,0:T(4,128)(2,1)S(1)}, bf16[4,3584]{1,0:T(4,128)(2,1)S(1)}, u32[]{:S(2)}, u32[]{:S(2)}) collective-permute-start(bf16[4,3584]{1,0:T(4,128)(2,1)S(1)} %get-tuple-element.70), channel_id=1, source_target_pairs={{0,1},{1,0},{2,3},{3,2},{4,5},{5,4},{6,7},{7,6},{8,9},{9,8},{10,11... | collective-permute-start | bytes 86024 | tf_op jit(solution)/shard_map/ppermute | solution.py:15
  35.6 8.9 %collective-permute-start.4 = (bf16[32,3584]{1,0:T(8,128)(2,1)S(1)}, bf16[32,3584]{1,0:T(8,128)(2,1)S(1)}, u32[]{:S(2)}, u32[]{:S(2)}) collective-permute-start(bf16[32,3584]{1,0:T(8,128)(2,1)S(1)} %get-tuple-element.42), channel_id=1, source_target_pairs={{0,8},{1,3},{2,10},{3,5},{4,12},{5,7},{6,14},{7,1},{8,16},{9,11},{... | collective-permute-start | bytes 688136 | tf_op jit(solution)/shard_map/ppermute | solution.py:35
  35.9 8.6 %collective-permute-start.5 = (bf16[32,3584]{1,0:T(8,128)(2,1)S(1)}, bf16[32,3584]{1,0:T(8,128)(2,1)S(1)}, u32[]{:S(2)}, u32[]{:S(2)}) collective-permute-start(bf16[32,3584]{1,0:T(8,128)(2,1)S(1)} %get-tuple-element.43), channel_id=1, source_target_pairs={{0,16},{1,5},{2,18},{3,7},{4,20},{5,1},{6,22},{7,3},{8,24},{9,13},... | collective-permute-start | bytes 688136 | tf_op jit(solution)/shard_map/ppermute | solution.py:35
  37.3 7.8 %collective-permute-start.6 = (bf16[32,3584]{1,0:T(8,128)(2,1)S(1)}, bf16[32,3584]{1,0:T(8,128)(2,1)S(1)}, u32[]{:S(2)}, u32[]{:S(2)}) collective-permute-start(bf16[32,3584]{1,0:T(8,128)(2,1)S(1)} %get-tuple-element.44), channel_id=1, source_target_pairs={{0,24},{1,7},{2,26},{3,1},{4,28},{5,3},{6,30},{7,5},{8,0},{9,15},{... | collective-permute-start | bytes 688136 | tf_op jit(solution)/shard_map/ppermute | solution.py:35
  38.5 17.1 %collective-permute-start.19 = (bf16[288,1792]{1,0:T(8,128)(2,1)S(1)}, bf16[288,1792]{1,0:T(8,128)(2,1)S(1)}, u32[]{:S(2)}, u32[]{:S(2)}) collective-permute-start(bf16[288,1792]{1,0:T(8,128)(2,1)S(1)} %copy-done.6), channel_id=1, source_target_pairs={{32,0},{96,1},{34,2},{98,3},{36,4},{100,5},{38,6},{102,7},{40,8},{... | collective-permute-start | bytes 3096584 | tf_op jit(solution)/shard_map/ppermute | solution.py:53
  45.3 15.6 %collective-permute-start.10 = (bf16[32,3584]{1,0:T(8,128)(2,1)S(1)}, bf16[32,3584]{1,0:T(8,128)(2,1)S(1)}, u32[]{:S(2)}, u32[]{:S(2)}) collective-permute-start(bf16[32,3584]{1,0:T(8,128)(2,1)S(1)} %fusion.1), channel_id=1, source_target_pairs={{0,4},{1,17},{2,6},{3,19},{4,0},{5,21},{6,2},{7,23},{8,12},{9,25},... | collective-permute-start | bytes 688136 | tf_op jit(solution)/shard_map/ppermute | solution.py:35
  45.9 14.9 %collective-permute-start.11 = (bf16[32,3584]{1,0:T(8,128)(2,1)S(1)}, bf16[32,3584]{1,0:T(8,128)(2,1)S(1)}, u32[]{:S(2)}, u32[]{:S(2)}) collective-permute-start(bf16[32,3584]{1,0:T(8,128)(2,1)S(1)} %fusion.1), channel_id=1, source_target_pairs={{0,6},{1,25},{2,0},{3,27},{4,2},{5,29},{6,4},{7,31},{8,14},{9,1},{... | collective-permute-start | bytes 688136 | tf_op jit(solution)/shard_map/ppermute | solution.py:35
  47.5 13.4 %collective-permute-start.9 = (bf16[32,3584]{1,0:T(8,128)(2,1)S(1)}, bf16[32,3584]{1,0:T(8,128)(2,1)S(1)}, u32[]{:S(2)}, u32[]{:S(2)}) collective-permute-start(bf16[32,3584]{1,0:T(8,128)(2,1)S(1)} %fusion.1), channel_id=1, source_target_pairs={{0,2},{1,9},{2,4},{3,11},{4,6},{5,13},{6,0},{7,15},{8,10},{9,17},{... | collective-permute-start | bytes 688136 | tf_op jit(solution)/shard_map/ppermute | solution.py:35
  55.6 20.7 %collective-permute-start.20 = (bf16[288,1792]{1,0:T(8,128)(2,1)S(1)}, bf16[288,1792]{1,0:T(8,128)(2,1)S(1)}, u32[]{:S(2)}, u32[]{:S(2)}) collective-permute-start(bf16[288,1792]{1,0:T(8,128)(2,1)S(1)} %copy-done.6), channel_id=1, source_target_pairs={{33,0},{97,1},{35,2},{99,3},{37,4},{101,5},{39,6},{103,7},{41,8},{... | collective-permute-start | bytes 3096584 | tf_op jit(solution)/shard_map/ppermute | solution.py:53
  61.0 5.2 %collective-permute-start.12 = (bf16[32,3584]{1,0:T(8,128)(2,1)S(1)}, bf16[32,3584]{1,0:T(8,128)(2,1)S(1)}, u32[]{:S(2)}, u32[]{:S(2)}) collective-permute-start(bf16[32,3584]{1,0:T(8,128)(2,1)S(1)} %add_convert_fusion.1.refs_0_), channel_id=1, source_target_pairs={{0,24},{1,7},{2,26},{3,1},{4,28},{5,3},{6,30},{7,5},{8,0},{9,15},{... | collective-permute-start | bytes 688136 | tf_op jit(solution)/shard_map/ppermute | solution.py:35
  62.0 6.6 %collective-permute-start.13 = (bf16[32,3584]{1,0:T(8,128)(2,1)S(1)}, bf16[32,3584]{1,0:T(8,128)(2,1)S(1)}, u32[]{:S(2)}, u32[]{:S(2)}) collective-permute-start(bf16[32,3584]{1,0:T(8,128)(2,1)S(1)} %add_convert_fusion.1.refs_0_), channel_id=1, source_target_pairs={{0,16},{1,5},{2,18},{3,7},{4,20},{5,1},{6,22},{7,3},{8,24},{9,13},... | collective-permute-start | bytes 688136 | tf_op jit(solution)/shard_map/ppermute | solution.py:35
  63.2 7.9 %collective-permute-start.14 = (bf16[32,3584]{1,0:T(8,128)(2,1)S(1)}, bf16[32,3584]{1,0:T(8,128)(2,1)S(1)}, u32[]{:S(2)}, u32[]{:S(2)}) collective-permute-start(bf16[32,3584]{1,0:T(8,128)(2,1)S(1)} %add_convert_fusion.1.refs_0_), channel_id=1, source_target_pairs={{0,8},{1,3},{2,10},{3,5},{4,12},{5,7},{6,14},{7,1},{8,16},{9,11},{... | collective-permute-start | bytes 688136 | tf_op jit(solution)/shard_map/ppermute | solution.py:35
  79.5 8.9 %collective-permute-start.22 = (bf16[32,3584]{1,0:T(8,128)(2,1)S(1)}, bf16[32,3584]{1,0:T(8,128)(2,1)S(1)}, u32[]{:S(2)}, u32[]{:S(2)}) collective-permute-start(bf16[32,3584]{1,0:T(8,128)(2,1)S(1)} %get-tuple-element.60), channel_id=1, source_target_pairs={{0,8},{1,3},{2,10},{3,5},{4,12},{5,7},{6,14},{7,1},{8,16},{9,11},{... | collective-permute-start | bytes 688136 | tf_op jit(solution)/shard_map/ppermute | solution.py:35
  79.8 8.7 %collective-permute-start.23 = (bf16[32,3584]{1,0:T(8,128)(2,1)S(1)}, bf16[32,3584]{1,0:T(8,128)(2,1)S(1)}, u32[]{:S(2)}, u32[]{:S(2)}) collective-permute-start(bf16[32,3584]{1,0:T(8,128)(2,1)S(1)} %get-tuple-element.61), channel_id=1, source_target_pairs={{0,16},{1,5},{2,18},{3,7},{4,20},{5,1},{6,22},{7,3},{8,24},{9,13},... | collective-permute-start | bytes 688136 | tf_op jit(solution)/shard_map/ppermute | solution.py:35
  81.6 7.5 %collective-permute-start.24 = (bf16[32,3584]{1,0:T(8,128)(2,1)S(1)}, bf16[32,3584]{1,0:T(8,128)(2,1)S(1)}, u32[]{:S(2)}, u32[]{:S(2)}) collective-permute-start(bf16[32,3584]{1,0:T(8,128)(2,1)S(1)} %get-tuple-element.62), channel_id=1, source_target_pairs={{0,24},{1,7},{2,26},{3,1},{4,28},{5,3},{6,30},{7,5},{8,0},{9,15},{... | collective-permute-start | bytes 688136 | tf_op jit(solution)/shard_map/ppermute | solution.py:35
  89.2 4.3 %collective-permute-start.25 = (bf16[8,3584]{1,0:T(8,128)(2,1)S(1)}, bf16[8,3584]{1,0:T(8,128)(2,1)S(1)}, u32[]{:S(2)}, u32[]{:S(2)}) collective-permute-start(bf16[8,3584]{1,0:T(8,128)(2,1)S(1)} %get-tuple-element.63), channel_id=1, source_target_pairs={{0,2},{1,9},{2,4},{3,11},{4,6},{5,13},{6,0},{7,15},{8,10},{9,17},{... | collective-permute-start | bytes 172040 | tf_op jit(solution)/shard_map/ppermute | solution.py:35
  89.7 4.5 %collective-permute-start.26 = (bf16[8,3584]{1,0:T(8,128)(2,1)S(1)}, bf16[8,3584]{1,0:T(8,128)(2,1)S(1)}, u32[]{:S(2)}, u32[]{:S(2)}) collective-permute-start(bf16[8,3584]{1,0:T(8,128)(2,1)S(1)} %get-tuple-element.65), channel_id=1, source_target_pairs={{0,4},{1,17},{2,6},{3,19},{4,0},{5,21},{6,2},{7,23},{8,12},{9,25},... | collective-permute-start | bytes 172040 | tf_op jit(solution)/shard_map/ppermute | solution.py:35
  91.1 3.6 %collective-permute-start.27 = (bf16[8,3584]{1,0:T(8,128)(2,1)S(1)}, bf16[8,3584]{1,0:T(8,128)(2,1)S(1)}, u32[]{:S(2)}, u32[]{:S(2)}) collective-permute-start(bf16[8,3584]{1,0:T(8,128)(2,1)S(1)} %get-tuple-element.64), channel_id=1, source_target_pairs={{0,6},{1,25},{2,0},{3,27},{4,2},{5,29},{6,4},{7,31},{8,14},{9,1},{... | collective-permute-start | bytes 172040 | tf_op jit(solution)/shard_map/ppermute | solution.py:35
  94.8 3.8 %collective-permute-start.28 = (bf16[4,3584]{1,0:T(4,128)(2,1)S(1)}, bf16[4,3584]{1,0:T(4,128)(2,1)S(1)}, u32[]{:S(2)}, u32[]{:S(2)}) collective-permute-start(bf16[4,3584]{1,0:T(4,128)(2,1)S(1)} %get-tuple-element.68), channel_id=1, source_target_pairs={{0,1},{1,0},{2,3},{3,2},{4,5},{5,4},{6,7},{7,6},{8,9},{9,8},{10,11... | collective-permute-start | bytes 86024 | tf_op jit(solution)/shard_map/ppermute | solution.py:15
  (13 other events, 181.5 us)

commit v12 on v11

--- a/solution.py
+++ b/solution.py
@@ -27,7 +27,7 @@
         for y in range(side):
             for x in range(side):
                 for core in range(2):
-                    if axis == core:
+                    if axis != core:
                         to = ((y + sign * k) % side) * side + x
                     else:
                         to = y * side + (x + sign * k) % side
@@ -151,7 +151,7 @@
         to = line_numbers(rows)
         along = (to // line + first) % side
         second = to // (2 * slots) % side
-        chip = jnp.where(core == 0, along * side + second, second * side + along)
+        chip = jnp.where(core == 1, along * side + second, second * side + along)
         from_other = (to // slots % 2 + core) % 2
         source = from_other * lines + chip * pairs + to % slots * heads
         latents = jnp.concatenate([mine_ref[...], other_ref[...]], axis=0)
@@ -334,7 +334,7 @@
     core = place % 2
     upper = core == 1
     at_y, at_x = place // (2 * side), place // 2 % side
-    first, second = jnp.where(upper, at_x, at_y), jnp.where(upper, at_y, at_x)
+    first, second = jnp.where(upper, at_y, at_x), jnp.where(upper, at_x, at_y)
     layer = lax.axis_index("dp")
     spot = jnp.stack([core, first, second, layer])
 

time: 99.7 us -> 100 us (level)
  transfers between devices with their start and end apart: 30 -> 30, of which waited for: 15 -> 14; matrix products, arithmetic and copies ran while one was open for 1% -> 1% of each run, Pallas kernels for 18% -> 17%
where the time goes in v12:
time: 100 us; the launch traced here: 99.7 us
  starting transfers between devices  43.4 us (43%)
  waiting for transfers between devices  34.5 us (34%)
  Pallas kernels  19.2 us (19%)
  other arithmetic  1.31 us (1%)
  between operations  1.04 us (1%)
    ppermute x15, waiting for transfers between devices, turn(): out.append(lax.ppermute(parts[k], 'tp', pairs))  18.5 us
    ppermute x15, starting transfers between devices, turn(): out.append(lax.ppermute(parts[k], 'tp', pairs))  14.3 us
    ppermute x4, starting transfers between devices, down_piece(): return lax.ppermute(down_weight, ('dp', 'tp'), pairs)  13.5 us
    ppermute x10, starting transfers between devices, core_swap(): return lax.ppermute(x, 'tp', [(i, i ^ 1) for i in range(width)])  8.82 us
    pallas_call x1, Pallas kernels, attend(): pl.pallas_call(kernel, in_specs=[in_smem, in_smem, in_vmem, in_hbm], out_...  8.65 us
    ppermute x4, waiting for transfers between devices, down_piece(): return lax.ppermute(down_weight, ('dp', 'tp'), pairs)  7.51 us
    all_to_all x1, starting transfers between devices, between_chips(): return lax.all_to_all(x, 'tp', 0, 0, tiled=True, axis_index_groups=groups)  6.77 us
    all_to_all x1, waiting for transfers between devices, between_chips(): return lax.all_to_all(x, 'tp', 0, 0, tiled=True, axis_index_groups=groups)  5.23 us
  transfers between devices with their start and end apart: 30, of which 14 were waited for; matrix products, arithmetic and copies ran while one was open for 1% of the time, Pallas kernels for 17%

profile of v12, /device:TPU:1, one launch (start us, length us, event | category | flops | bytes accessed | tf_op | source)
XLA Modules:
  0.0 99.7 jit_solution(3006341429260938556)
XLA Ops:
  1.4 3.5 %collective-permute-start.1 = (bf16[288,1792]{1,0:T(8,128)(2,1)}, bf16[288,1792]{1,0:T(8,128)(2,1)S(1)}, u32[]{:S(2)}, u32[]{:S(2)}) collective-permute-start(bf16[288,1792]{1,0:T(8,128)(2,1)} %param.21), channel_id=1, source_target_pairs={{0,0},{64,1},{2,2},{66,3},{4,4},{68,5},{6,6},{70,7},{8,8},{72,9},{... | collective-permute-start | bytes 3096584 | tf_op jit(solution)/shard_map/ppermute | solution.py:53
  5.7 8.6 %shard_map.109 = bf16[256,512]{1,0:T(8,128)(2,1)} custom-call(s32[4]{0:T(128)} %lengths_ref.1, s32[1]{0:T(128)} %copy.12.counts_ref, bf16[4,64,576]{2,1,0:T(8,128)(2,1)} %q_ref, bf16[4,576,2048]{2,1,0:T(8,128)(2,1)} %bitcast.27), custom_call_target="tpu_custom_call" | custom-call | flops 1140850688 | bytes 9437184 | tf_op jit(solution)/shard_map/pallas_call | solution.py:122
  14.4 6.8 %all-to-all-start = ((bf16[16,16,512]{2,1,0:T(8,128)(2,1)}), bf16[16,16,512]{2,1,0:T(8,128)(2,1)S(1)}, u32[]{:S(2)}, u32[]{:S(2)}) async-start(bf16[16,16,512]{2,1,0:T(8,128)(2,1)} %bitcast.28), calls=%async_computation | async-start | bytes 524288 | tf_op jit(solution)/shard_map/all_to_all | solution.py:20
  21.3 2.6 %collective-permute-start.2 = (bf16[2,512,128]{2,1,0:T(8,128)(2,1)S(1)}, bf16[2,512,128]{2,1,0:T(8,128)(2,1)S(1)}, u32[]{:S(2)}, u32[]{:S(2)}) collective-permute-start(bf16[2,512,128]{2,1,0:T(8,128)(2,1)S(1)} %copy-done.4), channel_id=1, source_target_pairs={{0,1},{1,0},{2,3},{3,2},{4,5},{5,4},{6,7},{7,6},{8,9},{9,8},{10,11... | collective-permute-start | bytes 786440 | tf_op jit(solution)/shard_map/ppermute | solution.py:15
  24.0 5.2 %all-to-all-done = bf16[16,16,512]{2,1,0:T(8,128)(2,1)S(1)} async-done(((bf16[16,16,512]{2,1,0:T(8,128)(2,1)}), bf16[16,16,512]{2,1,0:T(8,128)(2,1)S(1)}, u32[]{:S(2)}, u32[]{:S(2)}) %all-to-all-start) | async-done | bytes 262176 | tf_op jit(solution)/shard_map/all_to_all | solution.py:20
  30.9 1.6 %shard_map.110.value_ref = bf16[128,512]{1,0:T(8,128)(2,1)S(1)} custom-call(s32[4]{0:T(128)S(1)} %pad_add_fusion.spot_ref, bf16[256,512]{1,0:T(8,128)(2,1)S(1)} %bitcast.23, bf16[256,512]{1,0:T(8,128)(2,1)S(1)} %bitcast.26, bf16[2,512,128]{2,1,0:T(8,128)(2,1)S(1)} %copy-done.4, bf16[2,512,128]{2,1,0:T(8,128)(2,1)S(1)} %collective-permute-done.2.vo_ref), custom_call_target="tpu_custom_call" | custom-call | flops 1610612736 | bytes 524288 | tf_op jit(solution)/shard_map/pallas_call | solution.py:167
  32.6 3.0 %shard_map.111 = (bf16[32,3584]{1,0:T(8,128)(2,1)S(1)}, bf16[32,3584]{1,0:T(8,128)(2,1)S(1)}, bf16[32,3584]{1,0:T(8,128)(2,1)S(1)}, bf16[32,3584]{1,0:T(8,128)(2,1)S(1)}) custom-call(s32[4]{0:T(128)S(1)} %pad_add_fusion.spot_ref, bf16[128,512]{1,0:T(8,128)(2,1)S(1)} %shard_map.110.value_ref, bf16[256,7168]{1,0:T(8,128)(2,1)S(1)} %copy-done.2, ...), custom_call_target="tpu_custom_call" | custom-call | flops 469762048 | bytes 3670016 | tf_op jit(solution)/shard_map/pallas_call | solution.py:203
  35.7 1.7 %collective-permute-start.5 = (bf16[32,3584]{1,0:T(8,128)(2,1)S(1)}, bf16[32,3584]{1,0:T(8,128)(2,1)S(1)}, u32[]{:S(2)}, u32[]{:S(2)}) collective-permute-start(bf16[32,3584]{1,0:T(8,128)(2,1)S(1)} %get-tuple-element.43), channel_id=1, source_target_pairs={{0,4},{1,17},{2,6},{3,19},{4,0},{5,21},{6,2},{7,23},{8,12},{9,25},... | collective-permute-start | bytes 688136 | tf_op jit(solution)/shard_map/ppermute | solution.py:35
  38.4 4.5 %collective-permute-start.19 = (bf16[288,1792]{1,0:T(8,128)(2,1)S(1)}, bf16[288,1792]{1,0:T(8,128)(2,1)S(1)}, u32[]{:S(2)}, u32[]{:S(2)}) collective-permute-start(bf16[288,1792]{1,0:T(8,128)(2,1)S(1)} %copy-done.6), channel_id=1, source_target_pairs={{32,0},{96,1},{34,2},{98,3},{36,4},{100,5},{38,6},{102,7},{40,8},{... | collective-permute-start | bytes 3096584 | tf_op jit(solution)/shard_map/ppermute | solution.py:53
  42.9 1.6 %collective-permute-done.4 = bf16[32,3584]{1,0:T(8,128)(2,1)S(1)} collective-permute-done((bf16[32,3584]{1,0:T(8,128)(2,1)S(1)}, bf16[32,3584]{1,0:T(8,128)(2,1)S(1)}, u32[]{:S(2)}, u32[]{:S(2)}) %collective-permute-start.4) | collective-permute-done | bytes 229408 | tf_op jit(solution)/shard_map/ppermute | solution.py:35
  46.0 2.0 %collective-permute-start.11 = (bf16[32,3584]{1,0:T(8,128)(2,1)S(1)}, bf16[32,3584]{1,0:T(8,128)(2,1)S(1)}, u32[]{:S(2)}, u32[]{:S(2)}) collective-permute-start(bf16[32,3584]{1,0:T(8,128)(2,1)S(1)} %fusion.1), channel_id=1, source_target_pairs={{0,24},{1,7},{2,26},{3,1},{4,28},{5,3},{6,30},{7,5},{8,0},{9,15},{... | collective-permute-start | bytes 688136 | tf_op jit(solution)/shard_map/ppermute | solution.py:35
  48.0 7.5 %collective-permute-done.19.c_ref = bf16[288,1792]{1,0:T(8,128)(2,1)S(1)} collective-permute-done((bf16[288,1792]{1,0:T(8,128)(2,1)S(1)}, bf16[288,1792]{1,0:T(8,128)(2,1)S(1)}, u32[]{:S(2)}, u32[]{:S(2)}) %collective-permute-start.19) | collective-permute-done | bytes 1032224 | tf_op jit(solution)/shard_map/ppermute | solution.py:53
  55.5 5.4 %collective-permute-start.20 = (bf16[288,1792]{1,0:T(8,128)(2,1)S(1)}, bf16[288,1792]{1,0:T(8,128)(2,1)S(1)}, u32[]{:S(2)}, u32[]{:S(2)}) collective-permute-start(bf16[288,1792]{1,0:T(8,128)(2,1)S(1)} %copy-done.6), channel_id=1, source_target_pairs={{33,0},{97,1},{35,2},{99,3},{37,4},{101,5},{39,6},{103,7},{41,8},{... | collective-permute-start | bytes 3096584 | tf_op jit(solution)/shard_map/ppermute | solution.py:53
  63.2 3.1 %collective-permute-done.12.refs_1_ = bf16[32,3584]{1,0:T(8,128)(2,1)S(1)} collective-permute-done((bf16[32,3584]{1,0:T(8,128)(2,1)S(1)}, bf16[32,3584]{1,0:T(8,128)(2,1)S(1)}, u32[]{:S(2)}, u32[]{:S(2)}) %collective-permute-start.12) | collective-permute-done | bytes 229408 | tf_op jit(solution)/shard_map/ppermute | solution.py:35
  66.3 2.4 %collective-permute-done.13.refs_2_ = bf16[32,3584]{1,0:T(8,128)(2,1)S(1)} collective-permute-done((bf16[32,3584]{1,0:T(8,128)(2,1)S(1)}, bf16[32,3584]{1,0:T(8,128)(2,1)S(1)}, u32[]{:S(2)}, u32[]{:S(2)}) %collective-permute-start.13) | collective-permute-done | bytes 229408 | tf_op jit(solution)/shard_map/ppermute | solution.py:35
  68.7 2.4 %collective-permute-done.14.refs_3_ = bf16[32,3584]{1,0:T(8,128)(2,1)S(1)} collective-permute-done((bf16[32,3584]{1,0:T(8,128)(2,1)S(1)}, bf16[32,3584]{1,0:T(8,128)(2,1)S(1)}, u32[]{:S(2)}, u32[]{:S(2)}) %collective-permute-start.14) | collective-permute-done | bytes 229408 | tf_op jit(solution)/shard_map/ppermute | solution.py:35
  72.3 1.9 %shard_map.112 = (f32[128,576]{1,0:T(8,128)S(1)}, f32[128,128]{1,0:T(8,128)S(1)}) custom-call(s32[4]{0:T(128)S(1)} %pad_add_fusion.spot_ref, bf16[32,3584]{1,0:T(8,128)(2,1)S(1)} %add_convert_fusion.1.refs_0_, bf16[32,3584]{1,0:T(8,128)(2,1)S(1)} %collective-permute-done.12.refs_1_, bf16[32,3584]{1,0:T(8,128)(2,1)S(1)} %collective-permute-done.13.refs_2_, ...), custom_call_target="tpu_custom_call" | custom-call | flops 528482304 | bytes 4128768 | tf_op jit(solution)/shard_map/pallas_call | solution.py:260
  74.3 2.3 %shard_map.113.inner_ref = bf16[128,288]{1,0:T(8,128)(2,1)S(1)} custom-call(s32[4]{0:T(128)S(1)} %pad_add_fusion.spot_ref, bf16[32,3584]{1,0:T(8,128)(2,1)S(1)} %collective-permute-done.15.refs_0_, bf16[32,3584]{1,0:T(8,128)(2,1)S(1)} %collective-permute-done.16.refs_1_, bf16[32,3584]{1,0:T(8,128)(2,1)S(1)} %collective-permute-done.17.refs_2_, ...), custom_call_target="tpu_custom_call" | custom-call | flops 528482304 | bytes 4128768 | tf_op jit(solution)/shard_map/pallas_call | solution.py:260
  78.1 1.8 %shard_map.114 = (bf16[32,3584]{1,0:T(8,128)(2,1)S(1)}, bf16[32,3584]{1,0:T(8,128)(2,1)S(1)}, bf16[32,3584]{1,0:T(8,128)(2,1)S(1)}, bf16[32,3584]{1,0:T(8,128)(2,1)S(1)}) custom-call(s32[4]{0:T(128)S(1)} %pad_add_fusion.spot_ref, bf16[128,288]{1,0:T(8,128)(2,1)S(1)} %shard_map.113.inner_ref, bf16[128,288]{1,0:T(8,128)(2,1)S(1)} %collective-permute-done.21.other_ref, ...), custom_call_target="tpu_custom_call" | custom-call | flops 528482304 | bytes 4128768 | tf_op jit(solution)/shard_map/pallas_call | solution.py:299
  80.0 1.7 %collective-permute-start.23 = (bf16[32,3584]{1,0:T(8,128)(2,1)S(1)}, bf16[32,3584]{1,0:T(8,128)(2,1)S(1)}, u32[]{:S(2)}, u32[]{:S(2)}) collective-permute-start(bf16[32,3584]{1,0:T(8,128)(2,1)S(1)} %get-tuple-element.61), channel_id=1, source_target_pairs={{0,4},{1,17},{2,6},{3,19},{4,0},{5,21},{6,2},{7,23},{8,12},{9,25},... | collective-permute-start | bytes 688136 | tf_op jit(solution)/shard_map/ppermute | solution.py:35
  83.0 5.8 %collective-permute-done.22 = bf16[32,3584]{1,0:T(8,128)(2,1)S(1)} collective-permute-done((bf16[32,3584]{1,0:T(8,128)(2,1)S(1)}, bf16[32,3584]{1,0:T(8,128)(2,1)S(1)}, u32[]{:S(2)}, u32[]{:S(2)}) %collective-permute-start.22) | collective-permute-done | bytes 229408 | tf_op jit(solution)/shard_map/ppermute | solution.py:35
  89.6 1.5 %collective-permute-start.26 = (bf16[8,3584]{1,0:T(8,128)(2,1)S(1)}, bf16[8,3584]{1,0:T(8,128)(2,1)S(1)}, u32[]{:S(2)}, u32[]{:S(2)}) collective-permute-start(bf16[8,3584]{1,0:T(8,128)(2,1)S(1)} %get-tuple-element.65), channel_id=1, source_target_pairs={{0,16},{1,5},{2,18},{3,7},{4,20},{5,1},{6,22},{7,3},{8,24},{9,13},... | collective-permute-start | bytes 172040 | tf_op jit(solution)/shard_map/ppermute | solution.py:35
  91.2 2.0 %collective-permute-start.27 = (bf16[8,3584]{1,0:T(8,128)(2,1)S(1)}, bf16[8,3584]{1,0:T(8,128)(2,1)S(1)}, u32[]{:S(2)}, u32[]{:S(2)}) collective-permute-start(bf16[8,3584]{1,0:T(8,128)(2,1)S(1)} %get-tuple-element.64), channel_id=1, source_target_pairs={{0,24},{1,7},{2,26},{3,1},{4,28},{5,3},{6,30},{7,5},{8,0},{9,15},{... | collective-permute-start | bytes 172040 | tf_op jit(solution)/shard_map/ppermute | solution.py:35
  95.2 3.0 %collective-permute-start.28 = (bf16[4,3584]{1,0:T(4,128)(2,1)S(1)}, bf16[4,3584]{1,0:T(4,128)(2,1)S(1)}, u32[]{:S(2)}, u32[]{:S(2)}) collective-permute-start(bf16[4,3584]{1,0:T(4,128)(2,1)S(1)} %get-tuple-element.68), channel_id=1, source_target_pairs={{0,1},{1,0},{2,3},{3,2},{4,5},{5,4},{6,7},{7,6},{8,9},{9,8},{10,11... | collective-permute-start | bytes 86024 | tf_op jit(solution)/shard_map/ppermute | solution.py:15
  (72 shorter events, 16.7 us)
Async XLA Ops:
  0.0 32.6 %collective-permute-start.3 = (bf16[256,7168]{1,0:T(8,128)(2,1)}, bf16[256,7168]{1,0:T(8,128)(2,1)}, u32[]{:S(2)}, u32[]{:S(2)}) collective-permute-start(bf16[256,7168]{1,0:T(8,128)(2,1)} %om_ref.1), channel_id=1, source_target_pairs={{0,1},{1,0},{2,3},{3,2},{4,5},{5,4},{6,7},{7,6},{8,9},{9,8},{10,11... | collective-permute-start | bytes 11010056 | tf_op jit(solution)/shard_map/ppermute | solution.py:15
  1.4 29.5 %collective-permute-start.1 = (bf16[288,1792]{1,0:T(8,128)(2,1)}, bf16[288,1792]{1,0:T(8,128)(2,1)S(1)}, u32[]{:S(2)}, u32[]{:S(2)}) collective-permute-start(bf16[288,1792]{1,0:T(8,128)(2,1)} %param.21), channel_id=1, source_target_pairs={{0,0},{64,1},{2,2},{66,3},{4,4},{68,5},{6,6},{70,7},{8,8},{72,9},{... | collective-permute-start | bytes 3096584 | tf_op jit(solution)/shard_map/ppermute | solution.py:53
  14.4 14.9 %all-to-all-start = ((bf16[16,16,512]{2,1,0:T(8,128)(2,1)}), bf16[16,16,512]{2,1,0:T(8,128)(2,1)S(1)}, u32[]{:S(2)}, u32[]{:S(2)}) async-start(bf16[16,16,512]{2,1,0:T(8,128)(2,1)} %bitcast.28), calls=%async_computation | async-start | bytes 524288 | tf_op jit(solution)/shard_map/all_to_all | solution.py:20
  21.2 24.1 %collective-permute-start.8 = (bf16[288,1792]{1,0:T(8,128)(2,1)}, bf16[288,1792]{1,0:T(8,128)(2,1)S(1)}, u32[]{:S(2)}, u32[]{:S(2)}) collective-permute-start(bf16[288,1792]{1,0:T(8,128)(2,1)} %param.21), channel_id=1, source_target_pairs={{1,0},{65,1},{3,2},{67,3},{5,4},{69,5},{7,6},{71,7},{9,8},{73,9},{... | collective-permute-start | bytes 3096584 | tf_op jit(solution)/shard_map/ppermute | solution.py:53
  21.3 9.6 %collective-permute-start.2 = (bf16[2,512,128]{2,1,0:T(8,128)(2,1)S(1)}, bf16[2,512,128]{2,1,0:T(8,128)(2,1)S(1)}, u32[]{:S(2)}, u32[]{:S(2)}) collective-permute-start(bf16[2,512,128]{2,1,0:T(8,128)(2,1)S(1)} %copy-done.4), channel_id=1, source_target_pairs={{0,1},{1,0},{2,3},{3,2},{4,5},{5,4},{6,7},{7,6},{8,9},{9,8},{10,11... | collective-permute-start | bytes 786440 | tf_op jit(solution)/shard_map/ppermute | solution.py:15
  30.8 7.6 %collective-permute-start.7 = (bf16[4,3584]{1,0:T(4,128)(2,1)S(1)}, bf16[4,3584]{1,0:T(4,128)(2,1)S(1)}, u32[]{:S(2)}, u32[]{:S(2)}) collective-permute-start(bf16[4,3584]{1,0:T(4,128)(2,1)S(1)} %get-tuple-element.70), channel_id=1, source_target_pairs={{0,1},{1,0},{2,3},{3,2},{4,5},{5,4},{6,7},{7,6},{8,9},{9,8},{10,11... | collective-permute-start | bytes 86024 | tf_op jit(solution)/shard_map/ppermute | solution.py:15
  35.6 8.9 %collective-permute-start.4 = (bf16[32,3584]{1,0:T(8,128)(2,1)S(1)}, bf16[32,3584]{1,0:T(8,128)(2,1)S(1)}, u32[]{:S(2)}, u32[]{:S(2)}) collective-permute-start(bf16[32,3584]{1,0:T(8,128)(2,1)S(1)} %get-tuple-element.42), channel_id=1, source_target_pairs={{0,2},{1,9},{2,4},{3,11},{4,6},{5,13},{6,0},{7,15},{8,10},{9,17},{... | collective-permute-start | bytes 688136 | tf_op jit(solution)/shard_map/ppermute | solution.py:35
  35.7 8.8 %collective-permute-start.5 = (bf16[32,3584]{1,0:T(8,128)(2,1)S(1)}, bf16[32,3584]{1,0:T(8,128)(2,1)S(1)}, u32[]{:S(2)}, u32[]{:S(2)}) collective-permute-start(bf16[32,3584]{1,0:T(8,128)(2,1)S(1)} %get-tuple-element.43), channel_id=1, source_target_pairs={{0,4},{1,17},{2,6},{3,19},{4,0},{5,21},{6,2},{7,23},{8,12},{9,25},... | collective-permute-start | bytes 688136 | tf_op jit(solution)/shard_map/ppermute | solution.py:35
  37.4 7.7 %collective-permute-start.6 = (bf16[32,3584]{1,0:T(8,128)(2,1)S(1)}, bf16[32,3584]{1,0:T(8,128)(2,1)S(1)}, u32[]{:S(2)}, u32[]{:S(2)}) collective-permute-start(bf16[32,3584]{1,0:T(8,128)(2,1)S(1)} %get-tuple-element.44), channel_id=1, source_target_pairs={{0,6},{1,25},{2,0},{3,27},{4,2},{5,29},{6,4},{7,31},{8,14},{9,1},{... | collective-permute-start | bytes 688136 | tf_op jit(solution)/shard_map/ppermute | solution.py:35
  38.4 17.1 %collective-permute-start.19 = (bf16[288,1792]{1,0:T(8,128)(2,1)S(1)}, bf16[288,1792]{1,0:T(8,128)(2,1)S(1)}, u32[]{:S(2)}, u32[]{:S(2)}) collective-permute-start(bf16[288,1792]{1,0:T(8,128)(2,1)S(1)} %copy-done.6), channel_id=1, source_target_pairs={{32,0},{96,1},{34,2},{98,3},{36,4},{100,5},{38,6},{102,7},{40,8},{... | collective-permute-start | bytes 3096584 | tf_op jit(solution)/shard_map/ppermute | solution.py:53
  45.3 15.7 %collective-permute-start.10 = (bf16[32,3584]{1,0:T(8,128)(2,1)S(1)}, bf16[32,3584]{1,0:T(8,128)(2,1)S(1)}, u32[]{:S(2)}, u32[]{:S(2)}) collective-permute-start(bf16[32,3584]{1,0:T(8,128)(2,1)S(1)} %fusion.1), channel_id=1, source_target_pairs={{0,16},{1,5},{2,18},{3,7},{4,20},{5,1},{6,22},{7,3},{8,24},{9,13},... | collective-permute-start | bytes 688136 | tf_op jit(solution)/shard_map/ppermute | solution.py:35
  46.0 14.9 %collective-permute-start.11 = (bf16[32,3584]{1,0:T(8,128)(2,1)S(1)}, bf16[32,3584]{1,0:T(8,128)(2,1)S(1)}, u32[]{:S(2)}, u32[]{:S(2)}) collective-permute-start(bf16[32,3584]{1,0:T(8,128)(2,1)S(1)} %fusion.1), channel_id=1, source_target_pairs={{0,24},{1,7},{2,26},{3,1},{4,28},{5,3},{6,30},{7,5},{8,0},{9,15},{... | collective-permute-start | bytes 688136 | tf_op jit(solution)/shard_map/ppermute | solution.py:35
  48.0 12.9 %collective-permute-start.9 = (bf16[32,3584]{1,0:T(8,128)(2,1)S(1)}, bf16[32,3584]{1,0:T(8,128)(2,1)S(1)}, u32[]{:S(2)}, u32[]{:S(2)}) collective-permute-start(bf16[32,3584]{1,0:T(8,128)(2,1)S(1)} %fusion.1), channel_id=1, source_target_pairs={{0,8},{1,3},{2,10},{3,5},{4,12},{5,7},{6,14},{7,1},{8,16},{9,11},{... | collective-permute-start | bytes 688136 | tf_op jit(solution)/shard_map/ppermute | solution.py:35
  55.5 21.0 %collective-permute-start.20 = (bf16[288,1792]{1,0:T(8,128)(2,1)S(1)}, bf16[288,1792]{1,0:T(8,128)(2,1)S(1)}, u32[]{:S(2)}, u32[]{:S(2)}) collective-permute-start(bf16[288,1792]{1,0:T(8,128)(2,1)S(1)} %copy-done.6), channel_id=1, source_target_pairs={{33,0},{97,1},{35,2},{99,3},{37,4},{101,5},{39,6},{103,7},{41,8},{... | collective-permute-start | bytes 3096584 | tf_op jit(solution)/shard_map/ppermute | solution.py:53
  61.1 5.2 %collective-permute-start.12 = (bf16[32,3584]{1,0:T(8,128)(2,1)S(1)}, bf16[32,3584]{1,0:T(8,128)(2,1)S(1)}, u32[]{:S(2)}, u32[]{:S(2)}) collective-permute-start(bf16[32,3584]{1,0:T(8,128)(2,1)S(1)} %add_convert_fusion.1.refs_0_), channel_id=1, source_target_pairs={{0,6},{1,25},{2,0},{3,27},{4,2},{5,29},{6,4},{7,31},{8,14},{9,1},{... | collective-permute-start | bytes 688136 | tf_op jit(solution)/shard_map/ppermute | solution.py:35
  62.0 6.7 %collective-permute-start.13 = (bf16[32,3584]{1,0:T(8,128)(2,1)S(1)}, bf16[32,3584]{1,0:T(8,128)(2,1)S(1)}, u32[]{:S(2)}, u32[]{:S(2)}) collective-permute-start(bf16[32,3584]{1,0:T(8,128)(2,1)S(1)} %add_convert_fusion.1.refs_0_), channel_id=1, source_target_pairs={{0,4},{1,17},{2,6},{3,19},{4,0},{5,21},{6,2},{7,23},{8,12},{9,25},... | collective-permute-start | bytes 688136 | tf_op jit(solution)/shard_map/ppermute | solution.py:35
  63.2 7.9 %collective-permute-start.14 = (bf16[32,3584]{1,0:T(8,128)(2,1)S(1)}, bf16[32,3584]{1,0:T(8,128)(2,1)S(1)}, u32[]{:S(2)}, u32[]{:S(2)}) collective-permute-start(bf16[32,3584]{1,0:T(8,128)(2,1)S(1)} %add_convert_fusion.1.refs_0_), channel_id=1, source_target_pairs={{0,2},{1,9},{2,4},{3,11},{4,6},{5,13},{6,0},{7,15},{8,10},{9,17},{... | collective-permute-start | bytes 688136 | tf_op jit(solution)/shard_map/ppermute | solution.py:35
  79.9 8.9 %collective-permute-start.22 = (bf16[32,3584]{1,0:T(8,128)(2,1)S(1)}, bf16[32,3584]{1,0:T(8,128)(2,1)S(1)}, u32[]{:S(2)}, u32[]{:S(2)}) collective-permute-start(bf16[32,3584]{1,0:T(8,128)(2,1)S(1)} %get-tuple-element.60), channel_id=1, source_target_pairs={{0,2},{1,9},{2,4},{3,11},{4,6},{5,13},{6,0},{7,15},{8,10},{9,17},{... | collective-permute-start | bytes 688136 | tf_op jit(solution)/shard_map/ppermute | solution.py:35
  80.0 8.8 %collective-permute-start.23 = (bf16[32,3584]{1,0:T(8,128)(2,1)S(1)}, bf16[32,3584]{1,0:T(8,128)(2,1)S(1)}, u32[]{:S(2)}, u32[]{:S(2)}) collective-permute-start(bf16[32,3584]{1,0:T(8,128)(2,1)S(1)} %get-tuple-element.61), channel_id=1, source_target_pairs={{0,4},{1,17},{2,6},{3,19},{4,0},{5,21},{6,2},{7,23},{8,12},{9,25},... | collective-permute-start | bytes 688136 | tf_op jit(solution)/shard_map/ppermute | solution.py:35
  81.7 7.7 %collective-permute-start.24 = (bf16[32,3584]{1,0:T(8,128)(2,1)S(1)}, bf16[32,3584]{1,0:T(8,128)(2,1)S(1)}, u32[]{:S(2)}, u32[]{:S(2)}) collective-permute-start(bf16[32,3584]{1,0:T(8,128)(2,1)S(1)} %get-tuple-element.62), channel_id=1, source_target_pairs={{0,6},{1,25},{2,0},{3,27},{4,2},{5,29},{6,4},{7,31},{8,14},{9,1},{... | collective-permute-start | bytes 688136 | tf_op jit(solution)/shard_map/ppermute | solution.py:35
  89.6 4.9 %collective-permute-start.25 = (bf16[8,3584]{1,0:T(8,128)(2,1)S(1)}, bf16[8,3584]{1,0:T(8,128)(2,1)S(1)}, u32[]{:S(2)}, u32[]{:S(2)}) collective-permute-start(bf16[8,3584]{1,0:T(8,128)(2,1)S(1)} %get-tuple-element.63), channel_id=1, source_target_pairs={{0,8},{1,3},{2,10},{3,5},{4,12},{5,7},{6,14},{7,1},{8,16},{9,11},{... | collective-permute-start | bytes 172040 | tf_op jit(solution)/shard_map/ppermute | solution.py:35
  89.6 4.8 %collective-permute-start.26 = (bf16[8,3584]{1,0:T(8,128)(2,1)S(1)}, bf16[8,3584]{1,0:T(8,128)(2,1)S(1)}, u32[]{:S(2)}, u32[]{:S(2)}) collective-permute-start(bf16[8,3584]{1,0:T(8,128)(2,1)S(1)} %get-tuple-element.65), channel_id=1, source_target_pairs={{0,16},{1,5},{2,18},{3,7},{4,20},{5,1},{6,22},{7,3},{8,24},{9,13},... | collective-permute-start | bytes 172040 | tf_op jit(solution)/shard_map/ppermute | solution.py:35
  91.2 3.9 %collective-permute-start.27 = (bf16[8,3584]{1,0:T(8,128)(2,1)S(1)}, bf16[8,3584]{1,0:T(8,128)(2,1)S(1)}, u32[]{:S(2)}, u32[]{:S(2)}) collective-permute-start(bf16[8,3584]{1,0:T(8,128)(2,1)S(1)} %get-tuple-element.64), channel_id=1, source_target_pairs={{0,24},{1,7},{2,26},{3,1},{4,28},{5,3},{6,30},{7,5},{8,0},{9,15},{... | collective-permute-start | bytes 172040 | tf_op jit(solution)/shard_map/ppermute | solution.py:35
  95.2 3.8 %collective-permute-start.28 = (bf16[4,3584]{1,0:T(4,128)(2,1)S(1)}, bf16[4,3584]{1,0:T(4,128)(2,1)S(1)}, u32[]{:S(2)}, u32[]{:S(2)}) collective-permute-start(bf16[4,3584]{1,0:T(4,128)(2,1)S(1)} %get-tuple-element.68), channel_id=1, source_target_pairs={{0,1},{1,0},{2,3},{3,2},{4,5},{5,4},{6,7},{7,6},{8,9},{9,8},{10,11... | collective-permute-start | bytes 86024 | tf_op jit(solution)/shard_map/ppermute | solution.py:15
  (13 other events, 182.2 us)

commit v13 on v11

--- a/solution.py
+++ b/solution.py
@@ -21,8 +21,8 @@
 
 
 def turn(parts, axis, side, sign):
-    out = [parts[0]]
-    for k in range(1, side):
+    out = list(parts)
+    for k in sorted(range(1, side), key=lambda step: min(step, side - step)):
         pairs = []
         for y in range(side):
             for x in range(side):
@@ -32,7 +32,7 @@
                     else:
                         to = y * side + (x + sign * k) % side
                     pairs.append(((y * side + x) * 2 + core, to * 2 + core))
-        out.append(lax.ppermute(parts[k], "tp", pairs))
+        out[k] = lax.ppermute(parts[k], "tp", pairs)
     return out
 
 

time: 99.7 us -> 99.7 us (level)
  no operation moved by 1% of the time
where the time goes in v13:
time: 99.7 us; the launch traced here: 99.4 us
  starting transfers between devices  43.1 us (43%)
  waiting for transfers between devices  34.4 us (35%)
  Pallas kernels  19.2 us (19%)
  other arithmetic  1.31 us (1%)
  between operations  1 us (1%)
    ppermute x15, waiting for transfers between devices, turn(): out[k] = lax.ppermute(parts[k], 'tp', pairs)  17.8 us
    ppermute x15, starting transfers between devices, turn(): out[k] = lax.ppermute(parts[k], 'tp', pairs)  14.4 us
    ppermute x4, starting transfers between devices, down_piece(): return lax.ppermute(down_weight, ('dp', 'tp'), pairs)  13.3 us
    pallas_call x1, Pallas kernels, attend(): pl.pallas_call(kernel, in_specs=[in_smem, in_smem, in_vmem, in_hbm], out_...  8.65 us
    ppermute x10, starting transfers between devices, core_swap(): return lax.ppermute(x, 'tp', [(i, i ^ 1) for i in range(width)])  8.59 us
    ppermute x4, waiting for transfers between devices, down_piece(): return lax.ppermute(down_weight, ('dp', 'tp'), pairs)  8.06 us
    all_to_all x1, starting transfers between devices, between_chips(): return lax.all_to_all(x, 'tp', 0, 0, tiled=True, axis_index_groups=groups)  6.77 us
    all_to_all x1, waiting for transfers between devices, between_chips(): return lax.all_to_all(x, 'tp', 0, 0, tiled=True, axis_index_groups=groups)  5.23 us
  transfers between devices with their start and end apart: 30, of which 15 were waited for; matrix products, arithmetic and copies ran while one was open for 1% of the time, Pallas kernels for 18%

profile of v13, /device:TPU:1, one launch (start us, length us, event | category | flops | bytes accessed | tf_op | source)
XLA Modules:
  0.0 99.4 jit_solution(14412155978200179435)
XLA Ops:
  1.4 3.5 %collective-permute-start.1 = (bf16[288,1792]{1,0:T(8,128)(2,1)}, bf16[288,1792]{1,0:T(8,128)(2,1)S(1)}, u32[]{:S(2)}, u32[]{:S(2)}) collective-permute-start(bf16[288,1792]{1,0:T(8,128)(2,1)} %param.21), channel_id=1, source_target_pairs={{0,0},{64,1},{2,2},{66,3},{4,4},{68,5},{6,6},{70,7},{8,8},{72,9},{... | collective-permute-start | bytes 3096584 | tf_op jit(solution)/shard_map/ppermute | solution.py:53
  5.7 8.6 %shard_map.109 = bf16[256,512]{1,0:T(8,128)(2,1)} custom-call(s32[4]{0:T(128)} %lengths_ref.1, s32[1]{0:T(128)} %copy.12.counts_ref, bf16[4,64,576]{2,1,0:T(8,128)(2,1)} %q_ref, bf16[4,576,2048]{2,1,0:T(8,128)(2,1)} %bitcast.27), custom_call_target="tpu_custom_call" | custom-call | flops 1140850688 | bytes 9437184 | tf_op jit(solution)/shard_map/pallas_call | solution.py:122
  14.4 6.8 %all-to-all-start = ((bf16[16,16,512]{2,1,0:T(8,128)(2,1)}), bf16[16,16,512]{2,1,0:T(8,128)(2,1)S(1)}, u32[]{:S(2)}, u32[]{:S(2)}) async-start(bf16[16,16,512]{2,1,0:T(8,128)(2,1)} %bitcast.28), calls=%async_computation | async-start | bytes 524288 | tf_op jit(solution)/shard_map/all_to_all | solution.py:20
  21.3 2.6 %collective-permute-start.2 = (bf16[2,512,128]{2,1,0:T(8,128)(2,1)S(1)}, bf16[2,512,128]{2,1,0:T(8,128)(2,1)S(1)}, u32[]{:S(2)}, u32[]{:S(2)}) collective-permute-start(bf16[2,512,128]{2,1,0:T(8,128)(2,1)S(1)} %copy-done.4), channel_id=1, source_target_pairs={{0,1},{1,0},{2,3},{3,2},{4,5},{5,4},{6,7},{7,6},{8,9},{9,8},{10,11... | collective-permute-start | bytes 786440 | tf_op jit(solution)/shard_map/ppermute | solution.py:15
  24.0 5.2 %all-to-all-done = bf16[16,16,512]{2,1,0:T(8,128)(2,1)S(1)} async-done(((bf16[16,16,512]{2,1,0:T(8,128)(2,1)}), bf16[16,16,512]{2,1,0:T(8,128)(2,1)S(1)}, u32[]{:S(2)}, u32[]{:S(2)}) %all-to-all-start) | async-done | bytes 262176 | tf_op jit(solution)/shard_map/all_to_all | solution.py:20
  29.3 1.5 %collective-permute-done = bf16[16,16,512]{2,1,0:T(8,128)(2,1)S(1)} collective-permute-done((bf16[16,16,512]{2,1,0:T(8,128)(2,1)S(1)}, bf16[16,16,512]{2,1,0:T(8,128)(2,1)S(1)}, u32[]{:S(2)}, u32[]{:S(2)}) %collective-permute-start) | collective-permute-done | bytes 262176 | tf_op jit(solution)/shard_map/ppermute | solution.py:15
  30.9 1.6 %shard_map.110.value_ref = bf16[128,512]{1,0:T(8,128)(2,1)S(1)} custom-call(s32[4]{0:T(128)S(1)} %pad_add_fusion.spot_ref, bf16[256,512]{1,0:T(8,128)(2,1)S(1)} %bitcast.23, bf16[256,512]{1,0:T(8,128)(2,1)S(1)} %bitcast.26, bf16[2,512,128]{2,1,0:T(8,128)(2,1)S(1)} %copy-done.4, bf16[2,512,128]{2,1,0:T(8,128)(2,1)S(1)} %collective-permute-done.2.vo_ref), custom_call_target="tpu_custom_call" | custom-call | flops 1610612736 | bytes 524288 | tf_op jit(solution)/shard_map/pallas_call | solution.py:167
  32.6 3.0 %shard_map.111 = (bf16[32,3584]{1,0:T(8,128)(2,1)S(1)}, bf16[32,3584]{1,0:T(8,128)(2,1)S(1)}, bf16[32,3584]{1,0:T(8,128)(2,1)S(1)}, bf16[32,3584]{1,0:T(8,128)(2,1)S(1)}) custom-call(s32[4]{0:T(128)S(1)} %pad_add_fusion.spot_ref, bf16[128,512]{1,0:T(8,128)(2,1)S(1)} %shard_map.110.value_ref, bf16[256,7168]{1,0:T(8,128)(2,1)S(1)} %copy-done.2, ...), custom_call_target="tpu_custom_call" | custom-call | flops 469762048 | bytes 3670016 | tf_op jit(solution)/shard_map/pallas_call | solution.py:203
  38.5 4.5 %collective-permute-start.19 = (bf16[288,1792]{1,0:T(8,128)(2,1)S(1)}, bf16[288,1792]{1,0:T(8,128)(2,1)S(1)}, u32[]{:S(2)}, u32[]{:S(2)}) collective-permute-start(bf16[288,1792]{1,0:T(8,128)(2,1)S(1)} %copy-done.6), channel_id=1, source_target_pairs={{32,0},{96,1},{34,2},{98,3},{36,4},{100,5},{38,6},{102,7},{40,8},{... | collective-permute-start | bytes 3096584 | tf_op jit(solution)/shard_map/ppermute | solution.py:53
  43.0 1.5 %collective-permute-done.4 = bf16[32,3584]{1,0:T(8,128)(2,1)S(1)} collective-permute-done((bf16[32,3584]{1,0:T(8,128)(2,1)S(1)}, bf16[32,3584]{1,0:T(8,128)(2,1)S(1)}, u32[]{:S(2)}, u32[]{:S(2)}) %collective-permute-start.4) | collective-permute-done | bytes 229408 | tf_op jit(solution)/shard_map/ppermute | solution.py:35
  45.9 1.6 %collective-permute-start.11 = (bf16[32,3584]{1,0:T(8,128)(2,1)S(1)}, bf16[32,3584]{1,0:T(8,128)(2,1)S(1)}, u32[]{:S(2)}, u32[]{:S(2)}) collective-permute-start(bf16[32,3584]{1,0:T(8,128)(2,1)S(1)} %fusion.1), channel_id=1, source_target_pairs={{0,6},{1,25},{2,0},{3,27},{4,2},{5,29},{6,4},{7,31},{8,14},{9,1},{... | collective-permute-start | bytes 688136 | tf_op jit(solution)/shard_map/ppermute | solution.py:35
  47.5 8.1 %collective-permute-done.19.c_ref = bf16[288,1792]{1,0:T(8,128)(2,1)S(1)} collective-permute-done((bf16[288,1792]{1,0:T(8,128)(2,1)S(1)}, bf16[288,1792]{1,0:T(8,128)(2,1)S(1)}, u32[]{:S(2)}, u32[]{:S(2)}) %collective-permute-start.19) | collective-permute-done | bytes 1032224 | tf_op jit(solution)/shard_map/ppermute | solution.py:53
  55.6 5.3 %collective-permute-start.20 = (bf16[288,1792]{1,0:T(8,128)(2,1)S(1)}, bf16[288,1792]{1,0:T(8,128)(2,1)S(1)}, u32[]{:S(2)}, u32[]{:S(2)}) collective-permute-start(bf16[288,1792]{1,0:T(8,128)(2,1)S(1)} %copy-done.6), channel_id=1, source_target_pairs={{33,0},{97,1},{35,2},{99,3},{37,4},{101,5},{39,6},{103,7},{41,8},{... | collective-permute-start | bytes 3096584 | tf_op jit(solution)/shard_map/ppermute | solution.py:53
  63.2 3.1 %collective-permute-done.12.refs_1_ = bf16[32,3584]{1,0:T(8,128)(2,1)S(1)} collective-permute-done((bf16[32,3584]{1,0:T(8,128)(2,1)S(1)}, bf16[32,3584]{1,0:T(8,128)(2,1)S(1)}, u32[]{:S(2)}, u32[]{:S(2)}) %collective-permute-start.12) | collective-permute-done | bytes 229408 | tf_op jit(solution)/shard_map/ppermute | solution.py:35
  66.2 2.3 %collective-permute-done.13.refs_2_ = bf16[32,3584]{1,0:T(8,128)(2,1)S(1)} collective-permute-done((bf16[32,3584]{1,0:T(8,128)(2,1)S(1)}, bf16[32,3584]{1,0:T(8,128)(2,1)S(1)}, u32[]{:S(2)}, u32[]{:S(2)}) %collective-permute-start.13) | collective-permute-done | bytes 229408 | tf_op jit(solution)/shard_map/ppermute | solution.py:35
  68.6 2.5 %collective-permute-done.14.refs_3_ = bf16[32,3584]{1,0:T(8,128)(2,1)S(1)} collective-permute-done((bf16[32,3584]{1,0:T(8,128)(2,1)S(1)}, bf16[32,3584]{1,0:T(8,128)(2,1)S(1)}, u32[]{:S(2)}, u32[]{:S(2)}) %collective-permute-start.14) | collective-permute-done | bytes 229408 | tf_op jit(solution)/shard_map/ppermute | solution.py:35
  72.0 1.9 %shard_map.112 = (f32[128,576]{1,0:T(8,128)S(1)}, f32[128,128]{1,0:T(8,128)S(1)}) custom-call(s32[4]{0:T(128)S(1)} %pad_add_fusion.spot_ref, bf16[32,3584]{1,0:T(8,128)(2,1)S(1)} %add_convert_fusion.1.refs_0_, bf16[32,3584]{1,0:T(8,128)(2,1)S(1)} %collective-permute-done.12.refs_1_, bf16[32,3584]{1,0:T(8,128)(2,1)S(1)} %collective-permute-done.13.refs_2_, ...), custom_call_target="tpu_custom_call" | custom-call | flops 528482304 | bytes 4128768 | tf_op jit(solution)/shard_map/pallas_call | solution.py:260
  74.0 2.3 %shard_map.113.inner_ref = bf16[128,288]{1,0:T(8,128)(2,1)S(1)} custom-call(s32[4]{0:T(128)S(1)} %pad_add_fusion.spot_ref, bf16[32,3584]{1,0:T(8,128)(2,1)S(1)} %collective-permute-done.15.refs_0_, bf16[32,3584]{1,0:T(8,128)(2,1)S(1)} %collective-permute-done.16.refs_1_, bf16[32,3584]{1,0:T(8,128)(2,1)S(1)} %collective-permute-done.17.refs_2_, ...), custom_call_target="tpu_custom_call" | custom-call | flops 528482304 | bytes 4128768 | tf_op jit(solution)/shard_map/pallas_call | solution.py:260
  77.7 1.8 %shard_map.114 = (bf16[32,3584]{1,0:T(8,128)(2,1)S(1)}, bf16[32,3584]{1,0:T(8,128)(2,1)S(1)}, bf16[32,3584]{1,0:T(8,128)(2,1)S(1)}, bf16[32,3584]{1,0:T(8,128)(2,1)S(1)}) custom-call(s32[4]{0:T(128)S(1)} %pad_add_fusion.spot_ref, bf16[128,288]{1,0:T(8,128)(2,1)S(1)} %shard_map.113.inner_ref, bf16[128,288]{1,0:T(8,128)(2,1)S(1)} %collective-permute-done.21.other_ref, ...), custom_call_target="tpu_custom_call" | custom-call | flops 528482304 | bytes 4128768 | tf_op jit(solution)/shard_map/pallas_call | solution.py:299
  79.8 1.8 %collective-permute-start.23 = (bf16[32,3584]{1,0:T(8,128)(2,1)S(1)}, bf16[32,3584]{1,0:T(8,128)(2,1)S(1)}, u32[]{:S(2)}, u32[]{:S(2)}) collective-permute-start(bf16[32,3584]{1,0:T(8,128)(2,1)S(1)} %get-tuple-element.61), channel_id=1, source_target_pairs={{0,16},{1,5},{2,18},{3,7},{4,20},{5,1},{6,22},{7,3},{8,24},{9,13},... | collective-permute-start | bytes 688136 | tf_op jit(solution)/shard_map/ppermute | solution.py:35
  82.9 5.5 %collective-permute-done.22 = bf16[32,3584]{1,0:T(8,128)(2,1)S(1)} collective-permute-done((bf16[32,3584]{1,0:T(8,128)(2,1)S(1)}, bf16[32,3584]{1,0:T(8,128)(2,1)S(1)}, u32[]{:S(2)}, u32[]{:S(2)}) %collective-permute-start.22) | collective-permute-done | bytes 229408 | tf_op jit(solution)/shard_map/ppermute | solution.py:35
  89.7 1.4 %collective-permute-start.26 = (bf16[8,3584]{1,0:T(8,128)(2,1)S(1)}, bf16[8,3584]{1,0:T(8,128)(2,1)S(1)}, u32[]{:S(2)}, u32[]{:S(2)}) collective-permute-start(bf16[8,3584]{1,0:T(8,128)(2,1)S(1)} %get-tuple-element.65), channel_id=1, source_target_pairs={{0,4},{1,17},{2,6},{3,19},{4,0},{5,21},{6,2},{7,23},{8,12},{9,25},... | collective-permute-start | bytes 172040 | tf_op jit(solution)/shard_map/ppermute | solution.py:35
  91.1 2.0 %collective-permute-start.27 = (bf16[8,3584]{1,0:T(8,128)(2,1)S(1)}, bf16[8,3584]{1,0:T(8,128)(2,1)S(1)}, u32[]{:S(2)}, u32[]{:S(2)}) collective-permute-start(bf16[8,3584]{1,0:T(8,128)(2,1)S(1)} %get-tuple-element.64), channel_id=1, source_target_pairs={{0,6},{1,25},{2,0},{3,27},{4,2},{5,29},{6,4},{7,31},{8,14},{9,1},{... | collective-permute-start | bytes 172040 | tf_op jit(solution)/shard_map/ppermute | solution.py:35
  94.8 3.0 %collective-permute-start.28 = (bf16[4,3584]{1,0:T(4,128)(2,1)S(1)}, bf16[4,3584]{1,0:T(4,128)(2,1)S(1)}, u32[]{:S(2)}, u32[]{:S(2)}) collective-permute-start(bf16[4,3584]{1,0:T(4,128)(2,1)S(1)} %get-tuple-element.68), channel_id=1, source_target_pairs={{0,1},{1,0},{2,3},{3,2},{4,5},{5,4},{6,7},{7,6},{8,9},{9,8},{10,11... | collective-permute-start | bytes 86024 | tf_op jit(solution)/shard_map/ppermute | solution.py:15
  (72 shorter events, 17.1 us)
Async XLA Ops:
  0.0 32.6 %collective-permute-start.3 = (bf16[256,7168]{1,0:T(8,128)(2,1)}, bf16[256,7168]{1,0:T(8,128)(2,1)}, u32[]{:S(2)}, u32[]{:S(2)}) collective-permute-start(bf16[256,7168]{1,0:T(8,128)(2,1)} %om_ref.1), channel_id=1, source_target_pairs={{0,1},{1,0},{2,3},{3,2},{4,5},{5,4},{6,7},{7,6},{8,9},{9,8},{10,11... | collective-permute-start | bytes 11010056 | tf_op jit(solution)/shard_map/ppermute | solution.py:15
  1.4 29.5 %collective-permute-start.1 = (bf16[288,1792]{1,0:T(8,128)(2,1)}, bf16[288,1792]{1,0:T(8,128)(2,1)S(1)}, u32[]{:S(2)}, u32[]{:S(2)}) collective-permute-start(bf16[288,1792]{1,0:T(8,128)(2,1)} %param.21), channel_id=1, source_target_pairs={{0,0},{64,1},{2,2},{66,3},{4,4},{68,5},{6,6},{70,7},{8,8},{72,9},{... | collective-permute-start | bytes 3096584 | tf_op jit(solution)/shard_map/ppermute | solution.py:53
  14.4 14.9 %all-to-all-start = ((bf16[16,16,512]{2,1,0:T(8,128)(2,1)}), bf16[16,16,512]{2,1,0:T(8,128)(2,1)S(1)}, u32[]{:S(2)}, u32[]{:S(2)}) async-start(bf16[16,16,512]{2,1,0:T(8,128)(2,1)} %bitcast.28), calls=%async_computation | async-start | bytes 524288 | tf_op jit(solution)/shard_map/all_to_all | solution.py:20
  21.2 24.1 %collective-permute-start.8 = (bf16[288,1792]{1,0:T(8,128)(2,1)}, bf16[288,1792]{1,0:T(8,128)(2,1)S(1)}, u32[]{:S(2)}, u32[]{:S(2)}) collective-permute-start(bf16[288,1792]{1,0:T(8,128)(2,1)} %param.21), channel_id=1, source_target_pairs={{1,0},{65,1},{3,2},{67,3},{5,4},{69,5},{7,6},{71,7},{9,8},{73,9},{... | collective-permute-start | bytes 3096584 | tf_op jit(solution)/shard_map/ppermute | solution.py:53
  21.3 9.6 %collective-permute-start.2 = (bf16[2,512,128]{2,1,0:T(8,128)(2,1)S(1)}, bf16[2,512,128]{2,1,0:T(8,128)(2,1)S(1)}, u32[]{:S(2)}, u32[]{:S(2)}) collective-permute-start(bf16[2,512,128]{2,1,0:T(8,128)(2,1)S(1)} %copy-done.4), channel_id=1, source_target_pairs={{0,1},{1,0},{2,3},{3,2},{4,5},{5,4},{6,7},{7,6},{8,9},{9,8},{10,11... | collective-permute-start | bytes 786440 | tf_op jit(solution)/shard_map/ppermute | solution.py:15
  30.8 7.6 %collective-permute-start.7 = (bf16[4,3584]{1,0:T(4,128)(2,1)S(1)}, bf16[4,3584]{1,0:T(4,128)(2,1)S(1)}, u32[]{:S(2)}, u32[]{:S(2)}) collective-permute-start(bf16[4,3584]{1,0:T(4,128)(2,1)S(1)} %get-tuple-element.70), channel_id=1, source_target_pairs={{0,1},{1,0},{2,3},{3,2},{4,5},{5,4},{6,7},{7,6},{8,9},{9,8},{10,11... | collective-permute-start | bytes 86024 | tf_op jit(solution)/shard_map/ppermute | solution.py:15
  35.6 8.9 %collective-permute-start.4 = (bf16[32,3584]{1,0:T(8,128)(2,1)S(1)}, bf16[32,3584]{1,0:T(8,128)(2,1)S(1)}, u32[]{:S(2)}, u32[]{:S(2)}) collective-permute-start(bf16[32,3584]{1,0:T(8,128)(2,1)S(1)} %get-tuple-element.42), channel_id=1, source_target_pairs={{0,8},{1,3},{2,10},{3,5},{4,12},{5,7},{6,14},{7,1},{8,16},{9,11},{... | collective-permute-start | bytes 688136 | tf_op jit(solution)/shard_map/ppermute | solution.py:35
  35.9 8.6 %collective-permute-start.5 = (bf16[32,3584]{1,0:T(8,128)(2,1)S(1)}, bf16[32,3584]{1,0:T(8,128)(2,1)S(1)}, u32[]{:S(2)}, u32[]{:S(2)}) collective-permute-start(bf16[32,3584]{1,0:T(8,128)(2,1)S(1)} %get-tuple-element.43), channel_id=1, source_target_pairs={{0,16},{1,5},{2,18},{3,7},{4,20},{5,1},{6,22},{7,3},{8,24},{9,13},... | collective-permute-start | bytes 688136 | tf_op jit(solution)/shard_map/ppermute | solution.py:35
  37.3 7.8 %collective-permute-start.6 = (bf16[32,3584]{1,0:T(8,128)(2,1)S(1)}, bf16[32,3584]{1,0:T(8,128)(2,1)S(1)}, u32[]{:S(2)}, u32[]{:S(2)}) collective-permute-start(bf16[32,3584]{1,0:T(8,128)(2,1)S(1)} %get-tuple-element.44), channel_id=1, source_target_pairs={{0,24},{1,7},{2,26},{3,1},{4,28},{5,3},{6,30},{7,5},{8,0},{9,15},{... | collective-permute-start | bytes 688136 | tf_op jit(solution)/shard_map/ppermute | solution.py:35
  38.5 17.1 %collective-permute-start.19 = (bf16[288,1792]{1,0:T(8,128)(2,1)S(1)}, bf16[288,1792]{1,0:T(8,128)(2,1)S(1)}, u32[]{:S(2)}, u32[]{:S(2)}) collective-permute-start(bf16[288,1792]{1,0:T(8,128)(2,1)S(1)} %copy-done.6), channel_id=1, source_target_pairs={{32,0},{96,1},{34,2},{98,3},{36,4},{100,5},{38,6},{102,7},{40,8},{... | collective-permute-start | bytes 3096584 | tf_op jit(solution)/shard_map/ppermute | solution.py:53
  45.3 15.6 %collective-permute-start.10 = (bf16[32,3584]{1,0:T(8,128)(2,1)S(1)}, bf16[32,3584]{1,0:T(8,128)(2,1)S(1)}, u32[]{:S(2)}, u32[]{:S(2)}) collective-permute-start(bf16[32,3584]{1,0:T(8,128)(2,1)S(1)} %fusion.1), channel_id=1, source_target_pairs={{0,4},{1,17},{2,6},{3,19},{4,0},{5,21},{6,2},{7,23},{8,12},{9,25},... | collective-permute-start | bytes 688136 | tf_op jit(solution)/shard_map/ppermute | solution.py:35
  45.9 14.9 %collective-permute-start.11 = (bf16[32,3584]{1,0:T(8,128)(2,1)S(1)}, bf16[32,3584]{1,0:T(8,128)(2,1)S(1)}, u32[]{:S(2)}, u32[]{:S(2)}) collective-permute-start(bf16[32,3584]{1,0:T(8,128)(2,1)S(1)} %fusion.1), channel_id=1, source_target_pairs={{0,6},{1,25},{2,0},{3,27},{4,2},{5,29},{6,4},{7,31},{8,14},{9,1},{... | collective-permute-start | bytes 688136 | tf_op jit(solution)/shard_map/ppermute | solution.py:35
  47.5 13.4 %collective-permute-start.9 = (bf16[32,3584]{1,0:T(8,128)(2,1)S(1)}, bf16[32,3584]{1,0:T(8,128)(2,1)S(1)}, u32[]{:S(2)}, u32[]{:S(2)}) collective-permute-start(bf16[32,3584]{1,0:T(8,128)(2,1)S(1)} %fusion.1), channel_id=1, source_target_pairs={{0,2},{1,9},{2,4},{3,11},{4,6},{5,13},{6,0},{7,15},{8,10},{9,17},{... | collective-permute-start | bytes 688136 | tf_op jit(solution)/shard_map/ppermute | solution.py:35
  55.6 20.7 %collective-permute-start.20 = (bf16[288,1792]{1,0:T(8,128)(2,1)S(1)}, bf16[288,1792]{1,0:T(8,128)(2,1)S(1)}, u32[]{:S(2)}, u32[]{:S(2)}) collective-permute-start(bf16[288,1792]{1,0:T(8,128)(2,1)S(1)} %copy-done.6), channel_id=1, source_target_pairs={{33,0},{97,1},{35,2},{99,3},{37,4},{101,5},{39,6},{103,7},{41,8},{... | collective-permute-start | bytes 3096584 | tf_op jit(solution)/shard_map/ppermute | solution.py:53
  61.0 5.2 %collective-permute-start.12 = (bf16[32,3584]{1,0:T(8,128)(2,1)S(1)}, bf16[32,3584]{1,0:T(8,128)(2,1)S(1)}, u32[]{:S(2)}, u32[]{:S(2)}) collective-permute-start(bf16[32,3584]{1,0:T(8,128)(2,1)S(1)} %add_convert_fusion.1.refs_0_), channel_id=1, source_target_pairs={{0,24},{1,7},{2,26},{3,1},{4,28},{5,3},{6,30},{7,5},{8,0},{9,15},{... | collective-permute-start | bytes 688136 | tf_op jit(solution)/shard_map/ppermute | solution.py:35
  62.0 6.6 %collective-permute-start.13 = (bf16[32,3584]{1,0:T(8,128)(2,1)S(1)}, bf16[32,3584]{1,0:T(8,128)(2,1)S(1)}, u32[]{:S(2)}, u32[]{:S(2)}) collective-permute-start(bf16[32,3584]{1,0:T(8,128)(2,1)S(1)} %add_convert_fusion.1.refs_0_), channel_id=1, source_target_pairs={{0,16},{1,5},{2,18},{3,7},{4,20},{5,1},{6,22},{7,3},{8,24},{9,13},... | collective-permute-start | bytes 688136 | tf_op jit(solution)/shard_map/ppermute | solution.py:35
  63.2 7.9 %collective-permute-start.14 = (bf16[32,3584]{1,0:T(8,128)(2,1)S(1)}, bf16[32,3584]{1,0:T(8,128)(2,1)S(1)}, u32[]{:S(2)}, u32[]{:S(2)}) collective-permute-start(bf16[32,3584]{1,0:T(8,128)(2,1)S(1)} %add_convert_fusion.1.refs_0_), channel_id=1, source_target_pairs={{0,8},{1,3},{2,10},{3,5},{4,12},{5,7},{6,14},{7,1},{8,16},{9,11},{... | collective-permute-start | bytes 688136 | tf_op jit(solution)/shard_map/ppermute | solution.py:35
  79.5 8.9 %collective-permute-start.22 = (bf16[32,3584]{1,0:T(8,128)(2,1)S(1)}, bf16[32,3584]{1,0:T(8,128)(2,1)S(1)}, u32[]{:S(2)}, u32[]{:S(2)}) collective-permute-start(bf16[32,3584]{1,0:T(8,128)(2,1)S(1)} %get-tuple-element.60), channel_id=1, source_target_pairs={{0,8},{1,3},{2,10},{3,5},{4,12},{5,7},{6,14},{7,1},{8,16},{9,11},{... | collective-permute-start | bytes 688136 | tf_op jit(solution)/shard_map/ppermute | solution.py:35
  79.8 8.7 %collective-permute-start.23 = (bf16[32,3584]{1,0:T(8,128)(2,1)S(1)}, bf16[32,3584]{1,0:T(8,128)(2,1)S(1)}, u32[]{:S(2)}, u32[]{:S(2)}) collective-permute-start(bf16[32,3584]{1,0:T(8,128)(2,1)S(1)} %get-tuple-element.61), channel_id=1, source_target_pairs={{0,16},{1,5},{2,18},{3,7},{4,20},{5,1},{6,22},{7,3},{8,24},{9,13},... | collective-permute-start | bytes 688136 | tf_op jit(solution)/shard_map/ppermute | solution.py:35
  81.6 7.5 %collective-permute-start.24 = (bf16[32,3584]{1,0:T(8,128)(2,1)S(1)}, bf16[32,3584]{1,0:T(8,128)(2,1)S(1)}, u32[]{:S(2)}, u32[]{:S(2)}) collective-permute-start(bf16[32,3584]{1,0:T(8,128)(2,1)S(1)} %get-tuple-element.62), channel_id=1, source_target_pairs={{0,24},{1,7},{2,26},{3,1},{4,28},{5,3},{6,30},{7,5},{8,0},{9,15},{... | collective-permute-start | bytes 688136 | tf_op jit(solution)/shard_map/ppermute | solution.py:35
  89.2 4.3 %collective-permute-start.25 = (bf16[8,3584]{1,0:T(8,128)(2,1)S(1)}, bf16[8,3584]{1,0:T(8,128)(2,1)S(1)}, u32[]{:S(2)}, u32[]{:S(2)}) collective-permute-start(bf16[8,3584]{1,0:T(8,128)(2,1)S(1)} %get-tuple-element.63), channel_id=1, source_target_pairs={{0,2},{1,9},{2,4},{3,11},{4,6},{5,13},{6,0},{7,15},{8,10},{9,17},{... | collective-permute-start | bytes 172040 | tf_op jit(solution)/shard_map/ppermute | solution.py:35
  89.7 4.5 %collective-permute-start.26 = (bf16[8,3584]{1,0:T(8,128)(2,1)S(1)}, bf16[8,3584]{1,0:T(8,128)(2,1)S(1)}, u32[]{:S(2)}, u32[]{:S(2)}) collective-permute-start(bf16[8,3584]{1,0:T(8,128)(2,1)S(1)} %get-tuple-element.65), channel_id=1, source_target_pairs={{0,4},{1,17},{2,6},{3,19},{4,0},{5,21},{6,2},{7,23},{8,12},{9,25},... | collective-permute-start | bytes 172040 | tf_op jit(solution)/shard_map/ppermute | solution.py:35
  91.1 3.6 %collective-permute-start.27 = (bf16[8,3584]{1,0:T(8,128)(2,1)S(1)}, bf16[8,3584]{1,0:T(8,128)(2,1)S(1)}, u32[]{:S(2)}, u32[]{:S(2)}) collective-permute-start(bf16[8,3584]{1,0:T(8,128)(2,1)S(1)} %get-tuple-element.64), channel_id=1, source_target_pairs={{0,6},{1,25},{2,0},{3,27},{4,2},{5,29},{6,4},{7,31},{8,14},{9,1},{... | collective-permute-start | bytes 172040 | tf_op jit(solution)/shard_map/ppermute | solution.py:35
  94.8 3.8 %collective-permute-start.28 = (bf16[4,3584]{1,0:T(4,128)(2,1)S(1)}, bf16[4,3584]{1,0:T(4,128)(2,1)S(1)}, u32[]{:S(2)}, u32[]{:S(2)}) collective-permute-start(bf16[4,3584]{1,0:T(4,128)(2,1)S(1)} %get-tuple-element.68), channel_id=1, source_target_pairs={{0,1},{1,0},{2,3},{3,2},{4,5},{5,4},{6,7},{7,6},{8,9},{9,8},{10,11... | collective-permute-start | bytes 86024 | tf_op jit(solution)/shard_map/ppermute | solution.py:15
  (13 other events, 181.5 us)

commit v14 on v13

--- a/solution.py
+++ b/solution.py
@@ -90,12 +90,12 @@
 
         def score(slot):
             copies[slot].wait()
-            place = lax.broadcasted_iota(jnp.int32, (heads, ctx), 1)
-            found = product(q_ref[slot], held_ref[slot]) * score_scale
-            return jnp.where(place < lengths_ref[slot], found, -1e30)
+            place = lax.broadcasted_iota(jnp.int32, (1, ctx), 1)
+            hidden = jnp.where(place < lengths_ref[slot], 0.0, -1e30)
+            return product(q_ref[slot], held_ref[slot]) * (score_scale * math.log2(math.e)) + hidden
 
         def gather(slot, scores):
-            raised = jnp.exp(scores - jnp.max(scores, axis=1, keepdims=True))
+            raised = jnp.exp2(scores - jnp.max(scores, axis=1, keepdims=True))
             latent = lax.dot_general(
                 raised.astype(jnp.bfloat16),
                 held_ref[slot, :latent_width],
@@ -187,25 +187,39 @@
     depth, model = output_mine.shape
     half = model // 2
     line = rows // side
+    cuts = 2
+    span = half // cuts
 
     def kernel(spot_ref, value_ref, om_ref, oo_ref, *refs):
-        outs, (held_ref, sem) = refs[:side], refs[side:]
+        outs, (held_ref, sems) = refs[:side], refs[side:]
+        copies = []
+        for cut in range(cuts):
+            start = pl.multiple_of(spot_ref[0] * half + cut * span, 128)
+            copies.append(
+                pltpu.make_async_copy(
+                    oo_ref.at[:, pl.ds(start, span)], held_ref.at[cut], sems.at[cut]
+                )
+            )
+            copies[-1].start()
         at = pl.ds(pl.multiple_of(spot_ref[0] * half, 128), half)
-        copy = pltpu.make_async_copy(oo_ref.at[:, at], held_ref, sem)
-        copy.start()
-        result = product(value_ref[:, :depth], om_ref[:, at])
-        copy.wait()
-        result = result + product(value_ref[:, depth:], held_ref[...])
-        result = result.astype(jnp.bfloat16)
-        for k in range(side):
-            outs[k][...] = result[k * line : (k + 1) * line]
+        mine = product(value_ref[:, :depth], om_ref[:, at])
+        for cut in range(cuts):
+            part = slice(cut * span, (cut + 1) * span)
+            copies[cut].wait()
+            result = mine[:, part] + product(value_ref[:, depth:], held_ref[cut])
+            result = result.astype(jnp.bfloat16)
+            for k in range(side):
+                outs[k][:, part] = result[k * line : (k + 1) * line]
 
     return pl.pallas_call(
         kernel,
         in_specs=[in_smem] + [in_vmem] * 2 + [in_hbm],
         out_specs=[in_vmem] * side,
         out_shape=[jax.ShapeDtypeStruct((line, half), jnp.bfloat16)] * side,
-        scratch_shapes=[pltpu.VMEM((depth, half), jnp.bfloat16), pltpu.SemaphoreType.DMA],
+        scratch_shapes=[
+            pltpu.VMEM((cuts, depth, span), jnp.bfloat16),
+            pltpu.SemaphoreType.DMA((cuts,)),
+        ],
         compiler_params=budget(24),
         cost_estimate=pl.CostEstimate(
             flops=4 * rows * depth * half, bytes_accessed=4 * depth * half, transcendentals=0

time: 99.7 us -> 99.3 us (level)
  transfers between devices with their start and end apart: 30 -> 30, of which waited for: 15 -> 15; matrix products, arithmetic and copies ran while one was open for 1% -> 1% of each run, Pallas kernels for 18% -> 17%
where the time goes in v14:
time: 99.3 us; the launch traced here: 99 us
  starting transfers between devices  43.2 us (44%)
  waiting for transfers between devices  34.4 us (35%)
  Pallas kernels  18.8 us (19%)
  other arithmetic  1.31 us (1%)
  between operations  1 us (1%)
    ppermute x15, waiting for transfers between devices, turn(): out[k] = lax.ppermute(parts[k], 'tp', pairs)  17.8 us
    ppermute x15, starting transfers between devices, turn(): out[k] = lax.ppermute(parts[k], 'tp', pairs)  14.4 us
    ppermute x4, starting transfers between devices, down_piece(): return lax.ppermute(down_weight, ('dp', 'tp'), pairs)  13.4 us
    pallas_call x1, Pallas kernels, attend(): pl.pallas_call(kernel, in_specs=[in_smem, in_smem, in_vmem, in_hbm], out_...  8.61 us
    ppermute x10, starting transfers between devices, core_swap(): return lax.ppermute(x, 'tp', [(i, i ^ 1) for i in range(width)])  8.58 us
    ppermute x4, waiting for transfers between devices, down_piece(): return lax.ppermute(down_weight, ('dp', 'tp'), pairs)  8.04 us
    all_to_all x1, starting transfers between devices, between_chips(): return lax.all_to_all(x, 'tp', 0, 0, tiled=True, axis_index_groups=groups)  6.78 us
    all_to_all x1, waiting for transfers between devices, between_chips(): return lax.all_to_all(x, 'tp', 0, 0, tiled=True, axis_index_groups=groups)  5.23 us
  transfers between devices with their start and end apart: 30, of which 15 were waited for; matrix products, arithmetic and copies ran while one was open for 1% of the time, Pallas kernels for 17%

profile of v14, /device:TPU:1, one launch (start us, length us, event | category | flops | bytes accessed | tf_op | source)
XLA Modules:
  0.0 99.0 jit_solution(11051344637048644413)
XLA Ops:
  1.4 3.5 %collective-permute-start.1 = (bf16[288,1792]{1,0:T(8,128)(2,1)}, bf16[288,1792]{1,0:T(8,128)(2,1)S(1)}, u32[]{:S(2)}, u32[]{:S(2)}) collective-permute-start(bf16[288,1792]{1,0:T(8,128)(2,1)} %param.21), channel_id=1, source_target_pairs={{0,0},{64,1},{2,2},{66,3},{4,4},{68,5},{6,6},{70,7},{8,8},{72,9},{... | collective-permute-start | bytes 3096584 | tf_op jit(solution)/shard_map/ppermute | solution.py:53
  5.7 8.6 %shard_map.109 = bf16[256,512]{1,0:T(8,128)(2,1)} custom-call(s32[4]{0:T(128)} %lengths_ref.1, s32[1]{0:T(128)} %copy.12.counts_ref, bf16[4,64,576]{2,1,0:T(8,128)(2,1)} %q_ref, bf16[4,576,2048]{2,1,0:T(8,128)(2,1)} %bitcast.27), custom_call_target="tpu_custom_call" | custom-call | flops 1140850688 | bytes 9437184 | tf_op jit(solution)/shard_map/pallas_call | solution.py:122
  14.4 6.8 %all-to-all-start = ((bf16[16,16,512]{2,1,0:T(8,128)(2,1)}), bf16[16,16,512]{2,1,0:T(8,128)(2,1)S(1)}, u32[]{:S(2)}, u32[]{:S(2)}) async-start(bf16[16,16,512]{2,1,0:T(8,128)(2,1)} %bitcast.28), calls=%async_computation | async-start | bytes 524288 | tf_op jit(solution)/shard_map/all_to_all | solution.py:20
  21.3 2.6 %collective-permute-start.2 = (bf16[2,512,128]{2,1,0:T(8,128)(2,1)S(1)}, bf16[2,512,128]{2,1,0:T(8,128)(2,1)S(1)}, u32[]{:S(2)}, u32[]{:S(2)}) collective-permute-start(bf16[2,512,128]{2,1,0:T(8,128)(2,1)S(1)} %copy-done.4), channel_id=1, source_target_pairs={{0,1},{1,0},{2,3},{3,2},{4,5},{5,4},{6,7},{7,6},{8,9},{9,8},{10,11... | collective-permute-start | bytes 786440 | tf_op jit(solution)/shard_map/ppermute | solution.py:15
  24.0 5.2 %all-to-all-done = bf16[16,16,512]{2,1,0:T(8,128)(2,1)S(1)} async-done(((bf16[16,16,512]{2,1,0:T(8,128)(2,1)}), bf16[16,16,512]{2,1,0:T(8,128)(2,1)S(1)}, u32[]{:S(2)}, u32[]{:S(2)}) %all-to-all-start) | async-done | bytes 262176 | tf_op jit(solution)/shard_map/all_to_all | solution.py:20
  29.3 1.5 %collective-permute-done = bf16[16,16,512]{2,1,0:T(8,128)(2,1)S(1)} collective-permute-done((bf16[16,16,512]{2,1,0:T(8,128)(2,1)S(1)}, bf16[16,16,512]{2,1,0:T(8,128)(2,1)S(1)}, u32[]{:S(2)}, u32[]{:S(2)}) %collective-permute-start) | collective-permute-done | bytes 262176 | tf_op jit(solution)/shard_map/ppermute | solution.py:15
  30.9 1.6 %shard_map.110.value_ref = bf16[128,512]{1,0:T(8,128)(2,1)S(1)} custom-call(s32[4]{0:T(128)S(1)} %pad_add_fusion.spot_ref, bf16[256,512]{1,0:T(8,128)(2,1)S(1)} %bitcast.23, bf16[256,512]{1,0:T(8,128)(2,1)S(1)} %bitcast.26, bf16[2,512,128]{2,1,0:T(8,128)(2,1)S(1)} %copy-done.4, bf16[2,512,128]{2,1,0:T(8,128)(2,1)S(1)} %collective-permute-done.2.vo_ref), custom_call_target="tpu_custom_call" | custom-call | flops 1610612736 | bytes 524288 | tf_op jit(solution)/shard_map/pallas_call | solution.py:167
  32.6 2.7 %shard_map.111 = (bf16[32,3584]{1,0:T(8,128)(2,1)S(1)}, bf16[32,3584]{1,0:T(8,128)(2,1)S(1)}, bf16[32,3584]{1,0:T(8,128)(2,1)S(1)}, bf16[32,3584]{1,0:T(8,128)(2,1)S(1)}) custom-call(s32[4]{0:T(128)S(1)} %pad_add_fusion.spot_ref, bf16[128,512]{1,0:T(8,128)(2,1)S(1)} %shard_map.110.value_ref, bf16[256,7168]{1,0:T(8,128)(2,1)S(1)} %copy-done.2, ...), custom_call_target="tpu_custom_call" | custom-call | flops 469762048 | bytes 3670016 | tf_op jit(solution)/shard_map/pallas_call | solution.py:214
  38.1 4.5 %collective-permute-start.19 = (bf16[288,1792]{1,0:T(8,128)(2,1)S(1)}, bf16[288,1792]{1,0:T(8,128)(2,1)S(1)}, u32[]{:S(2)}, u32[]{:S(2)}) collective-permute-start(bf16[288,1792]{1,0:T(8,128)(2,1)S(1)} %copy-done.6), channel_id=1, source_target_pairs={{32,0},{96,1},{34,2},{98,3},{36,4},{100,5},{38,6},{102,7},{40,8},{... | collective-permute-start | bytes 3096584 | tf_op jit(solution)/shard_map/ppermute | solution.py:53
  42.6 1.5 %collective-permute-done.4 = bf16[32,3584]{1,0:T(8,128)(2,1)S(1)} collective-permute-done((bf16[32,3584]{1,0:T(8,128)(2,1)S(1)}, bf16[32,3584]{1,0:T(8,128)(2,1)S(1)}, u32[]{:S(2)}, u32[]{:S(2)}) %collective-permute-start.4) | collective-permute-done | bytes 229408 | tf_op jit(solution)/shard_map/ppermute | solution.py:35
  45.6 1.6 %collective-permute-start.11 = (bf16[32,3584]{1,0:T(8,128)(2,1)S(1)}, bf16[32,3584]{1,0:T(8,128)(2,1)S(1)}, u32[]{:S(2)}, u32[]{:S(2)}) collective-permute-start(bf16[32,3584]{1,0:T(8,128)(2,1)S(1)} %fusion.1), channel_id=1, source_target_pairs={{0,6},{1,25},{2,0},{3,27},{4,2},{5,29},{6,4},{7,31},{8,14},{9,1},{... | collective-permute-start | bytes 688136 | tf_op jit(solution)/shard_map/ppermute | solution.py:35
  47.2 8.0 %collective-permute-done.19.c_ref = bf16[288,1792]{1,0:T(8,128)(2,1)S(1)} collective-permute-done((bf16[288,1792]{1,0:T(8,128)(2,1)S(1)}, bf16[288,1792]{1,0:T(8,128)(2,1)S(1)}, u32[]{:S(2)}, u32[]{:S(2)}) %collective-permute-start.19) | collective-permute-done | bytes 1032224 | tf_op jit(solution)/shard_map/ppermute | solution.py:53
  55.2 5.3 %collective-permute-start.20 = (bf16[288,1792]{1,0:T(8,128)(2,1)S(1)}, bf16[288,1792]{1,0:T(8,128)(2,1)S(1)}, u32[]{:S(2)}, u32[]{:S(2)}) collective-permute-start(bf16[288,1792]{1,0:T(8,128)(2,1)S(1)} %copy-done.6), channel_id=1, source_target_pairs={{33,0},{97,1},{35,2},{99,3},{37,4},{101,5},{39,6},{103,7},{41,8},{... | collective-permute-start | bytes 3096584 | tf_op jit(solution)/shard_map/ppermute | solution.py:53
  62.8 3.1 %collective-permute-done.12.refs_1_ = bf16[32,3584]{1,0:T(8,128)(2,1)S(1)} collective-permute-done((bf16[32,3584]{1,0:T(8,128)(2,1)S(1)}, bf16[32,3584]{1,0:T(8,128)(2,1)S(1)}, u32[]{:S(2)}, u32[]{:S(2)}) %collective-permute-start.12) | collective-permute-done | bytes 229408 | tf_op jit(solution)/shard_map/ppermute | solution.py:35
  65.9 2.3 %collective-permute-done.13.refs_2_ = bf16[32,3584]{1,0:T(8,128)(2,1)S(1)} collective-permute-done((bf16[32,3584]{1,0:T(8,128)(2,1)S(1)}, bf16[32,3584]{1,0:T(8,128)(2,1)S(1)}, u32[]{:S(2)}, u32[]{:S(2)}) %collective-permute-start.13) | collective-permute-done | bytes 229408 | tf_op jit(solution)/shard_map/ppermute | solution.py:35
  68.2 2.5 %collective-permute-done.14.refs_3_ = bf16[32,3584]{1,0:T(8,128)(2,1)S(1)} collective-permute-done((bf16[32,3584]{1,0:T(8,128)(2,1)S(1)}, bf16[32,3584]{1,0:T(8,128)(2,1)S(1)}, u32[]{:S(2)}, u32[]{:S(2)}) %collective-permute-start.14) | collective-permute-done | bytes 229408 | tf_op jit(solution)/shard_map/ppermute | solution.py:35
  71.7 1.9 %shard_map.112 = (f32[128,576]{1,0:T(8,128)S(1)}, f32[128,128]{1,0:T(8,128)S(1)}) custom-call(s32[4]{0:T(128)S(1)} %pad_add_fusion.spot_ref, bf16[32,3584]{1,0:T(8,128)(2,1)S(1)} %add_convert_fusion.1.refs_0_, bf16[32,3584]{1,0:T(8,128)(2,1)S(1)} %collective-permute-done.12.refs_1_, bf16[32,3584]{1,0:T(8,128)(2,1)S(1)} %collective-permute-done.13.refs_2_, ...), custom_call_target="tpu_custom_call" | custom-call | flops 528482304 | bytes 4128768 | tf_op jit(solution)/shard_map/pallas_call | solution.py:274
  73.7 2.3 %shard_map.113.inner_ref = bf16[128,288]{1,0:T(8,128)(2,1)S(1)} custom-call(s32[4]{0:T(128)S(1)} %pad_add_fusion.spot_ref, bf16[32,3584]{1,0:T(8,128)(2,1)S(1)} %collective-permute-done.15.refs_0_, bf16[32,3584]{1,0:T(8,128)(2,1)S(1)} %collective-permute-done.16.refs_1_, bf16[32,3584]{1,0:T(8,128)(2,1)S(1)} %collective-permute-done.17.refs_2_, ...), custom_call_target="tpu_custom_call" | custom-call | flops 528482304 | bytes 4128768 | tf_op jit(solution)/shard_map/pallas_call | solution.py:274
  77.4 1.8 %shard_map.114 = (bf16[32,3584]{1,0:T(8,128)(2,1)S(1)}, bf16[32,3584]{1,0:T(8,128)(2,1)S(1)}, bf16[32,3584]{1,0:T(8,128)(2,1)S(1)}, bf16[32,3584]{1,0:T(8,128)(2,1)S(1)}) custom-call(s32[4]{0:T(128)S(1)} %pad_add_fusion.spot_ref, bf16[128,288]{1,0:T(8,128)(2,1)S(1)} %shard_map.113.inner_ref, bf16[128,288]{1,0:T(8,128)(2,1)S(1)} %collective-permute-done.21.other_ref, ...), custom_call_target="tpu_custom_call" | custom-call | flops 528482304 | bytes 4128768 | tf_op jit(solution)/shard_map/pallas_call | solution.py:313
  79.5 1.7 %collective-permute-start.23 = (bf16[32,3584]{1,0:T(8,128)(2,1)S(1)}, bf16[32,3584]{1,0:T(8,128)(2,1)S(1)}, u32[]{:S(2)}, u32[]{:S(2)}) collective-permute-start(bf16[32,3584]{1,0:T(8,128)(2,1)S(1)} %get-tuple-element.61), channel_id=1, source_target_pairs={{0,16},{1,5},{2,18},{3,7},{4,20},{5,1},{6,22},{7,3},{8,24},{9,13},... | collective-permute-start | bytes 688136 | tf_op jit(solution)/shard_map/ppermute | solution.py:35
  82.5 5.5 %collective-permute-done.22 = bf16[32,3584]{1,0:T(8,128)(2,1)S(1)} collective-permute-done((bf16[32,3584]{1,0:T(8,128)(2,1)S(1)}, bf16[32,3584]{1,0:T(8,128)(2,1)S(1)}, u32[]{:S(2)}, u32[]{:S(2)}) %collective-permute-start.22) | collective-permute-done | bytes 229408 | tf_op jit(solution)/shard_map/ppermute | solution.py:35
  89.3 1.4 %collective-permute-start.26 = (bf16[8,3584]{1,0:T(8,128)(2,1)S(1)}, bf16[8,3584]{1,0:T(8,128)(2,1)S(1)}, u32[]{:S(2)}, u32[]{:S(2)}) collective-permute-start(bf16[8,3584]{1,0:T(8,128)(2,1)S(1)} %get-tuple-element.65), channel_id=1, source_target_pairs={{0,4},{1,17},{2,6},{3,19},{4,0},{5,21},{6,2},{7,23},{8,12},{9,25},... | collective-permute-start | bytes 172040 | tf_op jit(solution)/shard_map/ppermute | solution.py:35
  90.7 2.0 %collective-permute-start.27 = (bf16[8,3584]{1,0:T(8,128)(2,1)S(1)}, bf16[8,3584]{1,0:T(8,128)(2,1)S(1)}, u32[]{:S(2)}, u32[]{:S(2)}) collective-permute-start(bf16[8,3584]{1,0:T(8,128)(2,1)S(1)} %get-tuple-element.64), channel_id=1, source_target_pairs={{0,6},{1,25},{2,0},{3,27},{4,2},{5,29},{6,4},{7,31},{8,14},{9,1},{... | collective-permute-start | bytes 172040 | tf_op jit(solution)/shard_map/ppermute | solution.py:35
  94.5 3.0 %collective-permute-start.28 = (bf16[4,3584]{1,0:T(4,128)(2,1)S(1)}, bf16[4,3584]{1,0:T(4,128)(2,1)S(1)}, u32[]{:S(2)}, u32[]{:S(2)}) collective-permute-start(bf16[4,3584]{1,0:T(4,128)(2,1)S(1)} %get-tuple-element.68), channel_id=1, source_target_pairs={{0,1},{1,0},{2,3},{3,2},{4,5},{5,4},{6,7},{7,6},{8,9},{9,8},{10,11... | collective-permute-start | bytes 86024 | tf_op jit(solution)/shard_map/ppermute | solution.py:15
  (72 shorter events, 17.2 us)
Async XLA Ops:
  0.0 32.5 %collective-permute-start.3 = (bf16[256,7168]{1,0:T(8,128)(2,1)}, bf16[256,7168]{1,0:T(8,128)(2,1)}, u32[]{:S(2)}, u32[]{:S(2)}) collective-permute-start(bf16[256,7168]{1,0:T(8,128)(2,1)} %om_ref.1), channel_id=1, source_target_pairs={{0,1},{1,0},{2,3},{3,2},{4,5},{5,4},{6,7},{7,6},{8,9},{9,8},{10,11... | collective-permute-start | bytes 11010056 | tf_op jit(solution)/shard_map/ppermute | solution.py:15
  1.4 29.5 %collective-permute-start.1 = (bf16[288,1792]{1,0:T(8,128)(2,1)}, bf16[288,1792]{1,0:T(8,128)(2,1)S(1)}, u32[]{:S(2)}, u32[]{:S(2)}) collective-permute-start(bf16[288,1792]{1,0:T(8,128)(2,1)} %param.21), channel_id=1, source_target_pairs={{0,0},{64,1},{2,2},{66,3},{4,4},{68,5},{6,6},{70,7},{8,8},{72,9},{... | collective-permute-start | bytes 3096584 | tf_op jit(solution)/shard_map/ppermute | solution.py:53
  14.4 14.9 %all-to-all-start = ((bf16[16,16,512]{2,1,0:T(8,128)(2,1)}), bf16[16,16,512]{2,1,0:T(8,128)(2,1)S(1)}, u32[]{:S(2)}, u32[]{:S(2)}) async-start(bf16[16,16,512]{2,1,0:T(8,128)(2,1)} %bitcast.28), calls=%async_computation | async-start | bytes 524288 | tf_op jit(solution)/shard_map/all_to_all | solution.py:20
  21.2 23.8 %collective-permute-start.8 = (bf16[288,1792]{1,0:T(8,128)(2,1)}, bf16[288,1792]{1,0:T(8,128)(2,1)S(1)}, u32[]{:S(2)}, u32[]{:S(2)}) collective-permute-start(bf16[288,1792]{1,0:T(8,128)(2,1)} %param.21), channel_id=1, source_target_pairs={{1,0},{65,1},{3,2},{67,3},{5,4},{69,5},{7,6},{71,7},{9,8},{73,9},{... | collective-permute-start | bytes 3096584 | tf_op jit(solution)/shard_map/ppermute | solution.py:53
  21.3 9.6 %collective-permute-start.2 = (bf16[2,512,128]{2,1,0:T(8,128)(2,1)S(1)}, bf16[2,512,128]{2,1,0:T(8,128)(2,1)S(1)}, u32[]{:S(2)}, u32[]{:S(2)}) collective-permute-start(bf16[2,512,128]{2,1,0:T(8,128)(2,1)S(1)} %copy-done.4), channel_id=1, source_target_pairs={{0,1},{1,0},{2,3},{3,2},{4,5},{5,4},{6,7},{7,6},{8,9},{9,8},{10,11... | collective-permute-start | bytes 786440 | tf_op jit(solution)/shard_map/ppermute | solution.py:15
  30.8 7.3 %collective-permute-start.7 = (bf16[4,3584]{1,0:T(4,128)(2,1)S(1)}, bf16[4,3584]{1,0:T(4,128)(2,1)S(1)}, u32[]{:S(2)}, u32[]{:S(2)}) collective-permute-start(bf16[4,3584]{1,0:T(4,128)(2,1)S(1)} %get-tuple-element.70), channel_id=1, source_target_pairs={{0,1},{1,0},{2,3},{3,2},{4,5},{5,4},{6,7},{7,6},{8,9},{9,8},{10,11... | collective-permute-start | bytes 86024 | tf_op jit(solution)/shard_map/ppermute | solution.py:15
  35.2 8.9 %collective-permute-start.4 = (bf16[32,3584]{1,0:T(8,128)(2,1)S(1)}, bf16[32,3584]{1,0:T(8,128)(2,1)S(1)}, u32[]{:S(2)}, u32[]{:S(2)}) collective-permute-start(bf16[32,3584]{1,0:T(8,128)(2,1)S(1)} %get-tuple-element.42), channel_id=1, source_target_pairs={{0,8},{1,3},{2,10},{3,5},{4,12},{5,7},{6,14},{7,1},{8,16},{9,11},{... | collective-permute-start | bytes 688136 | tf_op jit(solution)/shard_map/ppermute | solution.py:35
  35.6 8.6 %collective-permute-start.5 = (bf16[32,3584]{1,0:T(8,128)(2,1)S(1)}, bf16[32,3584]{1,0:T(8,128)(2,1)S(1)}, u32[]{:S(2)}, u32[]{:S(2)}) collective-permute-start(bf16[32,3584]{1,0:T(8,128)(2,1)S(1)} %get-tuple-element.43), channel_id=1, source_target_pairs={{0,16},{1,5},{2,18},{3,7},{4,20},{5,1},{6,22},{7,3},{8,24},{9,13},... | collective-permute-start | bytes 688136 | tf_op jit(solution)/shard_map/ppermute | solution.py:35
  37.0 7.8 %collective-permute-start.6 = (bf16[32,3584]{1,0:T(8,128)(2,1)S(1)}, bf16[32,3584]{1,0:T(8,128)(2,1)S(1)}, u32[]{:S(2)}, u32[]{:S(2)}) collective-permute-start(bf16[32,3584]{1,0:T(8,128)(2,1)S(1)} %get-tuple-element.44), channel_id=1, source_target_pairs={{0,24},{1,7},{2,26},{3,1},{4,28},{5,3},{6,30},{7,5},{8,0},{9,15},{... | collective-permute-start | bytes 688136 | tf_op jit(solution)/shard_map/ppermute | solution.py:35
  38.1 17.1 %collective-permute-start.19 = (bf16[288,1792]{1,0:T(8,128)(2,1)S(1)}, bf16[288,1792]{1,0:T(8,128)(2,1)S(1)}, u32[]{:S(2)}, u32[]{:S(2)}) collective-permute-start(bf16[288,1792]{1,0:T(8,128)(2,1)S(1)} %copy-done.6), channel_id=1, source_target_pairs={{32,0},{96,1},{34,2},{98,3},{36,4},{100,5},{38,6},{102,7},{40,8},{... | collective-permute-start | bytes 3096584 | tf_op jit(solution)/shard_map/ppermute | solution.py:53
  44.9 15.6 %collective-permute-start.10 = (bf16[32,3584]{1,0:T(8,128)(2,1)S(1)}, bf16[32,3584]{1,0:T(8,128)(2,1)S(1)}, u32[]{:S(2)}, u32[]{:S(2)}) collective-permute-start(bf16[32,3584]{1,0:T(8,128)(2,1)S(1)} %fusion.1), channel_id=1, source_target_pairs={{0,4},{1,17},{2,6},{3,19},{4,0},{5,21},{6,2},{7,23},{8,12},{9,25},... | collective-permute-start | bytes 688136 | tf_op jit(solution)/shard_map/ppermute | solution.py:35
  45.6 14.9 %collective-permute-start.11 = (bf16[32,3584]{1,0:T(8,128)(2,1)S(1)}, bf16[32,3584]{1,0:T(8,128)(2,1)S(1)}, u32[]{:S(2)}, u32[]{:S(2)}) collective-permute-start(bf16[32,3584]{1,0:T(8,128)(2,1)S(1)} %fusion.1), channel_id=1, source_target_pairs={{0,6},{1,25},{2,0},{3,27},{4,2},{5,29},{6,4},{7,31},{8,14},{9,1},{... | collective-permute-start | bytes 688136 | tf_op jit(solution)/shard_map/ppermute | solution.py:35
  47.2 13.4 %collective-permute-start.9 = (bf16[32,3584]{1,0:T(8,128)(2,1)S(1)}, bf16[32,3584]{1,0:T(8,128)(2,1)S(1)}, u32[]{:S(2)}, u32[]{:S(2)}) collective-permute-start(bf16[32,3584]{1,0:T(8,128)(2,1)S(1)} %fusion.1), channel_id=1, source_target_pairs={{0,2},{1,9},{2,4},{3,11},{4,6},{5,13},{6,0},{7,15},{8,10},{9,17},{... | collective-permute-start | bytes 688136 | tf_op jit(solution)/shard_map/ppermute | solution.py:35
  55.2 20.7 %collective-permute-start.20 = (bf16[288,1792]{1,0:T(8,128)(2,1)S(1)}, bf16[288,1792]{1,0:T(8,128)(2,1)S(1)}, u32[]{:S(2)}, u32[]{:S(2)}) collective-permute-start(bf16[288,1792]{1,0:T(8,128)(2,1)S(1)} %copy-done.6), channel_id=1, source_target_pairs={{33,0},{97,1},{35,2},{99,3},{37,4},{101,5},{39,6},{103,7},{41,8},{... | collective-permute-start | bytes 3096584 | tf_op jit(solution)/shard_map/ppermute | solution.py:53
  60.7 5.2 %collective-permute-start.12 = (bf16[32,3584]{1,0:T(8,128)(2,1)S(1)}, bf16[32,3584]{1,0:T(8,128)(2,1)S(1)}, u32[]{:S(2)}, u32[]{:S(2)}) collective-permute-start(bf16[32,3584]{1,0:T(8,128)(2,1)S(1)} %add_convert_fusion.1.refs_0_), channel_id=1, source_target_pairs={{0,24},{1,7},{2,26},{3,1},{4,28},{5,3},{6,30},{7,5},{8,0},{9,15},{... | collective-permute-start | bytes 688136 | tf_op jit(solution)/shard_map/ppermute | solution.py:35
  61.6 6.6 %collective-permute-start.13 = (bf16[32,3584]{1,0:T(8,128)(2,1)S(1)}, bf16[32,3584]{1,0:T(8,128)(2,1)S(1)}, u32[]{:S(2)}, u32[]{:S(2)}) collective-permute-start(bf16[32,3584]{1,0:T(8,128)(2,1)S(1)} %add_convert_fusion.1.refs_0_), channel_id=1, source_target_pairs={{0,16},{1,5},{2,18},{3,7},{4,20},{5,1},{6,22},{7,3},{8,24},{9,13},... | collective-permute-start | bytes 688136 | tf_op jit(solution)/shard_map/ppermute | solution.py:35
  62.8 7.9 %collective-permute-start.14 = (bf16[32,3584]{1,0:T(8,128)(2,1)S(1)}, bf16[32,3584]{1,0:T(8,128)(2,1)S(1)}, u32[]{:S(2)}, u32[]{:S(2)}) collective-permute-start(bf16[32,3584]{1,0:T(8,128)(2,1)S(1)} %add_convert_fusion.1.refs_0_), channel_id=1, source_target_pairs={{0,8},{1,3},{2,10},{3,5},{4,12},{5,7},{6,14},{7,1},{8,16},{9,11},{... | collective-permute-start | bytes 688136 | tf_op jit(solution)/shard_map/ppermute | solution.py:35
  79.2 8.9 %collective-permute-start.22 = (bf16[32,3584]{1,0:T(8,128)(2,1)S(1)}, bf16[32,3584]{1,0:T(8,128)(2,1)S(1)}, u32[]{:S(2)}, u32[]{:S(2)}) collective-permute-start(bf16[32,3584]{1,0:T(8,128)(2,1)S(1)} %get-tuple-element.60), channel_id=1, source_target_pairs={{0,8},{1,3},{2,10},{3,5},{4,12},{5,7},{6,14},{7,1},{8,16},{9,11},{... | collective-permute-start | bytes 688136 | tf_op jit(solution)/shard_map/ppermute | solution.py:35
  79.5 8.6 %collective-permute-start.23 = (bf16[32,3584]{1,0:T(8,128)(2,1)S(1)}, bf16[32,3584]{1,0:T(8,128)(2,1)S(1)}, u32[]{:S(2)}, u32[]{:S(2)}) collective-permute-start(bf16[32,3584]{1,0:T(8,128)(2,1)S(1)} %get-tuple-element.61), channel_id=1, source_target_pairs={{0,16},{1,5},{2,18},{3,7},{4,20},{5,1},{6,22},{7,3},{8,24},{9,13},... | collective-permute-start | bytes 688136 | tf_op jit(solution)/shard_map/ppermute | solution.py:35
  81.2 7.5 %collective-permute-start.24 = (bf16[32,3584]{1,0:T(8,128)(2,1)S(1)}, bf16[32,3584]{1,0:T(8,128)(2,1)S(1)}, u32[]{:S(2)}, u32[]{:S(2)}) collective-permute-start(bf16[32,3584]{1,0:T(8,128)(2,1)S(1)} %get-tuple-element.62), channel_id=1, source_target_pairs={{0,24},{1,7},{2,26},{3,1},{4,28},{5,3},{6,30},{7,5},{8,0},{9,15},{... | collective-permute-start | bytes 688136 | tf_op jit(solution)/shard_map/ppermute | solution.py:35
  88.8 4.3 %collective-permute-start.25 = (bf16[8,3584]{1,0:T(8,128)(2,1)S(1)}, bf16[8,3584]{1,0:T(8,128)(2,1)S(1)}, u32[]{:S(2)}, u32[]{:S(2)}) collective-permute-start(bf16[8,3584]{1,0:T(8,128)(2,1)S(1)} %get-tuple-element.63), channel_id=1, source_target_pairs={{0,2},{1,9},{2,4},{3,11},{4,6},{5,13},{6,0},{7,15},{8,10},{9,17},{... | collective-permute-start | bytes 172040 | tf_op jit(solution)/shard_map/ppermute | solution.py:35
  89.3 4.5 %collective-permute-start.26 = (bf16[8,3584]{1,0:T(8,128)(2,1)S(1)}, bf16[8,3584]{1,0:T(8,128)(2,1)S(1)}, u32[]{:S(2)}, u32[]{:S(2)}) collective-permute-start(bf16[8,3584]{1,0:T(8,128)(2,1)S(1)} %get-tuple-element.65), channel_id=1, source_target_pairs={{0,4},{1,17},{2,6},{3,19},{4,0},{5,21},{6,2},{7,23},{8,12},{9,25},... | collective-permute-start | bytes 172040 | tf_op jit(solution)/shard_map/ppermute | solution.py:35
  90.7 3.6 %collective-permute-start.27 = (bf16[8,3584]{1,0:T(8,128)(2,1)S(1)}, bf16[8,3584]{1,0:T(8,128)(2,1)S(1)}, u32[]{:S(2)}, u32[]{:S(2)}) collective-permute-start(bf16[8,3584]{1,0:T(8,128)(2,1)S(1)} %get-tuple-element.64), channel_id=1, source_target_pairs={{0,6},{1,25},{2,0},{3,27},{4,2},{5,29},{6,4},{7,31},{8,14},{9,1},{... | collective-permute-start | bytes 172040 | tf_op jit(solution)/shard_map/ppermute | solution.py:35
  94.5 3.8 %collective-permute-start.28 = (bf16[4,3584]{1,0:T(4,128)(2,1)S(1)}, bf16[4,3584]{1,0:T(4,128)(2,1)S(1)}, u32[]{:S(2)}, u32[]{:S(2)}) collective-permute-start(bf16[4,3584]{1,0:T(4,128)(2,1)S(1)} %get-tuple-element.68), channel_id=1, source_target_pairs={{0,1},{1,0},{2,3},{3,2},{4,5},{5,4},{6,7},{7,6},{8,9},{9,8},{10,11... | collective-permute-start | bytes 86024 | tf_op jit(solution)/shard_map/ppermute | solution.py:15
  (13 other events, 180.1 us)

commit v15 on v14

--- a/solution.py
+++ b/solution.py
@@ -76,13 +76,13 @@
     return pltpu.CompilerParams(vmem_limit_bytes=mib * 2**20)
 
 
-def attend(query, cache, lengths, counts, latent_width, chips):
+def attend(query, cache, lengths, latent_width, chips):
     slots, heads, wide = query.shape
     ctx = cache.shape[1]
     group = heads // chips
     rows = slots * heads
 
-    def kernel(lengths_ref, counts_ref, q_ref, cache_ref, out_ref, held_ref, sems):
+    def kernel(lengths_ref, q_ref, cache_ref, out_ref, held_ref, sems):
         copies = [
             pltpu.make_async_copy(cache_ref.at[slot], held_ref.at[slot], sems.at[slot])
             for slot in range(slots)
@@ -103,7 +103,7 @@
                 preferred_element_type=jnp.float32,
             )
             latent = latent / jnp.sum(raised, axis=1, keepdims=True)
-            return jnp.where(slot < counts_ref[0], latent, 0.0).astype(jnp.bfloat16)
+            return latent.astype(jnp.bfloat16)
 
         for copy in copies:
             copy.start()
@@ -121,7 +121,7 @@
 
     out = pl.pallas_call(
         kernel,
-        in_specs=[in_smem, in_smem, in_vmem, in_hbm],
+        in_specs=[in_smem, in_vmem, in_hbm],
         out_specs=in_vmem,
         out_shape=jax.ShapeDtypeStruct((rows, latent_width), jnp.bfloat16),
         scratch_shapes=[
@@ -134,7 +134,7 @@
             bytes_accessed=2 * cache.size,
             transcendentals=rows * ctx,
         ),
-    )(lengths, counts, query, jnp.swapaxes(cache, 1, 2))
+    )(lengths, query, jnp.swapaxes(cache, 1, 2))
     return out.reshape(chips, slots * group, latent_width)
 
 
@@ -366,7 +366,7 @@
     ).astype(jnp.float32)
 
     query, spot = lax.optimization_barrier((query, spot))
-    latent = attend(query, cache, lengths, counts, latent_width, chips)
+    latent = attend(query, cache, lengths, latent_width, chips)
     arrived = between_chips(latent, width)
     arrived_other = core_swap(arrived, width)
     arrived_other, pieces[0] = lax.optimization_barrier((arrived_other, pieces[0]))

time: 99.3 us -> 98.6 us (level)
  transfers between devices with their start and end apart: 30 -> 30, of which waited for: 15 -> 14; matrix products, arithmetic and copies ran while one was open for 1% -> 1% of each run, Pallas kernels for 17% -> 17%
where the time goes in v15:
time: 98.6 us; the launch traced here: 98.3 us
  starting transfers between devices  43.1 us (44%)
  waiting for transfers between devices  33.7 us (34%)
  Pallas kernels  18.9 us (19%)
  other arithmetic  1.31 us (1%)
  between operations  1 us (1%)
    ppermute x15, waiting for transfers between devices, turn(): out[k] = lax.ppermute(parts[k], 'tp', pairs)  17.1 us
    ppermute x15, starting transfers between devices, turn(): out[k] = lax.ppermute(parts[k], 'tp', pairs)  14.5 us
    ppermute x4, starting transfers between devices, down_piece(): return lax.ppermute(down_weight, ('dp', 'tp'), pairs)  13.4 us
    pallas_call x1, Pallas kernels, attend(): pl.pallas_call(kernel, in_specs=[in_smem, in_vmem, in_hbm], out_specs=in_...  8.62 us
    ppermute x10, starting transfers between devices, core_swap(): return lax.ppermute(x, 'tp', [(i, i ^ 1) for i in range(width)])  8.55 us
    ppermute x4, waiting for transfers between devices, down_piece(): return lax.ppermute(down_weight, ('dp', 'tp'), pairs)  8.05 us
    all_to_all x1, starting transfers between devices, between_chips(): return lax.all_to_all(x, 'tp', 0, 0, tiled=True, axis_index_groups=groups)  6.76 us
    all_to_all x1, waiting for transfers between devices, between_chips(): return lax.all_to_all(x, 'tp', 0, 0, tiled=True, axis_index_groups=groups)  5.23 us
  transfers between devices with their start and end apart: 30, of which 14 were waited for; matrix products, arithmetic and copies ran while one was open for 1% of the time, Pallas kernels for 17%

profile of v15, /device:TPU:1, one launch (start us, length us, event | category | flops | bytes accessed | tf_op | source)
XLA Modules:
  0.0 98.3 jit_solution(5853958658166008740)
XLA Ops:
  1.4 3.5 %collective-permute-start.1 = (bf16[288,1792]{1,0:T(8,128)(2,1)}, bf16[288,1792]{1,0:T(8,128)(2,1)S(1)}, u32[]{:S(2)}, u32[]{:S(2)}) collective-permute-start(bf16[288,1792]{1,0:T(8,128)(2,1)} %param.21), channel_id=1, source_target_pairs={{0,0},{64,1},{2,2},{66,3},{4,4},{68,5},{6,6},{70,7},{8,8},{72,9},{... | collective-permute-start | bytes 3096584 | tf_op jit(solution)/shard_map/ppermute | solution.py:53
  5.1 8.6 %shard_map.109 = bf16[256,512]{1,0:T(8,128)(2,1)} custom-call(s32[4]{0:T(128)} %lengths_ref.1, bf16[4,64,576]{2,1,0:T(8,128)(2,1)} %q_ref, bf16[4,576,2048]{2,1,0:T(8,128)(2,1)} %bitcast.27), custom_call_target="tpu_custom_call" | custom-call | flops 1140850688 | bytes 9437184 | tf_op jit(solution)/shard_map/pallas_call | solution.py:122
  13.7 6.8 %all-to-all-start = ((bf16[16,16,512]{2,1,0:T(8,128)(2,1)}), bf16[16,16,512]{2,1,0:T(8,128)(2,1)S(1)}, u32[]{:S(2)}, u32[]{:S(2)}) async-start(bf16[16,16,512]{2,1,0:T(8,128)(2,1)} %bitcast.28), calls=%async_computation | async-start | bytes 524288 | tf_op jit(solution)/shard_map/all_to_all | solution.py:20
  20.6 2.6 %collective-permute-start.2 = (bf16[2,512,128]{2,1,0:T(8,128)(2,1)S(1)}, bf16[2,512,128]{2,1,0:T(8,128)(2,1)S(1)}, u32[]{:S(2)}, u32[]{:S(2)}) collective-permute-start(bf16[2,512,128]{2,1,0:T(8,128)(2,1)S(1)} %copy-done.4), channel_id=1, source_target_pairs={{0,1},{1,0},{2,3},{3,2},{4,5},{5,4},{6,7},{7,6},{8,9},{9,8},{10,11... | collective-permute-start | bytes 786440 | tf_op jit(solution)/shard_map/ppermute | solution.py:15
  23.3 5.2 %all-to-all-done = bf16[16,16,512]{2,1,0:T(8,128)(2,1)S(1)} async-done(((bf16[16,16,512]{2,1,0:T(8,128)(2,1)}), bf16[16,16,512]{2,1,0:T(8,128)(2,1)S(1)}, u32[]{:S(2)}, u32[]{:S(2)}) %all-to-all-start) | async-done | bytes 262176 | tf_op jit(solution)/shard_map/all_to_all | solution.py:20
  28.6 1.5 %collective-permute-done = bf16[16,16,512]{2,1,0:T(8,128)(2,1)S(1)} collective-permute-done((bf16[16,16,512]{2,1,0:T(8,128)(2,1)S(1)}, bf16[16,16,512]{2,1,0:T(8,128)(2,1)S(1)}, u32[]{:S(2)}, u32[]{:S(2)}) %collective-permute-start) | collective-permute-done | bytes 262176 | tf_op jit(solution)/shard_map/ppermute | solution.py:15
  30.2 1.6 %shard_map.110.value_ref = bf16[128,512]{1,0:T(8,128)(2,1)S(1)} custom-call(s32[4]{0:T(128)S(1)} %pad_add_fusion.spot_ref, bf16[256,512]{1,0:T(8,128)(2,1)S(1)} %bitcast.23, bf16[256,512]{1,0:T(8,128)(2,1)S(1)} %bitcast.26, bf16[2,512,128]{2,1,0:T(8,128)(2,1)S(1)} %copy-done.4, bf16[2,512,128]{2,1,0:T(8,128)(2,1)S(1)} %collective-permute-done.2.vo_ref), custom_call_target="tpu_custom_call" | custom-call | flops 1610612736 | bytes 524288 | tf_op jit(solution)/shard_map/pallas_call | solution.py:167
  31.9 2.7 %shard_map.111 = (bf16[32,3584]{1,0:T(8,128)(2,1)S(1)}, bf16[32,3584]{1,0:T(8,128)(2,1)S(1)}, bf16[32,3584]{1,0:T(8,128)(2,1)S(1)}, bf16[32,3584]{1,0:T(8,128)(2,1)S(1)}) custom-call(s32[4]{0:T(128)S(1)} %pad_add_fusion.spot_ref, bf16[128,512]{1,0:T(8,128)(2,1)S(1)} %shard_map.110.value_ref, bf16[256,7168]{1,0:T(8,128)(2,1)S(1)} %copy-done.2, ...), custom_call_target="tpu_custom_call" | custom-call | flops 469762048 | bytes 3670016 | tf_op jit(solution)/shard_map/pallas_call | solution.py:214
  37.5 4.5 %collective-permute-start.19 = (bf16[288,1792]{1,0:T(8,128)(2,1)S(1)}, bf16[288,1792]{1,0:T(8,128)(2,1)S(1)}, u32[]{:S(2)}, u32[]{:S(2)}) collective-permute-start(bf16[288,1792]{1,0:T(8,128)(2,1)S(1)} %copy-done.6), channel_id=1, source_target_pairs={{32,0},{96,1},{34,2},{98,3},{36,4},{100,5},{38,6},{102,7},{40,8},{... | collective-permute-start | bytes 3096584 | tf_op jit(solution)/shard_map/ppermute | solution.py:53
  41.9 1.5 %collective-permute-done.4 = bf16[32,3584]{1,0:T(8,128)(2,1)S(1)} collective-permute-done((bf16[32,3584]{1,0:T(8,128)(2,1)S(1)}, bf16[32,3584]{1,0:T(8,128)(2,1)S(1)}, u32[]{:S(2)}, u32[]{:S(2)}) %collective-permute-start.4) | collective-permute-done | bytes 229408 | tf_op jit(solution)/shard_map/ppermute | solution.py:35
  44.9 1.6 %collective-permute-start.11 = (bf16[32,3584]{1,0:T(8,128)(2,1)S(1)}, bf16[32,3584]{1,0:T(8,128)(2,1)S(1)}, u32[]{:S(2)}, u32[]{:S(2)}) collective-permute-start(bf16[32,3584]{1,0:T(8,128)(2,1)S(1)} %fusion.1), channel_id=1, source_target_pairs={{0,6},{1,25},{2,0},{3,27},{4,2},{5,29},{6,4},{7,31},{8,14},{9,1},{... | collective-permute-start | bytes 688136 | tf_op jit(solution)/shard_map/ppermute | solution.py:35
  46.5 8.0 %collective-permute-done.19.c_ref = bf16[288,1792]{1,0:T(8,128)(2,1)S(1)} collective-permute-done((bf16[288,1792]{1,0:T(8,128)(2,1)S(1)}, bf16[288,1792]{1,0:T(8,128)(2,1)S(1)}, u32[]{:S(2)}, u32[]{:S(2)}) %collective-permute-start.19) | collective-permute-done | bytes 1032224 | tf_op jit(solution)/shard_map/ppermute | solution.py:53
  54.5 5.3 %collective-permute-start.20 = (bf16[288,1792]{1,0:T(8,128)(2,1)S(1)}, bf16[288,1792]{1,0:T(8,128)(2,1)S(1)}, u32[]{:S(2)}, u32[]{:S(2)}) collective-permute-start(bf16[288,1792]{1,0:T(8,128)(2,1)S(1)} %copy-done.6), channel_id=1, source_target_pairs={{33,0},{97,1},{35,2},{99,3},{37,4},{101,5},{39,6},{103,7},{41,8},{... | collective-permute-start | bytes 3096584 | tf_op jit(solution)/shard_map/ppermute | solution.py:53
  62.1 3.1 %collective-permute-done.12.refs_1_ = bf16[32,3584]{1,0:T(8,128)(2,1)S(1)} collective-permute-done((bf16[32,3584]{1,0:T(8,128)(2,1)S(1)}, bf16[32,3584]{1,0:T(8,128)(2,1)S(1)}, u32[]{:S(2)}, u32[]{:S(2)}) %collective-permute-start.12) | collective-permute-done | bytes 229408 | tf_op jit(solution)/shard_map/ppermute | solution.py:35
  65.2 2.3 %collective-permute-done.13.refs_2_ = bf16[32,3584]{1,0:T(8,128)(2,1)S(1)} collective-permute-done((bf16[32,3584]{1,0:T(8,128)(2,1)S(1)}, bf16[32,3584]{1,0:T(8,128)(2,1)S(1)}, u32[]{:S(2)}, u32[]{:S(2)}) %collective-permute-start.13) | collective-permute-done | bytes 229408 | tf_op jit(solution)/shard_map/ppermute | solution.py:35
  67.5 2.5 %collective-permute-done.14.refs_3_ = bf16[32,3584]{1,0:T(8,128)(2,1)S(1)} collective-permute-done((bf16[32,3584]{1,0:T(8,128)(2,1)S(1)}, bf16[32,3584]{1,0:T(8,128)(2,1)S(1)}, u32[]{:S(2)}, u32[]{:S(2)}) %collective-permute-start.14) | collective-permute-done | bytes 229408 | tf_op jit(solution)/shard_map/ppermute | solution.py:35
  71.0 1.9 %shard_map.112 = (f32[128,576]{1,0:T(8,128)S(1)}, f32[128,128]{1,0:T(8,128)S(1)}) custom-call(s32[4]{0:T(128)S(1)} %pad_add_fusion.spot_ref, bf16[32,3584]{1,0:T(8,128)(2,1)S(1)} %add_convert_fusion.1.refs_0_, bf16[32,3584]{1,0:T(8,128)(2,1)S(1)} %collective-permute-done.12.refs_1_, bf16[32,3584]{1,0:T(8,128)(2,1)S(1)} %collective-permute-done.13.refs_2_, ...), custom_call_target="tpu_custom_call" | custom-call | flops 528482304 | bytes 4128768 | tf_op jit(solution)/shard_map/pallas_call | solution.py:274
  73.0 2.3 %shard_map.113.inner_ref = bf16[128,288]{1,0:T(8,128)(2,1)S(1)} custom-call(s32[4]{0:T(128)S(1)} %pad_add_fusion.spot_ref, bf16[32,3584]{1,0:T(8,128)(2,1)S(1)} %collective-permute-done.15.refs_0_, bf16[32,3584]{1,0:T(8,128)(2,1)S(1)} %collective-permute-done.16.refs_1_, bf16[32,3584]{1,0:T(8,128)(2,1)S(1)} %collective-permute-done.17.refs_2_, ...), custom_call_target="tpu_custom_call" | custom-call | flops 528482304 | bytes 4128768 | tf_op jit(solution)/shard_map/pallas_call | solution.py:274
  76.7 1.8 %shard_map.114 = (bf16[32,3584]{1,0:T(8,128)(2,1)S(1)}, bf16[32,3584]{1,0:T(8,128)(2,1)S(1)}, bf16[32,3584]{1,0:T(8,128)(2,1)S(1)}, bf16[32,3584]{1,0:T(8,128)(2,1)S(1)}) custom-call(s32[4]{0:T(128)S(1)} %pad_add_fusion.spot_ref, bf16[128,288]{1,0:T(8,128)(2,1)S(1)} %shard_map.113.inner_ref, bf16[128,288]{1,0:T(8,128)(2,1)S(1)} %collective-permute-done.21.other_ref, ...), custom_call_target="tpu_custom_call" | custom-call | flops 528482304 | bytes 4128768 | tf_op jit(solution)/shard_map/pallas_call | solution.py:313
  78.7 1.8 %collective-permute-start.23 = (bf16[32,3584]{1,0:T(8,128)(2,1)S(1)}, bf16[32,3584]{1,0:T(8,128)(2,1)S(1)}, u32[]{:S(2)}, u32[]{:S(2)}) collective-permute-start(bf16[32,3584]{1,0:T(8,128)(2,1)S(1)} %get-tuple-element.61), channel_id=1, source_target_pairs={{0,16},{1,5},{2,18},{3,7},{4,20},{5,1},{6,22},{7,3},{8,24},{9,13},... | collective-permute-start | bytes 688136 | tf_op jit(solution)/shard_map/ppermute | solution.py:35
  81.9 5.5 %collective-permute-done.22 = bf16[32,3584]{1,0:T(8,128)(2,1)S(1)} collective-permute-done((bf16[32,3584]{1,0:T(8,128)(2,1)S(1)}, bf16[32,3584]{1,0:T(8,128)(2,1)S(1)}, u32[]{:S(2)}, u32[]{:S(2)}) %collective-permute-start.22) | collective-permute-done | bytes 229408 | tf_op jit(solution)/shard_map/ppermute | solution.py:35
  88.6 1.4 %collective-permute-start.26 = (bf16[8,3584]{1,0:T(8,128)(2,1)S(1)}, bf16[8,3584]{1,0:T(8,128)(2,1)S(1)}, u32[]{:S(2)}, u32[]{:S(2)}) collective-permute-start(bf16[8,3584]{1,0:T(8,128)(2,1)S(1)} %get-tuple-element.65), channel_id=1, source_target_pairs={{0,4},{1,17},{2,6},{3,19},{4,0},{5,21},{6,2},{7,23},{8,12},{9,25},... | collective-permute-start | bytes 172040 | tf_op jit(solution)/shard_map/ppermute | solution.py:35
  90.1 2.0 %collective-permute-start.27 = (bf16[8,3584]{1,0:T(8,128)(2,1)S(1)}, bf16[8,3584]{1,0:T(8,128)(2,1)S(1)}, u32[]{:S(2)}, u32[]{:S(2)}) collective-permute-start(bf16[8,3584]{1,0:T(8,128)(2,1)S(1)} %get-tuple-element.64), channel_id=1, source_target_pairs={{0,6},{1,25},{2,0},{3,27},{4,2},{5,29},{6,4},{7,31},{8,14},{9,1},{... | collective-permute-start | bytes 172040 | tf_op jit(solution)/shard_map/ppermute | solution.py:35
  93.8 3.0 %collective-permute-start.28 = (bf16[4,3584]{1,0:T(4,128)(2,1)S(1)}, bf16[4,3584]{1,0:T(4,128)(2,1)S(1)}, u32[]{:S(2)}, u32[]{:S(2)}) collective-permute-start(bf16[4,3584]{1,0:T(4,128)(2,1)S(1)} %get-tuple-element.68), channel_id=1, source_target_pairs={{0,1},{1,0},{2,3},{3,2},{4,5},{5,4},{6,7},{7,6},{8,9},{9,8},{10,11... | collective-permute-start | bytes 86024 | tf_op jit(solution)/shard_map/ppermute | solution.py:15
  (72 shorter events, 16.4 us)
Async XLA Ops:
  0.0 31.9 %collective-permute-start.3 = (bf16[256,7168]{1,0:T(8,128)(2,1)}, bf16[256,7168]{1,0:T(8,128)(2,1)}, u32[]{:S(2)}, u32[]{:S(2)}) collective-permute-start(bf16[256,7168]{1,0:T(8,128)(2,1)} %om_ref.1), channel_id=1, source_target_pairs={{0,1},{1,0},{2,3},{3,2},{4,5},{5,4},{6,7},{7,6},{8,9},{9,8},{10,11... | collective-permute-start | bytes 11010056 | tf_op jit(solution)/shard_map/ppermute | solution.py:15
  1.4 28.8 %collective-permute-start.1 = (bf16[288,1792]{1,0:T(8,128)(2,1)}, bf16[288,1792]{1,0:T(8,128)(2,1)S(1)}, u32[]{:S(2)}, u32[]{:S(2)}) collective-permute-start(bf16[288,1792]{1,0:T(8,128)(2,1)} %param.21), channel_id=1, source_target_pairs={{0,0},{64,1},{2,2},{66,3},{4,4},{68,5},{6,6},{70,7},{8,8},{72,9},{... | collective-permute-start | bytes 3096584 | tf_op jit(solution)/shard_map/ppermute | solution.py:53
  13.7 14.8 %all-to-all-start = ((bf16[16,16,512]{2,1,0:T(8,128)(2,1)}), bf16[16,16,512]{2,1,0:T(8,128)(2,1)S(1)}, u32[]{:S(2)}, u32[]{:S(2)}) async-start(bf16[16,16,512]{2,1,0:T(8,128)(2,1)} %bitcast.28), calls=%async_computation | async-start | bytes 524288 | tf_op jit(solution)/shard_map/all_to_all | solution.py:20
  20.5 23.8 %collective-permute-start.8 = (bf16[288,1792]{1,0:T(8,128)(2,1)}, bf16[288,1792]{1,0:T(8,128)(2,1)S(1)}, u32[]{:S(2)}, u32[]{:S(2)}) collective-permute-start(bf16[288,1792]{1,0:T(8,128)(2,1)} %param.21), channel_id=1, source_target_pairs={{1,0},{65,1},{3,2},{67,3},{5,4},{69,5},{7,6},{71,7},{9,8},{73,9},{... | collective-permute-start | bytes 3096584 | tf_op jit(solution)/shard_map/ppermute | solution.py:53
  20.6 9.6 %collective-permute-start.2 = (bf16[2,512,128]{2,1,0:T(8,128)(2,1)S(1)}, bf16[2,512,128]{2,1,0:T(8,128)(2,1)S(1)}, u32[]{:S(2)}, u32[]{:S(2)}) collective-permute-start(bf16[2,512,128]{2,1,0:T(8,128)(2,1)S(1)} %copy-done.4), channel_id=1, source_target_pairs={{0,1},{1,0},{2,3},{3,2},{4,5},{5,4},{6,7},{7,6},{8,9},{9,8},{10,11... | collective-permute-start | bytes 786440 | tf_op jit(solution)/shard_map/ppermute | solution.py:15
  30.1 7.3 %collective-permute-start.7 = (bf16[4,3584]{1,0:T(4,128)(2,1)S(1)}, bf16[4,3584]{1,0:T(4,128)(2,1)S(1)}, u32[]{:S(2)}, u32[]{:S(2)}) collective-permute-start(bf16[4,3584]{1,0:T(4,128)(2,1)S(1)} %get-tuple-element.70), channel_id=1, source_target_pairs={{0,1},{1,0},{2,3},{3,2},{4,5},{5,4},{6,7},{7,6},{8,9},{9,8},{10,11... | collective-permute-start | bytes 86024 | tf_op jit(solution)/shard_map/ppermute | solution.py:15
  34.6 8.9 %collective-permute-start.4 = (bf16[32,3584]{1,0:T(8,128)(2,1)S(1)}, bf16[32,3584]{1,0:T(8,128)(2,1)S(1)}, u32[]{:S(2)}, u32[]{:S(2)}) collective-permute-start(bf16[32,3584]{1,0:T(8,128)(2,1)S(1)} %get-tuple-element.42), channel_id=1, source_target_pairs={{0,8},{1,3},{2,10},{3,5},{4,12},{5,7},{6,14},{7,1},{8,16},{9,11},{... | collective-permute-start | bytes 688136 | tf_op jit(solution)/shard_map/ppermute | solution.py:35
  34.9 8.6 %collective-permute-start.5 = (bf16[32,3584]{1,0:T(8,128)(2,1)S(1)}, bf16[32,3584]{1,0:T(8,128)(2,1)S(1)}, u32[]{:S(2)}, u32[]{:S(2)}) collective-permute-start(bf16[32,3584]{1,0:T(8,128)(2,1)S(1)} %get-tuple-element.43), channel_id=1, source_target_pairs={{0,16},{1,5},{2,18},{3,7},{4,20},{5,1},{6,22},{7,3},{8,24},{9,13},... | collective-permute-start | bytes 688136 | tf_op jit(solution)/shard_map/ppermute | solution.py:35
  36.3 7.8 %collective-permute-start.6 = (bf16[32,3584]{1,0:T(8,128)(2,1)S(1)}, bf16[32,3584]{1,0:T(8,128)(2,1)S(1)}, u32[]{:S(2)}, u32[]{:S(2)}) collective-permute-start(bf16[32,3584]{1,0:T(8,128)(2,1)S(1)} %get-tuple-element.44), channel_id=1, source_target_pairs={{0,24},{1,7},{2,26},{3,1},{4,28},{5,3},{6,30},{7,5},{8,0},{9,15},{... | collective-permute-start | bytes 688136 | tf_op jit(solution)/shard_map/ppermute | solution.py:35
  37.5 17.1 %collective-permute-start.19 = (bf16[288,1792]{1,0:T(8,128)(2,1)S(1)}, bf16[288,1792]{1,0:T(8,128)(2,1)S(1)}, u32[]{:S(2)}, u32[]{:S(2)}) collective-permute-start(bf16[288,1792]{1,0:T(8,128)(2,1)S(1)} %copy-done.6), channel_id=1, source_target_pairs={{32,0},{96,1},{34,2},{98,3},{36,4},{100,5},{38,6},{102,7},{40,8},{... | collective-permute-start | bytes 3096584 | tf_op jit(solution)/shard_map/ppermute | solution.py:53
  44.3 15.6 %collective-permute-start.10 = (bf16[32,3584]{1,0:T(8,128)(2,1)S(1)}, bf16[32,3584]{1,0:T(8,128)(2,1)S(1)}, u32[]{:S(2)}, u32[]{:S(2)}) collective-permute-start(bf16[32,3584]{1,0:T(8,128)(2,1)S(1)} %fusion.1), channel_id=1, source_target_pairs={{0,4},{1,17},{2,6},{3,19},{4,0},{5,21},{6,2},{7,23},{8,12},{9,25},... | collective-permute-start | bytes 688136 | tf_op jit(solution)/shard_map/ppermute | solution.py:35
  44.9 14.9 %collective-permute-start.11 = (bf16[32,3584]{1,0:T(8,128)(2,1)S(1)}, bf16[32,3584]{1,0:T(8,128)(2,1)S(1)}, u32[]{:S(2)}, u32[]{:S(2)}) collective-permute-start(bf16[32,3584]{1,0:T(8,128)(2,1)S(1)} %fusion.1), channel_id=1, source_target_pairs={{0,6},{1,25},{2,0},{3,27},{4,2},{5,29},{6,4},{7,31},{8,14},{9,1},{... | collective-permute-start | bytes 688136 | tf_op jit(solution)/shard_map/ppermute | solution.py:35
  46.5 13.4 %collective-permute-start.9 = (bf16[32,3584]{1,0:T(8,128)(2,1)S(1)}, bf16[32,3584]{1,0:T(8,128)(2,1)S(1)}, u32[]{:S(2)}, u32[]{:S(2)}) collective-permute-start(bf16[32,3584]{1,0:T(8,128)(2,1)S(1)} %fusion.1), channel_id=1, source_target_pairs={{0,2},{1,9},{2,4},{3,11},{4,6},{5,13},{6,0},{7,15},{8,10},{9,17},{... | collective-permute-start | bytes 688136 | tf_op jit(solution)/shard_map/ppermute | solution.py:35
  54.5 20.7 %collective-permute-start.20 = (bf16[288,1792]{1,0:T(8,128)(2,1)S(1)}, bf16[288,1792]{1,0:T(8,128)(2,1)S(1)}, u32[]{:S(2)}, u32[]{:S(2)}) collective-permute-start(bf16[288,1792]{1,0:T(8,128)(2,1)S(1)} %copy-done.6), channel_id=1, source_target_pairs={{33,0},{97,1},{35,2},{99,3},{37,4},{101,5},{39,6},{103,7},{41,8},{... | collective-permute-start | bytes 3096584 | tf_op jit(solution)/shard_map/ppermute | solution.py:53
  60.0 5.2 %collective-permute-start.12 = (bf16[32,3584]{1,0:T(8,128)(2,1)S(1)}, bf16[32,3584]{1,0:T(8,128)(2,1)S(1)}, u32[]{:S(2)}, u32[]{:S(2)}) collective-permute-start(bf16[32,3584]{1,0:T(8,128)(2,1)S(1)} %add_convert_fusion.1.refs_0_), channel_id=1, source_target_pairs={{0,24},{1,7},{2,26},{3,1},{4,28},{5,3},{6,30},{7,5},{8,0},{9,15},{... | collective-permute-start | bytes 688136 | tf_op jit(solution)/shard_map/ppermute | solution.py:35
  61.0 6.6 %collective-permute-start.13 = (bf16[32,3584]{1,0:T(8,128)(2,1)S(1)}, bf16[32,3584]{1,0:T(8,128)(2,1)S(1)}, u32[]{:S(2)}, u32[]{:S(2)}) collective-permute-start(bf16[32,3584]{1,0:T(8,128)(2,1)S(1)} %add_convert_fusion.1.refs_0_), channel_id=1, source_target_pairs={{0,16},{1,5},{2,18},{3,7},{4,20},{5,1},{6,22},{7,3},{8,24},{9,13},... | collective-permute-start | bytes 688136 | tf_op jit(solution)/shard_map/ppermute | solution.py:35
  62.1 7.9 %collective-permute-start.14 = (bf16[32,3584]{1,0:T(8,128)(2,1)S(1)}, bf16[32,3584]{1,0:T(8,128)(2,1)S(1)}, u32[]{:S(2)}, u32[]{:S(2)}) collective-permute-start(bf16[32,3584]{1,0:T(8,128)(2,1)S(1)} %add_convert_fusion.1.refs_0_), channel_id=1, source_target_pairs={{0,8},{1,3},{2,10},{3,5},{4,12},{5,7},{6,14},{7,1},{8,16},{9,11},{... | collective-permute-start | bytes 688136 | tf_op jit(solution)/shard_map/ppermute | solution.py:35
  78.5 8.9 %collective-permute-start.22 = (bf16[32,3584]{1,0:T(8,128)(2,1)S(1)}, bf16[32,3584]{1,0:T(8,128)(2,1)S(1)}, u32[]{:S(2)}, u32[]{:S(2)}) collective-permute-start(bf16[32,3584]{1,0:T(8,128)(2,1)S(1)} %get-tuple-element.60), channel_id=1, source_target_pairs={{0,8},{1,3},{2,10},{3,5},{4,12},{5,7},{6,14},{7,1},{8,16},{9,11},{... | collective-permute-start | bytes 688136 | tf_op jit(solution)/shard_map/ppermute | solution.py:35
  78.7 8.6 %collective-permute-start.23 = (bf16[32,3584]{1,0:T(8,128)(2,1)S(1)}, bf16[32,3584]{1,0:T(8,128)(2,1)S(1)}, u32[]{:S(2)}, u32[]{:S(2)}) collective-permute-start(bf16[32,3584]{1,0:T(8,128)(2,1)S(1)} %get-tuple-element.61), channel_id=1, source_target_pairs={{0,16},{1,5},{2,18},{3,7},{4,20},{5,1},{6,22},{7,3},{8,24},{9,13},... | collective-permute-start | bytes 688136 | tf_op jit(solution)/shard_map/ppermute | solution.py:35
  80.5 7.5 %collective-permute-start.24 = (bf16[32,3584]{1,0:T(8,128)(2,1)S(1)}, bf16[32,3584]{1,0:T(8,128)(2,1)S(1)}, u32[]{:S(2)}, u32[]{:S(2)}) collective-permute-start(bf16[32,3584]{1,0:T(8,128)(2,1)S(1)} %get-tuple-element.62), channel_id=1, source_target_pairs={{0,24},{1,7},{2,26},{3,1},{4,28},{5,3},{6,30},{7,5},{8,0},{9,15},{... | collective-permute-start | bytes 688136 | tf_op jit(solution)/shard_map/ppermute | solution.py:35
  88.1 4.5 %collective-permute-start.25 = (bf16[8,3584]{1,0:T(8,128)(2,1)S(1)}, bf16[8,3584]{1,0:T(8,128)(2,1)S(1)}, u32[]{:S(2)}, u32[]{:S(2)}) collective-permute-start(bf16[8,3584]{1,0:T(8,128)(2,1)S(1)} %get-tuple-element.63), channel_id=1, source_target_pairs={{0,2},{1,9},{2,4},{3,11},{4,6},{5,13},{6,0},{7,15},{8,10},{9,17},{... | collective-permute-start | bytes 172040 | tf_op jit(solution)/shard_map/ppermute | solution.py:35
  88.6 4.5 %collective-permute-start.26 = (bf16[8,3584]{1,0:T(8,128)(2,1)S(1)}, bf16[8,3584]{1,0:T(8,128)(2,1)S(1)}, u32[]{:S(2)}, u32[]{:S(2)}) collective-permute-start(bf16[8,3584]{1,0:T(8,128)(2,1)S(1)} %get-tuple-element.65), channel_id=1, source_target_pairs={{0,4},{1,17},{2,6},{3,19},{4,0},{5,21},{6,2},{7,23},{8,12},{9,25},... | collective-permute-start | bytes 172040 | tf_op jit(solution)/shard_map/ppermute | solution.py:35
  90.1 3.6 %collective-permute-start.27 = (bf16[8,3584]{1,0:T(8,128)(2,1)S(1)}, bf16[8,3584]{1,0:T(8,128)(2,1)S(1)}, u32[]{:S(2)}, u32[]{:S(2)}) collective-permute-start(bf16[8,3584]{1,0:T(8,128)(2,1)S(1)} %get-tuple-element.64), channel_id=1, source_target_pairs={{0,6},{1,25},{2,0},{3,27},{4,2},{5,29},{6,4},{7,31},{8,14},{9,1},{... | collective-permute-start | bytes 172040 | tf_op jit(solution)/shard_map/ppermute | solution.py:35
  93.8 3.8 %collective-permute-start.28 = (bf16[4,3584]{1,0:T(4,128)(2,1)S(1)}, bf16[4,3584]{1,0:T(4,128)(2,1)S(1)}, u32[]{:S(2)}, u32[]{:S(2)}) collective-permute-start(bf16[4,3584]{1,0:T(4,128)(2,1)S(1)} %get-tuple-element.68), channel_id=1, source_target_pairs={{0,1},{1,0},{2,3},{3,2},{4,5},{5,4},{6,7},{7,6},{8,9},{9,8},{10,11... | collective-permute-start | bytes 86024 | tf_op jit(solution)/shard_map/ppermute | solution.py:15
  (13 other events, 180.1 us)

commit v16 on v15

--- a/solution.py
+++ b/solution.py
@@ -138,47 +138,49 @@
     return out.reshape(chips, slots * group, latent_width)
 
 
-def project(mine, other, value_mine, value_other, spot, side, slots):
-    chips, pairs, latent_width = mine.shape
+def project(latents, swapped, value_mine, value_other, spot, side, slots, before):
+    chips, pairs, latent_width = latents.shape
     heads_here, _, head = value_mine.shape
     heads = 2 * heads_here
     rows = 2 * chips * slots
     line = rows // side
     lines = chips * pairs
 
-    def kernel(spot_ref, mine_ref, other_ref, vm_ref, vo_ref, out_ref):
+    def kernel(spot_ref, latent_ref, vm_ref, vo_ref, *refs):
+        out_ref = refs[-1]
         core, first = spot_ref[0], spot_ref[1]
         to = line_numbers(rows)
         along = (to // line + first) % side
         second = to // (2 * slots) % side
         chip = jnp.where(core == 0, along * side + second, second * side + along)
         from_other = (to // slots % 2 + core) % 2
-        source = from_other * lines + chip * pairs + to % slots * heads
-        latents = jnp.concatenate([mine_ref[...], other_ref[...]], axis=0)
+        source = chip * pairs + to % slots * heads + (from_other != swapped) * (2 * lines)
         for index in range(heads):
             owner, weight_ref = (core, vm_ref) if index < heads_here else (1 - core, vo_ref)
             place = index % heads_here
-            pick = one_hot(source + owner * heads_here + place, 2 * lines)
-            picked = product(pick, latents).astype(jnp.bfloat16)
-            out_ref[:, index * head : (index + 1) * head] = product(
-                picked, weight_ref[place]
-            ).astype(jnp.bfloat16)
+            pick = one_hot(source + owner * heads_here + place, lines)
+            picked = product(pick, latent_ref[...]).astype(jnp.bfloat16)
+            value = product(picked, weight_ref[place]).astype(jnp.bfloat16)
+            part = slice(index * head, (index + 1) * head)
+            if swapped:
+                value = jnp.where(from_other == swapped, value, refs[0][:, part])
+            out_ref[:, part] = value
 
     return pl.pallas_call(
         kernel,
-        in_specs=[in_smem] + [in_vmem] * 4,
+        in_specs=[in_smem] + [in_vmem] * (3 + swapped),
         out_specs=in_vmem,
         out_shape=jax.ShapeDtypeStruct((rows, heads * head), jnp.bfloat16),
         compiler_params=budget(16),
         cost_estimate=pl.CostEstimate(
-            flops=64 * rows * latent_width * (lines + head), bytes_accessed=4 * mine.size, transcendentals=0
+            flops=64 * rows * latent_width * (lines + head), bytes_accessed=2 * latents.size, transcendentals=0
         ),
     )(
         spot,
-        mine.reshape(lines, latent_width),
-        other.reshape(lines, latent_width),
+        latents.reshape(lines, latent_width),
         value_mine,
         value_other,
+        *([before] if swapped else []),
     )
 
 
@@ -370,7 +372,8 @@
     arrived = between_chips(latent, width)
     arrived_other = core_swap(arrived, width)
     arrived_other, pieces[0] = lax.optimization_barrier((arrived_other, pieces[0]))
-    values = project(arrived, arrived_other, value_weight, value_other, spot, side, slots)
+    values = project(arrived, 0, value_weight, value_other, spot, side, slots, None)
+    values = project(arrived_other, 1, value_weight, value_other, spot, side, slots, values)
     attended_parts = sum_heads(values, output_weight, output_other, spot, side)
 
     attended_parts, later = lax.optimization_barrier((attended_parts, down_weight))

time: 98.6 us -> 101 us (1.024)
  Pallas kernels: 18.9 us -> 20.2 us
    ppermute x15, waiting for transfers between devices: 17.1 us -> 20 us  [turn(): out[k] = lax.ppermute(parts[k], 'tp', pairs)]
    ppermute x10, starting transfers between devices: 8.55 us -> 11.3 us  [core_swap(): return lax.ppermute(x, 'tp', [(i, i ^ 1) for i in range(width)])]
    ppermute x4, starting transfers between devices: 13.4 us -> 11.4 us  [down_piece(): return lax.ppermute(down_weight, ('dp', 'tp'), pairs)]
    ppermute x4, waiting for transfers between devices: 8.05 us -> 6.73 us  [down_piece(): return lax.ppermute(down_weight, ('dp', 'tp'), pairs)]
    pallas_call x1 -> x2, Pallas kernels: 1.59 us -> 2.82 us  [project(): pl.pallas_call(kernel, in_specs=[in_smem] + [in_vmem] * (3 + swapped), ou...]
    ppermute x10, waiting for transfers between devices: 3.3 us -> 2.14 us  [core_swap(): return lax.ppermute(x, 'tp', [(i, i ^ 1) for i in range(width)])]
  transfers between devices with their start and end apart: 30 -> 30, of which waited for: 14 -> 13; matrix products, arithmetic and copies ran while one was open for 1% -> 1% of each run, Pallas kernels for 17% -> 18%
where the time goes in v16:
time: 101 us
  starting transfers between devices  43.9 us (43%)
  waiting for transfers between devices  33.7 us (33%)
  Pallas kernels  20.2 us (20%)
  other arithmetic  1.3 us (1%)
  between operations  1.04 us (1%)
    ppermute x15, waiting for transfers between devices, turn(): out[k] = lax.ppermute(parts[k], 'tp', pairs)  20 us
    ppermute x15, starting transfers between devices, turn(): out[k] = lax.ppermute(parts[k], 'tp', pairs)  14.4 us
    ppermute x4, starting transfers between devices, down_piece(): return lax.ppermute(down_weight, ('dp', 'tp'), pairs)  11.4 us
    ppermute x10, starting transfers between devices, core_swap(): return lax.ppermute(x, 'tp', [(i, i ^ 1) for i in range(width)])  11.3 us
    pallas_call x1, Pallas kernels, attend(): pl.pallas_call(kernel, in_specs=[in_smem, in_vmem, in_hbm], out_specs=in_...  8.62 us
    all_to_all x1, starting transfers between devices, between_chips(): return lax.all_to_all(x, 'tp', 0, 0, tiled=True, axis_index_groups=groups)  6.76 us
    ppermute x4, waiting for transfers between devices, down_piece(): return lax.ppermute(down_weight, ('dp', 'tp'), pairs)  6.73 us
    all_to_all x1, waiting for transfers between devices, between_chips(): return lax.all_to_all(x, 'tp', 0, 0, tiled=True, axis_index_groups=groups)  4.91 us
  transfers between devices with their start and end apart: 30, of which 13 were waited for; matrix products, arithmetic and copies ran while one was open for 1% of the time, Pallas kernels for 18%

profile of v16, /device:TPU:1, one launch (start us, length us, event | category | flops | bytes accessed | tf_op | source)
XLA Modules:
  0.0 101.1 jit_solution(13397515628992742696)
XLA Ops:
  0.0 1.4 %collective-permute-start.3 = (bf16[256,7168]{1,0:T(8,128)(2,1)}, bf16[256,7168]{1,0:T(8,128)(2,1)}, u32[]{:S(2)}, u32[]{:S(2)}) collective-permute-start(bf16[256,7168]{1,0:T(8,128)(2,1)} %om_ref.1), channel_id=1, source_target_pairs={{0,1},{1,0},{2,3},{3,2},{4,5},{5,4},{6,7},{7,6},{8,9},{9,8},{10,11... | collective-permute-start | bytes 11010056 | tf_op jit(solution)/shard_map/ppermute | solution.py:15
  1.4 3.5 %collective-permute-start.1 = (bf16[288,1792]{1,0:T(8,128)(2,1)}, bf16[288,1792]{1,0:T(8,128)(2,1)S(1)}, u32[]{:S(2)}, u32[]{:S(2)}) collective-permute-start(bf16[288,1792]{1,0:T(8,128)(2,1)} %param.21), channel_id=1, source_target_pairs={{0,0},{64,1},{2,2},{66,3},{4,4},{68,5},{6,6},{70,7},{8,8},{72,9},{... | collective-permute-start | bytes 3096584 | tf_op jit(solution)/shard_map/ppermute | solution.py:53
  5.2 8.6 %shard_map.109 = bf16[256,512]{1,0:T(8,128)(2,1)} custom-call(s32[4]{0:T(128)} %lengths_ref.1, bf16[4,64,576]{2,1,0:T(8,128)(2,1)} %q_ref, bf16[4,576,2048]{2,1,0:T(8,128)(2,1)} %bitcast.27), custom_call_target="tpu_custom_call" | custom-call | flops 1140850688 | bytes 9437184 | tf_op jit(solution)/shard_map/pallas_call | solution.py:122
  13.8 6.8 %all-to-all-start = ((bf16[16,16,512]{2,1,0:T(8,128)(2,1)}), bf16[16,16,512]{2,1,0:T(8,128)(2,1)S(1)}, u32[]{:S(2)}, u32[]{:S(2)}) async-start(bf16[16,16,512]{2,1,0:T(8,128)(2,1)} %bitcast.28), calls=%async_computation | async-start | bytes 524288 | tf_op jit(solution)/shard_map/all_to_all | solution.py:20
  20.6 2.6 %collective-permute-start.2 = (bf16[2,512,128]{2,1,0:T(8,128)(2,1)S(1)}, bf16[2,512,128]{2,1,0:T(8,128)(2,1)S(1)}, u32[]{:S(2)}, u32[]{:S(2)}) collective-permute-start(bf16[2,512,128]{2,1,0:T(8,128)(2,1)S(1)} %copy-done.4), channel_id=1, source_target_pairs={{0,1},{1,0},{2,3},{3,2},{4,5},{5,4},{6,7},{7,6},{8,9},{9,8},{10,11... | collective-permute-start | bytes 786440 | tf_op jit(solution)/shard_map/ppermute | solution.py:15
  23.2 4.9 %all-to-all-done = bf16[16,16,512]{2,1,0:T(8,128)(2,1)S(1)} async-done(((bf16[16,16,512]{2,1,0:T(8,128)(2,1)}), bf16[16,16,512]{2,1,0:T(8,128)(2,1)S(1)}, u32[]{:S(2)}, u32[]{:S(2)}) %all-to-all-start) | async-done | bytes 262176 | tf_op jit(solution)/shard_map/all_to_all | solution.py:20
  28.1 3.7 %collective-permute-start = (bf16[16,16,512]{2,1,0:T(8,128)(2,1)S(1)}, bf16[16,16,512]{2,1,0:T(8,128)(2,1)S(1)}, u32[]{:S(2)}, u32[]{:S(2)}) collective-permute-start(bf16[16,16,512]{2,1,0:T(8,128)(2,1)S(1)} %all-to-all-done), channel_id=1, source_target_pairs={{0,1},{1,0},{2,3},{3,2},{4,5},{5,4},{6,7},{7,6},{8,9},{9,8},{10,11... | collective-permute-start | bytes 786440 | tf_op jit(solution)/shard_map/ppermute | solution.py:15
  35.4 2.8 %shard_map.112 = (bf16[32,3584]{1,0:T(8,128)(2,1)S(1)}, bf16[32,3584]{1,0:T(8,128)(2,1)S(1)}, bf16[32,3584]{1,0:T(8,128)(2,1)S(1)}, bf16[32,3584]{1,0:T(8,128)(2,1)S(1)}) custom-call(s32[4]{0:T(128)S(1)} %pad_add_fusion.spot_ref, bf16[128,512]{1,0:T(8,128)(2,1)S(1)} %shard_map.111.value_ref, bf16[256,7168]{1,0:T(8,128)(2,1)S(1)} %copy-done.2, ...), custom_call_target="tpu_custom_call" | custom-call | flops 469762048 | bytes 3670016 | tf_op jit(solution)/shard_map/pallas_call | solution.py:216
  41.2 1.7 %collective-permute-start.19 = (bf16[288,1792]{1,0:T(8,128)(2,1)S(1)}, bf16[288,1792]{1,0:T(8,128)(2,1)S(1)}, u32[]{:S(2)}, u32[]{:S(2)}) collective-permute-start(bf16[288,1792]{1,0:T(8,128)(2,1)S(1)} %copy-done.6), channel_id=1, source_target_pairs={{32,0},{96,1},{34,2},{98,3},{36,4},{100,5},{38,6},{102,7},{40,8},{... | collective-permute-start | bytes 3096584 | tf_op jit(solution)/shard_map/ppermute | solution.py:53
  42.9 4.3 %collective-permute-done.4 = bf16[32,3584]{1,0:T(8,128)(2,1)S(1)} collective-permute-done((bf16[32,3584]{1,0:T(8,128)(2,1)S(1)}, bf16[32,3584]{1,0:T(8,128)(2,1)S(1)}, u32[]{:S(2)}, u32[]{:S(2)}) %collective-permute-start.4) | collective-permute-done | bytes 229408 | tf_op jit(solution)/shard_map/ppermute | solution.py:35
  50.1 6.7 %collective-permute-done.19.c_ref = bf16[288,1792]{1,0:T(8,128)(2,1)S(1)} collective-permute-done((bf16[288,1792]{1,0:T(8,128)(2,1)S(1)}, bf16[288,1792]{1,0:T(8,128)(2,1)S(1)}, u32[]{:S(2)}, u32[]{:S(2)}) %collective-permute-start.19) | collective-permute-done | bytes 1032224 | tf_op jit(solution)/shard_map/ppermute | solution.py:53
  56.8 6.1 %collective-permute-start.20 = (bf16[288,1792]{1,0:T(8,128)(2,1)S(1)}, bf16[288,1792]{1,0:T(8,128)(2,1)S(1)}, u32[]{:S(2)}, u32[]{:S(2)}) collective-permute-start(bf16[288,1792]{1,0:T(8,128)(2,1)S(1)} %copy-done.6), channel_id=1, source_target_pairs={{33,0},{97,1},{35,2},{99,3},{37,4},{101,5},{39,6},{103,7},{41,8},{... | collective-permute-start | bytes 3096584 | tf_op jit(solution)/shard_map/ppermute | solution.py:53
  65.3 3.1 %collective-permute-done.12.refs_1_ = bf16[32,3584]{1,0:T(8,128)(2,1)S(1)} collective-permute-done((bf16[32,3584]{1,0:T(8,128)(2,1)S(1)}, bf16[32,3584]{1,0:T(8,128)(2,1)S(1)}, u32[]{:S(2)}, u32[]{:S(2)}) %collective-permute-start.12) | collective-permute-done | bytes 229408 | tf_op jit(solution)/shard_map/ppermute | solution.py:35
  68.4 2.3 %collective-permute-done.13.refs_2_ = bf16[32,3584]{1,0:T(8,128)(2,1)S(1)} collective-permute-done((bf16[32,3584]{1,0:T(8,128)(2,1)S(1)}, bf16[32,3584]{1,0:T(8,128)(2,1)S(1)}, u32[]{:S(2)}, u32[]{:S(2)}) %collective-permute-start.13) | collective-permute-done | bytes 229408 | tf_op jit(solution)/shard_map/ppermute | solution.py:35
  70.6 2.4 %collective-permute-done.14.refs_3_ = bf16[32,3584]{1,0:T(8,128)(2,1)S(1)} collective-permute-done((bf16[32,3584]{1,0:T(8,128)(2,1)S(1)}, bf16[32,3584]{1,0:T(8,128)(2,1)S(1)}, u32[]{:S(2)}, u32[]{:S(2)}) %collective-permute-start.14) | collective-permute-done | bytes 229408 | tf_op jit(solution)/shard_map/ppermute | solution.py:35
  74.0 1.9 %shard_map.113 = (f32[128,576]{1,0:T(8,128)S(1)}, f32[128,128]{1,0:T(8,128)S(1)}) custom-call(s32[4]{0:T(128)S(1)} %pad_add_fusion.spot_ref, bf16[32,3584]{1,0:T(8,128)(2,1)S(1)} %add_convert_fusion.1.refs_0_, bf16[32,3584]{1,0:T(8,128)(2,1)S(1)} %collective-permute-done.12.refs_1_, bf16[32,3584]{1,0:T(8,128)(2,1)S(1)} %collective-permute-done.13.refs_2_, ...), custom_call_target="tpu_custom_call" | custom-call | flops 528482304 | bytes 4128768 | tf_op jit(solution)/shard_map/pallas_call | solution.py:276
  76.0 2.3 %shard_map.114.inner_ref = bf16[128,288]{1,0:T(8,128)(2,1)S(1)} custom-call(s32[4]{0:T(128)S(1)} %pad_add_fusion.spot_ref, bf16[32,3584]{1,0:T(8,128)(2,1)S(1)} %collective-permute-done.15.refs_0_, bf16[32,3584]{1,0:T(8,128)(2,1)S(1)} %collective-permute-done.16.refs_1_, bf16[32,3584]{1,0:T(8,128)(2,1)S(1)} %collective-permute-done.17.refs_2_, ...), custom_call_target="tpu_custom_call" | custom-call | flops 528482304 | bytes 4128768 | tf_op jit(solution)/shard_map/pallas_call | solution.py:276
  79.6 1.8 %shard_map.115 = (bf16[32,3584]{1,0:T(8,128)(2,1)S(1)}, bf16[32,3584]{1,0:T(8,128)(2,1)S(1)}, bf16[32,3584]{1,0:T(8,128)(2,1)S(1)}, bf16[32,3584]{1,0:T(8,128)(2,1)S(1)}) custom-call(s32[4]{0:T(128)S(1)} %pad_add_fusion.spot_ref, bf16[128,288]{1,0:T(8,128)(2,1)S(1)} %shard_map.114.inner_ref, bf16[128,288]{1,0:T(8,128)(2,1)S(1)} %collective-permute-done.21.other_ref, ...), custom_call_target="tpu_custom_call" | custom-call | flops 528482304 | bytes 4128768 | tf_op jit(solution)/shard_map/pallas_call | solution.py:315
  81.5 1.8 %collective-permute-start.23 = (bf16[32,3584]{1,0:T(8,128)(2,1)S(1)}, bf16[32,3584]{1,0:T(8,128)(2,1)S(1)}, u32[]{:S(2)}, u32[]{:S(2)}) collective-permute-start(bf16[32,3584]{1,0:T(8,128)(2,1)S(1)} %get-tuple-element.61), channel_id=1, source_target_pairs={{0,16},{1,5},{2,18},{3,7},{4,20},{5,1},{6,22},{7,3},{8,24},{9,13},... | collective-permute-start | bytes 688136 | tf_op jit(solution)/shard_map/ppermute | solution.py:35
  83.3 1.4 %collective-permute-start.24 = (bf16[32,3584]{1,0:T(8,128)(2,1)S(1)}, bf16[32,3584]{1,0:T(8,128)(2,1)S(1)}, u32[]{:S(2)}, u32[]{:S(2)}) collective-permute-start(bf16[32,3584]{1,0:T(8,128)(2,1)S(1)} %get-tuple-element.62), channel_id=1, source_target_pairs={{0,24},{1,7},{2,26},{3,1},{4,28},{5,3},{6,30},{7,5},{8,0},{9,15},{... | collective-permute-start | bytes 688136 | tf_op jit(solution)/shard_map/ppermute | solution.py:35
  84.7 5.6 %collective-permute-done.22 = bf16[32,3584]{1,0:T(8,128)(2,1)S(1)} collective-permute-done((bf16[32,3584]{1,0:T(8,128)(2,1)S(1)}, bf16[32,3584]{1,0:T(8,128)(2,1)S(1)}, u32[]{:S(2)}, u32[]{:S(2)}) %collective-permute-start.22) | collective-permute-done | bytes 229408 | tf_op jit(solution)/shard_map/ppermute | solution.py:35
  91.5 1.7 %collective-permute-start.26 = (bf16[8,3584]{1,0:T(8,128)(2,1)S(1)}, bf16[8,3584]{1,0:T(8,128)(2,1)S(1)}, u32[]{:S(2)}, u32[]{:S(2)}) collective-permute-start(bf16[8,3584]{1,0:T(8,128)(2,1)S(1)} %get-tuple-element.65), channel_id=1, source_target_pairs={{0,4},{1,17},{2,6},{3,19},{4,0},{5,21},{6,2},{7,23},{8,12},{9,25},... | collective-permute-start | bytes 172040 | tf_op jit(solution)/shard_map/ppermute | solution.py:35
  93.2 2.0 %collective-permute-start.27 = (bf16[8,3584]{1,0:T(8,128)(2,1)S(1)}, bf16[8,3584]{1,0:T(8,128)(2,1)S(1)}, u32[]{:S(2)}, u32[]{:S(2)}) collective-permute-start(bf16[8,3584]{1,0:T(8,128)(2,1)S(1)} %get-tuple-element.64), channel_id=1, source_target_pairs={{0,6},{1,25},{2,0},{3,27},{4,2},{5,29},{6,4},{7,31},{8,14},{9,1},{... | collective-permute-start | bytes 172040 | tf_op jit(solution)/shard_map/ppermute | solution.py:35
  97.0 2.5 %collective-permute-start.28 = (bf16[4,3584]{1,0:T(4,128)(2,1)S(1)}, bf16[4,3584]{1,0:T(4,128)(2,1)S(1)}, u32[]{:S(2)}, u32[]{:S(2)}) collective-permute-start(bf16[4,3584]{1,0:T(4,128)(2,1)S(1)} %get-tuple-element.68), channel_id=1, source_target_pairs={{0,1},{1,0},{2,3},{3,2},{4,5},{5,4},{6,7},{7,6},{8,9},{9,8},{10,11... | collective-permute-start | bytes 86024 | tf_op jit(solution)/shard_map/ppermute | solution.py:15
  (73 shorter events, 18.2 us)
Async XLA Ops:
  0.0 34.9 %collective-permute-start.3 = (bf16[256,7168]{1,0:T(8,128)(2,1)}, bf16[256,7168]{1,0:T(8,128)(2,1)}, u32[]{:S(2)}, u32[]{:S(2)}) collective-permute-start(bf16[256,7168]{1,0:T(8,128)(2,1)} %om_ref.1), channel_id=1, source_target_pairs={{0,1},{1,0},{2,3},{3,2},{4,5},{5,4},{6,7},{7,6},{8,9},{9,8},{10,11... | collective-permute-start | bytes 11010056 | tf_op jit(solution)/shard_map/ppermute | solution.py:15
  1.4 32.0 %collective-permute-start.1 = (bf16[288,1792]{1,0:T(8,128)(2,1)}, bf16[288,1792]{1,0:T(8,128)(2,1)S(1)}, u32[]{:S(2)}, u32[]{:S(2)}) collective-permute-start(bf16[288,1792]{1,0:T(8,128)(2,1)} %param.21), channel_id=1, source_target_pairs={{0,0},{64,1},{2,2},{66,3},{4,4},{68,5},{6,6},{70,7},{8,8},{72,9},{... | collective-permute-start | bytes 3096584 | tf_op jit(solution)/shard_map/ppermute | solution.py:53
  4.9 43.0 %collective-permute-start.8 = (bf16[288,1792]{1,0:T(8,128)(2,1)}, bf16[288,1792]{1,0:T(8,128)(2,1)S(1)}, u32[]{:S(2)}, u32[]{:S(2)}) collective-permute-start(bf16[288,1792]{1,0:T(8,128)(2,1)} %param.21), channel_id=1, source_target_pairs={{1,0},{65,1},{3,2},{67,3},{5,4},{69,5},{7,6},{71,7},{9,8},{73,9},{... | collective-permute-start | bytes 3096584 | tf_op jit(solution)/shard_map/ppermute | solution.py:53
  13.8 14.3 %all-to-all-start = ((bf16[16,16,512]{2,1,0:T(8,128)(2,1)}), bf16[16,16,512]{2,1,0:T(8,128)(2,1)S(1)}, u32[]{:S(2)}, u32[]{:S(2)}) async-start(bf16[16,16,512]{2,1,0:T(8,128)(2,1)} %bitcast.28), calls=%async_computation | async-start | bytes 524288 | tf_op jit(solution)/shard_map/all_to_all | solution.py:20
  20.6 11.4 %collective-permute-start.2 = (bf16[2,512,128]{2,1,0:T(8,128)(2,1)S(1)}, bf16[2,512,128]{2,1,0:T(8,128)(2,1)S(1)}, u32[]{:S(2)}, u32[]{:S(2)}) collective-permute-start(bf16[2,512,128]{2,1,0:T(8,128)(2,1)S(1)} %copy-done.4), channel_id=1, source_target_pairs={{0,1},{1,0},{2,3},{3,2},{4,5},{5,4},{6,7},{7,6},{8,9},{9,8},{10,11... | collective-permute-start | bytes 786440 | tf_op jit(solution)/shard_map/ppermute | solution.py:15
  28.1 5.3 %collective-permute-start = (bf16[16,16,512]{2,1,0:T(8,128)(2,1)S(1)}, bf16[16,16,512]{2,1,0:T(8,128)(2,1)S(1)}, u32[]{:S(2)}, u32[]{:S(2)}) collective-permute-start(bf16[16,16,512]{2,1,0:T(8,128)(2,1)S(1)} %all-to-all-done), channel_id=1, source_target_pairs={{0,1},{1,0},{2,3},{3,2},{4,5},{5,4},{6,7},{7,6},{8,9},{9,8},{10,11... | collective-permute-start | bytes 786440 | tf_op jit(solution)/shard_map/ppermute | solution.py:15
  32.0 9.2 %collective-permute-start.7 = (bf16[4,3584]{1,0:T(4,128)(2,1)S(1)}, bf16[4,3584]{1,0:T(4,128)(2,1)S(1)}, u32[]{:S(2)}, u32[]{:S(2)}) collective-permute-start(bf16[4,3584]{1,0:T(4,128)(2,1)S(1)} %get-tuple-element.70), channel_id=1, source_target_pairs={{0,1},{1,0},{2,3},{3,2},{4,5},{5,4},{6,7},{7,6},{8,9},{9,8},{10,11... | collective-permute-start | bytes 86024 | tf_op jit(solution)/shard_map/ppermute | solution.py:15
  38.3 8.9 %collective-permute-start.4 = (bf16[32,3584]{1,0:T(8,128)(2,1)S(1)}, bf16[32,3584]{1,0:T(8,128)(2,1)S(1)}, u32[]{:S(2)}, u32[]{:S(2)}) collective-permute-start(bf16[32,3584]{1,0:T(8,128)(2,1)S(1)} %get-tuple-element.42), channel_id=1, source_target_pairs={{0,8},{1,3},{2,10},{3,5},{4,12},{5,7},{6,14},{7,1},{8,16},{9,11},{... | collective-permute-start | bytes 688136 | tf_op jit(solution)/shard_map/ppermute | solution.py:35
  38.6 8.6 %collective-permute-start.5 = (bf16[32,3584]{1,0:T(8,128)(2,1)S(1)}, bf16[32,3584]{1,0:T(8,128)(2,1)S(1)}, u32[]{:S(2)}, u32[]{:S(2)}) collective-permute-start(bf16[32,3584]{1,0:T(8,128)(2,1)S(1)} %get-tuple-element.43), channel_id=1, source_target_pairs={{0,16},{1,5},{2,18},{3,7},{4,20},{5,1},{6,22},{7,3},{8,24},{9,13},... | collective-permute-start | bytes 688136 | tf_op jit(solution)/shard_map/ppermute | solution.py:35
  40.0 7.8 %collective-permute-start.6 = (bf16[32,3584]{1,0:T(8,128)(2,1)S(1)}, bf16[32,3584]{1,0:T(8,128)(2,1)S(1)}, u32[]{:S(2)}, u32[]{:S(2)}) collective-permute-start(bf16[32,3584]{1,0:T(8,128)(2,1)S(1)} %get-tuple-element.44), channel_id=1, source_target_pairs={{0,24},{1,7},{2,26},{3,1},{4,28},{5,3},{6,30},{7,5},{8,0},{9,15},{... | collective-permute-start | bytes 688136 | tf_op jit(solution)/shard_map/ppermute | solution.py:35
  41.2 15.6 %collective-permute-start.19 = (bf16[288,1792]{1,0:T(8,128)(2,1)S(1)}, bf16[288,1792]{1,0:T(8,128)(2,1)S(1)}, u32[]{:S(2)}, u32[]{:S(2)}) collective-permute-start(bf16[288,1792]{1,0:T(8,128)(2,1)S(1)} %copy-done.6), channel_id=1, source_target_pairs={{32,0},{96,1},{34,2},{98,3},{36,4},{100,5},{38,6},{102,7},{40,8},{... | collective-permute-start | bytes 3096584 | tf_op jit(solution)/shard_map/ppermute | solution.py:53
  48.0 15.0 %collective-permute-start.10 = (bf16[32,3584]{1,0:T(8,128)(2,1)S(1)}, bf16[32,3584]{1,0:T(8,128)(2,1)S(1)}, u32[]{:S(2)}, u32[]{:S(2)}) collective-permute-start(bf16[32,3584]{1,0:T(8,128)(2,1)S(1)} %fusion.1), channel_id=1, source_target_pairs={{0,4},{1,17},{2,6},{3,19},{4,0},{5,21},{6,2},{7,23},{8,12},{9,25},... | collective-permute-start | bytes 688136 | tf_op jit(solution)/shard_map/ppermute | solution.py:35
  48.6 14.3 %collective-permute-start.11 = (bf16[32,3584]{1,0:T(8,128)(2,1)S(1)}, bf16[32,3584]{1,0:T(8,128)(2,1)S(1)}, u32[]{:S(2)}, u32[]{:S(2)}) collective-permute-start(bf16[32,3584]{1,0:T(8,128)(2,1)S(1)} %fusion.1), channel_id=1, source_target_pairs={{0,6},{1,25},{2,0},{3,27},{4,2},{5,29},{6,4},{7,31},{8,14},{9,1},{... | collective-permute-start | bytes 688136 | tf_op jit(solution)/shard_map/ppermute | solution.py:35
  50.0 13.0 %collective-permute-start.9 = (bf16[32,3584]{1,0:T(8,128)(2,1)S(1)}, bf16[32,3584]{1,0:T(8,128)(2,1)S(1)}, u32[]{:S(2)}, u32[]{:S(2)}) collective-permute-start(bf16[32,3584]{1,0:T(8,128)(2,1)S(1)} %fusion.1), channel_id=1, source_target_pairs={{0,2},{1,9},{2,4},{3,11},{4,6},{5,13},{6,0},{7,15},{8,10},{9,17},{... | collective-permute-start | bytes 688136 | tf_op jit(solution)/shard_map/ppermute | solution.py:35
  56.8 21.4 %collective-permute-start.20 = (bf16[288,1792]{1,0:T(8,128)(2,1)S(1)}, bf16[288,1792]{1,0:T(8,128)(2,1)S(1)}, u32[]{:S(2)}, u32[]{:S(2)}) collective-permute-start(bf16[288,1792]{1,0:T(8,128)(2,1)S(1)} %copy-done.6), channel_id=1, source_target_pairs={{33,0},{97,1},{35,2},{99,3},{37,4},{101,5},{39,6},{103,7},{41,8},{... | collective-permute-start | bytes 3096584 | tf_op jit(solution)/shard_map/ppermute | solution.py:53
  63.1 5.2 %collective-permute-start.12 = (bf16[32,3584]{1,0:T(8,128)(2,1)S(1)}, bf16[32,3584]{1,0:T(8,128)(2,1)S(1)}, u32[]{:S(2)}, u32[]{:S(2)}) collective-permute-start(bf16[32,3584]{1,0:T(8,128)(2,1)S(1)} %add_convert_fusion.1.refs_0_), channel_id=1, source_target_pairs={{0,24},{1,7},{2,26},{3,1},{4,28},{5,3},{6,30},{7,5},{8,0},{9,15},{... | collective-permute-start | bytes 688136 | tf_op jit(solution)/shard_map/ppermute | solution.py:35
  64.2 6.5 %collective-permute-start.13 = (bf16[32,3584]{1,0:T(8,128)(2,1)S(1)}, bf16[32,3584]{1,0:T(8,128)(2,1)S(1)}, u32[]{:S(2)}, u32[]{:S(2)}) collective-permute-start(bf16[32,3584]{1,0:T(8,128)(2,1)S(1)} %add_convert_fusion.1.refs_0_), channel_id=1, source_target_pairs={{0,16},{1,5},{2,18},{3,7},{4,20},{5,1},{6,22},{7,3},{8,24},{9,13},... | collective-permute-start | bytes 688136 | tf_op jit(solution)/shard_map/ppermute | solution.py:35
  65.3 7.7 %collective-permute-start.14 = (bf16[32,3584]{1,0:T(8,128)(2,1)S(1)}, bf16[32,3584]{1,0:T(8,128)(2,1)S(1)}, u32[]{:S(2)}, u32[]{:S(2)}) collective-permute-start(bf16[32,3584]{1,0:T(8,128)(2,1)S(1)} %add_convert_fusion.1.refs_0_), channel_id=1, source_target_pairs={{0,8},{1,3},{2,10},{3,5},{4,12},{5,7},{6,14},{7,1},{8,16},{9,11},{... | collective-permute-start | bytes 688136 | tf_op jit(solution)/shard_map/ppermute | solution.py:35
  81.4 8.9 %collective-permute-start.22 = (bf16[32,3584]{1,0:T(8,128)(2,1)S(1)}, bf16[32,3584]{1,0:T(8,128)(2,1)S(1)}, u32[]{:S(2)}, u32[]{:S(2)}) collective-permute-start(bf16[32,3584]{1,0:T(8,128)(2,1)S(1)} %get-tuple-element.60), channel_id=1, source_target_pairs={{0,8},{1,3},{2,10},{3,5},{4,12},{5,7},{6,14},{7,1},{8,16},{9,11},{... | collective-permute-start | bytes 688136 | tf_op jit(solution)/shard_map/ppermute | solution.py:35
  81.5 8.8 %collective-permute-start.23 = (bf16[32,3584]{1,0:T(8,128)(2,1)S(1)}, bf16[32,3584]{1,0:T(8,128)(2,1)S(1)}, u32[]{:S(2)}, u32[]{:S(2)}) collective-permute-start(bf16[32,3584]{1,0:T(8,128)(2,1)S(1)} %get-tuple-element.61), channel_id=1, source_target_pairs={{0,16},{1,5},{2,18},{3,7},{4,20},{5,1},{6,22},{7,3},{8,24},{9,13},... | collective-permute-start | bytes 688136 | tf_op jit(solution)/shard_map/ppermute | solution.py:35
  83.3 7.7 %collective-permute-start.24 = (bf16[32,3584]{1,0:T(8,128)(2,1)S(1)}, bf16[32,3584]{1,0:T(8,128)(2,1)S(1)}, u32[]{:S(2)}, u32[]{:S(2)}) collective-permute-start(bf16[32,3584]{1,0:T(8,128)(2,1)S(1)} %get-tuple-element.62), channel_id=1, source_target_pairs={{0,24},{1,7},{2,26},{3,1},{4,28},{5,3},{6,30},{7,5},{8,0},{9,15},{... | collective-permute-start | bytes 688136 | tf_op jit(solution)/shard_map/ppermute | solution.py:35
  91.1 4.7 %collective-permute-start.25 = (bf16[8,3584]{1,0:T(8,128)(2,1)S(1)}, bf16[8,3584]{1,0:T(8,128)(2,1)S(1)}, u32[]{:S(2)}, u32[]{:S(2)}) collective-permute-start(bf16[8,3584]{1,0:T(8,128)(2,1)S(1)} %get-tuple-element.63), channel_id=1, source_target_pairs={{0,2},{1,9},{2,4},{3,11},{4,6},{5,13},{6,0},{7,15},{8,10},{9,17},{... | collective-permute-start | bytes 172040 | tf_op jit(solution)/shard_map/ppermute | solution.py:35
  91.5 4.5 %collective-permute-start.26 = (bf16[8,3584]{1,0:T(8,128)(2,1)S(1)}, bf16[8,3584]{1,0:T(8,128)(2,1)S(1)}, u32[]{:S(2)}, u32[]{:S(2)}) collective-permute-start(bf16[8,3584]{1,0:T(8,128)(2,1)S(1)} %get-tuple-element.65), channel_id=1, source_target_pairs={{0,4},{1,17},{2,6},{3,19},{4,0},{5,21},{6,2},{7,23},{8,12},{9,25},... | collective-permute-start | bytes 172040 | tf_op jit(solution)/shard_map/ppermute | solution.py:35
  93.2 3.7 %collective-permute-start.27 = (bf16[8,3584]{1,0:T(8,128)(2,1)S(1)}, bf16[8,3584]{1,0:T(8,128)(2,1)S(1)}, u32[]{:S(2)}, u32[]{:S(2)}) collective-permute-start(bf16[8,3584]{1,0:T(8,128)(2,1)S(1)} %get-tuple-element.64), channel_id=1, source_target_pairs={{0,6},{1,25},{2,0},{3,27},{4,2},{5,29},{6,4},{7,31},{8,14},{9,1},{... | collective-permute-start | bytes 172040 | tf_op jit(solution)/shard_map/ppermute | solution.py:35
  (13 other events, 176.1 us)

commit v17 on v15

--- a/solution.py
+++ b/solution.py
@@ -187,7 +187,7 @@
     depth, model = output_mine.shape
     half = model // 2
     line = rows // side
-    cuts = 2
+    cuts = 4
     span = half // cuts
 
     def kernel(spot_ref, value_ref, om_ref, oo_ref, *refs):

time: 98.6 us -> 99.2 us (level)
  transfers between devices with their start and end apart: 30 -> 30, of which waited for: 14 -> 14; matrix products, arithmetic and copies ran while one was open for 1% -> 1% of each run, Pallas kernels for 17% -> 18%
where the time goes in v17:
time: 99.2 us; the launch traced here: 98.9 us
  starting transfers between devices  43.2 us (44%)
  waiting for transfers between devices  33.7 us (34%)
  Pallas kernels  19.4 us (20%)
  other arithmetic  1.31 us (1%)
  between operations  1 us (1%)
    ppermute x15, waiting for transfers between devices, turn(): out[k] = lax.ppermute(parts[k], 'tp', pairs)  17.1 us
    ppermute x15, starting transfers between devices, turn(): out[k] = lax.ppermute(parts[k], 'tp', pairs)  14.5 us
    ppermute x4, starting transfers between devices, down_piece(): return lax.ppermute(down_weight, ('dp', 'tp'), pairs)  13.3 us
    pallas_call x1, Pallas kernels, attend(): pl.pallas_call(kernel, in_specs=[in_smem, in_vmem, in_hbm], out_specs=in_...  8.62 us
    ppermute x10, starting transfers between devices, core_swap(): return lax.ppermute(x, 'tp', [(i, i ^ 1) for i in range(width)])  8.56 us
    ppermute x4, waiting for transfers between devices, down_piece(): return lax.ppermute(down_weight, ('dp', 'tp'), pairs)  8.05 us
    all_to_all x1, starting transfers between devices, between_chips(): return lax.all_to_all(x, 'tp', 0, 0, tiled=True, axis_index_groups=groups)  6.76 us
    all_to_all x1, waiting for transfers between devices, between_chips(): return lax.all_to_all(x, 'tp', 0, 0, tiled=True, axis_index_groups=groups)  5.23 us
  transfers between devices with their start and end apart: 30, of which 14 were waited for; matrix products, arithmetic and copies ran while one was open for 1% of the time, Pallas kernels for 18%

profile of v17, /device:TPU:1, one launch (start us, length us, event | category | flops | bytes accessed | tf_op | source)
XLA Modules:
  0.0 98.9 jit_solution(16733953876818864602)
XLA Ops:
  0.0 1.4 %collective-permute-start.3 = (bf16[256,7168]{1,0:T(8,128)(2,1)}, bf16[256,7168]{1,0:T(8,128)(2,1)}, u32[]{:S(2)}, u32[]{:S(2)}) collective-permute-start(bf16[256,7168]{1,0:T(8,128)(2,1)} %om_ref.1), channel_id=1, source_target_pairs={{0,1},{1,0},{2,3},{3,2},{4,5},{5,4},{6,7},{7,6},{8,9},{9,8},{10,11... | collective-permute-start | bytes 11010056 | tf_op jit(solution)/shard_map/ppermute | solution.py:15
  1.4 3.5 %collective-permute-start.1 = (bf16[288,1792]{1,0:T(8,128)(2,1)}, bf16[288,1792]{1,0:T(8,128)(2,1)S(1)}, u32[]{:S(2)}, u32[]{:S(2)}) collective-permute-start(bf16[288,1792]{1,0:T(8,128)(2,1)} %param.21), channel_id=1, source_target_pairs={{0,0},{64,1},{2,2},{66,3},{4,4},{68,5},{6,6},{70,7},{8,8},{72,9},{... | collective-permute-start | bytes 3096584 | tf_op jit(solution)/shard_map/ppermute | solution.py:53
  5.1 8.6 %shard_map.109 = bf16[256,512]{1,0:T(8,128)(2,1)} custom-call(s32[4]{0:T(128)} %lengths_ref.1, bf16[4,64,576]{2,1,0:T(8,128)(2,1)} %q_ref, bf16[4,576,2048]{2,1,0:T(8,128)(2,1)} %bitcast.27), custom_call_target="tpu_custom_call" | custom-call | flops 1140850688 | bytes 9437184 | tf_op jit(solution)/shard_map/pallas_call | solution.py:122
  13.7 6.8 %all-to-all-start = ((bf16[16,16,512]{2,1,0:T(8,128)(2,1)}), bf16[16,16,512]{2,1,0:T(8,128)(2,1)S(1)}, u32[]{:S(2)}, u32[]{:S(2)}) async-start(bf16[16,16,512]{2,1,0:T(8,128)(2,1)} %bitcast.28), calls=%async_computation | async-start | bytes 524288 | tf_op jit(solution)/shard_map/all_to_all | solution.py:20
  20.6 2.6 %collective-permute-start.2 = (bf16[2,512,128]{2,1,0:T(8,128)(2,1)S(1)}, bf16[2,512,128]{2,1,0:T(8,128)(2,1)S(1)}, u32[]{:S(2)}, u32[]{:S(2)}) collective-permute-start(bf16[2,512,128]{2,1,0:T(8,128)(2,1)S(1)} %copy-done.4), channel_id=1, source_target_pairs={{0,1},{1,0},{2,3},{3,2},{4,5},{5,4},{6,7},{7,6},{8,9},{9,8},{10,11... | collective-permute-start | bytes 786440 | tf_op jit(solution)/shard_map/ppermute | solution.py:15
  23.3 5.2 %all-to-all-done = bf16[16,16,512]{2,1,0:T(8,128)(2,1)S(1)} async-done(((bf16[16,16,512]{2,1,0:T(8,128)(2,1)}), bf16[16,16,512]{2,1,0:T(8,128)(2,1)S(1)}, u32[]{:S(2)}, u32[]{:S(2)}) %all-to-all-start) | async-done | bytes 262176 | tf_op jit(solution)/shard_map/all_to_all | solution.py:20
  28.6 1.5 %collective-permute-done = bf16[16,16,512]{2,1,0:T(8,128)(2,1)S(1)} collective-permute-done((bf16[16,16,512]{2,1,0:T(8,128)(2,1)S(1)}, bf16[16,16,512]{2,1,0:T(8,128)(2,1)S(1)}, u32[]{:S(2)}, u32[]{:S(2)}) %collective-permute-start) | collective-permute-done | bytes 262176 | tf_op jit(solution)/shard_map/ppermute | solution.py:15
  30.2 1.6 %shard_map.110.value_ref = bf16[128,512]{1,0:T(8,128)(2,1)S(1)} custom-call(s32[4]{0:T(128)S(1)} %pad_add_fusion.spot_ref, bf16[256,512]{1,0:T(8,128)(2,1)S(1)} %bitcast.23, bf16[256,512]{1,0:T(8,128)(2,1)S(1)} %bitcast.26, bf16[2,512,128]{2,1,0:T(8,128)(2,1)S(1)} %copy-done.4, bf16[2,512,128]{2,1,0:T(8,128)(2,1)S(1)} %collective-permute-done.2.vo_ref), custom_call_target="tpu_custom_call" | custom-call | flops 1610612736 | bytes 524288 | tf_op jit(solution)/shard_map/pallas_call | solution.py:167
  31.9 3.2 %shard_map.111 = (bf16[32,3584]{1,0:T(8,128)(2,1)S(1)}, bf16[32,3584]{1,0:T(8,128)(2,1)S(1)}, bf16[32,3584]{1,0:T(8,128)(2,1)S(1)}, bf16[32,3584]{1,0:T(8,128)(2,1)S(1)}) custom-call(s32[4]{0:T(128)S(1)} %pad_add_fusion.spot_ref, bf16[128,512]{1,0:T(8,128)(2,1)S(1)} %shard_map.110.value_ref, bf16[256,7168]{1,0:T(8,128)(2,1)S(1)} %copy-done.2, ...), custom_call_target="tpu_custom_call" | custom-call | flops 469762048 | bytes 3670016 | tf_op jit(solution)/shard_map/pallas_call | solution.py:214
  38.1 4.5 %collective-permute-start.19 = (bf16[288,1792]{1,0:T(8,128)(2,1)S(1)}, bf16[288,1792]{1,0:T(8,128)(2,1)S(1)}, u32[]{:S(2)}, u32[]{:S(2)}) collective-permute-start(bf16[288,1792]{1,0:T(8,128)(2,1)S(1)} %copy-done.6), channel_id=1, source_target_pairs={{32,0},{96,1},{34,2},{98,3},{36,4},{100,5},{38,6},{102,7},{40,8},{... | collective-permute-start | bytes 3096584 | tf_op jit(solution)/shard_map/ppermute | solution.py:53
  42.5 1.5 %collective-permute-done.4 = bf16[32,3584]{1,0:T(8,128)(2,1)S(1)} collective-permute-done((bf16[32,3584]{1,0:T(8,128)(2,1)S(1)}, bf16[32,3584]{1,0:T(8,128)(2,1)S(1)}, u32[]{:S(2)}, u32[]{:S(2)}) %collective-permute-start.4) | collective-permute-done | bytes 229408 | tf_op jit(solution)/shard_map/ppermute | solution.py:35
  45.5 1.6 %collective-permute-start.11 = (bf16[32,3584]{1,0:T(8,128)(2,1)S(1)}, bf16[32,3584]{1,0:T(8,128)(2,1)S(1)}, u32[]{:S(2)}, u32[]{:S(2)}) collective-permute-start(bf16[32,3584]{1,0:T(8,128)(2,1)S(1)} %fusion.1), channel_id=1, source_target_pairs={{0,6},{1,25},{2,0},{3,27},{4,2},{5,29},{6,4},{7,31},{8,14},{9,1},{... | collective-permute-start | bytes 688136 | tf_op jit(solution)/shard_map/ppermute | solution.py:35
  47.1 8.0 %collective-permute-done.19.c_ref = bf16[288,1792]{1,0:T(8,128)(2,1)S(1)} collective-permute-done((bf16[288,1792]{1,0:T(8,128)(2,1)S(1)}, bf16[288,1792]{1,0:T(8,128)(2,1)S(1)}, u32[]{:S(2)}, u32[]{:S(2)}) %collective-permute-start.19) | collective-permute-done | bytes 1032224 | tf_op jit(solution)/shard_map/ppermute | solution.py:53
  55.1 5.3 %collective-permute-start.20 = (bf16[288,1792]{1,0:T(8,128)(2,1)S(1)}, bf16[288,1792]{1,0:T(8,128)(2,1)S(1)}, u32[]{:S(2)}, u32[]{:S(2)}) collective-permute-start(bf16[288,1792]{1,0:T(8,128)(2,1)S(1)} %copy-done.6), channel_id=1, source_target_pairs={{33,0},{97,1},{35,2},{99,3},{37,4},{101,5},{39,6},{103,7},{41,8},{... | collective-permute-start | bytes 3096584 | tf_op jit(solution)/shard_map/ppermute | solution.py:53
  62.7 3.1 %collective-permute-done.12.refs_1_ = bf16[32,3584]{1,0:T(8,128)(2,1)S(1)} collective-permute-done((bf16[32,3584]{1,0:T(8,128)(2,1)S(1)}, bf16[32,3584]{1,0:T(8,128)(2,1)S(1)}, u32[]{:S(2)}, u32[]{:S(2)}) %collective-permute-start.12) | collective-permute-done | bytes 229408 | tf_op jit(solution)/shard_map/ppermute | solution.py:35
  65.8 2.3 %collective-permute-done.13.refs_2_ = bf16[32,3584]{1,0:T(8,128)(2,1)S(1)} collective-permute-done((bf16[32,3584]{1,0:T(8,128)(2,1)S(1)}, bf16[32,3584]{1,0:T(8,128)(2,1)S(1)}, u32[]{:S(2)}, u32[]{:S(2)}) %collective-permute-start.13) | collective-permute-done | bytes 229408 | tf_op jit(solution)/shard_map/ppermute | solution.py:35
  68.1 2.5 %collective-permute-done.14.refs_3_ = bf16[32,3584]{1,0:T(8,128)(2,1)S(1)} collective-permute-done((bf16[32,3584]{1,0:T(8,128)(2,1)S(1)}, bf16[32,3584]{1,0:T(8,128)(2,1)S(1)}, u32[]{:S(2)}, u32[]{:S(2)}) %collective-permute-start.14) | collective-permute-done | bytes 229408 | tf_op jit(solution)/shard_map/ppermute | solution.py:35
  71.6 1.9 %shard_map.112 = (f32[128,576]{1,0:T(8,128)S(1)}, f32[128,128]{1,0:T(8,128)S(1)}) custom-call(s32[4]{0:T(128)S(1)} %pad_add_fusion.spot_ref, bf16[32,3584]{1,0:T(8,128)(2,1)S(1)} %add_convert_fusion.1.refs_0_, bf16[32,3584]{1,0:T(8,128)(2,1)S(1)} %collective-permute-done.12.refs_1_, bf16[32,3584]{1,0:T(8,128)(2,1)S(1)} %collective-permute-done.13.refs_2_, ...), custom_call_target="tpu_custom_call" | custom-call | flops 528482304 | bytes 4128768 | tf_op jit(solution)/shard_map/pallas_call | solution.py:274
  73.6 2.3 %shard_map.113.inner_ref = bf16[128,288]{1,0:T(8,128)(2,1)S(1)} custom-call(s32[4]{0:T(128)S(1)} %pad_add_fusion.spot_ref, bf16[32,3584]{1,0:T(8,128)(2,1)S(1)} %collective-permute-done.15.refs_0_, bf16[32,3584]{1,0:T(8,128)(2,1)S(1)} %collective-permute-done.16.refs_1_, bf16[32,3584]{1,0:T(8,128)(2,1)S(1)} %collective-permute-done.17.refs_2_, ...), custom_call_target="tpu_custom_call" | custom-call | flops 528482304 | bytes 4128768 | tf_op jit(solution)/shard_map/pallas_call | solution.py:274
  77.3 1.8 %shard_map.114 = (bf16[32,3584]{1,0:T(8,128)(2,1)S(1)}, bf16[32,3584]{1,0:T(8,128)(2,1)S(1)}, bf16[32,3584]{1,0:T(8,128)(2,1)S(1)}, bf16[32,3584]{1,0:T(8,128)(2,1)S(1)}) custom-call(s32[4]{0:T(128)S(1)} %pad_add_fusion.spot_ref, bf16[128,288]{1,0:T(8,128)(2,1)S(1)} %shard_map.113.inner_ref, bf16[128,288]{1,0:T(8,128)(2,1)S(1)} %collective-permute-done.21.other_ref, ...), custom_call_target="tpu_custom_call" | custom-call | flops 528482304 | bytes 4128768 | tf_op jit(solution)/shard_map/pallas_call | solution.py:313
  79.3 1.8 %collective-permute-start.23 = (bf16[32,3584]{1,0:T(8,128)(2,1)S(1)}, bf16[32,3584]{1,0:T(8,128)(2,1)S(1)}, u32[]{:S(2)}, u32[]{:S(2)}) collective-permute-start(bf16[32,3584]{1,0:T(8,128)(2,1)S(1)} %get-tuple-element.61), channel_id=1, source_target_pairs={{0,16},{1,5},{2,18},{3,7},{4,20},{5,1},{6,22},{7,3},{8,24},{9,13},... | collective-permute-start | bytes 688136 | tf_op jit(solution)/shard_map/ppermute | solution.py:35
  82.5 5.5 %collective-permute-done.22 = bf16[32,3584]{1,0:T(8,128)(2,1)S(1)} collective-permute-done((bf16[32,3584]{1,0:T(8,128)(2,1)S(1)}, bf16[32,3584]{1,0:T(8,128)(2,1)S(1)}, u32[]{:S(2)}, u32[]{:S(2)}) %collective-permute-start.22) | collective-permute-done | bytes 229408 | tf_op jit(solution)/shard_map/ppermute | solution.py:35
  90.6 2.0 %collective-permute-start.27 = (bf16[8,3584]{1,0:T(8,128)(2,1)S(1)}, bf16[8,3584]{1,0:T(8,128)(2,1)S(1)}, u32[]{:S(2)}, u32[]{:S(2)}) collective-permute-start(bf16[8,3584]{1,0:T(8,128)(2,1)S(1)} %get-tuple-element.64), channel_id=1, source_target_pairs={{0,6},{1,25},{2,0},{3,27},{4,2},{5,29},{6,4},{7,31},{8,14},{9,1},{... | collective-permute-start | bytes 172040 | tf_op jit(solution)/shard_map/ppermute | solution.py:35
  94.4 3.0 %collective-permute-start.28 = (bf16[4,3584]{1,0:T(4,128)(2,1)S(1)}, bf16[4,3584]{1,0:T(4,128)(2,1)S(1)}, u32[]{:S(2)}, u32[]{:S(2)}) collective-permute-start(bf16[4,3584]{1,0:T(4,128)(2,1)S(1)} %get-tuple-element.68), channel_id=1, source_target_pairs={{0,1},{1,0},{2,3},{3,2},{4,5},{5,4},{6,7},{7,6},{8,9},{9,8},{10,11... | collective-permute-start | bytes 86024 | tf_op jit(solution)/shard_map/ppermute | solution.py:15
  (72 shorter events, 16.5 us)
Async XLA Ops:
  0.0 31.9 %collective-permute-start.3 = (bf16[256,7168]{1,0:T(8,128)(2,1)}, bf16[256,7168]{1,0:T(8,128)(2,1)}, u32[]{:S(2)}, u32[]{:S(2)}) collective-permute-start(bf16[256,7168]{1,0:T(8,128)(2,1)} %om_ref.1), channel_id=1, source_target_pairs={{0,1},{1,0},{2,3},{3,2},{4,5},{5,4},{6,7},{7,6},{8,9},{9,8},{10,11... | collective-permute-start | bytes 11010056 | tf_op jit(solution)/shard_map/ppermute | solution.py:15
  1.4 28.8 %collective-permute-start.1 = (bf16[288,1792]{1,0:T(8,128)(2,1)}, bf16[288,1792]{1,0:T(8,128)(2,1)S(1)}, u32[]{:S(2)}, u32[]{:S(2)}) collective-permute-start(bf16[288,1792]{1,0:T(8,128)(2,1)} %param.21), channel_id=1, source_target_pairs={{0,0},{64,1},{2,2},{66,3},{4,4},{68,5},{6,6},{70,7},{8,8},{72,9},{... | collective-permute-start | bytes 3096584 | tf_op jit(solution)/shard_map/ppermute | solution.py:53
  13.7 14.8 %all-to-all-start = ((bf16[16,16,512]{2,1,0:T(8,128)(2,1)}), bf16[16,16,512]{2,1,0:T(8,128)(2,1)S(1)}, u32[]{:S(2)}, u32[]{:S(2)}) async-start(bf16[16,16,512]{2,1,0:T(8,128)(2,1)} %bitcast.28), calls=%async_computation | async-start | bytes 524288 | tf_op jit(solution)/shard_map/all_to_all | solution.py:20
  20.5 24.4 %collective-permute-start.8 = (bf16[288,1792]{1,0:T(8,128)(2,1)}, bf16[288,1792]{1,0:T(8,128)(2,1)S(1)}, u32[]{:S(2)}, u32[]{:S(2)}) collective-permute-start(bf16[288,1792]{1,0:T(8,128)(2,1)} %param.21), channel_id=1, source_target_pairs={{1,0},{65,1},{3,2},{67,3},{5,4},{69,5},{7,6},{71,7},{9,8},{73,9},{... | collective-permute-start | bytes 3096584 | tf_op jit(solution)/shard_map/ppermute | solution.py:53
  20.6 9.6 %collective-permute-start.2 = (bf16[2,512,128]{2,1,0:T(8,128)(2,1)S(1)}, bf16[2,512,128]{2,1,0:T(8,128)(2,1)S(1)}, u32[]{:S(2)}, u32[]{:S(2)}) collective-permute-start(bf16[2,512,128]{2,1,0:T(8,128)(2,1)S(1)} %copy-done.4), channel_id=1, source_target_pairs={{0,1},{1,0},{2,3},{3,2},{4,5},{5,4},{6,7},{7,6},{8,9},{9,8},{10,11... | collective-permute-start | bytes 786440 | tf_op jit(solution)/shard_map/ppermute | solution.py:15
  30.1 7.9 %collective-permute-start.7 = (bf16[4,3584]{1,0:T(4,128)(2,1)S(1)}, bf16[4,3584]{1,0:T(4,128)(2,1)S(1)}, u32[]{:S(2)}, u32[]{:S(2)}) collective-permute-start(bf16[4,3584]{1,0:T(4,128)(2,1)S(1)} %get-tuple-element.70), channel_id=1, source_target_pairs={{0,1},{1,0},{2,3},{3,2},{4,5},{5,4},{6,7},{7,6},{8,9},{9,8},{10,11... | collective-permute-start | bytes 86024 | tf_op jit(solution)/shard_map/ppermute | solution.py:15
  35.1 8.9 %collective-permute-start.4 = (bf16[32,3584]{1,0:T(8,128)(2,1)S(1)}, bf16[32,3584]{1,0:T(8,128)(2,1)S(1)}, u32[]{:S(2)}, u32[]{:S(2)}) collective-permute-start(bf16[32,3584]{1,0:T(8,128)(2,1)S(1)} %get-tuple-element.42), channel_id=1, source_target_pairs={{0,8},{1,3},{2,10},{3,5},{4,12},{5,7},{6,14},{7,1},{8,16},{9,11},{... | collective-permute-start | bytes 688136 | tf_op jit(solution)/shard_map/ppermute | solution.py:35
  35.5 8.6 %collective-permute-start.5 = (bf16[32,3584]{1,0:T(8,128)(2,1)S(1)}, bf16[32,3584]{1,0:T(8,128)(2,1)S(1)}, u32[]{:S(2)}, u32[]{:S(2)}) collective-permute-start(bf16[32,3584]{1,0:T(8,128)(2,1)S(1)} %get-tuple-element.43), channel_id=1, source_target_pairs={{0,16},{1,5},{2,18},{3,7},{4,20},{5,1},{6,22},{7,3},{8,24},{9,13},... | collective-permute-start | bytes 688136 | tf_op jit(solution)/shard_map/ppermute | solution.py:35
  36.9 7.8 %collective-permute-start.6 = (bf16[32,3584]{1,0:T(8,128)(2,1)S(1)}, bf16[32,3584]{1,0:T(8,128)(2,1)S(1)}, u32[]{:S(2)}, u32[]{:S(2)}) collective-permute-start(bf16[32,3584]{1,0:T(8,128)(2,1)S(1)} %get-tuple-element.44), channel_id=1, source_target_pairs={{0,24},{1,7},{2,26},{3,1},{4,28},{5,3},{6,30},{7,5},{8,0},{9,15},{... | collective-permute-start | bytes 688136 | tf_op jit(solution)/shard_map/ppermute | solution.py:35
  38.1 17.1 %collective-permute-start.19 = (bf16[288,1792]{1,0:T(8,128)(2,1)S(1)}, bf16[288,1792]{1,0:T(8,128)(2,1)S(1)}, u32[]{:S(2)}, u32[]{:S(2)}) collective-permute-start(bf16[288,1792]{1,0:T(8,128)(2,1)S(1)} %copy-done.6), channel_id=1, source_target_pairs={{32,0},{96,1},{34,2},{98,3},{36,4},{100,5},{38,6},{102,7},{40,8},{... | collective-permute-start | bytes 3096584 | tf_op jit(solution)/shard_map/ppermute | solution.py:53
  44.8 15.6 %collective-permute-start.10 = (bf16[32,3584]{1,0:T(8,128)(2,1)S(1)}, bf16[32,3584]{1,0:T(8,128)(2,1)S(1)}, u32[]{:S(2)}, u32[]{:S(2)}) collective-permute-start(bf16[32,3584]{1,0:T(8,128)(2,1)S(1)} %fusion.1), channel_id=1, source_target_pairs={{0,4},{1,17},{2,6},{3,19},{4,0},{5,21},{6,2},{7,23},{8,12},{9,25},... | collective-permute-start | bytes 688136 | tf_op jit(solution)/shard_map/ppermute | solution.py:35
  45.5 14.9 %collective-permute-start.11 = (bf16[32,3584]{1,0:T(8,128)(2,1)S(1)}, bf16[32,3584]{1,0:T(8,128)(2,1)S(1)}, u32[]{:S(2)}, u32[]{:S(2)}) collective-permute-start(bf16[32,3584]{1,0:T(8,128)(2,1)S(1)} %fusion.1), channel_id=1, source_target_pairs={{0,6},{1,25},{2,0},{3,27},{4,2},{5,29},{6,4},{7,31},{8,14},{9,1},{... | collective-permute-start | bytes 688136 | tf_op jit(solution)/shard_map/ppermute | solution.py:35
  47.1 13.4 %collective-permute-start.9 = (bf16[32,3584]{1,0:T(8,128)(2,1)S(1)}, bf16[32,3584]{1,0:T(8,128)(2,1)S(1)}, u32[]{:S(2)}, u32[]{:S(2)}) collective-permute-start(bf16[32,3584]{1,0:T(8,128)(2,1)S(1)} %fusion.1), channel_id=1, source_target_pairs={{0,2},{1,9},{2,4},{3,11},{4,6},{5,13},{6,0},{7,15},{8,10},{9,17},{... | collective-permute-start | bytes 688136 | tf_op jit(solution)/shard_map/ppermute | solution.py:35
  55.1 20.7 %collective-permute-start.20 = (bf16[288,1792]{1,0:T(8,128)(2,1)S(1)}, bf16[288,1792]{1,0:T(8,128)(2,1)S(1)}, u32[]{:S(2)}, u32[]{:S(2)}) collective-permute-start(bf16[288,1792]{1,0:T(8,128)(2,1)S(1)} %copy-done.6), channel_id=1, source_target_pairs={{33,0},{97,1},{35,2},{99,3},{37,4},{101,5},{39,6},{103,7},{41,8},{... | collective-permute-start | bytes 3096584 | tf_op jit(solution)/shard_map/ppermute | solution.py:53
  60.6 5.2 %collective-permute-start.12 = (bf16[32,3584]{1,0:T(8,128)(2,1)S(1)}, bf16[32,3584]{1,0:T(8,128)(2,1)S(1)}, u32[]{:S(2)}, u32[]{:S(2)}) collective-permute-start(bf16[32,3584]{1,0:T(8,128)(2,1)S(1)} %add_convert_fusion.1.refs_0_), channel_id=1, source_target_pairs={{0,24},{1,7},{2,26},{3,1},{4,28},{5,3},{6,30},{7,5},{8,0},{9,15},{... | collective-permute-start | bytes 688136 | tf_op jit(solution)/shard_map/ppermute | solution.py:35
  61.5 6.6 %collective-permute-start.13 = (bf16[32,3584]{1,0:T(8,128)(2,1)S(1)}, bf16[32,3584]{1,0:T(8,128)(2,1)S(1)}, u32[]{:S(2)}, u32[]{:S(2)}) collective-permute-start(bf16[32,3584]{1,0:T(8,128)(2,1)S(1)} %add_convert_fusion.1.refs_0_), channel_id=1, source_target_pairs={{0,16},{1,5},{2,18},{3,7},{4,20},{5,1},{6,22},{7,3},{8,24},{9,13},... | collective-permute-start | bytes 688136 | tf_op jit(solution)/shard_map/ppermute | solution.py:35
  62.7 7.9 %collective-permute-start.14 = (bf16[32,3584]{1,0:T(8,128)(2,1)S(1)}, bf16[32,3584]{1,0:T(8,128)(2,1)S(1)}, u32[]{:S(2)}, u32[]{:S(2)}) collective-permute-start(bf16[32,3584]{1,0:T(8,128)(2,1)S(1)} %add_convert_fusion.1.refs_0_), channel_id=1, source_target_pairs={{0,8},{1,3},{2,10},{3,5},{4,12},{5,7},{6,14},{7,1},{8,16},{9,11},{... | collective-permute-start | bytes 688136 | tf_op jit(solution)/shard_map/ppermute | solution.py:35
  79.0 8.9 %collective-permute-start.22 = (bf16[32,3584]{1,0:T(8,128)(2,1)S(1)}, bf16[32,3584]{1,0:T(8,128)(2,1)S(1)}, u32[]{:S(2)}, u32[]{:S(2)}) collective-permute-start(bf16[32,3584]{1,0:T(8,128)(2,1)S(1)} %get-tuple-element.60), channel_id=1, source_target_pairs={{0,8},{1,3},{2,10},{3,5},{4,12},{5,7},{6,14},{7,1},{8,16},{9,11},{... | collective-permute-start | bytes 688136 | tf_op jit(solution)/shard_map/ppermute | solution.py:35
  79.3 8.6 %collective-permute-start.23 = (bf16[32,3584]{1,0:T(8,128)(2,1)S(1)}, bf16[32,3584]{1,0:T(8,128)(2,1)S(1)}, u32[]{:S(2)}, u32[]{:S(2)}) collective-permute-start(bf16[32,3584]{1,0:T(8,128)(2,1)S(1)} %get-tuple-element.61), channel_id=1, source_target_pairs={{0,16},{1,5},{2,18},{3,7},{4,20},{5,1},{6,22},{7,3},{8,24},{9,13},... | collective-permute-start | bytes 688136 | tf_op jit(solution)/shard_map/ppermute | solution.py:35
  81.1 7.5 %collective-permute-start.24 = (bf16[32,3584]{1,0:T(8,128)(2,1)S(1)}, bf16[32,3584]{1,0:T(8,128)(2,1)S(1)}, u32[]{:S(2)}, u32[]{:S(2)}) collective-permute-start(bf16[32,3584]{1,0:T(8,128)(2,1)S(1)} %get-tuple-element.62), channel_id=1, source_target_pairs={{0,24},{1,7},{2,26},{3,1},{4,28},{5,3},{6,30},{7,5},{8,0},{9,15},{... | collective-permute-start | bytes 688136 | tf_op jit(solution)/shard_map/ppermute | solution.py:35
  88.7 4.5 %collective-permute-start.25 = (bf16[8,3584]{1,0:T(8,128)(2,1)S(1)}, bf16[8,3584]{1,0:T(8,128)(2,1)S(1)}, u32[]{:S(2)}, u32[]{:S(2)}) collective-permute-start(bf16[8,3584]{1,0:T(8,128)(2,1)S(1)} %get-tuple-element.63), channel_id=1, source_target_pairs={{0,2},{1,9},{2,4},{3,11},{4,6},{5,13},{6,0},{7,15},{8,10},{9,17},{... | collective-permute-start | bytes 172040 | tf_op jit(solution)/shard_map/ppermute | solution.py:35
  89.2 4.5 %collective-permute-start.26 = (bf16[8,3584]{1,0:T(8,128)(2,1)S(1)}, bf16[8,3584]{1,0:T(8,128)(2,1)S(1)}, u32[]{:S(2)}, u32[]{:S(2)}) collective-permute-start(bf16[8,3584]{1,0:T(8,128)(2,1)S(1)} %get-tuple-element.65), channel_id=1, source_target_pairs={{0,4},{1,17},{2,6},{3,19},{4,0},{5,21},{6,2},{7,23},{8,12},{9,25},... | collective-permute-start | bytes 172040 | tf_op jit(solution)/shard_map/ppermute | solution.py:35
  90.6 3.6 %collective-permute-start.27 = (bf16[8,3584]{1,0:T(8,128)(2,1)S(1)}, bf16[8,3584]{1,0:T(8,128)(2,1)S(1)}, u32[]{:S(2)}, u32[]{:S(2)}) collective-permute-start(bf16[8,3584]{1,0:T(8,128)(2,1)S(1)} %get-tuple-element.64), channel_id=1, source_target_pairs={{0,6},{1,25},{2,0},{3,27},{4,2},{5,29},{6,4},{7,31},{8,14},{9,1},{... | collective-permute-start | bytes 172040 | tf_op jit(solution)/shard_map/ppermute | solution.py:35
  94.4 3.8 %collective-permute-start.28 = (bf16[4,3584]{1,0:T(4,128)(2,1)S(1)}, bf16[4,3584]{1,0:T(4,128)(2,1)S(1)}, u32[]{:S(2)}, u32[]{:S(2)}) collective-permute-start(bf16[4,3584]{1,0:T(4,128)(2,1)S(1)} %get-tuple-element.68), channel_id=1, source_target_pairs={{0,1},{1,0},{2,3},{3,2},{4,5},{5,4},{6,7},{7,6},{8,9},{9,8},{10,11... | collective-permute-start | bytes 86024 | tf_op jit(solution)/shard_map/ppermute | solution.py:15
  (13 other events, 182.4 us)
